TPU v7x, 128 devices: a whole 4x4x4 slice. The times are simulated.
128 devices in a mesh: sec: 16 (over x_lo, y, core), tile: 8 (over z, x_hi).
Axes of the slice: x: 4 (x_hi: 2, x_lo: 2; x = x_hi * 2 + x_lo), y: 4, z: 4, core: 2. Of those that a mesh axis runs over, the one named last changes fastest.
Arguments:
- sections: float32 [16, 8, 128, 128, 128], P('sec', None, 'tile'), may hold values from -6 to 6
- node_mask: int32 [16, 8, 128], P('sec', None, 'tile'), may hold values 0 or 1
- box_row: int32 [16, 8, 128, 4], P('sec', None, 'tile'), may hold values from 0 to 7, as said below
- box_shift: int32 [16, 8, 128, 4], P('sec', None, 'tile'), may hold values from -2 to 2
- box_count: int32 [16, 8, 128], P('sec', None, 'tile'), may hold values from 1 to 4, as said below
- blend_weight: float32 [16, 8, 128, 4], P('sec', None, 'tile'), may hold values from 0.25 to 4
Outputs:
- rendered: bfloat16 [16, 8, 128, 128, 128], P('sec', None, 'tile')
- node_field: float32 [16, 2, 8, 128], P('sec', None, None, 'tile')
Inputs may be any that keep to these rules, and one draw needn't show every extreme that they name: Within a cell's 4 slots the pairs (box_row, box_shift) are all different. `box_count`: in every section a band of columns around a drawn centre (wrapping around, a quarter of the width to each side) has 3 or 4 live boxes per cell, all other cells 1 or 2.
All inputs are finite; a program needn't handle non-finite values. No bound on the sum of `node_mask` on one device may be relied on, other than what follows from the above.
Results may differ from a plain program's by a relative error of at most 0.0054.
Values may be sent and summed in bfloat16 or wider, within the bound.
No kernel may reach another device: no remote copies, remote signals or barrier semaphores. Data moves between devices by JAX's collectives and lax.ppermute only.
A program may use at most 192 MiB of HBM per device.

v0:
```python
import functools

import jax
import jax.numpy as jnp
import numpy as np
from jax import lax
from jax.experimental import pallas as pl
from jax.experimental.pallas import tpu as pltpu
from jax.sharding import PartitionSpec as P

K = 4
HB = 2
STEPS = 3
N = 128
HALF = N // 2
PAD = 72
SPRING = 0.2
EPS = 1e-06
MIB = 1024 * 1024


def split(x):
    high = x.astype(jnp.bfloat16)
    return high, (x - high.astype(jnp.float32)).astype(jnp.bfloat16)


def tables():
    grid = np.arange(N)[:, None] * np.arange(N)[None, :] % N
    cosine = np.cos(2.0 * np.pi * grid / N)
    sine = np.sin(2.0 * np.pi * grid / N)
    rows = np.concatenate([cosine[:HALF], sine[:HALF]])
    rows[HALF] = cosine[HALF]
    cols = np.block([[cosine, -sine], [-sine, -cosine]])
    back_cols = np.block([[cosine, sine], [-sine, cosine]]) / N
    weight = np.where(np.arange(HALF) == 0, 1.0, 2.0)
    back_rows = np.concatenate([cosine[:, :HALF] * weight, -2.0 * sine[:, :HALF]], axis=1) / N
    back_rows[:, HALF] = cosine[:, HALF] / N
    return [jnp.asarray(t, jnp.float32) for t in (rows, cols, back_cols, back_rows)]


def first_row(shape):
    return lax.broadcasted_iota(jnp.int32, shape, len(shape) - 2) == 0


def dot(a, b):
    return jnp.dot(a, b, preferred_element_type=jnp.float32)


def forward_kernel(x_ref, rows_ref, cols_ref, spec_ref, src_ref):
    patches = x_ref.shape[2]
    rows2 = rows_ref[...]
    cols = cols_ref[...]
    for pair in range(patches // 2):
        x = jnp.concatenate([x_ref[0, 0, 2 * pair], x_ref[0, 0, 2 * pair + 1]], axis=1)
        high, low = split(x)
        src_ref[0, 2 * pair] = high[:, :N]
        src_ref[0, 2 * pair + 1] = high[:, N:]
        y = dot(rows2, jnp.concatenate([high, low], axis=0))
        left = jnp.concatenate([y[:HALF, :N], y[HALF:, :N]], axis=1)
        right = jnp.concatenate([y[:HALF, N:], y[HALF:, N:]], axis=1)
        lines = jnp.concatenate([left, right], axis=0)
        lines_high, lines_low = split(lines)
        freq = dot(lines_high, cols) + dot(lines_low, cols)
        freq = freq.reshape(2, HALF, 2 * N)
        keep = lines.reshape(2, HALF, 2 * N)
        out = jnp.where(first_row(freq.shape), keep, freq)
        spec_ref[0, 2 * pair] = out[0].astype(jnp.bfloat16)
        spec_ref[0, 2 * pair + 1] = out[1].astype(jnp.bfloat16)


def forward(sections, rows, cols):
    _, ny, nx, _, _ = sections.shape
    rows2 = jnp.concatenate([rows, rows], axis=1).astype(jnp.bfloat16)
    whole = lambda shape: pl.BlockSpec(shape, lambda y: (0,) * len(shape))
    return pl.pallas_call(
        forward_kernel,
        grid=(ny,),
        in_specs=[
            pl.BlockSpec((1, 1, nx, N, N), lambda y: (0, y, 0, 0, 0)),
            whole((N, 2 * N)),
            whole((2 * N, 2 * N)),
        ],
        out_specs=[
            pl.BlockSpec((1, nx, HALF, 2 * N), lambda y: (y, 0, 0, 0)),
            pl.BlockSpec((1, nx, N, N), lambda y: (y, 0, 0, 0)),
        ],
        out_shape=[
            jax.ShapeDtypeStruct((ny, nx, HALF, 2 * N), jnp.bfloat16),
            jax.ShapeDtypeStruct((ny, nx, N, N), jnp.bfloat16),
        ],
        compiler_params=pltpu.CompilerParams(vmem_limit_bytes=32 * MIB),
        cost_estimate=pl.CostEstimate(flops=4_000_000_000, bytes_accessed=16 * MIB, transcendentals=0),
        name="forward",
    )(sections, rows2, cols.astype(jnp.bfloat16))


def times_conj(a, b, sign):
    ar, ai, br, bi = a[:, :N], a[:, N:], b[:, :N], b[:, N:]
    real = ar * br + ai * bi
    imag = ai * br - ar * bi if sign > 0 else ar * bi - ai * br
    return jnp.concatenate([real, imag], axis=1).astype(jnp.bfloat16)


def flow_kernel(sign, own_ref, other_ref, cols_ref, back_cols_ref, back_rows_ref, flow_ref, sums, moments):
    y = pl.program_id(0)
    patches = own_ref.shape[1]
    cols = cols_ref[...]
    back_cols = back_cols_ref[...]
    back_rows = back_rows_ref[...]
    own = own_ref[0]
    other = other_ref[0]
    lines = jnp.concatenate(
        [r[:, 0, :].astype(jnp.float32) for r in (own, other)], axis=0
    ).astype(jnp.bfloat16)
    edge = jnp.concatenate([lines[:, :N], lines[:, N:]], axis=0)
    edge = dot(edge, cols[:N])
    quarter = edge.reshape(4, patches, 2 * N)
    low = times_conj(quarter[0], quarter[1], sign)
    high = times_conj(quarter[2], quarter[3], sign)
    sides = dot(jnp.concatenate([low, high], axis=0), back_cols[:, :N])
    shift_rows = lax.broadcasted_iota(jnp.int32, (N, N), 0)
    offset_rows = (((shift_rows + HALF) % N) - HALF).astype(jnp.float32)
    offset_rows = jnp.concatenate([offset_rows, offset_rows], axis=1)
    for pair in range(patches // 2):
        a = own_ref[0, 2 * pair : 2 * pair + 2].reshape(2 * HALF, 2 * N).astype(jnp.float32)
        b = other_ref[0, 2 * pair : 2 * pair + 2].reshape(2 * HALF, 2 * N).astype(jnp.float32)
        back = dot(times_conj(a, b, sign), back_cols)
        halves = []
        for side in range(2):
            p = 2 * pair + side
            real = back[side * HALF : (side + 1) * HALF, :N]
            imag = back[side * HALF : (side + 1) * HALF, N:]
            real = jnp.where(first_row(real.shape), sides[p : p + 1], real)
            imag = jnp.where(first_row(imag.shape), sides[patches + p : patches + p + 1], imag)
            halves.append(jnp.concatenate([real, imag], axis=0).astype(jnp.bfloat16))
        corr = dot(back_rows, jnp.concatenate(halves, axis=1))
        power = corr * corr
        total = power.sum(0, keepdims=True)
        moment = (power * offset_rows).sum(0, keepdims=True)
        for side in range(2):
            p = 2 * pair + side
            sums[p : p + 1, :] = total[:, side * N : (side + 1) * N]
            moments[p : p + 1, :] = moment[:, side * N : (side + 1) * N]
    lane = lax.broadcasted_iota(jnp.int32, (8, N), 1)
    row = lax.broadcasted_iota(jnp.int32, (8, N), 0)
    offset_cols = (((lane + HALF) % N) - HALF).astype(jnp.float32)
    reduce_by = jnp.where(row == 0, 1.0, jnp.where(row == 1, offset_cols, 0.0))
    over_lanes = lambda m: lax.dot_general(
        reduce_by, m, (((1,), (1,)), ((), ())),
        precision=lax.Precision.HIGHEST, preferred_element_type=jnp.float32,
    )
    by_sums = over_lanes(sums[...])
    by_moments = over_lanes(moments[...])
    total = by_sums[0:1] + EPS
    flow_ref[0, pl.ds(y, 1), :] = by_moments[0:1] / total
    flow_ref[1, pl.ds(y, 1), :] = by_sums[1:2] / total


def flow_of(own, first, other, sign, cols, back_cols, back_rows):
    ny, nx = other.shape[:2]
    whole = lambda shape: pl.BlockSpec(shape, lambda y: (0,) * len(shape))
    block = (1, nx, HALF, 2 * N)
    return pl.pallas_call(
        functools.partial(flow_kernel, sign),
        grid=(ny,),
        in_specs=[
            pl.BlockSpec(block, lambda y: (y + first, 0, 0, 0)),
            pl.BlockSpec(block, lambda y: (y, 0, 0, 0)),
            whole((2 * N, 2 * N)),
            whole((2 * N, 2 * N)),
            whole((N, N)),
        ],
        out_specs=whole((2, ny, nx)),
        out_shape=jax.ShapeDtypeStruct((2, ny, nx), jnp.float32),
        scratch_shapes=[pltpu.VMEM((nx, N), jnp.float32), pltpu.VMEM((nx, N), jnp.float32)],
        compiler_params=pltpu.CompilerParams(vmem_limit_bytes=32 * MIB),
        cost_estimate=pl.CostEstimate(flops=2_000_000_000, bytes_accessed=8 * MIB, transcendentals=0),
        name="flow",
    )(own, other, *(t.astype(jnp.bfloat16) for t in (cols, back_cols, back_rows)))


def blend_kernel(target_ref, share_ref, src_ref, low_ref, high_ref, out_ref, window, sems):
    y = pl.program_id(0)
    nx = src_ref.shape[1]

    @pl.when(y == 0)
    def _():
        copies = [
            pltpu.make_async_copy(src_ref, window.at[:, HB : HB + nx], sems.at[0]),
            pltpu.make_async_copy(low_ref, window.at[:, :HB], sems.at[1]),
            pltpu.make_async_copy(high_ref, window.at[:, HB + nx :], sems.at[2]),
        ]
        for copy in copies:
            copy.start()
        for copy in copies:
            copy.wait()

    def cell(x, carry):
        base = (y * nx + x) * K
        total = None
        for k in range(K):
            spot = target_ref[base + k]
            piece = window[spot // (nx + 2 * HB), spot % (nx + 2 * HB)].astype(jnp.float32) * share_ref[base + k]
            total = piece if total is None else total + piece
        out_ref[0, x] = total
        return carry

    lax.fori_loop(0, nx, cell, 0, unroll=2)


def blend(target, share, source, low, high):
    ny, nx = source.shape[:2]
    return pl.pallas_call(
        blend_kernel,
        grid=(ny,),
        in_specs=[
            pl.BlockSpec(memory_space=pltpu.SMEM),
            pl.BlockSpec(memory_space=pltpu.SMEM),
            pl.BlockSpec(memory_space=pl.ANY),
            pl.BlockSpec(memory_space=pl.ANY),
            pl.BlockSpec(memory_space=pl.ANY),
        ],
        out_specs=pl.BlockSpec((1, nx, N, N), lambda y: (y, 0, 0, 0)),
        out_shape=jax.ShapeDtypeStruct((ny, nx, N, N), jnp.float32),
        scratch_shapes=[
            pltpu.VMEM((ny, nx + 2 * HB, N, N), jnp.bfloat16),
            pltpu.SemaphoreType.DMA((3,)),
        ],
        compiler_params=pltpu.CompilerParams(vmem_limit_bytes=32 * MIB),
        cost_estimate=pl.CostEstimate(flops=20_000_000, bytes_accessed=13 * MIB, transcendentals=0),
        name="blend",
    )(target, share, source, low, high)


def relax_kernel(flow_ref, trust_ref, valid_ref, out_ref):
    ny = flow_ref.shape[1]
    trust = trust_ref[...]
    valid = valid_ref[...]
    row = lax.broadcasted_iota(jnp.int32, trust.shape, 0)
    for component in range(2):
        flow = flow_ref[component]
        field = trust * flow
        for _ in range(STEPS):
            below = jnp.where(row == 0, 0.0, pltpu.roll(field, 1, 0))
            above = jnp.where(row == ny - 1, 0.0, pltpu.roll(field, ny - 1, 0))
            beside = pltpu.roll(field, 1, 1) + pltpu.roll(field, field.shape[1] - 1, 1)
            lap = above + below + beside - 4.0 * field
            field = (field + SPRING * (lap + trust * (flow - field))) * valid
        out_ref[component] = field


def relax(flow, trust, valid):
    return pl.pallas_call(
        relax_kernel,
        out_shape=jax.ShapeDtypeStruct(flow.shape, jnp.float32),
        name="relax",
    )(flow, trust, valid)


def warp_kernel(field_ref, blended_ref, out_ref, padded, sems):
    y = pl.program_id(0)
    ny = pl.num_programs(0)
    nx = out_ref.shape[2]
    slot = y % 2

    def fetch(row, into):
        return pltpu.make_async_copy(
            blended_ref.at[row], padded.at[into, :, PAD : PAD + N], sems.at[into]
        )

    @pl.when(y == 0)
    def _():
        padded[:, :, :PAD] = jnp.zeros((2, nx, PAD, N), jnp.float32)
        padded[:, :, PAD + N :] = jnp.zeros((2, nx, PAD, N), jnp.float32)
        fetch(0, 0).start()

    @pl.when(y + 1 < ny)
    def _():
        fetch(y + 1, 1 - slot).start()

    fetch(y, slot).wait()
    lane = lax.broadcasted_iota(jnp.int32, (1, N), 1)

    def whole_and_part(shift):
        whole = jnp.clip((shift + 256.0).astype(jnp.int32) - 256, 4 - PAD, PAD - 6)
        return whole, shift - whole.astype(jnp.float32)

    def cell(x, carry):
        down, part = whole_and_part(field_ref[0, y, x])
        upper = padded[slot, x, pl.ds(PAD + down, N), :]
        lower = padded[slot, x, pl.ds(PAD + 1 + down, N), :]
        image = upper + part * (lower - upper)
        right, part = whole_and_part(field_ref[1, y, x])
        spot = lane + right
        near = jnp.where((spot >= 0) & (spot < N), 1.0 - part, 0.0)
        far = jnp.where((spot >= -1) & (spot < N - 1), part, 0.0)
        turn = (2 * N - right) % N
        turned = pltpu.roll(image, turn, 1)
        out = turned * near + pltpu.roll(turned, N - 1, 1) * far
        out_ref[0, 0, x] = out.astype(jnp.bfloat16)
        return carry

    lax.fori_loop(0, nx, cell, 0, unroll=2)


def warp(field, blended):
    ny, nx = blended.shape[:2]
    return pl.pallas_call(
        warp_kernel,
        grid=(ny,),
        in_specs=[
            pl.BlockSpec(memory_space=pltpu.SMEM),
            pl.BlockSpec(memory_space=pl.ANY),
        ],
        out_specs=pl.BlockSpec((1, 1, nx, N, N), lambda y: (0, y, 0, 0, 0)),
        out_shape=jax.ShapeDtypeStruct((1, ny, nx, N, N), jnp.bfloat16),
        scratch_shapes=[
            pltpu.VMEM((2, nx, 2 * PAD + N, N), jnp.float32),
            pltpu.SemaphoreType.DMA((2,)),
        ],
        compiler_params=pltpu.CompilerParams(vmem_limit_bytes=32 * MIB),
        cost_estimate=pl.CostEstimate(flops=20_000_000, bytes_accessed=12 * MIB, transcendentals=0),
        name="warp",
    )(field, blended)


def from_behind(x, axis, by):
    length = lax.axis_size(axis)
    pairs = [(i, i + by) for i in range(length) if 0 <= i + by < length]
    return lax.ppermute(x, axis, pairs)


def bordered(x, width):
    low = from_behind(x[..., x.shape[-1] - width :], "tile", 1)
    high = from_behind(x[..., :width], "tile", -1)
    return jnp.concatenate([low, x, high], axis=-1)


def to_lanes(x):
    return jnp.pad(x, ((0, 0),) * (x.ndim - 1) + ((0, N - x.shape[-1]),))


def per_device(sections, node_mask, box_row, box_shift, box_count, blend_weight):
    ny, nx = sections.shape[1:3]
    rows, cols, back_cols, back_rows = tables()
    half = ny // 2
    spectra, source = forward(sections, rows, cols)
    from_next = from_behind(spectra[:half], "sec", -1)
    from_last = from_behind(spectra[half:], "sec", 1)
    low = from_behind(source[:, nx - HB :], "tile", 1)
    high = from_behind(source[:, :HB], "tile", -1)
    trust = node_mask[0].astype(jnp.float32)
    known = to_lanes(bordered(jnp.stack([trust, jnp.ones_like(trust)]), STEPS))

    live = jnp.arange(K)[None, None, :] < box_count[0][..., None]
    weights = jnp.where(live, blend_weight[0], 0.0)
    share = (weights / weights.sum(-1, keepdims=True)).astype(jnp.bfloat16).astype(jnp.float32)
    local_col = jnp.arange(nx)[None, :, None]
    target = box_row[0] * (nx + 2 * HB) + local_col + HB + box_shift[0]
    blended = blend(target.reshape(-1), share.reshape(-1), source, low, high)

    flow_high = flow_of(spectra, half, from_last, -1, cols, back_cols, back_rows)
    flow_high = from_behind(flow_high, "sec", -1)
    flow_low = flow_of(spectra, 0, from_next, 1, cols, back_cols, back_rows)
    flow = to_lanes(bordered(jnp.concatenate([flow_low, flow_high], axis=1), STEPS))
    field = relax(flow, known[0], known[1])[:, :, STEPS : STEPS + nx]
    rendered = warp(field, blended)
    return (rendered, field[None])


def solution(mesh):
    return jax.shard_map(
        per_device,
        mesh=mesh,
        in_specs=(
            P("sec", None, "tile", None, None),
            P("sec", None, "tile"),
            P("sec", None, "tile", None),
            P("sec", None, "tile", None),
            P("sec", None, "tile"),
            P("sec", None, "tile", None),
        ),
        out_specs=(P("sec", None, "tile", None, None), P("sec", None, None, "tile")),
        check_vma=False,
    )
```

profile of v0, /device:TPU:66, one launch (start us, length us, event | category | flops | bytes accessed | tf_op | source)
XLA Modules:
  0.0 120.3 jit_solution(16169590800654496812)
XLA Ops:
  0.6 3.4 %copy-done.6 = f32[1,8,16,128,128]{4,3,2,1,0:T(8,128)S(1)} copy-done((f32[1,8,16,128,128]{4,3,2,1,0:T(8,128)S(1)}, f32[1,8,16,128,128]{4,3,2,1,0:T(8,128)}, u32[]{:S(2)}) %copy-start.6) | copy-done | bytes 8388632
  4.0 0.9 copy-done.7
  4.9 0.8 copy-done.10
  5.8 8.8 %forward.1 = (bf16[8,16,64,256]{3,2,1,0:T(8,128)(2,1)S(1)}, bf16[8,16,128,128]{3,2,1,0:T(8,128)(2,1)S(1)}) custom-call(f32[1,8,16,128,128]{4,3,2,1,0:T(8,128)S(1)} %copy-done.6, bf16[128,256]{1,0:T(8,128)(2,1)S(1)} %copy-done.10, bf16[256,256]{1,0:T(8,128)(2,1)S(1)} %copy-done.7), custom_call_target="tpu_custom_call" | custom-call | flops 4000000000 | bytes 16777216 | tf_op jit(solution)/shard_map/forward/pallas_call | solution.py:75
  14.7 2.6 %fusion.7 = (bf16[4,16,64,256]{3,2,1,0:T(8,128)(2,1)}, bf16[4,16,64,256]{3,2,1,0:T(8,128)(2,1)}) fusion(bf16[8,16,64,256]{3,2,1,0:T(8,128)(2,1)S(1)} %get-tuple-element.4.own_ref), kind=kLoop, calls=%fused_computation.24 | loop fusion | bytes 8388608 | tf_op jit(solution)/shard_map/slice | solution.py:348
  17.9 1.9 %collective-permute-start.1 = (bf16[4,16,64,256]{3,2,1,0:T(8,128)(2,1)}, bf16[4,16,64,256]{3,2,1,0:T(8,128)(2,1)}, u32[]{:S(2)}, u32[]{:S(2)}) collective-permute-start(bf16[4,16,64,256]{3,2,1,0:T(8,128)(2,1)} %get-tuple-element.9), channel_id=1, source_target_pairs={{0,8},{8,16},{16,24},{24,32},{32,40},{40,48},{48,56},{56,64},{64,7... | collective-permute-start | bytes 6291464 | tf_op jit(solution)/shard_map/ppermute | solution.py:330
  19.8 5.8 %collective-permute-start = (bf16[4,16,64,256]{3,2,1,0:T(8,128)(2,1)}, bf16[4,16,64,256]{3,2,1,0:T(8,128)(2,1)S(1)}, u32[]{:S(2)}, u32[]{:S(2)}) collective-permute-start(bf16[4,16,64,256]{3,2,1,0:T(8,128)(2,1)} %get-tuple-element.8), channel_id=1, source_target_pairs={{8,0},{16,8},{24,16},{32,24},{40,32},{48,40},{56,48},{64,56},{72,6... | collective-permute-start | bytes 6291464 | tf_op jit(solution)/shard_map/ppermute | solution.py:330
  25.6 0.7 pad_slice_fusion.1
  26.2 4.0 %collective-permute-start.5 = (f32[2,8,3]{2,1,0:T(8,128)}, f32[2,8,3]{2,1,0:T(8,128)}, u32[]{:S(2)}, u32[]{:S(2)}) collective-permute-start(f32[2,8,3]{2,1,0:T(8,128)} %get-tuple-element.16), channel_id=1, source_target_pairs={{0,1},{1,2},{2,3},{3,4},{4,5},{5,6},{6,7},{8,9},{9,10},{10,11},{11... | collective-permute-start | bytes 584 | tf_op jit(solution)/shard_map/ppermute | solution.py:330
  30.3 4.2 %collective-permute-start.6 = (f32[2,8,3]{2,1,0:T(8,128)}, f32[2,8,3]{2,1,0:T(8,128)}, u32[]{:S(2)}, u32[]{:S(2)}) collective-permute-start(f32[2,8,3]{2,1,0:T(8,128)} %get-tuple-element.17), channel_id=1, source_target_pairs={{1,0},{2,1},{3,2},{4,3},{5,4},{6,5},{7,6},{9,8},{10,9},{11,10},{12... | collective-permute-start | bytes 584 | tf_op jit(solution)/shard_map/ppermute | solution.py:330
  34.5 0.9 fusion.6
  35.4 3.1 %collective-permute-start.7 = (bf16[8,2,128,128]{3,2,1,0:T(8,128)(2,1)}, bf16[8,2,128,128]{3,2,1,0:T(8,128)(2,1)S(1)}, u32[]{:S(2)}, u32[]{:S(2)}) collective-permute-start(bf16[8,2,128,128]{3,2,1,0:T(8,128)(2,1)} %get-tuple-element.7), channel_id=1, source_target_pairs={{0,1},{1,2},{2,3},{3,4},{4,5},{5,6},{6,7},{8,9},{9,10},{10,11},{11... | collective-permute-start | bytes 1572872 | tf_op jit(solution)/shard_map/ppermute | solution.py:330
  38.7 0.7 div.11
  39.4 0.9 div.12
  40.5 0.6 lt.23
  41.3 0.7 broadcast_multiply_fusion
  43.2 19.8 %collective-permute-done.5 = f32[2,8,3]{2,1,0:T(8,128)} collective-permute-done((f32[2,8,3]{2,1,0:T(8,128)}, f32[2,8,3]{2,1,0:T(8,128)}, u32[]{:S(2)}, u32[]{:S(2)}) %collective-permute-start.5) | collective-permute-done | bytes 224 | tf_op jit(solution)/shard_map/ppermute | solution.py:330
  63.0 3.3 %collective-permute-start.8 = (bf16[8,2,128,128]{3,2,1,0:T(8,128)(2,1)S(1)}, bf16[8,2,128,128]{3,2,1,0:T(8,128)(2,1)S(1)}, u32[]{:S(2)}, u32[]{:S(2)}) collective-permute-start(bf16[8,2,128,128]{3,2,1,0:T(8,128)(2,1)S(1)} %get-tuple-element.6), channel_id=1, source_target_pairs={{1,0},{2,1},{3,2},{4,3},{5,4},{6,5},{7,6},{9,8},{10,9},{11,10},{12... | collective-permute-start | bytes 1572872 | tf_op jit(solution)/shard_map/ppermute | solution.py:330
  66.3 0.8 select_maximum_fusion
  67.8 2.2 %copy-done.5 = bf16[8,16,64,256]{3,2,1,0:T(8,128)(2,1)S(1)} copy-done((bf16[8,16,64,256]{3,2,1,0:T(8,128)(2,1)S(1)}, bf16[8,16,64,256]{3,2,1,0:T(8,128)(2,1)}, u32[]{:S(2)}) %copy-start.5) | copy-done | bytes 4194328
  70.0 5.0 %flow.3 = f32[2,4,16]{2,1,0:T(4,128)S(1)} custom-call(bf16[8,16,64,256]{3,2,1,0:T(8,128)(2,1)S(1)} %copy-done.5, bf16[4,16,64,256]{3,2,1,0:T(8,128)(2,1)} %collective-permute-done.1.other_ref, bf16[256,256]{1,0:T(8,128)(2,1)S(1)} %copy-done.8, bf16[256,256]{1,0:T(8,128)(2,1)S(1)} %copy-done.9, bf16[128,128]{1,0:T(8,128)(2,1)S(1)} %copy-done.11), custom_call_target="tpu_custom_call" | custom-call | flops 2000000000 | bytes 8388608 | tf_op jit(solution)/shard_map/flow/pallas_call | solution.py:163
  75.0 2.2 %collective-permute-start.2 = (f32[2,4,16]{2,1,0:T(4,128)S(1)}, f32[2,4,16]{2,1,0:T(4,128)S(1)}, u32[]{:S(2)}, u32[]{:S(2)}) collective-permute-start(f32[2,4,16]{2,1,0:T(4,128)S(1)} %flow.3), channel_id=1, source_target_pairs={{8,0},{16,8},{24,16},{32,24},{40,32},{48,40},{56,48},{64,56},{72,6... | collective-permute-start | bytes 1544 | tf_op jit(solution)/shard_map/ppermute | solution.py:330
  77.2 4.0 %flow.2 = f32[2,4,16]{2,1,0:T(4,128)S(1)} custom-call(bf16[8,16,64,256]{3,2,1,0:T(8,128)(2,1)S(1)} %copy-done.5, bf16[4,16,64,256]{3,2,1,0:T(8,128)(2,1)S(1)} %collective-permute-done.other_ref, bf16[256,256]{1,0:T(8,128)(2,1)S(1)} %copy-done.8, bf16[256,256]{1,0:T(8,128)(2,1)S(1)} %copy-done.9, bf16[128,128]{1,0:T(8,128)(2,1)S(1)} %copy-done.11), custom_call_target="tpu_custom_call" | custom-call | flops 2000000000 | bytes 8388608 | tf_op jit(solution)/shard_map/flow/pallas_call | solution.py:163
  81.3 4.0 %collective-permute-start.3 = (f32[2,8,3]{2,1,0:T(8,128)S(1)}, f32[2,8,3]{2,1,0:T(8,128)S(1)}, u32[]{:S(2)}, u32[]{:S(2)}) collective-permute-start(f32[2,8,3]{2,1,0:T(8,128)S(1)} %get-tuple-element.14), channel_id=1, source_target_pairs={{0,1},{1,2},{2,3},{3,4},{4,5},{5,6},{6,7},{8,9},{9,10},{10,11},{11... | collective-permute-start | bytes 584 | tf_op jit(solution)/shard_map/ppermute | solution.py:330
  85.3 4.2 %collective-permute-start.4 = (f32[2,8,3]{2,1,0:T(8,128)S(1)}, f32[2,8,3]{2,1,0:T(8,128)S(1)}, u32[]{:S(2)}, u32[]{:S(2)}) collective-permute-start(f32[2,8,3]{2,1,0:T(8,128)S(1)} %get-tuple-element.15), channel_id=1, source_target_pairs={{1,0},{2,1},{3,2},{4,3},{5,4},{6,5},{7,6},{9,8},{10,9},{11,10},{12... | collective-permute-start | bytes 584 | tf_op jit(solution)/shard_map/ppermute | solution.py:330
  89.6 6.2 %blend.1.blended_ref = f32[8,16,128,128]{3,2,1,0:T(8,128)S(1)} custom-call(s32[512]{0:T(512)S(1)} %add_add_fusion.target_ref, f32[512]{0:T(512)S(1)} %fusion.5.share_ref, bf16[8,16,128,128]{3,2,1,0:T(8,128)(2,1)S(1)} %copy-done.3, bf16[8,2,128,128]{3,2,1,0:T(8,128)(2,1)S(1)} %collective-permute-done.7.low_ref, ...), custom_call_target="tpu_custom_call" | custom-call | flops 20000000 | bytes 13631488 | tf_op jit(solution)/shard_map/blend/pallas_call | solution.py:213
  95.8 3.3 %copy-done = f32[8,16,128,128]{3,2,1,0:T(8,128)} copy-done((f32[8,16,128,128]{3,2,1,0:T(8,128)}, f32[8,16,128,128]{3,2,1,0:T(8,128)S(1)}, u32[]{:S(2)}) %copy-start) | copy-done | bytes 8388632
  99.0 0.7 select_maximum_fusion.2.flow_ref
  99.7 1.5 %relax.1 = f32[2,8,128]{2,1,0:T(8,128)} custom-call(f32[2,8,128]{2,1,0:T(8,128)} %select_maximum_fusion.2.flow_ref, f32[8,128]{1,0:T(8,128)} %get-tuple-element.13.trust_ref, f32[8,128]{1,0:T(8,128)} %get-tuple-element.12.valid_ref), custom_call_target="tpu_custom_call" | custom-call | tf_op jit(solution)/shard_map/relax/pallas_call | solution.py:253
  101.3 1.4 %slice_bitcast_fusion.2 = (f32[1,2,8,16]{3,2,1,0:T(8,128)}, f32[2,8,16]{2,1,0:T(8,128)S(1)}) fusion(f32[2,8,128]{2,1,0:T(8,128)} %relax.1), kind=kLoop, calls=%fused_computation.22 | loop fusion | bytes 3072 | tf_op jit(solution)/shard_map/broadcast_in_dim | solution.py:368
  102.6 3.4 %copy-done.1 = f32[8,16,128,128]{3,2,1,0:T(8,128)S(1)} copy-done((f32[8,16,128,128]{3,2,1,0:T(8,128)S(1)}, f32[8,16,128,128]{3,2,1,0:T(8,128)}, u32[]{:S(2)}) %copy-start.1) | copy-done | bytes 8388632
  106.0 14.3 %warp.1 = bf16[1,8,16,128,128]{4,3,2,1,0:T(8,128)(2,1)} custom-call(f32[2,8,16]{2,1,0:T(8,128)S(1)} %get-tuple-element.11.field_ref, f32[8,16,128,128]{3,2,1,0:T(8,128)S(1)} %copy-done.1), custom_call_target="tpu_custom_call" | custom-call | flops 20000000 | bytes 12582912 | tf_op jit(solution)/shard_map/warp/pallas_call | solution.py:308
  (51 shorter events, 2.9 us)
Async XLA Ops:
  0.6 3.4 %copy-start.6 = (f32[1,8,16,128,128]{4,3,2,1,0:T(8,128)S(1)}, f32[1,8,16,128,128]{4,3,2,1,0:T(8,128)}, u32[]{:S(2)}) copy-start(f32[1,8,16,128,128]{4,3,2,1,0:T(8,128)} %x_ref.1) | copy-start | bytes 25165828
  4.0 0.9 copy-start.7
  4.9 0.8 copy-start.10
  14.6 3.3 %copy-start.4 = (bf16[8,16,64,256]{3,2,1,0:T(8,128)(2,1)}, bf16[8,16,64,256]{3,2,1,0:T(8,128)(2,1)S(1)}, u32[]{:S(2)}) copy-start(bf16[8,16,64,256]{3,2,1,0:T(8,128)(2,1)S(1)} %get-tuple-element.4.own_ref) | copy-start | bytes 12582916
  14.6 19.9 %copy-start.2 = (bf16[8,16,128,128]{3,2,1,0:T(8,128)(2,1)}, bf16[8,16,128,128]{3,2,1,0:T(8,128)(2,1)S(1)}, u32[]{:S(2)}) copy-start(bf16[8,16,128,128]{3,2,1,0:T(8,128)(2,1)S(1)} %get-tuple-element.5.src_ref) | copy-start | bytes 12582916
  14.6 10.9 %copy-start.15 = (s32[1,8,16]{2,1,0:T(8,128)S(1)}, s32[1,8,16]{2,1,0:T(8,128)}, u32[]{:S(2)}) copy-start(s32[1,8,16]{2,1,0:T(8,128)} %param.11) | copy-start | bytes 1540
  14.6 23.9 %copy-start.12 = (f32[1,8,16,4]{2,3,1,0:T(4,128)S(1)}, f32[1,8,16,4]{2,3,1,0:T(4,128)}, u32[]{:S(2)}) copy-start(f32[1,8,16,4]{2,3,1,0:T(4,128)} %param.15) | copy-start | bytes 6148
  14.6 24.1 %copy-start.14 = (s32[1,8,16]{2,1,0:T(8,128)S(1)}, s32[1,8,16]{2,1,0:T(8,128)}, u32[]{:S(2)}) copy-start(s32[1,8,16]{2,1,0:T(8,128)} %param.14) | copy-start | bytes 1540
  14.7 27.7 %copy-start.13 = (s32[1,8,16,4]{2,3,1,0:T(4,128)S(1)}, s32[1,8,16,4]{2,3,1,0:T(4,128)}, u32[]{:S(2)}) copy-start(s32[1,8,16,4]{2,3,1,0:T(4,128)} %param.13) | copy-start | bytes 6148
  14.7 53.1 %copy-start.8 = (bf16[256,256]{1,0:T(8,128)(2,1)S(1)}, bf16[256,256]{1,0:T(8,128)(2,1)}, u32[]{:S(2)}) copy-start(bf16[256,256]{1,0:T(8,128)(2,1)} %constant.36.cols_ref) | copy-start | bytes 393220
  14.7 53.1 %copy-start.9 = (bf16[256,256]{1,0:T(8,128)(2,1)S(1)}, bf16[256,256]{1,0:T(8,128)(2,1)}, u32[]{:S(2)}) copy-start(bf16[256,256]{1,0:T(8,128)(2,1)} %constant.37.back_cols_ref) | copy-start | bytes 393220
  14.7 53.1 %copy-start.11 = (bf16[128,128]{1,0:T(8,128)(2,1)S(1)}, bf16[128,128]{1,0:T(8,128)(2,1)}, u32[]{:S(2)}) copy-start(bf16[128,128]{1,0:T(8,128)(2,1)} %constant.38.back_rows_ref) | copy-start | bytes 98308
  17.9 49.9 %collective-permute-start.1 = (bf16[4,16,64,256]{3,2,1,0:T(8,128)(2,1)}, bf16[4,16,64,256]{3,2,1,0:T(8,128)(2,1)}, u32[]{:S(2)}, u32[]{:S(2)}) collective-permute-start(bf16[4,16,64,256]{3,2,1,0:T(8,128)(2,1)} %get-tuple-element.9), channel_id=1, source_target_pairs={{0,8},{8,16},{16,24},{24,32},{32,40},{40,48},{48,56},{56,64},{64,7... | collective-permute-start | bytes 6291464 | tf_op jit(solution)/shard_map/ppermute | solution.py:330
  19.8 57.4 %collective-permute-start = (bf16[4,16,64,256]{3,2,1,0:T(8,128)(2,1)}, bf16[4,16,64,256]{3,2,1,0:T(8,128)(2,1)S(1)}, u32[]{:S(2)}, u32[]{:S(2)}) collective-permute-start(bf16[4,16,64,256]{3,2,1,0:T(8,128)(2,1)} %get-tuple-element.8), channel_id=1, source_target_pairs={{8,0},{16,8},{24,16},{32,24},{40,32},{48,40},{56,48},{64,56},{72,6... | collective-permute-start | bytes 6291464 | tf_op jit(solution)/shard_map/ppermute | solution.py:330
  26.2 36.8 %collective-permute-start.5 = (f32[2,8,3]{2,1,0:T(8,128)}, f32[2,8,3]{2,1,0:T(8,128)}, u32[]{:S(2)}, u32[]{:S(2)}) collective-permute-start(f32[2,8,3]{2,1,0:T(8,128)} %get-tuple-element.16), channel_id=1, source_target_pairs={{0,1},{1,2},{2,3},{3,4},{4,5},{5,6},{6,7},{8,9},{9,10},{10,11},{11... | collective-permute-start | bytes 584 | tf_op jit(solution)/shard_map/ppermute | solution.py:330
  30.3 36.1 %collective-permute-start.6 = (f32[2,8,3]{2,1,0:T(8,128)}, f32[2,8,3]{2,1,0:T(8,128)}, u32[]{:S(2)}, u32[]{:S(2)}) collective-permute-start(f32[2,8,3]{2,1,0:T(8,128)} %get-tuple-element.17), channel_id=1, source_target_pairs={{1,0},{2,1},{3,2},{4,3},{5,4},{6,5},{7,6},{9,8},{10,9},{11,10},{12... | collective-permute-start | bytes 584 | tf_op jit(solution)/shard_map/ppermute | solution.py:330
  35.4 54.1 %collective-permute-start.7 = (bf16[8,2,128,128]{3,2,1,0:T(8,128)(2,1)}, bf16[8,2,128,128]{3,2,1,0:T(8,128)(2,1)S(1)}, u32[]{:S(2)}, u32[]{:S(2)}) collective-permute-start(bf16[8,2,128,128]{3,2,1,0:T(8,128)(2,1)} %get-tuple-element.7), channel_id=1, source_target_pairs={{0,1},{1,2},{2,3},{3,4},{4,5},{5,6},{6,7},{8,9},{9,10},{10,11},{11... | collective-permute-start | bytes 1572872 | tf_op jit(solution)/shard_map/ppermute | solution.py:330
  63.0 26.5 %collective-permute-start.8 = (bf16[8,2,128,128]{3,2,1,0:T(8,128)(2,1)S(1)}, bf16[8,2,128,128]{3,2,1,0:T(8,128)(2,1)S(1)}, u32[]{:S(2)}, u32[]{:S(2)}) collective-permute-start(bf16[8,2,128,128]{3,2,1,0:T(8,128)(2,1)S(1)} %get-tuple-element.6), channel_id=1, source_target_pairs={{1,0},{2,1},{3,2},{4,3},{5,4},{6,5},{7,6},{9,8},{10,9},{11,10},{12... | collective-permute-start | bytes 1572872 | tf_op jit(solution)/shard_map/ppermute | solution.py:330
  67.8 2.2 %copy-start.5 = (bf16[8,16,64,256]{3,2,1,0:T(8,128)(2,1)S(1)}, bf16[8,16,64,256]{3,2,1,0:T(8,128)(2,1)}, u32[]{:S(2)}) copy-start(bf16[8,16,64,256]{3,2,1,0:T(8,128)(2,1)} %copy-done.4) | copy-start | bytes 12582916
  75.0 14.5 %copy-start.3 = (bf16[8,16,128,128]{3,2,1,0:T(8,128)(2,1)S(1)}, bf16[8,16,128,128]{3,2,1,0:T(8,128)(2,1)}, u32[]{:S(2)}) copy-start(bf16[8,16,128,128]{3,2,1,0:T(8,128)(2,1)} %copy-done.2) | copy-start | bytes 12582916
  75.0 6.2 %collective-permute-start.2 = (f32[2,4,16]{2,1,0:T(4,128)S(1)}, f32[2,4,16]{2,1,0:T(4,128)S(1)}, u32[]{:S(2)}, u32[]{:S(2)}) collective-permute-start(f32[2,4,16]{2,1,0:T(4,128)S(1)} %flow.3), channel_id=1, source_target_pairs={{8,0},{16,8},{24,16},{32,24},{40,32},{48,40},{56,48},{64,56},{72,6... | collective-permute-start | bytes 1544 | tf_op jit(solution)/shard_map/ppermute | solution.py:330
  81.3 17.8 %collective-permute-start.3 = (f32[2,8,3]{2,1,0:T(8,128)S(1)}, f32[2,8,3]{2,1,0:T(8,128)S(1)}, u32[]{:S(2)}, u32[]{:S(2)}) collective-permute-start(f32[2,8,3]{2,1,0:T(8,128)S(1)} %get-tuple-element.14), channel_id=1, source_target_pairs={{0,1},{1,2},{2,3},{3,4},{4,5},{5,6},{6,7},{8,9},{9,10},{10,11},{11... | collective-permute-start | bytes 584 | tf_op jit(solution)/shard_map/ppermute | solution.py:330
  85.3 13.8 %collective-permute-start.4 = (f32[2,8,3]{2,1,0:T(8,128)S(1)}, f32[2,8,3]{2,1,0:T(8,128)S(1)}, u32[]{:S(2)}, u32[]{:S(2)}) collective-permute-start(f32[2,8,3]{2,1,0:T(8,128)S(1)} %get-tuple-element.15), channel_id=1, source_target_pairs={{1,0},{2,1},{3,2},{4,3},{5,4},{6,5},{7,6},{9,8},{10,9},{11,10},{12... | collective-permute-start | bytes 584 | tf_op jit(solution)/shard_map/ppermute | solution.py:330
  95.8 3.3 %copy-start = (f32[8,16,128,128]{3,2,1,0:T(8,128)}, f32[8,16,128,128]{3,2,1,0:T(8,128)S(1)}, u32[]{:S(2)}) copy-start(f32[8,16,128,128]{3,2,1,0:T(8,128)S(1)} %blend.1.blended_ref) | copy-start | bytes 25165828
  102.6 3.4 %copy-start.1 = (f32[8,16,128,128]{3,2,1,0:T(8,128)S(1)}, f32[8,16,128,128]{3,2,1,0:T(8,128)}, u32[]{:S(2)}) copy-start(f32[8,16,128,128]{3,2,1,0:T(8,128)} %copy-done) | copy-start | bytes 25165828
where the time goes:
time: 122 us; the launch traced here: 120 us
  Pallas kernels  39.9 us (33%)
  starting transfers between devices  32.8 us (27%)
  local copies, waits for them, and re-layouts  24 us (20%)
  waiting for transfers between devices  19.8 us (16%)
  other arithmetic  2.94 us (2%)
    ppermute x9, starting transfers between devices, from_behind(): return lax.ppermute(x, axis, pairs)  32.8 us
    ppermute x9, waiting for transfers between devices, from_behind(): return lax.ppermute(x, axis, pairs)  19.8 us
    unnamed x34, local copies, waits for them, and re-layouts  14.8 us
    pallas_call x1, Pallas kernels, warp(): pl.pallas_call(warp_kernel, grid=(ny,), in_specs=[pl.BlockSpec(memory_spa...  14.3 us
    pallas_call x2, Pallas kernels, flow_of(): pl.pallas_call(functools.partial(flow_kernel, sign), grid=(ny,), in_specs...  9 us
    pallas_call x1, Pallas kernels, forward(): pl.pallas_call(forward_kernel, grid=(ny,), in_specs=[pl.BlockSpec((1, 1,...  8.83 us
    pallas_call x1, Pallas kernels, blend(): pl.pallas_call(blend_kernel, grid=(ny,), in_specs=[pl.BlockSpec(memory_sp...  6.2 us
    slice x1, local copies, waits for them, and re-layouts, per_device(): from_next = from_behind(spectra[:half], 'sec', -1)  2.62 us
  transfers between devices with their start and end apart: 9, of which 1 were waited for; matrix products, arithmetic and copies ran while one was open for 6% of the time, Pallas kernels for 13%

commit v1 on v0

v1 whole, which is shorter than its diff:
```python
import functools

import jax
import jax.numpy as jnp
import numpy as np
from jax import lax
from jax.experimental import pallas as pl
from jax.experimental.pallas import tpu as pltpu
from jax.sharding import PartitionSpec as P

K = 4
HB = 2
STEPS = 3
N = 128
HALF = N // 2
PAD = 72
ROW = 32
DEPTH = 3
SPRING = 0.2
EPS = 1e-06
MIB = 1024 * 1024
VMEM = 56 * MIB


def split(x):
    high = x.astype(jnp.bfloat16)
    return high, (x - high.astype(jnp.float32)).astype(jnp.bfloat16)


def tables():
    grid = np.arange(N)[:, None] * np.arange(N)[None, :] % N
    cosine = np.cos(2.0 * np.pi * grid / N)
    sine = np.sin(2.0 * np.pi * grid / N)
    rows = np.concatenate([cosine[:HALF], sine[:HALF]])
    rows[HALF] = cosine[HALF]
    cols = np.block([[cosine, -sine], [-sine, -cosine]])
    back_cols = np.block([[cosine, sine], [-sine, cosine]]) / N
    weight = np.where(np.arange(HALF) == 0, 1.0, 2.0)
    back_rows = np.concatenate([cosine[:, :HALF] * weight, -2.0 * sine[:, :HALF]], axis=1) / N
    back_rows[:, HALF] = cosine[:, HALF] / N
    return [jnp.asarray(t, jnp.float32) for t in (rows, cols, back_cols, back_rows)]


def first_row(shape):
    return lax.broadcasted_iota(jnp.int32, shape, len(shape) - 2) == 0


def dot(a, b):
    return jnp.dot(a, b, preferred_element_type=jnp.float32)


def ahead(fetch, rows, depth):
    y = pl.program_id(0)

    @pl.when(y == 0)
    def _():
        for row in range(depth):
            for copy in fetch(row):
                copy.start()

    @pl.when(y + depth < rows)
    def _():
        for copy in fetch(y + depth):
            copy.start()

    for copy in fetch(y):
        copy.wait()


def wait_all(copies):
    @pl.when(pl.program_id(0) == pl.num_programs(0) - 1)
    def _():
        for copy in copies:
            copy.wait()


def forward_kernel(x_hbm, rows_ref, cols_ref, *refs):
    *out_hbm, x_ref, lines_ref, spec, strip, in_sems, out_sems = refs
    y = pl.program_id(0)
    ny, patches = x_ref.shape[:2]
    half = ny // 2
    fetch = lambda row: [pltpu.make_async_copy(x_hbm.at[0, row], x_ref.at[row], in_sems.at[row])]
    ahead(fetch, ny, DEPTH)

    rows2 = rows_ref[...]
    cols = cols_ref[...]
    cols2 = jnp.concatenate([cols, cols], axis=0)
    for pair in range(patches // 2):
        x = jnp.concatenate([x_ref[y, 2 * pair], x_ref[y, 2 * pair + 1]], axis=1)
        high, low = split(x)
        part = {0: 0, 1: 1, patches // 2 - 2: 2, patches // 2 - 1: 3}.get(pair)
        if part is not None:
            strip[y, part, 0] = high[:, :N]
            strip[y, part, 1] = high[:, N:]
        both = dot(rows2, jnp.concatenate([high, low], axis=0))
        for side in range(2):
            here = both[:, side * N : (side + 1) * N]
            lines = jnp.concatenate([here[:HALF], here[HALF:]], axis=1)
            first = (2 * pair + side) * HALF
            high, low = split(lines)
            lines_ref[first : first + HALF, : 2 * N] = high
            lines_ref[first : first + HALF, 2 * N :] = low
    step = 4
    for first in range(0, patches, step):
        lines = lines_ref[first * HALF : (first + step) * HALF, :]
        freq = dot(lines, cols2).reshape(step, HALF, 2 * N)
        keep = lines[:, : 2 * N].astype(jnp.float32).reshape(step, HALF, 2 * N)
        out = jnp.where(first_row(freq.shape), keep, freq)
        spec[y, first : first + step] = out.astype(jnp.bfloat16)

    def spectra_to(row):
        ref = out_hbm[0].at[row] if row < half else out_hbm[1].at[row - half]
        return pltpu.make_async_copy(spec.at[row], ref, out_sems.at[row])

    strips_to = [
        pltpu.make_async_copy(strip.at[:, i], ref, out_sems.at[ny + i]) for i, ref in enumerate(out_hbm[2:])
    ]
    for row in range(ny):
        pl.when(y == row)(spectra_to(row).start)
    pl.when(y == ny - 1)(lambda: [copy.start() for copy in strips_to] and None)
    wait_all([spectra_to(row) for row in range(ny)] + strips_to)


def forward(sections, rows, cols):
    _, ny, nx, _, _ = sections.shape
    half = ny // 2
    rows2 = jnp.concatenate([rows, rows], axis=1).astype(jnp.bfloat16)
    whole = lambda shape: pl.BlockSpec(shape, lambda y: (0,) * len(shape))
    return pl.pallas_call(
        forward_kernel,
        grid=(ny,),
        in_specs=[
            pl.BlockSpec(memory_space=pl.ANY),
            whole((N, 2 * N)),
            whole((2 * N, 2 * N)),
        ],
        out_specs=[pl.BlockSpec(memory_space=pl.ANY)] * 6,
        out_shape=[jax.ShapeDtypeStruct((half, nx, HALF, 2 * N), jnp.bfloat16)] * 2
        + [jax.ShapeDtypeStruct((ny, HB, N, N), jnp.bfloat16)] * 4,
        scratch_shapes=[
            pltpu.VMEM(sections.shape[1:], jnp.float32),
            pltpu.VMEM((nx * HALF, 4 * N), jnp.bfloat16),
            pltpu.VMEM((ny, nx, HALF, 2 * N), jnp.bfloat16),
            pltpu.VMEM((ny, 4, HB, N, N), jnp.bfloat16),
            pltpu.SemaphoreType.DMA((ny,)),
            pltpu.SemaphoreType.DMA((ny + 4,)),
        ],
        compiler_params=pltpu.CompilerParams(vmem_limit_bytes=VMEM),
        cost_estimate=pl.CostEstimate(flops=4_000_000_000, bytes_accessed=14 * MIB, transcendentals=0),
        name="forward",
    )(sections, rows2, cols.astype(jnp.bfloat16))


def times_conj(a, b, sign):
    ar, ai, br, bi = a[:, :N], a[:, N:], b[:, :N], b[:, N:]
    real = ar * br + ai * bi
    imag = ai * br - ar * bi if sign > 0 else ar * bi - ai * br
    return jnp.concatenate([real, imag], axis=1).astype(jnp.bfloat16)


def flow_kernel(sign, own_hbm, other_hbm, cols_ref, back_cols_ref, back_rows_ref, flow_ref, sums, moments, product_ref, own_all, other_all, sems):
    y = pl.program_id(0)
    ny, patches = own_all.shape[:2]
    fetch = lambda row: [
        pltpu.make_async_copy(source.at[row], target.at[row], sems.at[row, i])
        for i, (source, target) in enumerate(((own_hbm, own_all), (other_hbm, other_all)))
    ]
    ahead(fetch, ny, DEPTH)
    own_ref = own_all.at[pl.ds(y, 1)]
    other_ref = other_all.at[pl.ds(y, 1)]
    cols = cols_ref[...]
    back_cols = back_cols_ref[...]
    back_rows = back_rows_ref[...]
    own = own_ref[0]
    other = other_ref[0]
    lines = jnp.concatenate(
        [r[:, 0, :].astype(jnp.float32) for r in (own, other)], axis=0
    ).astype(jnp.bfloat16)
    edge = jnp.concatenate([lines[:, :N], lines[:, N:]], axis=0)
    edge = dot(edge, cols[:N])
    quarter = edge.reshape(4, patches, 2 * N)
    low = times_conj(quarter[0], quarter[1], sign)
    high = times_conj(quarter[2], quarter[3], sign)
    sides = dot(jnp.concatenate([low, high], axis=0), back_cols[:, :N])
    shift_rows = lax.broadcasted_iota(jnp.int32, (N, N), 0)
    offset_rows = (((shift_rows + HALF) % N) - HALF).astype(jnp.float32)
    offset_rows = jnp.concatenate([offset_rows, offset_rows], axis=1)
    step = 4
    for first in range(0, patches, step):
        a = own_ref[0, first : first + step].reshape(step * HALF, 2 * N).astype(jnp.float32)
        b = other_ref[0, first : first + step].reshape(step * HALF, 2 * N).astype(jnp.float32)
        product_ref[first * HALF : (first + step) * HALF, :] = times_conj(a, b, sign)
    for first in range(0, patches, step):
        back = dot(product_ref[first * HALF : (first + step) * HALF, :], back_cols)
        halves = []
        for p in range(first, first + step):
            here = back[(p - first) * HALF : (p - first + 1) * HALF]
            parts = []
            for i, side in enumerate((p, patches + p)):
                part = here[:, i * N : (i + 1) * N]
                top = jnp.where(first_row((16, N)), sides[side : side + 1], part[:16])
                parts += [top.astype(jnp.bfloat16), part[16:].astype(jnp.bfloat16)]
            halves.append(jnp.concatenate(parts, axis=0))
        for i in range(0, step, 2):
            corr = dot(back_rows, jnp.concatenate(halves[i : i + 2], axis=1))
            power = corr * corr
            total = power.sum(0, keepdims=True)
            moment = (power * offset_rows).sum(0, keepdims=True)
            for side in range(2):
                p = first + i + side
                sums[p : p + 1, :] = total[:, side * N : (side + 1) * N]
                moments[p : p + 1, :] = moment[:, side * N : (side + 1) * N]
    lane = lax.broadcasted_iota(jnp.int32, (8, N), 1)
    row = lax.broadcasted_iota(jnp.int32, (8, N), 0)
    offset_cols = (((lane + HALF) % N) - HALF).astype(jnp.float32)
    reduce_by = jnp.where(row == 0, 1.0, jnp.where(row == 1, offset_cols, 0.0))
    over_lanes = lambda m: lax.dot_general(
        reduce_by, m, (((1,), (1,)), ((), ())),
        precision=lax.Precision.HIGHEST, preferred_element_type=jnp.float32,
    )
    by_sums = over_lanes(sums[...])
    by_moments = over_lanes(moments[...])
    total = by_sums[0:1] + EPS
    flow_ref[0, pl.ds(y, 1), :] = by_moments[0:1] / total
    flow_ref[1, pl.ds(y, 1), :] = by_sums[1:2] / total


def flow_of(own, other, sign, cols, back_cols, back_rows):
    ny, nx = other.shape[:2]
    whole = lambda shape: pl.BlockSpec(shape, lambda y: (0,) * len(shape))
    return pl.pallas_call(
        functools.partial(flow_kernel, sign),
        grid=(ny,),
        in_specs=[
            pl.BlockSpec(memory_space=pl.ANY),
            pl.BlockSpec(memory_space=pl.ANY),
            whole((2 * N, 2 * N)),
            whole((2 * N, 2 * N)),
            whole((N, N)),
        ],
        out_specs=whole((2, ny, nx)),
        out_shape=jax.ShapeDtypeStruct((2, ny, nx), jnp.float32),
        scratch_shapes=[
            pltpu.VMEM((nx, N), jnp.float32),
            pltpu.VMEM((nx, N), jnp.float32),
            pltpu.VMEM((nx * HALF, 2 * N), jnp.bfloat16),
            pltpu.VMEM(own.shape, own.dtype),
            pltpu.VMEM(own.shape, own.dtype),
            pltpu.SemaphoreType.DMA((ny, 2)),
        ],
        compiler_params=pltpu.CompilerParams(vmem_limit_bytes=VMEM),
        cost_estimate=pl.CostEstimate(flops=2_000_000_000, bytes_accessed=8 * MIB, transcendentals=0),
        name="flow",
    )(own, other, *(t.astype(jnp.bfloat16) for t in (cols, back_cols, back_rows)))


def slots_kernel(rows_ref, shifts_ref, count_ref, weight_ref, target_ref, share_ref):
    ny, _, nx = rows_ref.shape[1:]
    live = [k < count_ref[0] for k in range(K)]
    weights = [jnp.where(live[k], weight_ref[0, :, k, :], 0.0) for k in range(K)]
    total = weights[0] + weights[1] + weights[2] + weights[3]
    share = [(w / total).astype(jnp.bfloat16).astype(jnp.float32) for w in weights]
    column = lax.broadcasted_iota(jnp.int32, (ny, nx), 1) + HB
    target = [rows_ref[0, :, k, :] * ROW + column + shifts_ref[0, :, k, :] for k in range(K)]
    rest = N - K * nx
    share_ref[...] = jnp.concatenate(share + [jnp.zeros((ny, rest), jnp.float32)], axis=1)
    target_ref[...] = jnp.concatenate(target + [jnp.zeros((ny, rest), jnp.int32)], axis=1)


def slots_of(box_row, box_shift, box_count, blend_weight):
    ny = box_row.shape[1]
    slots_first = lambda x: jnp.transpose(x, (0, 1, 3, 2))
    return pl.pallas_call(
        slots_kernel,
        out_shape=[
            jax.ShapeDtypeStruct((ny, N), jnp.int32),
            jax.ShapeDtypeStruct((ny, N), jnp.float32),
        ],
        compiler_params=pltpu.CompilerParams(vmem_limit_bytes=VMEM),
        name="slots",
    )(slots_first(box_row), slots_first(box_shift), box_count, slots_first(blend_weight))


def blend_cell(y, x, nx, target_ref, share_ref, window):
    total = None
    for k in range(K):
        spot = target_ref[y, k * nx + x]
        piece = window[spot // ROW, spot % ROW].astype(jnp.float32) * share_ref[y, k * nx + x]
        total = piece if total is None else total + piece
    return total


def blend_kernel(target_ref, share_ref, x_hbm, out_hbm, window, staging, mid, in_sems, out_sems):
    y = pl.program_id(0)
    ny, nx = staging.shape[:2]

    @pl.when(y == 0)
    def _():
        copies = [
            pltpu.make_async_copy(x_hbm.at[0, row], staging.at[row], in_sems.at[row]) for row in range(ny)
        ]
        for copy in copies:
            copy.start()
        for row, copy in enumerate(copies):
            copy.wait()
            for x in range(nx):
                window[row, HB + x] = staging[row, x].astype(jnp.bfloat16)

    for x in range(HB, nx - HB):
        mid[y, x - HB] = blend_cell(y, x, nx, target_ref, share_ref, window)
    store = lambda row: pltpu.make_async_copy(mid.at[row], out_hbm.at[row], out_sems.at[row])
    store(y).start()
    wait_all([store(row) for row in range(ny)])


def blend(target, share, sections):
    _, ny, nx, _, _ = sections.shape
    mid = (ny, nx - 2 * HB, N, N)
    return pl.pallas_call(
        blend_kernel,
        grid=(ny,),
        in_specs=[pl.BlockSpec(memory_space=pltpu.SMEM)] * 2 + [pl.BlockSpec(memory_space=pl.ANY)],
        out_specs=pl.BlockSpec(memory_space=pl.ANY),
        out_shape=jax.ShapeDtypeStruct(mid, jnp.float32),
        scratch_shapes=[
            pltpu.VMEM((ny, nx + 2 * HB, N, N), jnp.bfloat16),
            pltpu.VMEM(sections.shape[1:], jnp.float32),
            pltpu.VMEM(mid, jnp.float32),
            pltpu.SemaphoreType.DMA((ny,)),
            pltpu.SemaphoreType.DMA((ny,)),
        ],
        compiler_params=pltpu.CompilerParams(vmem_limit_bytes=VMEM),
        cost_estimate=pl.CostEstimate(flops=20_000_000, bytes_accessed=14 * MIB, transcendentals=0),
        name="blend",
    )(target, share, sections)


def relax_kernel(low_ref, high_ref, mask_ref, left_ref, right_ref, out_ref):
    ny, nx = mask_ref.shape[1:]
    rest = jnp.zeros((ny, N - nx - 2 * STEPS), jnp.float32)

    def across(left, own, right):
        return jnp.concatenate([left[:, nx - STEPS :], own, right[:, :STEPS], rest], axis=1)

    known = across(left_ref[2], mask_ref[0].astype(jnp.float32) + 1.0, right_ref[2])
    valid = jnp.where(known > 0.5, 1.0, 0.0)
    trust = jnp.where(known > 1.5, 1.0, 0.0)
    row = lax.broadcasted_iota(jnp.int32, trust.shape, 0)
    for component in range(2):
        own = jnp.concatenate([low_ref[component], high_ref[component]], axis=0)
        flow = across(left_ref[component], own, right_ref[component])
        field = trust * flow
        for _ in range(STEPS):
            below = jnp.where(row == 0, 0.0, pltpu.roll(field, 1, 0))
            above = jnp.where(row == ny - 1, 0.0, pltpu.roll(field, ny - 1, 0))
            beside = pltpu.roll(field, 1, 1) + pltpu.roll(field, N - 1, 1)
            lap = above + below + beside - 4.0 * field
            field = (field + SPRING * (lap + trust * (flow - field))) * valid
        out_ref[0, component] = field[:, STEPS : STEPS + nx]


def relax(low, high, mask, left, right):
    return pl.pallas_call(
        relax_kernel,
        out_shape=jax.ShapeDtypeStruct((1, 2) + mask.shape[1:], jnp.float32),
        compiler_params=pltpu.CompilerParams(vmem_limit_bytes=VMEM),
        name="relax",
    )(low, high, mask, left, right)


def warp_kernel(field_ref, target_ref, share_ref, mid_hbm, *refs):
    *strips, out_hbm, window, padded, out, in_sems, out_sems = refs
    y = pl.program_id(0)
    ny, nx = out.shape[:2]
    places = (0, HB, 2 * HB, nx - HB, nx, nx + HB)
    strip_copies = [
        pltpu.make_async_copy(ref, window.at[:, into : into + HB], in_sems.at[ny + i])
        for i, (ref, into) in enumerate(zip(strips, places, strict=True))
    ]
    fetch = lambda row: [
        pltpu.make_async_copy(
            mid_hbm.at[row], padded.at[row, HB : nx - HB, PAD : PAD + N], in_sems.at[row]
        )
    ]

    @pl.when(y == 0)
    def _():
        for copy in strip_copies:
            copy.start()

    ahead(fetch, ny, DEPTH)
    padded[y, :, :PAD] = jnp.zeros((nx, PAD, N), jnp.float32)
    padded[y, :, PAD + N :] = jnp.zeros((nx, PAD, N), jnp.float32)

    @pl.when(y == 0)
    def _():
        for copy in strip_copies:
            copy.wait()

    for x in (*range(HB), *range(nx - HB, nx)):
        padded[y, x, PAD : PAD + N] = blend_cell(y, x, nx, target_ref, share_ref, window)
    apart = lax.broadcasted_iota(jnp.int32, (N, N), 0) - lax.broadcasted_iota(jnp.int32, (N, N), 1)
    apart = apart.astype(jnp.float32)
    for x in range(nx):
        shift = field_ref[0, 0, y, x]
        down = jnp.clip((shift + 256.0).astype(jnp.int32) - 256, 4 - PAD, PAD - 6)
        part = shift - down.astype(jnp.float32)
        upper = padded[y, x, pl.ds(PAD + down, N), :]
        lower = padded[y, x, pl.ds(PAD + 1 + down, N), :]
        image = upper + part * (lower - upper)
        hat = jnp.maximum(0.0, 1.0 - jnp.abs(apart - field_ref[0, 1, y, x])).astype(jnp.bfloat16)
        warped = dot(jnp.concatenate(split(image), axis=1), jnp.concatenate([hat, hat], axis=0))
        out[y, x] = warped.astype(jnp.bfloat16)
    store = lambda row: pltpu.make_async_copy(out.at[row], out_hbm.at[0, row], out_sems.at[row])
    store(y).start()
    wait_all([store(row) for row in range(ny)])


def warp(field, target, share, mid, strips):
    ny, nx = field.shape[2:]
    return pl.pallas_call(
        warp_kernel,
        grid=(ny,),
        in_specs=[pl.BlockSpec(memory_space=pltpu.SMEM)] * 3
        + [pl.BlockSpec(memory_space=pl.ANY)] * (1 + len(strips)),
        out_specs=pl.BlockSpec(memory_space=pl.ANY),
        out_shape=jax.ShapeDtypeStruct((1, ny, nx, N, N), jnp.bfloat16),
        scratch_shapes=[
            pltpu.VMEM((ny, nx + 2 * HB, N, N), jnp.bfloat16),
            pltpu.VMEM((ny, nx, 2 * PAD + N, N), jnp.float32),
            pltpu.VMEM((ny, nx, N, N), jnp.bfloat16),
            pltpu.SemaphoreType.DMA((ny + len(strips),)),
            pltpu.SemaphoreType.DMA((ny,)),
        ],
        compiler_params=pltpu.CompilerParams(vmem_limit_bytes=VMEM),
        cost_estimate=pl.CostEstimate(flops=20_000_000, bytes_accessed=12 * MIB, transcendentals=0),
        name="warp",
    )(field, target, share, mid, *strips)


def from_behind(x, axis, by):
    length = lax.axis_size(axis)
    pairs = [(i, i + by) for i in range(length) if 0 <= i + by < length]
    return lax.ppermute(x, axis, pairs)


def per_device(sections, node_mask, box_row, box_shift, box_count, blend_weight):
    ny, nx = sections.shape[1:3]
    rows, cols, back_cols, back_rows = tables()
    half = ny // 2
    spectra_low, spectra_high, left, after, before, right = forward(sections, rows, cols)
    from_next = from_behind(spectra_low, "sec", -1)
    from_last = from_behind(spectra_high, "sec", 1)
    low = from_behind(right, "tile", 1)
    high = from_behind(left, "tile", -1)
    target, share = slots_of(box_row, box_shift, box_count, blend_weight)
    mid = blend(target, share, sections)

    flow_low = flow_of(spectra_low, from_next, 1, cols, back_cols, back_rows)
    flow_high = flow_of(spectra_high, from_last, -1, cols, back_cols, back_rows)
    flow_high = from_behind(flow_high, "sec", -1)
    flow = jnp.concatenate([flow_low, flow_high], axis=1)
    flow = jnp.concatenate([flow, node_mask.astype(jnp.float32) + 1.0], axis=0)
    flow_left = from_behind(flow, "tile", 1)
    flow_right = from_behind(flow, "tile", -1)
    strips = (low, left, after, before, right, high)
    field = relax(flow_low, flow_high, node_mask, flow_left, flow_right)
    return (warp(field, target, share, mid, strips), field)


def solution(mesh):
    return jax.shard_map(
        per_device,
        mesh=mesh,
        in_specs=(
            P("sec", None, "tile", None, None),
            P("sec", None, "tile"),
            P("sec", None, "tile", None),
            P("sec", None, "tile", None),
            P("sec", None, "tile"),
            P("sec", None, "tile", None),
        ),
        out_specs=(P("sec", None, "tile", None, None), P("sec", None, None, "tile")),
        check_vma=False,
    )
```

time: 122 us -> 101 us (0.83); the launches traced: 120 us -> 101 us
  local copies, waits for them, and re-layouts: 24 us -> 4.89 us
  starting transfers between devices: 32.8 us -> 26.1 us
  Pallas kernels: 39.9 us -> 44.8 us
  waiting for transfers between devices: 19.8 us -> 23.5 us
  other arithmetic: 2.94 us -> 0.69 us
    unnamed x34 -> x16, local copies, waits for them, and re-layouts: 14.8 us -> 4.89 us
    ppermute x9 -> x7, starting transfers between devices: 32.8 us -> 26.1 us  [from_behind(): return lax.ppermute(x, axis, pairs)]
    pallas_call x2, Pallas kernels: 9 us -> 13.6 us  [flow_of(): pl.pallas_call(functools.partial(flow_kernel, sign), grid=(ny,), in_specs...]
    slice x3 -> x0, local copies, waits for them, and re-layouts: 4.22 us -> none  [the longest x1 2.62 us: per_device(): from_next = from_behind(spectra[:half], 'sec', -1)]
    pallas_call x1, Pallas kernels: 14.3 us -> 10.4 us  [warp(): pl.pallas_call(warp_kernel, grid=(ny,), in_specs=[pl.BlockSpec(memory_spa...]
    ppermute x9 -> x7, waiting for transfers between devices: 19.8 us -> 23.5 us  [from_behind(): return lax.ppermute(x, axis, pairs)]
    pallas_call x1, Pallas kernels: 6.2 us -> 8.44 us  [blend(): pl.pallas_call(blend_kernel, grid=(ny,), in_specs=[pl.BlockSpec(memory_sp...]
    pallas_call x2 -> x3, Pallas kernels: 10.4 us -> 12.4 us  [the longest x1 9.17 us: forward(): pl.pallas_call(forward_kernel, grid=(ny,), in_specs=[pl.BlockSpec(memory_...]
  transfers between devices with their start and end apart: 9 -> 7, of which waited for: 1 -> 1; matrix products, arithmetic and copies ran while one was open for 6% -> 1% of each run, Pallas kernels for 13% -> 25%
where the time goes in v1:
time: 101 us
  Pallas kernels  44.8 us (44%)
  starting transfers between devices  26.1 us (26%)
  waiting for transfers between devices  23.5 us (23%)
  local copies, waits for them, and re-layouts  4.89 us (5%)
    ppermute x7, starting transfers between devices, from_behind(): return lax.ppermute(x, axis, pairs)  26.1 us
    ppermute x7, waiting for transfers between devices, from_behind(): return lax.ppermute(x, axis, pairs)  23.5 us
    pallas_call x2, Pallas kernels, flow_of(): pl.pallas_call(functools.partial(flow_kernel, sign), grid=(ny,), in_specs...  13.6 us
    pallas_call x1, Pallas kernels, warp(): pl.pallas_call(warp_kernel, grid=(ny,), in_specs=[pl.BlockSpec(memory_spa...  10.4 us
    pallas_call x1, Pallas kernels, forward(): pl.pallas_call(forward_kernel, grid=(ny,), in_specs=[pl.BlockSpec(memory_...  9.17 us
    pallas_call x1, Pallas kernels, blend(): pl.pallas_call(blend_kernel, grid=(ny,), in_specs=[pl.BlockSpec(memory_sp...  8.44 us
    unnamed x16, local copies, waits for them, and re-layouts  4.89 us
  transfers between devices with their start and end apart: 7, of which 1 were waited for; matrix products, arithmetic and copies ran while one was open for 1% of the time, Pallas kernels for 25%

profile of v1, /device:TPU:66, one launch (start us, length us, event | category | flops | bytes accessed | tf_op | source)
XLA Modules:
  0.0 100.7 jit_solution(1650423522714450488)
XLA Ops:
  0.6 0.0 copy-start.2
  0.6 9.2 %forward.1 = (bf16[4,16,64,256]{3,2,1,0:T(8,128)(2,1)}, bf16[4,16,64,256]{3,2,1,0:T(8,128)(2,1)}, bf16[8,2,128,128]{3,2,1,0:T(8,128)(2,1)}, bf16[8,2,128,128]{3,...) custom-call(f32[1,8,16,128,128]{4,3,2,1,0:T(8,128)} %x_hbm.3, ...), custom_call_target="tpu_custom_call" | custom-call | flops 4000000000 | bytes 14680064 | tf_op jit(solution)/shard_map/forward/pallas_call | solution.py:129
  9.8 1.9 %collective-permute-start.1 = (bf16[4,16,64,256]{3,2,1,0:T(8,128)(2,1)}, bf16[4,16,64,256]{3,2,1,0:T(8,128)(2,1)S(1)}, u32[]{:S(2)}, u32[]{:S(2)}) collective-permute-start(bf16[4,16,64,256]{3,2,1,0:T(8,128)(2,1)} %get-tuple-element.11.own_hbm), channel_id=1, source_target_pairs={{0,8},{8,16},{16,24},{24,32},{32,40},{40,48},{48,56},{56,64},{64,7... | collective-permute-start | bytes 6291464 | tf_op jit(solution)/shard_map/ppermute | solution.py:444
  11.7 5.8 %collective-permute-start = (bf16[4,16,64,256]{3,2,1,0:T(8,128)(2,1)}, bf16[4,16,64,256]{3,2,1,0:T(8,128)(2,1)S(1)}, u32[]{:S(2)}, u32[]{:S(2)}) collective-permute-start(bf16[4,16,64,256]{3,2,1,0:T(8,128)(2,1)} %get-tuple-element.10.own_hbm), channel_id=1, source_target_pairs={{8,0},{16,8},{24,16},{32,24},{40,32},{48,40},{56,48},{64,56},{72,6... | collective-permute-start | bytes 6291464 | tf_op jit(solution)/shard_map/ppermute | solution.py:444
  17.5 4.0 %collective-permute-start.5 = (bf16[8,2,128,128]{3,2,1,0:T(8,128)(2,1)}, bf16[8,2,128,128]{3,2,1,0:T(8,128)(2,1)S(1)}, u32[]{:S(2)}, u32[]{:S(2)}) collective-permute-start(bf16[8,2,128,128]{3,2,1,0:T(8,128)(2,1)} %get-tuple-element.14.refs_4_), channel_id=1, source_target_pairs={{0,1},{1,2},{2,3},{3,4},{4,5},{5,6},{6,7},{8,9},{9,10},{10,11},{11... | collective-permute-start | bytes 1572872 | tf_op jit(solution)/shard_map/ppermute | solution.py:444
  21.5 4.2 %collective-permute-start.6 = (bf16[8,2,128,128]{3,2,1,0:T(8,128)(2,1)}, bf16[8,2,128,128]{3,2,1,0:T(8,128)(2,1)S(1)}, u32[]{:S(2)}, u32[]{:S(2)}) collective-permute-start(bf16[8,2,128,128]{3,2,1,0:T(8,128)(2,1)} %get-tuple-element.15.refs_1_), channel_id=1, source_target_pairs={{1,0},{2,1},{3,2},{4,3},{5,4},{6,5},{7,6},{9,8},{10,9},{11,10},{12... | collective-permute-start | bytes 1572872 | tf_op jit(solution)/shard_map/ppermute | solution.py:444
  25.8 0.0 copy-done.2
  25.8 1.5 %slots.1 = (s32[8,128]{1,0:T(8,128)}, f32[8,128]{1,0:T(8,128)}) custom-call(s32[1,8,4,16]{3,2,1,0:T(4,128)} %bitcast.3, s32[1,8,4,16]{3,2,1,0:T(4,128)} %bitcast.4, s32[1,8,16]{2,1,0:T(8,128)} %count_ref.1, f32[1,8,4,16]{3,2,1,0:T(4,128)} %bitcast.5), custom_call_target="tpu_custom_call" | custom-call | tf_op jit(solution)/shard_map/slots/pallas_call | solution.py:273
  27.3 23.5 %collective-permute-done.1.other_hbm = bf16[4,16,64,256]{3,2,1,0:T(8,128)(2,1)S(1)} collective-permute-done((bf16[4,16,64,256]{3,2,1,0:T(8,128)(2,1)}, bf16[4,16,64,256]{3,2,1,0:T(8,128)(2,1)S(1)}, u32[]{:S(2)}, u32[]{:S(2)}) %collective-permute-start.1) | collective-permute-done | bytes 2097184 | tf_op jit(solution)/shard_map/ppermute | solution.py:444
  50.7 1.3 %copy-done.7 = bf16[4,16,64,256]{3,2,1,0:T(8,128)(2,1)} copy-done((bf16[4,16,64,256]{3,2,1,0:T(8,128)(2,1)}, bf16[4,16,64,256]{3,2,1,0:T(8,128)(2,1)S(1)}, u32[]{:S(2)}) %copy-start.7) | copy-done | bytes 2097176
  52.1 6.8 %flow.3 = f32[2,4,16]{2,1,0:T(4,128)} custom-call(bf16[4,16,64,256]{3,2,1,0:T(8,128)(2,1)} %get-tuple-element.11.own_hbm, bf16[4,16,64,256]{3,2,1,0:T(8,128)(2,1)} %copy-done.7, bf16[256,256]{1,0:T(8,128)(2,1)} %constant.22.cols_ref, bf16[256,256]{1,0:T(8,128)(2,1)} %constant.23.back_cols_ref, bf16[128,128]{1,0:T(8,128)(2,1)} %constant.24.back_rows_ref), custom_call_target="tpu_custom_call" | custom-call | flops 2000000000 | bytes 8388608 | tf_op jit(solution)/shard_map/flow/pallas_call | solution.py:231
  58.9 1.9 %collective-permute-start.2 = (f32[2,4,16]{2,1,0:T(4,128)}, f32[2,4,16]{2,1,0:T(4,128)S(1)}, u32[]{:S(2)}, u32[]{:S(2)}) collective-permute-start(f32[2,4,16]{2,1,0:T(4,128)} %flow.3), channel_id=1, source_target_pairs={{8,0},{16,8},{24,16},{32,24},{40,32},{48,40},{56,48},{64,56},{72,6... | collective-permute-start | bytes 1544 | tf_op jit(solution)/shard_map/ppermute | solution.py:444
  60.8 0.0 collective-permute-done.other_hbm
  60.8 0.0 copy-start.6
  60.8 1.3 %copy-done.6 = bf16[4,16,64,256]{3,2,1,0:T(8,128)(2,1)} copy-done((bf16[4,16,64,256]{3,2,1,0:T(8,128)(2,1)}, bf16[4,16,64,256]{3,2,1,0:T(8,128)(2,1)S(1)}, u32[]{:S(2)}) %copy-start.6) | copy-done | bytes 2097176
  62.1 6.8 %flow.2.low_ref = f32[2,4,16]{2,1,0:T(4,128)} custom-call(bf16[4,16,64,256]{3,2,1,0:T(8,128)(2,1)} %get-tuple-element.10.own_hbm, bf16[4,16,64,256]{3,2,1,0:T(8,128)(2,1)} %copy-done.6, bf16[256,256]{1,0:T(8,128)(2,1)} %constant.22.cols_ref, bf16[256,256]{1,0:T(8,128)(2,1)} %constant.23.back_cols_ref, bf16[128,128]{1,0:T(8,128)(2,1)} %constant.24.back_rows_ref), custom_call_target="tpu_custom_call" | custom-call | flops 2000000000 | bytes 8388608 | tf_op jit(solution)/shard_map/flow/pallas_call | solution.py:231
  69.0 0.0 collective-permute-done.2.high_ref
  69.0 0.7 pad_maximum_fusion
  69.7 4.0 %collective-permute-start.3 = (f32[3,8,16]{2,1,0:T(8,128)S(1)}, f32[3,8,16]{2,1,0:T(8,128)S(1)}, u32[]{:S(2)}, u32[]{:S(2)}) collective-permute-start(f32[3,8,16]{2,1,0:T(8,128)S(1)} %pad_maximum_fusion), channel_id=1, source_target_pairs={{0,1},{1,2},{2,3},{3,4},{4,5},{5,6},{6,7},{8,9},{9,10},{10,11},{11... | collective-permute-start | bytes 4616 | tf_op jit(solution)/shard_map/ppermute | solution.py:444
  73.7 4.2 %collective-permute-start.4 = (f32[3,8,16]{2,1,0:T(8,128)S(1)}, f32[3,8,16]{2,1,0:T(8,128)S(1)}, u32[]{:S(2)}, u32[]{:S(2)}) collective-permute-start(f32[3,8,16]{2,1,0:T(8,128)S(1)} %pad_maximum_fusion), channel_id=1, source_target_pairs={{1,0},{2,1},{3,2},{4,3},{5,4},{6,5},{7,6},{9,8},{10,9},{11,10},{12... | collective-permute-start | bytes 4616 | tf_op jit(solution)/shard_map/ppermute | solution.py:444
  77.9 8.4 %blend.1.mid_hbm = f32[8,12,128,128]{3,2,1,0:T(8,128)} custom-call(s32[8,128]{1,0:T(8,128)} %get-tuple-element.12.target_ref, f32[8,128]{1,0:T(8,128)} %get-tuple-element.13.share_ref, f32[1,8,16,128,128]{4,3,2,1,0:T(8,128)} %x_hbm.3), custom_call_target="tpu_custom_call" | custom-call | flops 20000000 | bytes 14680064 | tf_op jit(solution)/shard_map/blend/pallas_call | solution.py:319
  86.4 0.0 collective-permute-done.3.left_ref
  86.4 0.0 copy-start.4
  86.4 0.0 collective-permute-done.4.right_ref
  86.4 0.6 copy-done.4
  87.0 0.6 copy-done.5
  87.6 1.7 %relax.1.field_ref = f32[1,2,8,16]{3,2,1,0:T(8,128)} custom-call(f32[2,4,16]{2,1,0:T(4,128)} %flow.2.low_ref, f32[2,4,16]{2,1,0:T(4,128)} %copy-done.3, s32[1,8,16]{2,1,0:T(8,128)} %mask_ref.1, f32[3,8,16]{2,1,0:T(8,128)} %copy-done.4, f32[3,8,16]{2,1,0:T(8,128)} %copy-done.5), custom_call_target="tpu_custom_call" | custom-call | tf_op jit(solution)/shard_map/relax/pallas_call | solution.py:363
  89.3 0.0 collective-permute-done.5.refs_0_
  89.3 0.0 collective-permute-done.6.refs_5_
  89.3 0.8 copy-done
  90.1 0.2 copy-done.1
  90.4 10.4 %warp.1 = bf16[1,8,16,128,128]{4,3,2,1,0:T(8,128)(2,1)} custom-call(f32[1,2,8,16]{3,2,1,0:T(8,128)} %relax.1.field_ref, s32[8,128]{1,0:T(8,128)} %get-tuple-element.12.target_ref, f32[8,128]{1,0:T(8,128)} %get-tuple-element.13.share_ref, f32[8,12,128,128]{3,2,1,0:T(8,128)} %blend.1.mid_hbm, bf16[8,2,128,128]{3,2,1,0:T(8,128)(2,1)} %copy-done, ...), custom_call_target="tpu_custom_call" | custom-call | flops 20000000 | bytes 12582912 | tf_op jit(solution)/shard_map/warp/pallas_call | solution.py:421
  (7 shorter events, 0.0 us)
Async XLA Ops:
  0.6 25.1 %copy-start.2 = (s32[1,8,16]{2,1,0:T(8,128)S(1)}, s32[1,8,16]{2,1,0:T(8,128)}, u32[]{:S(2)}) copy-start(s32[1,8,16]{2,1,0:T(8,128)} %mask_ref.1) | copy-start | bytes 1540
  9.8 40.9 %collective-permute-start.1 = (bf16[4,16,64,256]{3,2,1,0:T(8,128)(2,1)}, bf16[4,16,64,256]{3,2,1,0:T(8,128)(2,1)S(1)}, u32[]{:S(2)}, u32[]{:S(2)}) collective-permute-start(bf16[4,16,64,256]{3,2,1,0:T(8,128)(2,1)} %get-tuple-element.11.own_hbm), channel_id=1, source_target_pairs={{0,8},{8,16},{16,24},{24,32},{32,40},{40,48},{48,56},{56,64},{64,7... | collective-permute-start | bytes 6291464 | tf_op jit(solution)/shard_map/ppermute | solution.py:444
  11.7 49.1 %collective-permute-start = (bf16[4,16,64,256]{3,2,1,0:T(8,128)(2,1)}, bf16[4,16,64,256]{3,2,1,0:T(8,128)(2,1)S(1)}, u32[]{:S(2)}, u32[]{:S(2)}) collective-permute-start(bf16[4,16,64,256]{3,2,1,0:T(8,128)(2,1)} %get-tuple-element.10.own_hbm), channel_id=1, source_target_pairs={{8,0},{16,8},{24,16},{32,24},{40,32},{48,40},{56,48},{64,56},{72,6... | collective-permute-start | bytes 6291464 | tf_op jit(solution)/shard_map/ppermute | solution.py:444
  17.5 71.8 %collective-permute-start.5 = (bf16[8,2,128,128]{3,2,1,0:T(8,128)(2,1)}, bf16[8,2,128,128]{3,2,1,0:T(8,128)(2,1)S(1)}, u32[]{:S(2)}, u32[]{:S(2)}) collective-permute-start(bf16[8,2,128,128]{3,2,1,0:T(8,128)(2,1)} %get-tuple-element.14.refs_4_), channel_id=1, source_target_pairs={{0,1},{1,2},{2,3},{3,4},{4,5},{5,6},{6,7},{8,9},{9,10},{10,11},{11... | collective-permute-start | bytes 1572872 | tf_op jit(solution)/shard_map/ppermute | solution.py:444
  21.5 67.8 %collective-permute-start.6 = (bf16[8,2,128,128]{3,2,1,0:T(8,128)(2,1)}, bf16[8,2,128,128]{3,2,1,0:T(8,128)(2,1)S(1)}, u32[]{:S(2)}, u32[]{:S(2)}) collective-permute-start(bf16[8,2,128,128]{3,2,1,0:T(8,128)(2,1)} %get-tuple-element.15.refs_1_), channel_id=1, source_target_pairs={{1,0},{2,1},{3,2},{4,3},{5,4},{6,5},{7,6},{9,8},{10,9},{11,10},{12... | collective-permute-start | bytes 1572872 | tf_op jit(solution)/shard_map/ppermute | solution.py:444
  50.7 1.3 %copy-start.7 = (bf16[4,16,64,256]{3,2,1,0:T(8,128)(2,1)}, bf16[4,16,64,256]{3,2,1,0:T(8,128)(2,1)S(1)}, u32[]{:S(2)}) copy-start(bf16[4,16,64,256]{3,2,1,0:T(8,128)(2,1)S(1)} %collective-permute-done.1.other_hbm) | copy-start | bytes 6291460
  58.9 10.1 %collective-permute-start.2 = (f32[2,4,16]{2,1,0:T(4,128)}, f32[2,4,16]{2,1,0:T(4,128)S(1)}, u32[]{:S(2)}, u32[]{:S(2)}) collective-permute-start(f32[2,4,16]{2,1,0:T(4,128)} %flow.3), channel_id=1, source_target_pairs={{8,0},{16,8},{24,16},{32,24},{40,32},{48,40},{56,48},{64,56},{72,6... | collective-permute-start | bytes 1544 | tf_op jit(solution)/shard_map/ppermute | solution.py:444
  60.8 1.3 %copy-start.6 = (bf16[4,16,64,256]{3,2,1,0:T(8,128)(2,1)}, bf16[4,16,64,256]{3,2,1,0:T(8,128)(2,1)S(1)}, u32[]{:S(2)}) copy-start(bf16[4,16,64,256]{3,2,1,0:T(8,128)(2,1)S(1)} %collective-permute-done.other_hbm) | copy-start | bytes 6291460
  69.0 17.4 %copy-start.3 = (f32[2,4,16]{2,1,0:T(4,128)}, f32[2,4,16]{2,1,0:T(4,128)S(1)}, u32[]{:S(2)}) copy-start(f32[2,4,16]{2,1,0:T(4,128)S(1)} %collective-permute-done.2.high_ref) | copy-start | bytes 1540
  69.7 16.7 %collective-permute-start.3 = (f32[3,8,16]{2,1,0:T(8,128)S(1)}, f32[3,8,16]{2,1,0:T(8,128)S(1)}, u32[]{:S(2)}, u32[]{:S(2)}) collective-permute-start(f32[3,8,16]{2,1,0:T(8,128)S(1)} %pad_maximum_fusion), channel_id=1, source_target_pairs={{0,1},{1,2},{2,3},{3,4},{4,5},{5,6},{6,7},{8,9},{9,10},{10,11},{11... | collective-permute-start | bytes 4616 | tf_op jit(solution)/shard_map/ppermute | solution.py:444
  73.7 12.7 %collective-permute-start.4 = (f32[3,8,16]{2,1,0:T(8,128)S(1)}, f32[3,8,16]{2,1,0:T(8,128)S(1)}, u32[]{:S(2)}, u32[]{:S(2)}) collective-permute-start(f32[3,8,16]{2,1,0:T(8,128)S(1)} %pad_maximum_fusion), channel_id=1, source_target_pairs={{1,0},{2,1},{3,2},{4,3},{5,4},{6,5},{7,6},{9,8},{10,9},{11,10},{12... | collective-permute-start | bytes 4616 | tf_op jit(solution)/shard_map/ppermute | solution.py:444
  86.4 0.6 copy-start.4
  87.0 0.6 copy-start.5
  89.3 0.8 copy-start
  89.3 1.1 %copy-start.1 = (bf16[8,2,128,128]{3,2,1,0:T(8,128)(2,1)}, bf16[8,2,128,128]{3,2,1,0:T(8,128)(2,1)S(1)}, u32[]{:S(2)}) copy-start(bf16[8,2,128,128]{3,2,1,0:T(8,128)(2,1)S(1)} %collective-permute-done.6.refs_5_) | copy-start | bytes 1572868

commit v2 on v1

v2 whole, which is shorter than its diff:
```python
import functools

import jax
import jax.numpy as jnp
import numpy as np
from jax import lax
from jax.experimental import pallas as pl
from jax.experimental.pallas import tpu as pltpu
from jax.sharding import PartitionSpec as P

K = 4
HB = 2
STEPS = 3
N = 128
HALF = N // 2
PAD = 72
ROW = 32
DEPTH = 3
SPRING = 0.2
EPS = 1e-06
MIB = 1024 * 1024
VMEM = 60 * MIB


def split(x):
    high = x.astype(jnp.bfloat16)
    return high, (x - high.astype(jnp.float32)).astype(jnp.bfloat16)


def tables():
    grid = np.arange(N)[:, None] * np.arange(N)[None, :] % N
    cosine = np.cos(2.0 * np.pi * grid / N)
    sine = np.sin(2.0 * np.pi * grid / N)
    rows = np.concatenate([cosine[:HALF], sine[:HALF]])
    rows[HALF] = cosine[HALF]
    cols = np.block([[cosine, -sine], [-sine, -cosine]])
    back_cols = np.block([[cosine, sine], [-sine, cosine]]) / N
    weight = np.where(np.arange(HALF) == 0, 1.0, 2.0)
    back_rows = np.concatenate([cosine[:, :HALF] * weight, -2.0 * sine[:, :HALF]], axis=1) / N
    back_rows[:, HALF] = cosine[:, HALF] / N
    return [jnp.asarray(t, jnp.float32) for t in (rows, cols, back_cols, back_rows)]


def first_row(shape):
    return lax.broadcasted_iota(jnp.int32, shape, len(shape) - 2) == 0


def dot(a, b):
    return jnp.dot(a, b, preferred_element_type=jnp.float32)


def ahead(fetch, rows, depth):
    y = pl.program_id(0)

    @pl.when(y == 0)
    def _():
        for row in range(depth):
            for copy in fetch(row):
                copy.start()

    @pl.when(y + depth < rows)
    def _():
        for copy in fetch(y + depth):
            copy.start()

    for copy in fetch(y):
        copy.wait()


def wait_all(copies):
    @pl.when(pl.program_id(0) == pl.num_programs(0) - 1)
    def _():
        for copy in copies:
            copy.wait()


def forward_kernel(x_hbm, rows_ref, cols_ref, low_hbm, high_hbm, x_ref, lines_ref, ends_ref, spec, in_sems, out_sems):
    y = pl.program_id(0)
    ny, patches = x_ref.shape[:2]
    half = ny // 2
    fetch = lambda row: [pltpu.make_async_copy(x_hbm.at[0, row], x_ref.at[row], in_sems.at[row])]
    ahead(fetch, ny, DEPTH)

    rows2 = rows_ref[...]
    cols = cols_ref[...]
    cols2 = jnp.concatenate([cols, cols], axis=0)
    for pair in range(patches // 2):
        x = jnp.concatenate([x_ref[y, 2 * pair], x_ref[y, 2 * pair + 1]], axis=1)
        both = dot(rows2, jnp.concatenate(split(x), axis=0))
        for side in range(2):
            here = both[:, side * N : (side + 1) * N]
            p = 2 * pair + side
            ends_ref[p : p + 1, :N] = here[:1]
            ends_ref[p : p + 1, N:] = here[HALF : HALF + 1]
            lines = jnp.concatenate([here[:HALF], here[HALF:]], axis=1)
            high, low = split(lines)
            lines_ref[p * HALF : (p + 1) * HALF, : 2 * N] = high
            lines_ref[p * HALF : (p + 1) * HALF, 2 * N :] = low
    part, row = y // half, y % half
    step = 4
    for first in range(0, patches, step):
        lines = lines_ref[first * HALF : (first + step) * HALF, :]
        freq = dot(lines, cols2).reshape(step, HALF, 2 * N)
        spec[part, pl.ds(row * patches + first, step)] = freq.astype(jnp.bfloat16)
    last = half * patches
    ends = ends_ref[...].astype(jnp.bfloat16)
    spec[part, last, pl.ds(pl.multiple_of(row * patches, patches), patches), :] = ends

    def spectra_to(row):
        first = row % half * patches
        count = patches + (row % half == half - 1)
        return pltpu.make_async_copy(
            spec.at[row // half, pl.ds(first, count)],
            (low_hbm, high_hbm)[row // half].at[pl.ds(first, count)],
            out_sems.at[row],
        )

    for row in range(ny):
        pl.when(y == row)(spectra_to(row).start)
    wait_all([spectra_to(row) for row in range(ny)])


def forward(sections, rows, cols):
    _, ny, nx, _, _ = sections.shape
    half = ny // 2
    rows2 = jnp.concatenate([rows, rows], axis=1).astype(jnp.bfloat16)
    whole = lambda shape: pl.BlockSpec(shape, lambda y: (0,) * len(shape))
    spectra = (half * nx + 1, HALF, 2 * N)
    return pl.pallas_call(
        forward_kernel,
        grid=(ny,),
        in_specs=[
            pl.BlockSpec(memory_space=pl.ANY),
            whole((N, 2 * N)),
            whole((2 * N, 2 * N)),
        ],
        out_specs=[pl.BlockSpec(memory_space=pl.ANY)] * 2,
        out_shape=[jax.ShapeDtypeStruct(spectra, jnp.bfloat16)] * 2,
        scratch_shapes=[
            pltpu.VMEM(sections.shape[1:], jnp.float32),
            pltpu.VMEM((nx * HALF, 4 * N), jnp.bfloat16),
            pltpu.VMEM((nx, 2 * N), jnp.float32),
            pltpu.VMEM((2,) + spectra, jnp.bfloat16),
            pltpu.SemaphoreType.DMA((ny,)),
            pltpu.SemaphoreType.DMA((ny,)),
        ],
        compiler_params=pltpu.CompilerParams(vmem_limit_bytes=VMEM),
        cost_estimate=pl.CostEstimate(flops=4_000_000_000, bytes_accessed=12 * MIB, transcendentals=0),
        name="forward",
    )(sections, rows2, cols.astype(jnp.bfloat16))


def times_conj(a, b, sign):
    ar, ai, br, bi = a[:, :N], a[:, N:], b[:, :N], b[:, N:]
    real = ar * br + ai * bi
    imag = ai * br - ar * bi if sign > 0 else ar * bi - ai * br
    return jnp.concatenate([real, imag], axis=1).astype(jnp.bfloat16)


def flow_kernel(sign, own_hbm, other_hbm, cols_ref, back_cols_ref, back_rows_ref, flow_ref, own, other, sides, sums, moments, sems):
    y = pl.program_id(0)
    ny, patches = sums.shape[:2]
    last = ny * patches
    pairs = ((own_hbm, own), (other_hbm, other))
    fetch = lambda row: [
        pltpu.make_async_copy(
            source.at[pl.ds(row * patches, patches)], target.at[pl.ds(row * patches, patches)], sems.at[row, i]
        )
        for i, (source, target) in enumerate(pairs)
    ]
    ends = [
        pltpu.make_async_copy(source.at[last], target.at[last], sems.at[ny, i])
        for i, (source, target) in enumerate(pairs)
    ]

    @pl.when(y == 0)
    def _():
        for copy in ends:
            copy.start()

    ahead(fetch, ny, DEPTH)
    cols = cols_ref[...]
    back_cols = back_cols_ref[...]
    back_rows = back_rows_ref[...]

    @pl.when(y == 0)
    def _():
        for copy in ends:
            copy.wait()
        lines = jnp.concatenate([own[last], other[last]], axis=0)
        edge = dot(jnp.concatenate([lines[:, :N], lines[:, N:]], axis=0), cols[:N])
        quarter = edge.reshape(4, last, 2 * N)
        low = times_conj(quarter[0], quarter[1], sign)
        high = times_conj(quarter[2], quarter[3], sign)
        back = dot(jnp.concatenate([low, high], axis=0), back_cols[:, :N])
        sides[...] = back.reshape(sides.shape)

    shift_rows = lax.broadcasted_iota(jnp.int32, (N, N), 0)
    offset_rows = (((shift_rows + HALF) % N) - HALF).astype(jnp.float32)
    offset_rows = jnp.concatenate([offset_rows, offset_rows], axis=1)
    step = 4
    for first in range(0, patches, step):
        here = pl.ds(y * patches + first, step)
        a = own[here].reshape(step * HALF, 2 * N).astype(jnp.float32)
        b = other[here].reshape(step * HALF, 2 * N).astype(jnp.float32)
        back = dot(times_conj(a, b, sign), back_cols)
        halves = []
        for i in range(step):
            p = first + i
            parts = []
            for side in range(2):
                part = back[i * HALF : (i + 1) * HALF, side * N : (side + 1) * N]
                top = jnp.where(first_row((16, N)), sides[side, y, p : p + 1, :], part[:16])
                parts += [top.astype(jnp.bfloat16), part[16:].astype(jnp.bfloat16)]
            halves.append(jnp.concatenate(parts, axis=0))
        for i in range(0, step, 2):
            corr = dot(back_rows, jnp.concatenate(halves[i : i + 2], axis=1))
            power = corr * corr
            total = power.sum(0, keepdims=True)
            moment = (power * offset_rows).sum(0, keepdims=True)
            for side in range(2):
                p = first + i + side
                sums[y, p : p + 1, :] = total[:, side * N : (side + 1) * N]
                moments[y, p : p + 1, :] = moment[:, side * N : (side + 1) * N]

    @pl.when(y == ny - 1)
    def _():
        lane = lax.broadcasted_iota(jnp.int32, (8, N), 1)
        row = lax.broadcasted_iota(jnp.int32, (8, N), 0)
        offset_cols = (((lane + HALF) % N) - HALF).astype(jnp.float32)
        reduce_by = jnp.where(row == 0, 1.0, jnp.where(row == 1, offset_cols, 0.0))
        over_lanes = lambda m: lax.dot_general(
            reduce_by, m.reshape(last, N), (((1,), (1,)), ((), ())),
            precision=lax.Precision.HIGHEST, preferred_element_type=jnp.float32,
        )
        by_sums = over_lanes(sums[...])
        by_moments = over_lanes(moments[...])
        total = by_sums[0:1] + EPS
        along_rows = by_moments[0:1] / total
        along_cols = by_sums[1:2] / total
        for row in range(ny):
            flow_ref[0, row : row + 1, :] = along_rows[:, row * patches : (row + 1) * patches]
            flow_ref[1, row : row + 1, :] = along_cols[:, row * patches : (row + 1) * patches]


def flow_of(own, other, sign, ny, nx, cols, back_cols, back_rows):
    whole = lambda shape: pl.BlockSpec(shape, lambda y: (0,) * len(shape))
    return pl.pallas_call(
        functools.partial(flow_kernel, sign),
        grid=(ny,),
        in_specs=[
            pl.BlockSpec(memory_space=pl.ANY),
            pl.BlockSpec(memory_space=pl.ANY),
            whole((2 * N, 2 * N)),
            whole((2 * N, 2 * N)),
            whole((N, N)),
        ],
        out_specs=whole((2, ny, nx)),
        out_shape=jax.ShapeDtypeStruct((2, ny, nx), jnp.float32),
        scratch_shapes=[
            pltpu.VMEM(own.shape, own.dtype),
            pltpu.VMEM(own.shape, own.dtype),
            pltpu.VMEM((2, ny, nx, N), jnp.float32),
            pltpu.VMEM((ny, nx, N), jnp.float32),
            pltpu.VMEM((ny, nx, N), jnp.float32),
            pltpu.SemaphoreType.DMA((ny + 1, 2)),
        ],
        compiler_params=pltpu.CompilerParams(vmem_limit_bytes=VMEM),
        cost_estimate=pl.CostEstimate(flops=2_000_000_000, bytes_accessed=4 * MIB, transcendentals=0),
        name="flow",
    )(own, other, *(t.astype(jnp.bfloat16) for t in (cols, back_cols, back_rows)))


def slots_kernel(tile_ref, rows_ref, shifts_ref, count_ref, weight_ref, target_ref, share_ref):
    ny, _, nx = rows_ref.shape[1:]
    tile, tiles = tile_ref[0], tile_ref[1]
    live = [k < count_ref[0] for k in range(K)]
    weights = [jnp.where(live[k], weight_ref[0, :, k, :], 0.0) for k in range(K)]
    total = weights[0] + weights[1] + weights[2] + weights[3]
    share = [(w / total).astype(jnp.bfloat16).astype(jnp.float32) for w in weights]
    columns = [lax.broadcasted_iota(jnp.int32, (ny, nx), 1) + shifts_ref[0, :, k, :] for k in range(K)]
    rows = [rows_ref[0, :, k, :] * ROW for k in range(K)]
    low = [c < 0 for c in columns]
    high = [c >= nx for c in columns]
    first, last = tile == 0, tile == tiles - 1
    inside = [jnp.where(l | h, 0.0, s) for l, h, s in zip(low, high, share, strict=True)]
    share_low = [jnp.where(first, 0.0, jnp.where(l, s, 0.0)) for l, s in zip(low, share, strict=True)]
    share_high = [jnp.where(last, 0.0, jnp.where(h, s, 0.0)) for h, s in zip(high, share, strict=True)]
    beyond = [l + h for l, h in zip(share_low, share_high, strict=True)]
    share_ref[...] = jnp.concatenate(inside + beyond, axis=1)
    target = [r + jnp.where(l | h, 0, c) for r, c, l, h in zip(rows, columns, low, high, strict=True)]
    away = [
        r + jnp.where(l, c + HB, jnp.where(h, c - nx + HB, 0))
        for r, c, l, h in zip(rows, columns, low, high, strict=True)
    ]
    target_ref[...] = jnp.concatenate(target + away, axis=1)


def slots_of(tile, box_row, box_shift, box_count, blend_weight):
    ny = box_row.shape[1]
    slots_first = lambda x: jnp.transpose(x, (0, 1, 3, 2))
    return pl.pallas_call(
        slots_kernel,
        in_specs=[pl.BlockSpec(memory_space=pltpu.SMEM)] + [pl.BlockSpec(memory_space=pltpu.VMEM)] * 4,
        out_shape=[
            jax.ShapeDtypeStruct((ny, N), jnp.int32),
            jax.ShapeDtypeStruct((ny, N), jnp.float32),
        ],
        compiler_params=pltpu.CompilerParams(vmem_limit_bytes=VMEM),
        name="slots",
    )(tile, slots_first(box_row), slots_first(box_shift), box_count, slots_first(blend_weight))


def blend_cell(y, first, nx, target_ref, share_ref, window):
    total = None
    for k in range(K):
        spot = target_ref[y, first + k * nx]
        piece = window[spot // ROW, spot % ROW].astype(jnp.float32) * share_ref[y, first + k * nx]
        total = piece if total is None else total + piece
    return total


def blend_kernel(target_ref, share_ref, x_hbm, out_hbm, window, staging, out, in_sems, out_sems):
    y = pl.program_id(0)
    ny, nx = staging.shape[:2]

    @pl.when(y == 0)
    def _():
        copies = [
            pltpu.make_async_copy(x_hbm.at[0, row], staging.at[row], in_sems.at[row]) for row in range(ny)
        ]
        for copy in copies:
            copy.start()
        for row, copy in enumerate(copies):
            copy.wait()
            for x in range(nx):
                window[row, x] = staging[row, x].astype(jnp.bfloat16)

    for x in range(nx):
        out[y, x] = blend_cell(y, x, nx, target_ref, share_ref, window)
    store = lambda row: pltpu.make_async_copy(out.at[row], out_hbm.at[row], out_sems.at[row])
    store(y).start()
    wait_all([store(row) for row in range(ny)])


def blend(target, share, sections):
    _, ny, nx, _, _ = sections.shape
    shape = sections.shape[1:]
    return pl.pallas_call(
        blend_kernel,
        grid=(ny,),
        in_specs=[pl.BlockSpec(memory_space=pltpu.SMEM)] * 2 + [pl.BlockSpec(memory_space=pl.ANY)],
        out_specs=pl.BlockSpec(memory_space=pl.ANY),
        out_shape=jax.ShapeDtypeStruct(shape, jnp.float32),
        scratch_shapes=[
            pltpu.VMEM(shape, jnp.bfloat16),
            pltpu.VMEM(shape, jnp.float32),
            pltpu.VMEM(shape, jnp.float32),
            pltpu.SemaphoreType.DMA((ny,)),
            pltpu.SemaphoreType.DMA((ny,)),
        ],
        compiler_params=pltpu.CompilerParams(vmem_limit_bytes=VMEM),
        cost_estimate=pl.CostEstimate(flops=20_000_000, bytes_accessed=16 * MIB, transcendentals=0),
        name="blend",
    )(target, share, sections)


def relax(low_ref, high_ref, mask_ref, left_ref, right_ref):
    ny, nx = mask_ref.shape[1:]
    rest = jnp.zeros((ny, N - nx - 2 * STEPS), jnp.float32)

    def across(left, own, right):
        return jnp.concatenate([left[:, nx - STEPS :], own, right[:, :STEPS], rest], axis=1)

    known = across(left_ref[2], mask_ref[0].astype(jnp.float32) + 1.0, right_ref[2])
    valid = jnp.where(known > 0.5, 1.0, 0.0)
    trust = jnp.where(known > 1.5, 1.0, 0.0)
    row = lax.broadcasted_iota(jnp.int32, trust.shape, 0)
    fields = []
    for component in range(2):
        own = jnp.concatenate([low_ref[component], high_ref[component]], axis=0)
        flow = across(left_ref[component], own, right_ref[component])
        field = trust * flow
        for _ in range(STEPS):
            below = jnp.where(row == 0, 0.0, pltpu.roll(field, 1, 0))
            above = jnp.where(row == ny - 1, 0.0, pltpu.roll(field, ny - 1, 0))
            beside = pltpu.roll(field, 1, 1) + pltpu.roll(field, N - 1, 1)
            lap = above + below + beside - 4.0 * field
            field = (field + SPRING * (lap + trust * (flow - field))) * valid
        fields.append(field)
    return fields


def warp_kernel(tile_ref, target_ref, share_ref, *refs):
    *flows, blended_hbm, on_hbm, off_hbm, out_hbm, field_ref, window, padded, out, wide, field, in_sems, out_sems = refs
    y = pl.program_id(0)
    ny, nx = out.shape[:2]
    even = tile_ref[0] % 2 == 0
    halos = {
        True: ((on_hbm, HB), (off_hbm.at[0], 0)),
        False: ((on_hbm, 0), (off_hbm.at[1], HB)),
    }
    halo_copies = {
        side: [
            pltpu.make_async_copy(ref, window.at[:, into : into + HB], in_sems.at[ny + i])
            for i, (ref, into) in enumerate(places)
        ]
        for side, places in halos.items()
    }
    fetch = lambda row: [
        pltpu.make_async_copy(blended_hbm.at[row], padded.at[row, :, PAD : PAD + N], in_sems.at[row])
    ]

    @pl.when((y == 0) & even)
    def _():
        for copy in halo_copies[True]:
            copy.start()

    @pl.when((y == 0) & jnp.logical_not(even))
    def _():
        for copy in halo_copies[False]:
            copy.start()

    padded[y, :, :PAD] = jnp.zeros((nx, PAD, N), jnp.float32)
    padded[y, :, PAD + N :] = jnp.zeros((nx, PAD, N), jnp.float32)

    @pl.when(y == 0)
    def _():
        for component, values in enumerate(relax(*flows)):
            wide[component] = values
            field_ref[0, component] = values[:, STEPS : STEPS + nx]
        scalars = pltpu.make_async_copy(wide, field, in_sems.at[ny + 2])
        scalars.start()
        scalars.wait()
        for copy in halo_copies[True]:
            copy.wait()

    ahead(fetch, ny, DEPTH)
    for x in (*range(HB), *range(nx - HB, nx)):
        more = blend_cell(y, K * nx + x, nx, target_ref, share_ref, window)
        padded[y, x, PAD : PAD + N] += more
    apart = lax.broadcasted_iota(jnp.int32, (N, N), 0) - lax.broadcasted_iota(jnp.int32, (N, N), 1)
    apart = apart.astype(jnp.float32)
    for x in range(nx):
        shift = field[0, y, STEPS + x]
        down = jnp.clip((shift + 256.0).astype(jnp.int32) - 256, 4 - PAD, PAD - 6)
        part = shift - down.astype(jnp.float32)
        upper = padded[y, x, pl.ds(PAD + down, N), :]
        lower = padded[y, x, pl.ds(PAD + 1 + down, N), :]
        image = upper + part * (lower - upper)
        hat = jnp.maximum(0.0, 1.0 - jnp.abs(apart - field[1, y, STEPS + x])).astype(jnp.bfloat16)
        warped = dot(jnp.concatenate(split(image), axis=1), jnp.concatenate([hat, hat], axis=0))
        out[y, x] = warped.astype(jnp.bfloat16)
    store = lambda row: pltpu.make_async_copy(out.at[row], out_hbm.at[0, row], out_sems.at[row])
    store(y).start()
    wait_all([store(row) for row in range(ny)])


def warp(tile, target, share, flows, blended, on, off):
    ny, nx = blended.shape[:2]
    whole = lambda shape: pl.BlockSpec(shape, lambda y: (0,) * len(shape))
    return pl.pallas_call(
        warp_kernel,
        grid=(ny,),
        in_specs=[pl.BlockSpec(memory_space=pltpu.SMEM)] * 3
        + [whole(x.shape) for x in flows]
        + [pl.BlockSpec(memory_space=pl.ANY)] * 3,
        out_specs=[pl.BlockSpec(memory_space=pl.ANY), whole((1, 2, ny, nx))],
        out_shape=[
            jax.ShapeDtypeStruct((1, ny, nx, N, N), jnp.bfloat16),
            jax.ShapeDtypeStruct((1, 2, ny, nx), jnp.float32),
        ],
        scratch_shapes=[
            pltpu.VMEM((ny, 2 * HB, N, N), jnp.bfloat16),
            pltpu.VMEM((ny, nx, 2 * PAD + N, N), jnp.float32),
            pltpu.VMEM((ny, nx, N, N), jnp.bfloat16),
            pltpu.VMEM((2, ny, N), jnp.float32),
            pltpu.SMEM((2, ny, N), jnp.float32),
            pltpu.SemaphoreType.DMA((ny + 3,)),
            pltpu.SemaphoreType.DMA((ny,)),
        ],
        compiler_params=pltpu.CompilerParams(vmem_limit_bytes=VMEM),
        cost_estimate=pl.CostEstimate(flops=20_000_000, bytes_accessed=12 * MIB, transcendentals=0),
        name="warp",
    )(tile, target, share, *flows, blended, on, off)


def from_behind(x, axis, by):
    length = lax.axis_size(axis)
    pairs = [(i, i + by) for i in range(length) if 0 <= i + by < length]
    return lax.ppermute(x, axis, pairs)


def swapped(x):
    pairs = [(i, i ^ 1) for i in range(lax.axis_size("tile"))]
    return lax.ppermute(x, "tile", pairs)


def gathered_across(x):
    tiles = lax.axis_size("tile")
    groups = [[i, (i + 1) % tiles] for i in range(1, tiles, 2)]
    return lax.all_gather(x, "tile", axis_index_groups=groups)


def per_device(sections, node_mask, box_row, box_shift, box_count, blend_weight):
    ny, nx = sections.shape[1:3]
    rows, cols, back_cols, back_rows = tables()
    half = ny // 2
    index = lax.axis_index("tile")
    odd = index % 2
    tile = jnp.stack([index, lax.axis_size("tile")]).astype(jnp.int32)

    def edge(high):
        strip = lax.dynamic_slice_in_dim(sections[0], high * (nx - HB), HB, axis=1)
        return strip.astype(jnp.bfloat16)

    edge_off, edge_on = edge(odd), edge(1 - odd)
    edge_off, edge_on, sections = lax.optimization_barrier((edge_off, edge_on, sections))
    off = gathered_across(edge_off)
    on = swapped(edge_on)

    spectra_low, spectra_high = forward(sections, rows, cols)
    from_last = from_behind(spectra_high, "sec", 1)
    from_next = from_behind(spectra_low, "sec", -1)
    target, share = slots_of(tile, box_row, box_shift, box_count, blend_weight)
    blended = blend(target, share, sections)
    from_last, blended = lax.optimization_barrier((from_last, blended))

    flow_high = flow_of(spectra_high, from_last, -1, half, nx, cols, back_cols, back_rows)
    flow_high = from_behind(flow_high, "sec", -1)
    flow_low = flow_of(spectra_low, from_next, 1, half, nx, cols, back_cols, back_rows)
    flow = jnp.concatenate([flow_low, flow_high], axis=1)
    flow = jnp.concatenate([flow, node_mask.astype(jnp.float32) + 1.0], axis=0)
    flow_left = from_behind(flow, "tile", 1)
    flow_right = from_behind(flow, "tile", -1)
    flows = (flow_low, flow_high, node_mask, flow_left, flow_right)
    return tuple(warp(tile, target, share, flows, blended, on, off))


def solution(mesh):
    return jax.shard_map(
        per_device,
        mesh=mesh,
        in_specs=(
            P("sec", None, "tile", None, None),
            P("sec", None, "tile"),
            P("sec", None, "tile", None),
            P("sec", None, "tile", None),
            P("sec", None, "tile"),
            P("sec", None, "tile", None),
        ),
        out_specs=(P("sec", None, "tile", None, None), P("sec", None, None, "tile")),
        check_vma=False,
    )
```

time: 101 us -> 114 us (1.13); the launches traced: 101 us -> 112 us
  between operations: 0.82 us -> 14.2 us
  starting transfers between devices: 26.1 us -> 20.1 us
  waiting for transfers between devices: 23.5 us -> 28.3 us
    ppermute x7 -> x5, starting transfers between devices: 26.1 us -> 17.8 us  [from_behind(): return lax.ppermute(x, axis, pairs)]
    ppermute x7 -> x5, waiting for transfers between devices: 23.5 us -> 28.3 us  [from_behind(): return lax.ppermute(x, axis, pairs)]
    unnamed x16 -> x12, local copies, waits for them, and re-layouts: 4.89 us -> 2 us
    convert_element_type x0 -> x1, local copies, waits for them, and re-layouts: none -> 2.52 us  [edge(): return strip.astype(jnp.bfloat16)]
    ppermute x0 -> x1, starting transfers between devices: none -> 2.21 us  [swapped(): return lax.ppermute(x, 'tile', pairs)]
    pallas_call x2 -> x1, Pallas kernels: 3.19 us -> 1.52 us  [slots_of(): pl.pallas_call(slots_kernel, in_specs=[pl.BlockSpec(memory_space=pltpu.SM...]
  transfers between devices with their start and end apart: 7 -> 7, of which waited for: 1 -> 2; matrix products, arithmetic and copies ran while one was open for 1% -> 1% of each run, Pallas kernels for 25% -> 22%
where the time goes in v2:
time: 114 us; the launch traced here: 112 us
  Pallas kernels  43.9 us (39%)
  waiting for transfers between devices  28.3 us (25%)
  starting transfers between devices  20.1 us (18%)
  between operations  14.2 us (12%)
  local copies, waits for them, and re-layouts  4.52 us (4%)
  other arithmetic  1.3 us (1%)
    ppermute x5, waiting for transfers between devices, from_behind(): return lax.ppermute(x, axis, pairs)  28.3 us
    ppermute x5, starting transfers between devices, from_behind(): return lax.ppermute(x, axis, pairs)  17.8 us
    pallas_call x2, Pallas kernels, flow_of(): pl.pallas_call(functools.partial(flow_kernel, sign), grid=(ny,), in_specs...  13.3 us
    pallas_call x1, Pallas kernels, warp(): pl.pallas_call(warp_kernel, grid=(ny,), in_specs=[pl.BlockSpec(memory_spa...  11.3 us
    pallas_call x1, Pallas kernels, blend(): pl.pallas_call(blend_kernel, grid=(ny,), in_specs=[pl.BlockSpec(memory_sp...  9.48 us
    pallas_call x1, Pallas kernels, forward(): pl.pallas_call(forward_kernel, grid=(ny,), in_specs=[pl.BlockSpec(memory_...  8.26 us
    convert_element_type x1, local copies, waits for them, and re-layouts, edge(): return strip.astype(jnp.bfloat16)  2.52 us
  transfers between devices with their start and end apart: 7, of which 2 were waited for; matrix products, arithmetic and copies ran while one was open for 1% of the time, Pallas kernels for 22%

profile of v2, /device:TPU:66, one launch (start us, length us, event | category | flops | bytes accessed | tf_op | source)
XLA Modules:
  0.0 112.3 jit_solution(8941939313405050149)
XLA Ops:
  7.2 0.0 all-gather.3.cloned.1.call-start
  7.2 2.5 %fusion.1 = (bf16[8,2,128,128]{3,2,1,0:T(8,128)(2,1)S(1)}, bf16[8,2,128,128]{3,2,1,0:T(8,128)(2,1)}) fusion(f32[1,8,16,128,128]{4,3,2,1,0:T(8,128)} %x_hbm.1, s32[]{:T(128)S(6)} %select_n.15, s32[]{:T(128)S(6)} %select_n.14), kind=kLoop, calls=%fused_computation.3 | loop fusion | bytes 2097160 | tf_op jit(solution)/shard_map/convert_element_type | solution.py:515
  9.8 8.3 %forward.1 = (bf16[65,64,256]{2,1,0:T(8,128)(2,1)}, bf16[65,64,256]{2,1,0:T(8,128)(2,1)}) custom-call(f32[1,8,16,128,128]{4,3,2,1,0:T(8,128)} %x_hbm.1, bf16[128,256]{1,0:T(8,128)(2,1)} %constant.48.rows_ref, bf16[256,256]{1,0:T(8,128)(2,1)} %constant.49.cols_ref), custom_call_target="tpu_custom_call" | custom-call | flops 4000000000 | bytes 12582912 | tf_op jit(solution)/shard_map/forward/pallas_call | solution.py:129
  18.0 1.9 %collective-permute-start.1 = (bf16[65,64,256]{2,1,0:T(8,128)(2,1)}, bf16[65,64,256]{2,1,0:T(8,128)(2,1)}, u32[]{:S(2)}, u32[]{:S(2)}) collective-permute-start(bf16[65,64,256]{2,1,0:T(8,128)(2,1)} %get-tuple-element.15.own_hbm), channel_id=1, source_target_pairs={{0,8},{8,16},{16,24},{24,32},{32,40},{40,48},{48,56},{56,64},{64,7... | collective-permute-start | bytes 6389768 | tf_op jit(solution)/shard_map/ppermute | solution.py:491
  20.0 5.8 %collective-permute-start = (bf16[65,64,256]{2,1,0:T(8,128)(2,1)}, bf16[65,64,256]{2,1,0:T(8,128)(2,1)S(1)}, u32[]{:S(2)}, u32[]{:S(2)}) collective-permute-start(bf16[65,64,256]{2,1,0:T(8,128)(2,1)} %get-tuple-element.14.own_hbm), channel_id=1, source_target_pairs={{8,0},{16,8},{24,16},{32,24},{40,32},{48,40},{56,48},{64,56},{72,6... | collective-permute-start | bytes 6389768 | tf_op jit(solution)/shard_map/ppermute | solution.py:491
  25.7 0.0 all-gather.3.cloned.1.call-update
  25.7 2.2 %collective-permute-start.5 = (bf16[8,2,128,128]{3,2,1,0:T(8,128)(2,1)S(1)}, bf16[8,2,128,128]{3,2,1,0:T(8,128)(2,1)S(1)}, u32[]{:S(2)}, u32[]{:S(2)}) collective-permute-start(bf16[8,2,128,128]{3,2,1,0:T(8,128)(2,1)S(1)} %get-tuple-element.18), channel_id=1, source_target_pairs={{0,1},{1,0},{2,3},{3,2},{4,5},{5,4},{6,7},{7,6},{8,9},{9,8},{10,11... | collective-permute-start | bytes 1572872 | tf_op jit(solution)/shard_map/ppermute | solution.py:496
  27.9 0.0 copy-done.1
  27.9 0.6 pad_add_fusion.tile_ref
  28.6 1.5 %slots.1 = (s32[8,128]{1,0:T(8,128)}, f32[8,128]{1,0:T(8,128)}) custom-call(s32[2]{0:T(128)} %pad_add_fusion.tile_ref, s32[1,8,4,16]{3,2,1,0:T(4,128)} %bitcast.10, s32[1,8,4,16]{3,2,1,0:T(4,128)} %bitcast.11, s32[1,8,16]{2,1,0:T(8,128)} %count_ref.1, f32[1,8,4,16]{3,2,1,0:T(4,128)} %bitcast.12), custom_call_target="tpu_custom_call" | custom-call | tf_op jit(solution)/shard_map/slots/pallas_call | solution.py:302
  30.1 9.5 %blend.1.refs_5_ = f32[8,16,128,128]{3,2,1,0:T(8,128)} custom-call(s32[8,128]{1,0:T(8,128)} %get-tuple-element.11.target_ref, f32[8,128]{1,0:T(8,128)} %get-tuple-element.12.share_ref, f32[1,8,16,128,128]{4,3,2,1,0:T(8,128)} %x_hbm.1), custom_call_target="tpu_custom_call" | custom-call | flops 20000000 | bytes 16777216 | tf_op jit(solution)/shard_map/blend/pallas_call | solution.py:349
  39.6 25.4 %collective-permute-done.1.other_hbm = bf16[65,64,256]{2,1,0:T(8,128)(2,1)} collective-permute-done((bf16[65,64,256]{2,1,0:T(8,128)(2,1)}, bf16[65,64,256]{2,1,0:T(8,128)(2,1)}, u32[]{:S(2)}, u32[]{:S(2)}) %collective-permute-start.1) | collective-permute-done | bytes 2129952 | tf_op jit(solution)/shard_map/ppermute | solution.py:491
  65.0 6.7 %flow.3 = f32[2,4,16]{2,1,0:T(4,128)} custom-call(bf16[65,64,256]{2,1,0:T(8,128)(2,1)} %get-tuple-element.15.own_hbm, bf16[65,64,256]{2,1,0:T(8,128)(2,1)} %collective-permute-done.1.other_hbm, bf16[256,256]{1,0:T(8,128)(2,1)} %constant.49.cols_ref, bf16[256,256]{1,0:T(8,128)(2,1)} %constant.50.back_cols_ref, bf16[128,128]{1,0:T(8,128)(2,1)} %constant.51.back_rows_ref), custom_call_target="tpu_custom_call" | custom-call | flops 2000000000 | bytes 4194304 | tf_op jit(solution)/shard_map/flow/pallas_call | solution.py:248
  71.7 1.9 %collective-permute-start.2 = (f32[2,4,16]{2,1,0:T(4,128)}, f32[2,4,16]{2,1,0:T(4,128)S(1)}, u32[]{:S(2)}, u32[]{:S(2)}) collective-permute-start(f32[2,4,16]{2,1,0:T(4,128)} %flow.3), channel_id=1, source_target_pairs={{8,0},{16,8},{24,16},{32,24},{40,32},{48,40},{56,48},{64,56},{72,6... | collective-permute-start | bytes 1544 | tf_op jit(solution)/shard_map/ppermute | solution.py:491
  73.6 0.0 collective-permute-done.other_hbm
  73.6 0.0 copy-start.5
  73.6 1.4 %copy-done.5 = bf16[65,64,256]{2,1,0:T(8,128)(2,1)} copy-done((bf16[65,64,256]{2,1,0:T(8,128)(2,1)}, bf16[65,64,256]{2,1,0:T(8,128)(2,1)S(1)}, u32[]{:S(2)}) %copy-start.5) | copy-done | bytes 2129944
  75.0 6.7 %flow.2.refs_0_ = f32[2,4,16]{2,1,0:T(4,128)} custom-call(bf16[65,64,256]{2,1,0:T(8,128)(2,1)} %get-tuple-element.14.own_hbm, bf16[65,64,256]{2,1,0:T(8,128)(2,1)} %copy-done.5, bf16[256,256]{1,0:T(8,128)(2,1)} %constant.49.cols_ref, bf16[256,256]{1,0:T(8,128)(2,1)} %constant.50.back_cols_ref, bf16[128,128]{1,0:T(8,128)(2,1)} %constant.51.back_rows_ref), custom_call_target="tpu_custom_call" | custom-call | flops 2000000000 | bytes 4194304 | tf_op jit(solution)/shard_map/flow/pallas_call | solution.py:248
  81.7 0.0 collective-permute-done.2.refs_1_
  81.7 0.0 copy-start.2
  81.7 0.7 pad_maximum_fusion
  82.4 4.0 %collective-permute-start.3 = (f32[3,8,16]{2,1,0:T(8,128)S(1)}, f32[3,8,16]{2,1,0:T(8,128)S(1)}, u32[]{:S(2)}, u32[]{:S(2)}) collective-permute-start(f32[3,8,16]{2,1,0:T(8,128)S(1)} %pad_maximum_fusion), channel_id=1, source_target_pairs={{0,1},{1,2},{2,3},{3,4},{4,5},{5,6},{6,7},{8,9},{9,10},{10,11},{11... | collective-permute-start | bytes 4616 | tf_op jit(solution)/shard_map/ppermute | solution.py:491
  86.4 4.2 %collective-permute-start.4 = (f32[3,8,16]{2,1,0:T(8,128)S(1)}, f32[3,8,16]{2,1,0:T(8,128)S(1)}, u32[]{:S(2)}, u32[]{:S(2)}) collective-permute-start(f32[3,8,16]{2,1,0:T(8,128)S(1)} %pad_maximum_fusion), channel_id=1, source_target_pairs={{1,0},{2,1},{3,2},{4,3},{5,4},{6,5},{7,6},{9,8},{10,9},{11,10},{12... | collective-permute-start | bytes 4616 | tf_op jit(solution)/shard_map/ppermute | solution.py:491
  90.7 0.0 collective-permute-done.5.refs_6_
  90.7 0.0 all-gather.3.cloned.1.call-done
  90.7 0.0 collective-permute-done.3.refs_3_
  90.7 0.0 copy-start.3
  90.7 2.8 %collective-permute-done.4.refs_4_ = f32[3,8,16]{2,1,0:T(8,128)S(1)} collective-permute-done((f32[3,8,16]{2,1,0:T(8,128)S(1)}, f32[3,8,16]{2,1,0:T(8,128)S(1)}, u32[]{:S(2)}, u32[]{:S(2)}) %collective-permute-start.4) | collective-permute-done | bytes 1568 | tf_op jit(solution)/shard_map/ppermute | solution.py:491
  93.5 0.0 copy-done.2
  93.5 0.0 copy-done.3
  93.5 0.6 copy-done.4
  94.1 11.3 %warp.1 = (bf16[1,8,16,128,128]{4,3,2,1,0:T(8,128)(2,1)}, f32[1,2,8,16]{3,2,1,0:T(8,128)}) custom-call(s32[2]{0:T(128)} %pad_add_fusion.tile_ref, s32[8,128]{1,0:T(8,128)} %get-tuple-element.11.target_ref, f32[8,128]{1,0:T(8,128)} %get-tuple-element.12.share_ref, f32[2,4,16]{2,1,0:T(4,128)} %flow.2.refs_0_, f32[2,4,16]{2,1,0:T(4,128)} %copy-done.2, ...), custom_call_target="tpu_custom_call" | custom-call | flops 20000000 | bytes 12582912 | tf_op jit(solution)/shard_map/warp/pallas_call | solution.py:462
  (5 shorter events, 0.0 us)
Async XLA Ops:
  7.2 83.5 %all-gather.3.cloned.1.call-start = ((), (), s32[]{:S(2)}) async-start(), calls=%async_computation | async-start | bytes 1572864 | tf_op jit(solution)/shard_map/all_gather | solution.py:502
  9.8 18.2 %copy-start.1 = (s32[1,8,16]{2,1,0:T(8,128)S(1)}, s32[1,8,16]{2,1,0:T(8,128)}, u32[]{:S(2)}) copy-start(s32[1,8,16]{2,1,0:T(8,128)} %refs_2_.1) | copy-start | bytes 1540
  18.0 47.0 %collective-permute-start.1 = (bf16[65,64,256]{2,1,0:T(8,128)(2,1)}, bf16[65,64,256]{2,1,0:T(8,128)(2,1)}, u32[]{:S(2)}, u32[]{:S(2)}) collective-permute-start(bf16[65,64,256]{2,1,0:T(8,128)(2,1)} %get-tuple-element.15.own_hbm), channel_id=1, source_target_pairs={{0,8},{8,16},{16,24},{24,32},{32,40},{40,48},{48,56},{56,64},{64,7... | collective-permute-start | bytes 6389768 | tf_op jit(solution)/shard_map/ppermute | solution.py:491
  20.0 53.7 %collective-permute-start = (bf16[65,64,256]{2,1,0:T(8,128)(2,1)}, bf16[65,64,256]{2,1,0:T(8,128)(2,1)S(1)}, u32[]{:S(2)}, u32[]{:S(2)}) collective-permute-start(bf16[65,64,256]{2,1,0:T(8,128)(2,1)} %get-tuple-element.14.own_hbm), channel_id=1, source_target_pairs={{8,0},{16,8},{24,16},{32,24},{40,32},{48,40},{56,48},{64,56},{72,6... | collective-permute-start | bytes 6389768 | tf_op jit(solution)/shard_map/ppermute | solution.py:491
  25.7 64.9 %collective-permute-start.5 = (bf16[8,2,128,128]{3,2,1,0:T(8,128)(2,1)S(1)}, bf16[8,2,128,128]{3,2,1,0:T(8,128)(2,1)S(1)}, u32[]{:S(2)}, u32[]{:S(2)}) collective-permute-start(bf16[8,2,128,128]{3,2,1,0:T(8,128)(2,1)S(1)} %get-tuple-element.18), channel_id=1, source_target_pairs={{0,1},{1,0},{2,3},{3,2},{4,5},{5,4},{6,7},{7,6},{8,9},{9,8},{10,11... | collective-permute-start | bytes 1572872 | tf_op jit(solution)/shard_map/ppermute | solution.py:496
  71.7 10.0 %collective-permute-start.2 = (f32[2,4,16]{2,1,0:T(4,128)}, f32[2,4,16]{2,1,0:T(4,128)S(1)}, u32[]{:S(2)}, u32[]{:S(2)}) collective-permute-start(f32[2,4,16]{2,1,0:T(4,128)} %flow.3), channel_id=1, source_target_pairs={{8,0},{16,8},{24,16},{32,24},{40,32},{48,40},{56,48},{64,56},{72,6... | collective-permute-start | bytes 1544 | tf_op jit(solution)/shard_map/ppermute | solution.py:491
  73.6 1.4 %copy-start.5 = (bf16[65,64,256]{2,1,0:T(8,128)(2,1)}, bf16[65,64,256]{2,1,0:T(8,128)(2,1)S(1)}, u32[]{:S(2)}) copy-start(bf16[65,64,256]{2,1,0:T(8,128)(2,1)S(1)} %collective-permute-done.other_hbm) | copy-start | bytes 6389764
  81.7 11.8 %copy-start.2 = (f32[2,4,16]{2,1,0:T(4,128)}, f32[2,4,16]{2,1,0:T(4,128)S(1)}, u32[]{:S(2)}) copy-start(f32[2,4,16]{2,1,0:T(4,128)S(1)} %collective-permute-done.2.refs_1_) | copy-start | bytes 1540
  82.4 8.3 %collective-permute-start.3 = (f32[3,8,16]{2,1,0:T(8,128)S(1)}, f32[3,8,16]{2,1,0:T(8,128)S(1)}, u32[]{:S(2)}, u32[]{:S(2)}) collective-permute-start(f32[3,8,16]{2,1,0:T(8,128)S(1)} %pad_maximum_fusion), channel_id=1, source_target_pairs={{0,1},{1,2},{2,3},{3,4},{4,5},{5,6},{6,7},{8,9},{9,10},{10,11},{11... | collective-permute-start | bytes 4616 | tf_op jit(solution)/shard_map/ppermute | solution.py:491
  86.4 7.1 %collective-permute-start.4 = (f32[3,8,16]{2,1,0:T(8,128)S(1)}, f32[3,8,16]{2,1,0:T(8,128)S(1)}, u32[]{:S(2)}, u32[]{:S(2)}) collective-permute-start(f32[3,8,16]{2,1,0:T(8,128)S(1)} %pad_maximum_fusion), channel_id=1, source_target_pairs={{1,0},{2,1},{3,2},{4,3},{5,4},{6,5},{7,6},{9,8},{10,9},{11,10},{12... | collective-permute-start | bytes 4616 | tf_op jit(solution)/shard_map/ppermute | solution.py:491
  90.7 2.9 %copy-start = (bf16[8,2,128,128]{3,2,1,0:T(8,128)(2,1)}, bf16[8,2,128,128]{3,2,1,0:T(8,128)(2,1)S(1)}, u32[]{:S(2)}) copy-start(bf16[8,2,128,128]{3,2,1,0:T(8,128)(2,1)S(1)} %collective-permute-done.5.refs_6_) | copy-start | bytes 1572868
  90.7 2.8 %copy-start.3 = (f32[3,8,16]{2,1,0:T(8,128)}, f32[3,8,16]{2,1,0:T(8,128)S(1)}, u32[]{:S(2)}) copy-start(f32[3,8,16]{2,1,0:T(8,128)S(1)} %collective-permute-done.3.refs_3_) | copy-start | bytes 4612
  93.5 0.6 copy-start.4
Sparse Core Ops, SparseCore 0:
  25.9 29.5 all-gather.2

commit v3 on v2

--- a/solution.py
+++ b/solution.py
@@ -19,7 +19,6 @@
 SPRING = 0.2
 EPS = 1e-06
 MIB = 1024 * 1024
-VMEM = 60 * MIB
 
 
 def split(x):
@@ -67,6 +66,14 @@
         copy.wait()
 
 
+def in_hbm(x):
+    return pltpu.with_memory_space_constraint(x, pltpu.HBM)
+
+
+def in_vmem(x):
+    return pltpu.with_memory_space_constraint(x, pltpu.VMEM)
+
+
 def wait_all(copies):
     @pl.when(pl.program_id(0) == pl.num_programs(0) - 1)
     def _():
@@ -74,12 +81,16 @@
             copy.wait()
 
 
-def forward_kernel(x_hbm, rows_ref, cols_ref, low_hbm, high_hbm, x_ref, lines_ref, ends_ref, spec, in_sems, out_sems):
+def forward_kernel(tile_ref, x_hbm, rows_ref, cols_ref, low_ref, high_ref, on_ref, off_ref, x_ref, lines_ref, ends_ref, in_sems):
     y = pl.program_id(0)
     ny, patches = x_ref.shape[:2]
     half = ny // 2
     fetch = lambda row: [pltpu.make_async_copy(x_hbm.at[0, row], x_ref.at[row], in_sems.at[row])]
     ahead(fetch, ny, DEPTH)
+    odd = tile_ref[0] % 2
+    for i in range(HB):
+        on_ref[y, i] = x_ref[y, (1 - odd) * (patches - HB) + i].astype(jnp.bfloat16)
+        off_ref[y, i] = x_ref[y, odd * (patches - HB) + i].astype(jnp.bfloat16)
 
     rows2 = rows_ref[...]
     cols = cols_ref[...]
@@ -96,31 +107,23 @@
             high, low = split(lines)
             lines_ref[p * HALF : (p + 1) * HALF, : 2 * N] = high
             lines_ref[p * HALF : (p + 1) * HALF, 2 * N :] = low
-    part, row = y // half, y % half
-    step = 4
-    for first in range(0, patches, step):
-        lines = lines_ref[first * HALF : (first + step) * HALF, :]
-        freq = dot(lines, cols2).reshape(step, HALF, 2 * N)
-        spec[part, pl.ds(row * patches + first, step)] = freq.astype(jnp.bfloat16)
+    row = y % half
     last = half * patches
     ends = ends_ref[...].astype(jnp.bfloat16)
-    spec[part, last, pl.ds(pl.multiple_of(row * patches, patches), patches), :] = ends
-
-    def spectra_to(row):
-        first = row % half * patches
-        count = patches + (row % half == half - 1)
-        return pltpu.make_async_copy(
-            spec.at[row // half, pl.ds(first, count)],
-            (low_hbm, high_hbm)[row // half].at[pl.ds(first, count)],
-            out_sems.at[row],
-        )
-
-    for row in range(ny):
-        pl.when(y == row)(spectra_to(row).start)
-    wait_all([spectra_to(row) for row in range(ny)])
-
-
-def forward(sections, rows, cols):
+    step = 4
+
+    def finish(spec_ref):
+        for first in range(0, patches, step):
+            lines = lines_ref[first * HALF : (first + step) * HALF, :]
+            freq = dot(lines, cols2).reshape(step, HALF, 2 * N)
+            spec_ref[pl.ds(row * patches + first, step)] = freq.astype(jnp.bfloat16)
+        spec_ref[last, pl.ds(pl.multiple_of(row * patches, patches), patches), :] = ends
+
+    pl.when(y < half)(lambda: finish(low_ref))
+    pl.when(y >= half)(lambda: finish(high_ref))
+
+
+def forward(tile, sections, rows, cols):
     _, ny, nx, _, _ = sections.shape
     half = ny // 2
     rows2 = jnp.concatenate([rows, rows], axis=1).astype(jnp.bfloat16)
@@ -130,24 +133,23 @@
         forward_kernel,
         grid=(ny,),
         in_specs=[
-            pl.BlockSpec(memory_space=pl.ANY),
+            pl.BlockSpec(memory_space=pltpu.SMEM),
+            pl.BlockSpec(memory_space=pltpu.HBM),
             whole((N, 2 * N)),
             whole((2 * N, 2 * N)),
         ],
-        out_specs=[pl.BlockSpec(memory_space=pl.ANY)] * 2,
-        out_shape=[jax.ShapeDtypeStruct(spectra, jnp.bfloat16)] * 2,
+        out_specs=[pl.BlockSpec(memory_space=pltpu.VMEM)] * 4,
+        out_shape=[pltpu.VMEM(spectra, jnp.bfloat16)] * 2 + [pltpu.VMEM((ny, HB, N, N), jnp.bfloat16)] * 2,
         scratch_shapes=[
             pltpu.VMEM(sections.shape[1:], jnp.float32),
             pltpu.VMEM((nx * HALF, 4 * N), jnp.bfloat16),
             pltpu.VMEM((nx, 2 * N), jnp.float32),
-            pltpu.VMEM((2,) + spectra, jnp.bfloat16),
             pltpu.SemaphoreType.DMA((ny,)),
-            pltpu.SemaphoreType.DMA((ny,)),
-        ],
-        compiler_params=pltpu.CompilerParams(vmem_limit_bytes=VMEM),
+        ],
+        compiler_params=pltpu.CompilerParams(vmem_limit_bytes=20 * MIB),
         cost_estimate=pl.CostEstimate(flops=4_000_000_000, bytes_accessed=12 * MIB, transcendentals=0),
         name="forward",
-    )(sections, rows2, cols.astype(jnp.bfloat16))
+    )(tile, in_hbm(sections), rows2, cols.astype(jnp.bfloat16))
 
 
 def times_conj(a, b, sign):
@@ -157,36 +159,16 @@
     return jnp.concatenate([real, imag], axis=1).astype(jnp.bfloat16)
 
 
-def flow_kernel(sign, own_hbm, other_hbm, cols_ref, back_cols_ref, back_rows_ref, flow_ref, own, other, sides, sums, moments, sems):
+def flow_kernel(sign, own, other, cols_ref, back_cols_ref, back_rows_ref, flow_ref, sides, sums, moments):
     y = pl.program_id(0)
     ny, patches = sums.shape[:2]
     last = ny * patches
-    pairs = ((own_hbm, own), (other_hbm, other))
-    fetch = lambda row: [
-        pltpu.make_async_copy(
-            source.at[pl.ds(row * patches, patches)], target.at[pl.ds(row * patches, patches)], sems.at[row, i]
-        )
-        for i, (source, target) in enumerate(pairs)
-    ]
-    ends = [
-        pltpu.make_async_copy(source.at[last], target.at[last], sems.at[ny, i])
-        for i, (source, target) in enumerate(pairs)
-    ]
-
-    @pl.when(y == 0)
-    def _():
-        for copy in ends:
-            copy.start()
-
-    ahead(fetch, ny, DEPTH)
     cols = cols_ref[...]
     back_cols = back_cols_ref[...]
     back_rows = back_rows_ref[...]
 
     @pl.when(y == 0)
     def _():
-        for copy in ends:
-            copy.wait()
         lines = jnp.concatenate([own[last], other[last]], axis=0)
         edge = dot(jnp.concatenate([lines[:, :N], lines[:, N:]], axis=0), cols[:N])
         quarter = edge.reshape(4, last, 2 * N)
@@ -249,8 +231,8 @@
         functools.partial(flow_kernel, sign),
         grid=(ny,),
         in_specs=[
-            pl.BlockSpec(memory_space=pl.ANY),
-            pl.BlockSpec(memory_space=pl.ANY),
+            pl.BlockSpec(memory_space=pltpu.VMEM),
+            pl.BlockSpec(memory_space=pltpu.VMEM),
             whole((2 * N, 2 * N)),
             whole((2 * N, 2 * N)),
             whole((N, N)),
@@ -258,17 +240,14 @@
         out_specs=whole((2, ny, nx)),
         out_shape=jax.ShapeDtypeStruct((2, ny, nx), jnp.float32),
         scratch_shapes=[
-            pltpu.VMEM(own.shape, own.dtype),
-            pltpu.VMEM(own.shape, own.dtype),
             pltpu.VMEM((2, ny, nx, N), jnp.float32),
             pltpu.VMEM((ny, nx, N), jnp.float32),
             pltpu.VMEM((ny, nx, N), jnp.float32),
-            pltpu.SemaphoreType.DMA((ny + 1, 2)),
-        ],
-        compiler_params=pltpu.CompilerParams(vmem_limit_bytes=VMEM),
+        ],
+        compiler_params=pltpu.CompilerParams(vmem_limit_bytes=8 * MIB),
         cost_estimate=pl.CostEstimate(flops=2_000_000_000, bytes_accessed=4 * MIB, transcendentals=0),
         name="flow",
-    )(own, other, *(t.astype(jnp.bfloat16) for t in (cols, back_cols, back_rows)))
+    )(in_vmem(own), in_vmem(other), *(t.astype(jnp.bfloat16) for t in (cols, back_cols, back_rows)))
 
 
 def slots_kernel(tile_ref, rows_ref, shifts_ref, count_ref, weight_ref, target_ref, share_ref):
@@ -306,7 +285,7 @@
             jax.ShapeDtypeStruct((ny, N), jnp.int32),
             jax.ShapeDtypeStruct((ny, N), jnp.float32),
         ],
-        compiler_params=pltpu.CompilerParams(vmem_limit_bytes=VMEM),
+        compiler_params=pltpu.CompilerParams(vmem_limit_bytes=4 * MIB),
         name="slots",
     )(tile, slots_first(box_row), slots_first(box_shift), box_count, slots_first(blend_weight))
 
@@ -320,9 +299,12 @@
     return total
 
 
-def blend_kernel(target_ref, share_ref, x_hbm, out_hbm, window, staging, out, in_sems, out_sems):
+def blend_kernel(target_ref, share_ref, x_hbm, out_ref, window, staging, in_sems):
     y = pl.program_id(0)
     ny, nx = staging.shape[:2]
+    border = jnp.zeros((nx, PAD, N), jnp.float32)
+    out_ref[y, :, :PAD] = border
+    out_ref[y, :, PAD + N :] = border
 
     @pl.when(y == 0)
     def _():
@@ -337,10 +319,7 @@
                 window[row, x] = staging[row, x].astype(jnp.bfloat16)
 
     for x in range(nx):
-        out[y, x] = blend_cell(y, x, nx, target_ref, share_ref, window)
-    store = lambda row: pltpu.make_async_copy(out.at[row], out_hbm.at[row], out_sems.at[row])
-    store(y).start()
-    wait_all([store(row) for row in range(ny)])
+        out_ref[y, x, PAD : PAD + N] = blend_cell(y, x, nx, target_ref, share_ref, window)
 
 
 def blend(target, share, sections):
@@ -349,20 +328,18 @@
     return pl.pallas_call(
         blend_kernel,
         grid=(ny,),
-        in_specs=[pl.BlockSpec(memory_space=pltpu.SMEM)] * 2 + [pl.BlockSpec(memory_space=pl.ANY)],
-        out_specs=pl.BlockSpec(memory_space=pl.ANY),
-        out_shape=jax.ShapeDtypeStruct(shape, jnp.float32),
+        in_specs=[pl.BlockSpec(memory_space=pltpu.SMEM)] * 2 + [pl.BlockSpec(memory_space=pltpu.HBM)],
+        out_specs=pl.BlockSpec(memory_space=pltpu.VMEM),
+        out_shape=pltpu.VMEM((ny, nx, N + 2 * PAD, N), jnp.float32),
         scratch_shapes=[
             pltpu.VMEM(shape, jnp.bfloat16),
             pltpu.VMEM(shape, jnp.float32),
-            pltpu.VMEM(shape, jnp.float32),
             pltpu.SemaphoreType.DMA((ny,)),
-            pltpu.SemaphoreType.DMA((ny,)),
-        ],
-        compiler_params=pltpu.CompilerParams(vmem_limit_bytes=VMEM),
+        ],
+        compiler_params=pltpu.CompilerParams(vmem_limit_bytes=16 * MIB),
         cost_estimate=pl.CostEstimate(flops=20_000_000, bytes_accessed=16 * MIB, transcendentals=0),
         name="blend",
-    )(target, share, sections)
+    )(target, share, in_hbm(sections))
 
 
 def relax(low_ref, high_ref, mask_ref, left_ref, right_ref):
@@ -392,24 +369,18 @@
 
 
 def warp_kernel(tile_ref, target_ref, share_ref, *refs):
-    *flows, blended_hbm, on_hbm, off_hbm, out_hbm, field_ref, window, padded, out, wide, field, in_sems, out_sems = refs
+    *flows, padded, on_hbm, off_hbm, out_hbm, field_ref, window, edges, out, wide, field, in_sems, out_sems = refs
     y = pl.program_id(0)
     ny, nx = out.shape[:2]
     even = tile_ref[0] % 2 == 0
-    halos = {
-        True: ((on_hbm, HB), (off_hbm.at[0], 0)),
-        False: ((on_hbm, 0), (off_hbm.at[1], HB)),
-    }
+    halos = {True: ((on_hbm, HB), (off_hbm, 0)), False: ((on_hbm, 0), (off_hbm, HB))}
     halo_copies = {
         side: [
-            pltpu.make_async_copy(ref, window.at[:, into : into + HB], in_sems.at[ny + i])
+            pltpu.make_async_copy(ref, window.at[:, into : into + HB], in_sems.at[i])
             for i, (ref, into) in enumerate(places)
         ]
         for side, places in halos.items()
     }
-    fetch = lambda row: [
-        pltpu.make_async_copy(blended_hbm.at[row], padded.at[row, :, PAD : PAD + N], in_sems.at[row])
-    ]
 
     @pl.when((y == 0) & even)
     def _():
@@ -420,33 +391,33 @@
     def _():
         for copy in halo_copies[False]:
             copy.start()
-
-    padded[y, :, :PAD] = jnp.zeros((nx, PAD, N), jnp.float32)
-    padded[y, :, PAD + N :] = jnp.zeros((nx, PAD, N), jnp.float32)
 
     @pl.when(y == 0)
     def _():
         for component, values in enumerate(relax(*flows)):
             wide[component] = values
             field_ref[0, component] = values[:, STEPS : STEPS + nx]
-        scalars = pltpu.make_async_copy(wide, field, in_sems.at[ny + 2])
+        scalars = pltpu.make_async_copy(wide, field, in_sems.at[2])
         scalars.start()
+        edges[:, :PAD] = jnp.zeros((2 * HB, PAD, N), jnp.float32)
+        edges[:, PAD + N :] = jnp.zeros((2 * HB, PAD, N), jnp.float32)
         scalars.wait()
         for copy in halo_copies[True]:
             copy.wait()
 
-    ahead(fetch, ny, DEPTH)
-    for x in (*range(HB), *range(nx - HB, nx)):
+    borders = (*range(HB), *range(nx - HB, nx))
+    for i, x in enumerate(borders):
         more = blend_cell(y, K * nx + x, nx, target_ref, share_ref, window)
-        padded[y, x, PAD : PAD + N] += more
+        edges[i, PAD : PAD + N] = padded[y, x, PAD : PAD + N] + more
     apart = lax.broadcasted_iota(jnp.int32, (N, N), 0) - lax.broadcasted_iota(jnp.int32, (N, N), 1)
     apart = apart.astype(jnp.float32)
     for x in range(nx):
+        cell = edges.at[borders.index(x)] if x in borders else padded.at[y, x]
         shift = field[0, y, STEPS + x]
         down = jnp.clip((shift + 256.0).astype(jnp.int32) - 256, 4 - PAD, PAD - 6)
         part = shift - down.astype(jnp.float32)
-        upper = padded[y, x, pl.ds(PAD + down, N), :]
-        lower = padded[y, x, pl.ds(PAD + 1 + down, N), :]
+        upper = cell[pl.ds(PAD + down, N), :]
+        lower = cell[pl.ds(PAD + 1 + down, N), :]
         image = upper + part * (lower - upper)
         hat = jnp.maximum(0.0, 1.0 - jnp.abs(apart - field[1, y, STEPS + x])).astype(jnp.bfloat16)
         warped = dot(jnp.concatenate(split(image), axis=1), jnp.concatenate([hat, hat], axis=0))
@@ -464,7 +435,8 @@
         grid=(ny,),
         in_specs=[pl.BlockSpec(memory_space=pltpu.SMEM)] * 3
         + [whole(x.shape) for x in flows]
-        + [pl.BlockSpec(memory_space=pl.ANY)] * 3,
+        + [pl.BlockSpec(memory_space=pltpu.VMEM)]
+        + [pl.BlockSpec(memory_space=pl.ANY)] * 2,
         out_specs=[pl.BlockSpec(memory_space=pl.ANY), whole((1, 2, ny, nx))],
         out_shape=[
             jax.ShapeDtypeStruct((1, ny, nx, N, N), jnp.bfloat16),
@@ -472,17 +444,17 @@
         ],
         scratch_shapes=[
             pltpu.VMEM((ny, 2 * HB, N, N), jnp.bfloat16),
-            pltpu.VMEM((ny, nx, 2 * PAD + N, N), jnp.float32),
+            pltpu.VMEM((2 * HB, 2 * PAD + N, N), jnp.float32),
             pltpu.VMEM((ny, nx, N, N), jnp.bfloat16),
             pltpu.VMEM((2, ny, N), jnp.float32),
             pltpu.SMEM((2, ny, N), jnp.float32),
-            pltpu.SemaphoreType.DMA((ny + 3,)),
+            pltpu.SemaphoreType.DMA((3,)),
             pltpu.SemaphoreType.DMA((ny,)),
         ],
-        compiler_params=pltpu.CompilerParams(vmem_limit_bytes=VMEM),
+        compiler_params=pltpu.CompilerParams(vmem_limit_bytes=12 * MIB),
         cost_estimate=pl.CostEstimate(flops=20_000_000, bytes_accessed=12 * MIB, transcendentals=0),
         name="warp",
-    )(tile, target, share, *flows, blended, on, off)
+    )(tile, target, share, *flows, in_vmem(blended), on, off)
 
 
 def from_behind(x, axis, by):
@@ -491,43 +463,47 @@
     return lax.ppermute(x, axis, pairs)
 
 
-def swapped(x):
-    pairs = [(i, i ^ 1) for i in range(lax.axis_size("tile"))]
-    return lax.ppermute(x, "tile", pairs)
-
-
-def gathered_across(x):
-    tiles = lax.axis_size("tile")
-    groups = [[i, (i + 1) % tiles] for i in range(1, tiles, 2)]
-    return lax.all_gather(x, "tile", axis_index_groups=groups)
+def hops(tiles, sections, across):
+    pairs = ([], [])
+    for section in range(sections):
+        x_low, rest = divmod(section, sections // 2)
+        way = 1 if rest < sections // 4 else -1
+        for tile in range(tiles):
+            z, x_high = divmod(tile, 2)
+            ends = [section * tiles + tile]
+            for hop in (1, 2):
+                x = (2 * x_high + x_low + hop * way) % 4
+                to_z = (z + 2 * x_high - 1) % (tiles // 2) if across and hop == 2 else z
+                ends.append((x % 2 * (sections // 2) + rest) * tiles + 2 * to_z + x // 2)
+            pairs[0].append((ends[0], ends[1]))
+            pairs[1].append((ends[1], ends[2]))
+    return pairs
 
 
 def per_device(sections, node_mask, box_row, box_shift, box_count, blend_weight):
     ny, nx = sections.shape[1:3]
     rows, cols, back_cols, back_rows = tables()
     half = ny // 2
-    index = lax.axis_index("tile")
-    odd = index % 2
-    tile = jnp.stack([index, lax.axis_size("tile")]).astype(jnp.int32)
-
-    def edge(high):
-        strip = lax.dynamic_slice_in_dim(sections[0], high * (nx - HB), HB, axis=1)
-        return strip.astype(jnp.bfloat16)
-
-    edge_off, edge_on = edge(odd), edge(1 - odd)
-    edge_off, edge_on, sections = lax.optimization_barrier((edge_off, edge_on, sections))
-    off = gathered_across(edge_off)
-    on = swapped(edge_on)
-
-    spectra_low, spectra_high = forward(sections, rows, cols)
+    tiles, count = lax.axis_size("tile"), lax.axis_size("sec")
+    tile = jnp.stack([lax.axis_index("tile"), tiles]).astype(jnp.int32)
+    on_hops, off_hops = hops(tiles, count, False), hops(tiles, count, True)
+    hop = lambda x, pairs: lax.ppermute(x, ("sec", "tile"), pairs)
+
+    spectra_low, spectra_high, on, off = forward(tile, sections, rows, cols)
     from_last = from_behind(spectra_high, "sec", 1)
     from_next = from_behind(spectra_low, "sec", -1)
+    off = hop(off, off_hops[0])
+    on = hop(on, on_hops[0])
     target, share = slots_of(tile, box_row, box_shift, box_count, blend_weight)
     blended = blend(target, share, sections)
+    off, blended = lax.optimization_barrier((off, blended))
+    off = hop(off, off_hops[1])
     from_last, blended = lax.optimization_barrier((from_last, blended))
 
     flow_high = flow_of(spectra_high, from_last, -1, half, nx, cols, back_cols, back_rows)
+    on, flow_high = lax.optimization_barrier((on, flow_high))
     flow_high = from_behind(flow_high, "sec", -1)
+    on = hop(on, on_hops[1])
     flow_low = flow_of(spectra_low, from_next, 1, half, nx, cols, back_cols, back_rows)
     flow = jnp.concatenate([flow_low, flow_high], axis=1)
     flow = jnp.concatenate([flow, node_mask.astype(jnp.float32) + 1.0], axis=0)

time: 114 us -> 76.1 us (0.67)
  the two profiles are of different devices: /device:TPU:66 before, /device:TPU:0 now
where the time goes in v3:
time: 76.1 us; the launch traced here: 75.8 us
  Pallas kernels  34.2 us (45%)
  starting transfers between devices  19.5 us (26%)
  waiting for transfers between devices  19.5 us (26%)
  local copies, waits for them, and re-layouts  1.78 us (2%)
    ppermute x4, waiting for transfers between devices, per_device(): hop = lambda x, pairs: lax.ppermute(x, ('sec', 'tile'), pairs)  13 us
    ppermute x5, starting transfers between devices, from_behind(): return lax.ppermute(x, axis, pairs)  9.94 us
    ppermute x4, starting transfers between devices, per_device(): hop = lambda x, pairs: lax.ppermute(x, ('sec', 'tile'), pairs)  9.52 us
    pallas_call x1, Pallas kernels, warp(): pl.pallas_call(warp_kernel, grid=(ny,), in_specs=[pl.BlockSpec(memory_spa...  9.04 us
    pallas_call x1, Pallas kernels, blend(): pl.pallas_call(blend_kernel, grid=(ny,), in_specs=[pl.BlockSpec(memory_sp...  8.7 us
    pallas_call x1, Pallas kernels, forward(): pl.pallas_call(forward_kernel, grid=(ny,), in_specs=[pl.BlockSpec(memory_...  8.37 us
    pallas_call x2, Pallas kernels, flow_of(): pl.pallas_call(functools.partial(flow_kernel, sign), grid=(ny,), in_specs...  7.42 us
    ppermute x5, waiting for transfers between devices, from_behind(): return lax.ppermute(x, axis, pairs)  6.57 us
  transfers between devices with their start and end apart: 9, of which 5 were waited for; matrix products, arithmetic and copies ran while one was open for 0% of the time, Pallas kernels for 22%

profile of v3, /device:TPU:0, one launch (start us, length us, event | category | flops | bytes accessed | tf_op | source)
XLA Modules:
  0.0 75.8 jit_solution(8245493959050818268)
XLA Ops:
  0.6 0.1 pad_add_fusion.tile_ref
  0.7 0.9 %copy-done.5 = bf16[256,256]{1,0:T(8,128)(2,1)S(1)} copy-done((bf16[256,256]{1,0:T(8,128)(2,1)S(1)}, bf16[256,256]{1,0:T(8,128)(2,1)}, u32[]{:S(2)}) %copy-start.5) | copy-done | bytes 131096
  1.6 0.8 %copy-done.7 = bf16[128,256]{1,0:T(8,128)(2,1)S(1)} copy-done((bf16[128,256]{1,0:T(8,128)(2,1)S(1)}, bf16[128,256]{1,0:T(8,128)(2,1)}, u32[]{:S(2)}) %copy-start.7) | copy-done | bytes 65560
  2.5 8.4 %forward.1 = (bf16[65,64,256]{2,1,0:T(8,128)(2,1)S(1)}, bf16[65,64,256]{2,1,0:T(8,128)(2,1)S(1)}, bf16[8,2,128,128]{3,2,1,0:T(8,128)(2,1)S(1)}, bf16[8,2,128,128]{3,2,1,0:T(8,128)(2,1)S(1)}) custom-call(s32[2]{0:T(128)S(1)} %pad_add_fusion.tile_ref, f32[1,8,16,128,128]{4,3,2,1,0:T(8,128)} %x_hbm.3, bf16[128,256]{1,0:T(8,128)(2,1)S(1)} %copy-done.7, ...), custom_call_target="tpu_custom_call" | custom-call | flops 4000000000 | bytes 12582912 | tf_op jit(solution)/shard_map/forward/pallas_call | solution.py:132
  10.8 1.4 %collective-permute-start.2 = (bf16[65,64,256]{2,1,0:T(8,128)(2,1)S(1)}, bf16[65,64,256]{2,1,0:T(8,128)(2,1)S(1)}, u32[]{:S(2)}, u32[]{:S(2)}) collective-permute-start(bf16[65,64,256]{2,1,0:T(8,128)(2,1)S(1)} %get-tuple-element.18.own), channel_id=1, source_target_pairs={{0,8},{8,16},{16,24},{24,32},{32,40},{40,48},{48,56},{56,64},{64,7... | collective-permute-start | bytes 6389768 | tf_op jit(solution)/shard_map/ppermute | solution.py:463
  12.3 1.3 %collective-permute-start = (bf16[65,64,256]{2,1,0:T(8,128)(2,1)S(1)}, bf16[65,64,256]{2,1,0:T(8,128)(2,1)S(1)}, u32[]{:S(2)}, u32[]{:S(2)}) collective-permute-start(bf16[65,64,256]{2,1,0:T(8,128)(2,1)S(1)} %get-tuple-element.16.own), channel_id=1, source_target_pairs={{8,0},{16,8},{24,16},{32,24},{40,32},{48,40},{56,48},{64,56},{72,6... | collective-permute-start | bytes 6389768 | tf_op jit(solution)/shard_map/ppermute | solution.py:463
  13.6 6.6 %collective-permute-start.3 = (bf16[8,2,128,128]{3,2,1,0:T(8,128)(2,1)S(1)}, bf16[8,2,128,128]{3,2,1,0:T(8,128)(2,1)S(1)}, u32[]{:S(2)}, u32[]{:S(2)}) collective-permute-start(bf16[8,2,128,128]{3,2,1,0:T(8,128)(2,1)S(1)} %get-tuple-element.19), channel_id=1, source_target_pairs={{0,64},{1,65},{2,66},{3,67},{4,68},{5,69},{6,70},{7,71},{8,72},{9,... | collective-permute-start | bytes 1572872 | tf_op jit(solution)/shard_map/ppermute | solution.py:490
  20.2 0.1 collective-permute-start.1
  20.3 0.0 copy-done.2
  20.3 0.6 slots.1
  20.9 0.0 copy-start.6
  20.9 0.0 copy-start.8
  20.9 8.7 %blend.1.refs_5_ = f32[8,16,272,128]{3,2,1,0:T(8,128)S(1)} custom-call(s32[8,128]{1,0:T(8,128)S(1)} %get-tuple-element.14.target_ref, f32[8,128]{1,0:T(8,128)S(1)} %get-tuple-element.15.share_ref, f32[1,8,16,128,128]{4,3,2,1,0:T(8,128)} %x_hbm.3), custom_call_target="tpu_custom_call" | custom-call | flops 20000000 | bytes 16777216 | tf_op jit(solution)/shard_map/blend/pallas_call | solution.py:328
  29.7 0.0 copy-start.3
  29.7 4.6 %collective-permute-done.3 = bf16[8,2,128,128]{3,2,1,0:T(8,128)(2,1)S(1)} collective-permute-done((bf16[8,2,128,128]{3,2,1,0:T(8,128)(2,1)S(1)}, bf16[8,2,128,128]{3,2,1,0:T(8,128)(2,1)S(1)}, u32[]{:S(2)}, u32[]{:S(2)}) %collective-permute-start.3) | collective-permute-done | bytes 524320 | tf_op jit(solution)/shard_map/ppermute | solution.py:490
  34.3 2.1 %collective-permute-start.8 = (bf16[8,2,128,128]{3,2,1,0:T(8,128)(2,1)S(1)}, bf16[8,2,128,128]{3,2,1,0:T(8,128)(2,1)S(1)}, u32[]{:S(2)}, u32[]{:S(2)}) collective-permute-start(bf16[8,2,128,128]{3,2,1,0:T(8,128)(2,1)S(1)} %collective-permute-done.3), channel_id=1, source_target_pairs={{64,7},{65,2},{66,1},{67,4},{68,3},{69,6},{70,5},{71,0},{72,15},{7... | collective-permute-start | bytes 1572872 | tf_op jit(solution)/shard_map/ppermute | solution.py:490
  36.4 0.0 collective-permute-done.2.other
  36.4 3.7 %flow.3 = f32[2,4,16]{2,1,0:T(4,128)S(1)} custom-call(bf16[65,64,256]{2,1,0:T(8,128)(2,1)S(1)} %get-tuple-element.18.own, bf16[65,64,256]{2,1,0:T(8,128)(2,1)S(1)} %collective-permute-done.2.other, bf16[256,256]{1,0:T(8,128)(2,1)S(1)} %copy-done.5, bf16[256,256]{1,0:T(8,128)(2,1)S(1)} %copy-done.6, bf16[128,128]{1,0:T(8,128)(2,1)S(1)} %copy-done.8), custom_call_target="tpu_custom_call" | custom-call | flops 2000000000 | bytes 4194304 | tf_op jit(solution)/shard_map/flow/pallas_call | solution.py:230
  40.1 5.4 %collective-permute-done.1 = bf16[8,2,128,128]{3,2,1,0:T(8,128)(2,1)S(1)} collective-permute-done((bf16[8,2,128,128]{3,2,1,0:T(8,128)(2,1)S(1)}, bf16[8,2,128,128]{3,2,1,0:T(8,128)(2,1)S(1)}, u32[]{:S(2)}, u32[]{:S(2)}) %collective-permute-start.1) | collective-permute-done | bytes 524320 | tf_op jit(solution)/shard_map/ppermute | solution.py:490
  45.5 0.7 collective-permute-start.7
  46.3 0.0 copy-done.3
  46.3 1.3 %collective-permute-start.4 = (f32[2,4,16]{2,1,0:T(4,128)S(1)}, f32[2,4,16]{2,1,0:T(4,128)S(1)}, u32[]{:S(2)}, u32[]{:S(2)}) collective-permute-start(f32[2,4,16]{2,1,0:T(4,128)S(1)} %flow.3), channel_id=1, source_target_pairs={{8,0},{16,8},{24,16},{32,24},{40,32},{48,40},{56,48},{64,56},{72,6... | collective-permute-start | bytes 1544 | tf_op jit(solution)/shard_map/ppermute | solution.py:463
  47.6 0.0 collective-permute-done.other
  47.6 3.7 %flow.2.refs_0_ = f32[2,4,16]{2,1,0:T(4,128)S(1)} custom-call(bf16[65,64,256]{2,1,0:T(8,128)(2,1)S(1)} %get-tuple-element.16.own, bf16[65,64,256]{2,1,0:T(8,128)(2,1)S(1)} %collective-permute-done.other, bf16[256,256]{1,0:T(8,128)(2,1)S(1)} %copy-done.5, bf16[256,256]{1,0:T(8,128)(2,1)S(1)} %copy-done.6, bf16[128,128]{1,0:T(8,128)(2,1)S(1)} %copy-done.8), custom_call_target="tpu_custom_call" | custom-call | flops 2000000000 | bytes 4194304 | tf_op jit(solution)/shard_map/flow/pallas_call | solution.py:230
  51.3 0.0 collective-permute-done.4.refs_1_
  51.3 4.7 %collective-permute-start.5 = (f32[3,8,16]{2,1,0:T(8,128)S(1)}, f32[3,8,16]{2,1,0:T(8,128)S(1)}, u32[]{:S(2)}, u32[]{:S(2)}) collective-permute-start(f32[3,8,16]{2,1,0:T(8,128)S(1)} %pad_maximum_fusion), channel_id=1, source_target_pairs={{0,1},{1,2},{2,3},{3,4},{4,5},{5,6},{6,7},{8,9},{9,10},{10,11},{11... | collective-permute-start | bytes 4616 | tf_op jit(solution)/shard_map/ppermute | solution.py:463
  56.0 1.3 %collective-permute-start.6 = (f32[3,8,16]{2,1,0:T(8,128)S(1)}, f32[3,8,16]{2,1,0:T(8,128)S(1)}, u32[]{:S(2)}, u32[]{:S(2)}) collective-permute-start(f32[3,8,16]{2,1,0:T(8,128)S(1)} %pad_maximum_fusion), channel_id=1, source_target_pairs={{1,0},{2,1},{3,2},{4,3},{5,4},{6,5},{7,6},{9,8},{10,9},{11,10},{12... | collective-permute-start | bytes 4616 | tf_op jit(solution)/shard_map/ppermute | solution.py:463
  57.3 3.0 %collective-permute-done.8.refs_7_ = bf16[8,2,128,128]{3,2,1,0:T(8,128)(2,1)S(1)} collective-permute-done((bf16[8,2,128,128]{3,2,1,0:T(8,128)(2,1)S(1)}, bf16[8,2,128,128]{3,2,1,0:T(8,128)(2,1)S(1)}, u32[]{:S(2)}, u32[]{:S(2)}) %collective-permute-start.8) | collective-permute-done | bytes 524320 | tf_op jit(solution)/shard_map/ppermute | solution.py:490
  60.2 3.1 %collective-permute-done.5.refs_3_ = f32[3,8,16]{2,1,0:T(8,128)S(1)} collective-permute-done((f32[3,8,16]{2,1,0:T(8,128)S(1)}, f32[3,8,16]{2,1,0:T(8,128)S(1)}, u32[]{:S(2)}, u32[]{:S(2)}) %collective-permute-start.5) | collective-permute-done | bytes 1568 | tf_op jit(solution)/shard_map/ppermute | solution.py:463
  63.3 3.5 %collective-permute-done.6.refs_4_ = f32[3,8,16]{2,1,0:T(8,128)S(1)} collective-permute-done((f32[3,8,16]{2,1,0:T(8,128)S(1)}, f32[3,8,16]{2,1,0:T(8,128)S(1)}, u32[]{:S(2)}, u32[]{:S(2)}) %collective-permute-start.6) | collective-permute-done | bytes 1568 | tf_op jit(solution)/shard_map/ppermute | solution.py:463
  66.8 0.0 collective-permute-done.7.refs_6_
  66.8 9.0 %warp.1 = (bf16[1,8,16,128,128]{4,3,2,1,0:T(8,128)(2,1)}, f32[1,2,8,16]{3,2,1,0:T(8,128)}) custom-call(s32[2]{0:T(128)S(1)} %pad_add_fusion.tile_ref, s32[8,128]{1,0:T(8,128)S(1)} %get-tuple-element.14.target_ref, f32[8,128]{1,0:T(8,128)S(1)} %get-tuple-element.15.share_ref, f32[2,4,16]{2,1,0:T(4,128)S(1)} %flow.2.refs_0_, ...), custom_call_target="tpu_custom_call" | custom-call | flops 20000000 | bytes 12582912 | tf_op jit(solution)/shard_map/warp/pallas_call | solution.py:433
  (13 shorter events, 0.0 us)
Async XLA Ops:
  0.7 0.9 %copy-start.5 = (bf16[256,256]{1,0:T(8,128)(2,1)S(1)}, bf16[256,256]{1,0:T(8,128)(2,1)}, u32[]{:S(2)}) copy-start(bf16[256,256]{1,0:T(8,128)(2,1)} %constant.28.cols_ref) | copy-start | bytes 393220
  1.6 0.8 %copy-start.7 = (bf16[128,256]{1,0:T(8,128)(2,1)S(1)}, bf16[128,256]{1,0:T(8,128)(2,1)}, u32[]{:S(2)}) copy-start(bf16[128,256]{1,0:T(8,128)(2,1)} %constant.27.rows_ref) | copy-start | bytes 196612
  2.5 17.8 %copy-start = (s32[1,8,16,4]{2,3,1,0:T(4,128)S(1)}, s32[1,8,16,4]{2,3,1,0:T(4,128)}, u32[]{:S(2)}) copy-start(s32[1,8,16,4]{2,3,1,0:T(4,128)} %param.12) | copy-start | bytes 6148
  2.5 17.8 %copy-start.1 = (s32[1,8,16,4]{2,3,1,0:T(4,128)S(1)}, s32[1,8,16,4]{2,3,1,0:T(4,128)}, u32[]{:S(2)}) copy-start(s32[1,8,16,4]{2,3,1,0:T(4,128)} %param.13) | copy-start | bytes 6148
  2.5 17.8 %copy-start.2 = (f32[1,8,16,4]{2,3,1,0:T(4,128)S(1)}, f32[1,8,16,4]{2,3,1,0:T(4,128)}, u32[]{:S(2)}) copy-start(f32[1,8,16,4]{2,3,1,0:T(4,128)} %param.15) | copy-start | bytes 6148
  2.5 17.8 %copy-start.4 = (s32[1,8,16]{2,1,0:T(8,128)S(1)}, s32[1,8,16]{2,1,0:T(8,128)}, u32[]{:S(2)}) copy-start(s32[1,8,16]{2,1,0:T(8,128)} %count_ref.1) | copy-start | bytes 1540
  10.8 25.6 %collective-permute-start.2 = (bf16[65,64,256]{2,1,0:T(8,128)(2,1)S(1)}, bf16[65,64,256]{2,1,0:T(8,128)(2,1)S(1)}, u32[]{:S(2)}, u32[]{:S(2)}) collective-permute-start(bf16[65,64,256]{2,1,0:T(8,128)(2,1)S(1)} %get-tuple-element.18.own), channel_id=1, source_target_pairs={{0,8},{8,16},{16,24},{24,32},{32,40},{40,48},{48,56},{56,64},{64,7... | collective-permute-start | bytes 6389768 | tf_op jit(solution)/shard_map/ppermute | solution.py:463
  12.3 35.3 %collective-permute-start = (bf16[65,64,256]{2,1,0:T(8,128)(2,1)S(1)}, bf16[65,64,256]{2,1,0:T(8,128)(2,1)S(1)}, u32[]{:S(2)}, u32[]{:S(2)}) collective-permute-start(bf16[65,64,256]{2,1,0:T(8,128)(2,1)S(1)} %get-tuple-element.16.own), channel_id=1, source_target_pairs={{8,0},{16,8},{24,16},{32,24},{40,32},{48,40},{56,48},{64,56},{72,6... | collective-permute-start | bytes 6389768 | tf_op jit(solution)/shard_map/ppermute | solution.py:463
  13.6 20.7 %collective-permute-start.3 = (bf16[8,2,128,128]{3,2,1,0:T(8,128)(2,1)S(1)}, bf16[8,2,128,128]{3,2,1,0:T(8,128)(2,1)S(1)}, u32[]{:S(2)}, u32[]{:S(2)}) collective-permute-start(bf16[8,2,128,128]{3,2,1,0:T(8,128)(2,1)S(1)} %get-tuple-element.19), channel_id=1, source_target_pairs={{0,64},{1,65},{2,66},{3,67},{4,68},{5,69},{6,70},{7,71},{8,72},{9,... | collective-permute-start | bytes 1572872 | tf_op jit(solution)/shard_map/ppermute | solution.py:490
  20.2 25.4 %collective-permute-start.1 = (bf16[8,2,128,128]{3,2,1,0:T(8,128)(2,1)S(1)}, bf16[8,2,128,128]{3,2,1,0:T(8,128)(2,1)S(1)}, u32[]{:S(2)}, u32[]{:S(2)}) collective-permute-start(bf16[8,2,128,128]{3,2,1,0:T(8,128)(2,1)S(1)} %get-tuple-element.17), channel_id=1, source_target_pairs={{0,64},{1,65},{2,66},{3,67},{4,68},{5,69},{6,70},{7,71},{8,72},{9,... | collective-permute-start | bytes 1572872 | tf_op jit(solution)/shard_map/ppermute | solution.py:490
  20.9 15.5 %copy-start.6 = (bf16[256,256]{1,0:T(8,128)(2,1)S(1)}, bf16[256,256]{1,0:T(8,128)(2,1)}, u32[]{:S(2)}) copy-start(bf16[256,256]{1,0:T(8,128)(2,1)} %constant.29.back_cols_ref) | copy-start | bytes 393220
  20.9 15.5 %copy-start.8 = (bf16[128,128]{1,0:T(8,128)(2,1)S(1)}, bf16[128,128]{1,0:T(8,128)(2,1)}, u32[]{:S(2)}) copy-start(bf16[128,128]{1,0:T(8,128)(2,1)} %constant.30.back_rows_ref) | copy-start | bytes 98308
  29.7 16.6 %copy-start.3 = (s32[1,8,16]{2,1,0:T(8,128)S(1)}, s32[1,8,16]{2,1,0:T(8,128)}, u32[]{:S(2)}) copy-start(s32[1,8,16]{2,1,0:T(8,128)} %refs_2_.1) | copy-start | bytes 1540
  34.3 25.9 %collective-permute-start.8 = (bf16[8,2,128,128]{3,2,1,0:T(8,128)(2,1)S(1)}, bf16[8,2,128,128]{3,2,1,0:T(8,128)(2,1)S(1)}, u32[]{:S(2)}, u32[]{:S(2)}) collective-permute-start(bf16[8,2,128,128]{3,2,1,0:T(8,128)(2,1)S(1)} %collective-permute-done.3), channel_id=1, source_target_pairs={{64,7},{65,2},{66,1},{67,4},{68,3},{69,6},{70,5},{71,0},{72,15},{7... | collective-permute-start | bytes 1572872 | tf_op jit(solution)/shard_map/ppermute | solution.py:490
  45.5 21.3 %collective-permute-start.7 = (bf16[8,2,128,128]{3,2,1,0:T(8,128)(2,1)S(1)}, bf16[8,2,128,128]{3,2,1,0:T(8,128)(2,1)S(1)}, u32[]{:S(2)}, u32[]{:S(2)}) collective-permute-start(bf16[8,2,128,128]{3,2,1,0:T(8,128)(2,1)S(1)} %collective-permute-done.1), channel_id=1, source_target_pairs={{64,1},{65,0},{66,3},{67,2},{68,5},{69,4},{70,7},{71,6},{72,9},{73... | collective-permute-start | bytes 1572872 | tf_op jit(solution)/shard_map/ppermute | solution.py:490
  46.3 5.0 %collective-permute-start.4 = (f32[2,4,16]{2,1,0:T(4,128)S(1)}, f32[2,4,16]{2,1,0:T(4,128)S(1)}, u32[]{:S(2)}, u32[]{:S(2)}) collective-permute-start(f32[2,4,16]{2,1,0:T(4,128)S(1)} %flow.3), channel_id=1, source_target_pairs={{8,0},{16,8},{24,16},{32,24},{40,32},{48,40},{56,48},{64,56},{72,6... | collective-permute-start | bytes 1544 | tf_op jit(solution)/shard_map/ppermute | solution.py:463
  51.3 12.0 %collective-permute-start.5 = (f32[3,8,16]{2,1,0:T(8,128)S(1)}, f32[3,8,16]{2,1,0:T(8,128)S(1)}, u32[]{:S(2)}, u32[]{:S(2)}) collective-permute-start(f32[3,8,16]{2,1,0:T(8,128)S(1)} %pad_maximum_fusion), channel_id=1, source_target_pairs={{0,1},{1,2},{2,3},{3,4},{4,5},{5,6},{6,7},{8,9},{9,10},{10,11},{11... | collective-permute-start | bytes 4616 | tf_op jit(solution)/shard_map/ppermute | solution.py:463
  56.0 10.8 %collective-permute-start.6 = (f32[3,8,16]{2,1,0:T(8,128)S(1)}, f32[3,8,16]{2,1,0:T(8,128)S(1)}, u32[]{:S(2)}, u32[]{:S(2)}) collective-permute-start(f32[3,8,16]{2,1,0:T(8,128)S(1)} %pad_maximum_fusion), channel_id=1, source_target_pairs={{1,0},{2,1},{3,2},{4,3},{5,4},{6,5},{7,6},{9,8},{10,9},{11,10},{12... | collective-permute-start | bytes 4616 | tf_op jit(solution)/shard_map/ppermute | solution.py:463

commit v4 on v3

--- a/solution.py
+++ b/solution.py
@@ -81,16 +81,52 @@
             copy.wait()
 
 
-def forward_kernel(tile_ref, x_hbm, rows_ref, cols_ref, low_ref, high_ref, on_ref, off_ref, x_ref, lines_ref, ends_ref, in_sems):
+def forward_kernel(start, strips, tile_ref, x_hbm, rows_hbm, cols_hbm, *refs):
+    spec_ref, refs = refs[0], refs[1:]
+    if strips:
+        on_ref, off_ref, on_x, off_x, strip_sems = refs[:2] + refs[-3:]
+        refs = refs[2:-3]
+    x_ref, lines_ref, ends_ref, rows_ref, cols_ref, in_sems, table_sems = refs
     y = pl.program_id(0)
-    ny, patches = x_ref.shape[:2]
-    half = ny // 2
-    fetch = lambda row: [pltpu.make_async_copy(x_hbm.at[0, row], x_ref.at[row], in_sems.at[row])]
-    ahead(fetch, ny, DEPTH)
-    odd = tile_ref[0] % 2
-    for i in range(HB):
-        on_ref[y, i] = x_ref[y, (1 - odd) * (patches - HB) + i].astype(jnp.bfloat16)
-        off_ref[y, i] = x_ref[y, odd * (patches - HB) + i].astype(jnp.bfloat16)
+    count, patches = x_ref.shape[:2]
+    fetch = lambda row: [pltpu.make_async_copy(x_hbm.at[0, start + row], x_ref.at[row], in_sems.at[row])]
+    tables_in = [
+        pltpu.make_async_copy(rows_hbm, rows_ref, table_sems.at[0]),
+        pltpu.make_async_copy(cols_hbm, cols_ref, table_sems.at[1]),
+    ]
+
+    @pl.when(y == 0)
+    def _():
+        for copy in tables_in:
+            copy.start()
+
+    ahead(fetch, count, min(DEPTH, count))
+
+    @pl.when(y == 0)
+    def _():
+        for copy in tables_in:
+            copy.wait()
+
+    if strips:
+        odd = tile_ref[0] % 2
+        strip_copies = [
+            pltpu.make_async_copy(x_hbm.at[0, :, pl.ds(column, HB)], target, strip_sems.at[i])
+            for i, (column, target) in enumerate(
+                (((1 - odd) * (patches - HB), on_x), (odd * (patches - HB), off_x))
+            )
+        ]
+
+        @pl.when(y == 0)
+        def _():
+            for copy in strip_copies:
+                copy.start()
+
+        @pl.when(y == count - 1)
+        def _():
+            for copy in strip_copies:
+                copy.wait()
+            on_ref[...] = on_x[...].astype(jnp.bfloat16)
+            off_ref[...] = off_x[...].astype(jnp.bfloat16)
 
     rows2 = rows_ref[...]
     cols = cols_ref[...]
@@ -107,49 +143,41 @@
             high, low = split(lines)
             lines_ref[p * HALF : (p + 1) * HALF, : 2 * N] = high
             lines_ref[p * HALF : (p + 1) * HALF, 2 * N :] = low
-    row = y % half
-    last = half * patches
+    step = 4
+    for first in range(0, patches, step):
+        lines = lines_ref[first * HALF : (first + step) * HALF, :]
+        freq = dot(lines, cols2).reshape(step, HALF, 2 * N)
+        spec_ref[pl.ds(y * patches + first, step)] = freq.astype(jnp.bfloat16)
     ends = ends_ref[...].astype(jnp.bfloat16)
-    step = 4
-
-    def finish(spec_ref):
-        for first in range(0, patches, step):
-            lines = lines_ref[first * HALF : (first + step) * HALF, :]
-            freq = dot(lines, cols2).reshape(step, HALF, 2 * N)
-            spec_ref[pl.ds(row * patches + first, step)] = freq.astype(jnp.bfloat16)
-        spec_ref[last, pl.ds(pl.multiple_of(row * patches, patches), patches), :] = ends
-
-    pl.when(y < half)(lambda: finish(low_ref))
-    pl.when(y >= half)(lambda: finish(high_ref))
-
-
-def forward(tile, sections, rows, cols):
+    spec_ref[count * patches, pl.ds(pl.multiple_of(y * patches, patches), patches), :] = ends
+
+
+def forward(tile, sections, start, count, strips, rows, cols):
     _, ny, nx, _, _ = sections.shape
-    half = ny // 2
     rows2 = jnp.concatenate([rows, rows], axis=1).astype(jnp.bfloat16)
-    whole = lambda shape: pl.BlockSpec(shape, lambda y: (0,) * len(shape))
-    spectra = (half * nx + 1, HALF, 2 * N)
+    spectra = (count * nx + 1, HALF, 2 * N)
+    strip = (ny, HB, N, N)
+    extra = [pltpu.VMEM(strip, jnp.float32)] * 2 + [pltpu.SemaphoreType.DMA((2,))]
     return pl.pallas_call(
-        forward_kernel,
-        grid=(ny,),
-        in_specs=[
-            pl.BlockSpec(memory_space=pltpu.SMEM),
-            pl.BlockSpec(memory_space=pltpu.HBM),
-            whole((N, 2 * N)),
-            whole((2 * N, 2 * N)),
-        ],
-        out_specs=[pl.BlockSpec(memory_space=pltpu.VMEM)] * 4,
-        out_shape=[pltpu.VMEM(spectra, jnp.bfloat16)] * 2 + [pltpu.VMEM((ny, HB, N, N), jnp.bfloat16)] * 2,
+        functools.partial(forward_kernel, start, strips),
+        grid=(count,),
+        in_specs=[pl.BlockSpec(memory_space=pltpu.SMEM)] + [pl.BlockSpec(memory_space=pltpu.HBM)] * 3,
+        out_specs=[pl.BlockSpec(memory_space=pltpu.VMEM)] * (3 if strips else 1),
+        out_shape=[pltpu.VMEM(spectra, jnp.bfloat16)] + [pltpu.VMEM(strip, jnp.bfloat16)] * (2 if strips else 0),
         scratch_shapes=[
-            pltpu.VMEM(sections.shape[1:], jnp.float32),
+            pltpu.VMEM((count, nx, N, N), jnp.float32),
             pltpu.VMEM((nx * HALF, 4 * N), jnp.bfloat16),
             pltpu.VMEM((nx, 2 * N), jnp.float32),
-            pltpu.SemaphoreType.DMA((ny,)),
-        ],
-        compiler_params=pltpu.CompilerParams(vmem_limit_bytes=20 * MIB),
-        cost_estimate=pl.CostEstimate(flops=4_000_000_000, bytes_accessed=12 * MIB, transcendentals=0),
+            pltpu.VMEM((N, 2 * N), jnp.bfloat16),
+            pltpu.VMEM((2 * N, 2 * N), jnp.bfloat16),
+            pltpu.SemaphoreType.DMA((count,)),
+            pltpu.SemaphoreType.DMA((2,)),
+        ]
+        + (extra if strips else []),
+        compiler_params=pltpu.CompilerParams(vmem_limit_bytes=16 * MIB),
+        cost_estimate=pl.CostEstimate(flops=2_000_000_000, bytes_accessed=6 * MIB, transcendentals=0),
         name="forward",
-    )(tile, in_hbm(sections), rows2, cols.astype(jnp.bfloat16))
+    )(tile, in_hbm(sections), in_hbm(rows2), in_hbm(cols.astype(jnp.bfloat16)))
 
 
 def times_conj(a, b, sign):
@@ -368,15 +396,14 @@
     return fields
 
 
-def warp_kernel(tile_ref, target_ref, share_ref, *refs):
-    *flows, padded, on_hbm, off_hbm, out_hbm, field_ref, window, edges, out, wide, field, in_sems, out_sems = refs
+def edge_kernel(tile_ref, target_ref, share_ref, on_ref, off_ref, padded, out_ref, window, sems):
     y = pl.program_id(0)
-    ny, nx = out.shape[:2]
+    ny, nx = padded.shape[:2]
     even = tile_ref[0] % 2 == 0
-    halos = {True: ((on_hbm, HB), (off_hbm, 0)), False: ((on_hbm, 0), (off_hbm, HB))}
-    halo_copies = {
+    halos = {True: ((on_ref, HB), (off_ref, 0)), False: ((on_ref, 0), (off_ref, HB))}
+    copies = {
         side: [
-            pltpu.make_async_copy(ref, window.at[:, into : into + HB], in_sems.at[i])
+            pltpu.make_async_copy(ref, window.at[:, into : into + HB], sems.at[i])
             for i, (ref, into) in enumerate(places)
         ]
         for side, places in halos.items()
@@ -384,35 +411,63 @@
 
     @pl.when((y == 0) & even)
     def _():
-        for copy in halo_copies[True]:
+        for copy in copies[True]:
             copy.start()
 
     @pl.when((y == 0) & jnp.logical_not(even))
     def _():
-        for copy in halo_copies[False]:
+        for copy in copies[False]:
             copy.start()
+
+    border = jnp.zeros((2 * HB, PAD, N), jnp.float32)
+    out_ref[y, :, :PAD] = border
+    out_ref[y, :, PAD + N :] = border
+
+    @pl.when(y == 0)
+    def _():
+        for copy in copies[True]:
+            copy.wait()
+
+    for i, x in enumerate((*range(HB), *range(nx - HB, nx))):
+        more = blend_cell(y, K * nx + x, nx, target_ref, share_ref, window)
+        out_ref[y, i, PAD : PAD + N] = padded[y, x, PAD : PAD + N] + more
+
+
+def edges_of(tile, target, share, on, off, blended):
+    ny, _, tall, _ = blended.shape
+    vmem = pl.BlockSpec(memory_space=pltpu.VMEM)
+    return pl.pallas_call(
+        edge_kernel,
+        grid=(ny,),
+        in_specs=[pl.BlockSpec(memory_space=pltpu.SMEM)] * 3 + [vmem] * 3,
+        out_specs=vmem,
+        out_shape=pltpu.VMEM((ny, 2 * HB, tall, N), jnp.float32),
+        scratch_shapes=[pltpu.VMEM((ny, 2 * HB, N, N), jnp.bfloat16), pltpu.SemaphoreType.DMA((2,))],
+        compiler_params=pltpu.CompilerParams(vmem_limit_bytes=4 * MIB),
+        cost_estimate=pl.CostEstimate(flops=5_000_000, bytes_accessed=4 * MIB, transcendentals=0),
+        name="edges",
+    )(tile, target, share, in_vmem(on), in_vmem(off), in_vmem(blended))
+
+
+def warp_kernel(*refs):
+    *flows, padded, edges, out_hbm, field_ref, out, wide, field, sem, out_sems = refs
+    y = pl.program_id(0)
+    ny, nx = out.shape[:2]
 
     @pl.when(y == 0)
     def _():
         for component, values in enumerate(relax(*flows)):
             wide[component] = values
             field_ref[0, component] = values[:, STEPS : STEPS + nx]
-        scalars = pltpu.make_async_copy(wide, field, in_sems.at[2])
+        scalars = pltpu.make_async_copy(wide, field, sem)
         scalars.start()
-        edges[:, :PAD] = jnp.zeros((2 * HB, PAD, N), jnp.float32)
-        edges[:, PAD + N :] = jnp.zeros((2 * HB, PAD, N), jnp.float32)
         scalars.wait()
-        for copy in halo_copies[True]:
-            copy.wait()
 
     borders = (*range(HB), *range(nx - HB, nx))
-    for i, x in enumerate(borders):
-        more = blend_cell(y, K * nx + x, nx, target_ref, share_ref, window)
-        edges[i, PAD : PAD + N] = padded[y, x, PAD : PAD + N] + more
     apart = lax.broadcasted_iota(jnp.int32, (N, N), 0) - lax.broadcasted_iota(jnp.int32, (N, N), 1)
     apart = apart.astype(jnp.float32)
     for x in range(nx):
-        cell = edges.at[borders.index(x)] if x in borders else padded.at[y, x]
+        cell = edges.at[y, borders.index(x)] if x in borders else padded.at[y, x]
         shift = field[0, y, STEPS + x]
         down = jnp.clip((shift + 256.0).astype(jnp.int32) - 256, 4 - PAD, PAD - 6)
         part = shift - down.astype(jnp.float32)
@@ -427,34 +482,29 @@
     wait_all([store(row) for row in range(ny)])
 
 
-def warp(tile, target, share, flows, blended, on, off):
+def warp(flows, blended, edges):
     ny, nx = blended.shape[:2]
     whole = lambda shape: pl.BlockSpec(shape, lambda y: (0,) * len(shape))
     return pl.pallas_call(
         warp_kernel,
         grid=(ny,),
-        in_specs=[pl.BlockSpec(memory_space=pltpu.SMEM)] * 3
-        + [whole(x.shape) for x in flows]
-        + [pl.BlockSpec(memory_space=pltpu.VMEM)]
-        + [pl.BlockSpec(memory_space=pl.ANY)] * 2,
+        in_specs=[whole(x.shape) for x in flows] + [pl.BlockSpec(memory_space=pltpu.VMEM)] * 2,
         out_specs=[pl.BlockSpec(memory_space=pl.ANY), whole((1, 2, ny, nx))],
         out_shape=[
             jax.ShapeDtypeStruct((1, ny, nx, N, N), jnp.bfloat16),
             jax.ShapeDtypeStruct((1, 2, ny, nx), jnp.float32),
         ],
         scratch_shapes=[
-            pltpu.VMEM((ny, 2 * HB, N, N), jnp.bfloat16),
-            pltpu.VMEM((2 * HB, 2 * PAD + N, N), jnp.float32),
             pltpu.VMEM((ny, nx, N, N), jnp.bfloat16),
             pltpu.VMEM((2, ny, N), jnp.float32),
             pltpu.SMEM((2, ny, N), jnp.float32),
-            pltpu.SemaphoreType.DMA((3,)),
+            pltpu.SemaphoreType.DMA,
             pltpu.SemaphoreType.DMA((ny,)),
         ],
-        compiler_params=pltpu.CompilerParams(vmem_limit_bytes=12 * MIB),
+        compiler_params=pltpu.CompilerParams(vmem_limit_bytes=8 * MIB),
         cost_estimate=pl.CostEstimate(flops=20_000_000, bytes_accessed=12 * MIB, transcendentals=0),
         name="warp",
-    )(tile, target, share, *flows, in_vmem(blended), on, off)
+    )(*flows, in_vmem(blended), in_vmem(edges))
 
 
 def from_behind(x, axis, by):
@@ -463,7 +513,11 @@
     return lax.ppermute(x, axis, pairs)
 
 
-def hops(tiles, sections, across):
+def swapped(x):
+    return lax.ppermute(x, "tile", [(i, i ^ 1) for i in range(lax.axis_size("tile"))])
+
+
+def hops(tiles, sections):
     pairs = ([], [])
     for section in range(sections):
         x_low, rest = divmod(section, sections // 2)
@@ -473,7 +527,7 @@
             ends = [section * tiles + tile]
             for hop in (1, 2):
                 x = (2 * x_high + x_low + hop * way) % 4
-                to_z = (z + 2 * x_high - 1) % (tiles // 2) if across and hop == 2 else z
+                to_z = (z + 2 * x_high - 1) % (tiles // 2) if hop == 2 else z
                 ends.append((x % 2 * (sections // 2) + rest) * tiles + 2 * to_z + x // 2)
             pairs[0].append((ends[0], ends[1]))
             pairs[1].append((ends[1], ends[2]))
@@ -486,14 +540,14 @@
     half = ny // 2
     tiles, count = lax.axis_size("tile"), lax.axis_size("sec")
     tile = jnp.stack([lax.axis_index("tile"), tiles]).astype(jnp.int32)
-    on_hops, off_hops = hops(tiles, count, False), hops(tiles, count, True)
+    off_hops = hops(tiles, count)
     hop = lambda x, pairs: lax.ppermute(x, ("sec", "tile"), pairs)
 
-    spectra_low, spectra_high, on, off = forward(tile, sections, rows, cols)
+    spectra_high, = forward(tile, sections, half, half, False, rows, cols)
     from_last = from_behind(spectra_high, "sec", 1)
+    spectra_low, on, off = forward(tile, sections, 0, half, True, rows, cols)
     from_next = from_behind(spectra_low, "sec", -1)
     off = hop(off, off_hops[0])
-    on = hop(on, on_hops[0])
     target, share = slots_of(tile, box_row, box_shift, box_count, blend_weight)
     blended = blend(target, share, sections)
     off, blended = lax.optimization_barrier((off, blended))
@@ -503,14 +557,15 @@
     flow_high = flow_of(spectra_high, from_last, -1, half, nx, cols, back_cols, back_rows)
     on, flow_high = lax.optimization_barrier((on, flow_high))
     flow_high = from_behind(flow_high, "sec", -1)
-    on = hop(on, on_hops[1])
+    on = swapped(on)
     flow_low = flow_of(spectra_low, from_next, 1, half, nx, cols, back_cols, back_rows)
     flow = jnp.concatenate([flow_low, flow_high], axis=1)
     flow = jnp.concatenate([flow, node_mask.astype(jnp.float32) + 1.0], axis=0)
     flow_left = from_behind(flow, "tile", 1)
     flow_right = from_behind(flow, "tile", -1)
     flows = (flow_low, flow_high, node_mask, flow_left, flow_right)
-    return tuple(warp(tile, target, share, flows, blended, on, off))
+    edges = edges_of(tile, target, share, on, off, blended)
+    return tuple(warp(flows, blended, edges))
 
 
 def solution(mesh):

time: 76.1 us -> 74.2 us (0.975)
  the two profiles are of different devices: /device:TPU:0 before, /device:TPU:66 now
where the time goes in v4:
time: 74.2 us; the launch traced here: 72.8 us
  Pallas kernels  36.4 us (49%)
  starting transfers between devices  20.3 us (27%)
  waiting for transfers between devices  15.1 us (20%)
  between operations  0.85 us (1%)
    ppermute x5, starting transfers between devices, from_behind(): return lax.ppermute(x, axis, pairs)  17 us
    ppermute x5, waiting for transfers between devices, from_behind(): return lax.ppermute(x, axis, pairs)  12.9 us
    pallas_call x2, Pallas kernels, forward(): pl.pallas_call(functools.partial(forward_kernel, start, strips), grid=(co...  10.2 us
    pallas_call x1, Pallas kernels, blend(): pl.pallas_call(blend_kernel, grid=(ny,), in_specs=[pl.BlockSpec(memory_sp...  8.7 us
    pallas_call x2, Pallas kernels, flow_of(): pl.pallas_call(functools.partial(flow_kernel, sign), grid=(ny,), in_specs...  7.4 us
    pallas_call x1, Pallas kernels, warp(): pl.pallas_call(warp_kernel, grid=(ny,), in_specs=[whole(x.shape) for x in...  7.14 us
    pallas_call x1, Pallas kernels, edges_of(): pl.pallas_call(edge_kernel, grid=(ny,), in_specs=[pl.BlockSpec(memory_spa...  2.32 us
    ppermute x2, waiting for transfers between devices, per_device(): hop = lambda x, pairs: lax.ppermute(x, ('sec', 'tile'), pairs)  2.21 us
  transfers between devices with their start and end apart: 8, of which 5 were waited for; matrix products, arithmetic and copies ran while one was open for 0% of the time, Pallas kernels for 33%

profile of v4, /device:TPU:66, one launch (start us, length us, event | category | flops | bytes accessed | tf_op | source)
XLA Modules:
  0.0 72.8 jit_solution(4417434544765999570)
XLA Ops:
  0.6 0.1 pad_add_fusion.tile_ref
  0.7 5.0 %forward.3.own = bf16[65,64,256]{2,1,0:T(8,128)(2,1)S(1)} custom-call(s32[2]{0:T(128)S(1)} %pad_add_fusion.tile_ref, f32[1,8,16,128,128]{4,3,2,1,0:T(8,128)} %x_hbm.5, bf16[128,256]{1,0:T(8,128)(2,1)} %constant.27.rows_hbm, bf16[256,256]{1,0:T(8,128)(2,1)} %constant.28.cols_hbm.cols_ref), custom_call_target="tpu_custom_call" | custom-call | flops 2000000000 | bytes 6291456 | tf_op jit(solution)/shard_map/forward/pallas_call | solution.py:161
  5.7 0.0 copy-start.2
  5.7 0.0 copy-start.3
  5.8 0.0 copy-start.4
  5.8 0.0 copy-start.5
  5.8 2.1 %collective-permute-start.1 = (bf16[65,64,256]{2,1,0:T(8,128)(2,1)S(1)}, bf16[65,64,256]{2,1,0:T(8,128)(2,1)S(1)}, u32[]{:S(2)}, u32[]{:S(2)}) collective-permute-start(bf16[65,64,256]{2,1,0:T(8,128)(2,1)S(1)} %forward.3.own), channel_id=1, source_target_pairs={{0,8},{8,16},{16,24},{24,32},{32,40},{40,48},{48,56},{56,64},{64,7... | collective-permute-start | bytes 6389768 | tf_op jit(solution)/shard_map/ppermute | solution.py:513
  7.8 5.2 %forward.2 = (bf16[65,64,256]{2,1,0:T(8,128)(2,1)S(1)}, bf16[8,2,128,128]{3,2,1,0:T(8,128)(2,1)S(1)}, bf16[8,2,128,128]{3,2,1,0:T(8,128)(2,1)S(1)}) custom-call(s32[2]{0:T(128)S(1)} %pad_add_fusion.tile_ref, f32[1,8,16,128,128]{4,3,2,1,0:T(8,128)} %x_hbm.5, bf16[128,256]{1,0:T(8,128)(2,1)} %constant.27.rows_hbm, bf16[256,256]{1,0:T(8,128)(2,1)} %constant.28.cols_hbm.cols_ref), custom_call_target="tpu_custom_call" | custom-call | flops 2000000000 | bytes 6291456 | tf_op jit(solution)/shard_map/forward/pallas_call | solution.py:161
  13.0 5.7 %collective-permute-start = (bf16[65,64,256]{2,1,0:T(8,128)(2,1)S(1)}, bf16[65,64,256]{2,1,0:T(8,128)(2,1)S(1)}, u32[]{:S(2)}, u32[]{:S(2)}) collective-permute-start(bf16[65,64,256]{2,1,0:T(8,128)(2,1)S(1)} %get-tuple-element.13.own), channel_id=1, source_target_pairs={{8,0},{16,8},{24,16},{32,24},{40,32},{48,40},{56,48},{64,56},{72,6... | collective-permute-start | bytes 6389768 | tf_op jit(solution)/shard_map/ppermute | solution.py:513
  18.8 0.1 collective-permute-start.2
  18.9 0.6 slots.1
  19.6 0.0 copy-start
  19.6 0.0 copy-start.6
  19.6 0.0 copy-start.7
  19.6 8.7 %blend.1.padded.refs_5_ = f32[8,16,272,128]{3,2,1,0:T(8,128)S(1)} custom-call(s32[8,128]{1,0:T(8,128)S(1)} %get-tuple-element.16.target_ref, f32[8,128]{1,0:T(8,128)S(1)} %get-tuple-element.17.share_ref, f32[1,8,16,128,128]{4,3,2,1,0:T(8,128)} %x_hbm.5), custom_call_target="tpu_custom_call" | custom-call | flops 20000000 | bytes 16777216 | tf_op jit(solution)/shard_map/blend/pallas_call | solution.py:356
  28.3 0.0 copy-start.1
  28.3 2.2 %collective-permute-done.2 = bf16[8,2,128,128]{3,2,1,0:T(8,128)(2,1)S(1)} collective-permute-done((bf16[8,2,128,128]{3,2,1,0:T(8,128)(2,1)S(1)}, bf16[8,2,128,128]{3,2,1,0:T(8,128)(2,1)S(1)}, u32[]{:S(2)}, u32[]{:S(2)}) %collective-permute-start.2) | collective-permute-done | bytes 524320 | tf_op jit(solution)/shard_map/ppermute | solution.py:544
  30.5 1.0 %collective-permute-start.7 = (bf16[8,2,128,128]{3,2,1,0:T(8,128)(2,1)S(1)}, bf16[8,2,128,128]{3,2,1,0:T(8,128)(2,1)S(1)}, u32[]{:S(2)}, u32[]{:S(2)}) collective-permute-start(bf16[8,2,128,128]{3,2,1,0:T(8,128)(2,1)S(1)} %collective-permute-done.2), channel_id=1, source_target_pairs={{64,7},{65,2},{66,1},{67,4},{68,3},{69,6},{70,5},{71,0},{72,15},{7... | collective-permute-start | bytes 1572872 | tf_op jit(solution)/shard_map/ppermute | solution.py:544
  31.6 4.1 %collective-permute-done.1.other = bf16[65,64,256]{2,1,0:T(8,128)(2,1)S(1)} collective-permute-done((bf16[65,64,256]{2,1,0:T(8,128)(2,1)S(1)}, bf16[65,64,256]{2,1,0:T(8,128)(2,1)S(1)}, u32[]{:S(2)}, u32[]{:S(2)}) %collective-permute-start.1) | collective-permute-done | bytes 2129952 | tf_op jit(solution)/shard_map/ppermute | solution.py:513
  35.7 3.7 %flow.3 = f32[2,4,16]{2,1,0:T(4,128)S(1)} custom-call(bf16[65,64,256]{2,1,0:T(8,128)(2,1)S(1)} %forward.3.own, bf16[65,64,256]{2,1,0:T(8,128)(2,1)S(1)} %collective-permute-done.1.other, bf16[256,256]{1,0:T(8,128)(2,1)S(1)} %copy-done, bf16[256,256]{1,0:T(8,128)(2,1)S(1)} %copy-done.6, bf16[128,128]{1,0:T(8,128)(2,1)S(1)} %copy-done.7), custom_call_target="tpu_custom_call" | custom-call | flops 2000000000 | bytes 4194304 | tf_op jit(solution)/shard_map/flow/pallas_call | solution.py:258
  39.4 2.2 %collective-permute-start.6 = (bf16[8,2,128,128]{3,2,1,0:T(8,128)(2,1)S(1)}, bf16[8,2,128,128]{3,2,1,0:T(8,128)(2,1)S(1)}, u32[]{:S(2)}, u32[]{:S(2)}) collective-permute-start(bf16[8,2,128,128]{3,2,1,0:T(8,128)(2,1)S(1)} %get-tuple-element.22), channel_id=1, source_target_pairs={{0,1},{1,0},{2,3},{3,2},{4,5},{5,4},{6,7},{7,6},{8,9},{9,8},{10,11... | collective-permute-start | bytes 1572872 | tf_op jit(solution)/shard_map/ppermute | solution.py:517
  41.6 1.9 %collective-permute-start.3 = (f32[2,4,16]{2,1,0:T(4,128)S(1)}, f32[2,4,16]{2,1,0:T(4,128)S(1)}, u32[]{:S(2)}, u32[]{:S(2)}) collective-permute-start(f32[2,4,16]{2,1,0:T(4,128)S(1)} %flow.3), channel_id=1, source_target_pairs={{8,0},{16,8},{24,16},{32,24},{40,32},{48,40},{56,48},{64,56},{72,6... | collective-permute-start | bytes 1544 | tf_op jit(solution)/shard_map/ppermute | solution.py:513
  43.5 3.0 %collective-permute-done.other = bf16[65,64,256]{2,1,0:T(8,128)(2,1)S(1)} collective-permute-done((bf16[65,64,256]{2,1,0:T(8,128)(2,1)S(1)}, bf16[65,64,256]{2,1,0:T(8,128)(2,1)S(1)}, u32[]{:S(2)}, u32[]{:S(2)}) %collective-permute-start) | collective-permute-done | bytes 2129952 | tf_op jit(solution)/shard_map/ppermute | solution.py:513
  46.5 3.7 %flow.2.refs_0_ = f32[2,4,16]{2,1,0:T(4,128)S(1)} custom-call(bf16[65,64,256]{2,1,0:T(8,128)(2,1)S(1)} %get-tuple-element.13.own, bf16[65,64,256]{2,1,0:T(8,128)(2,1)S(1)} %collective-permute-done.other, bf16[256,256]{1,0:T(8,128)(2,1)S(1)} %copy-done, bf16[256,256]{1,0:T(8,128)(2,1)S(1)} %copy-done.6, bf16[128,128]{1,0:T(8,128)(2,1)S(1)} %copy-done.7), custom_call_target="tpu_custom_call" | custom-call | flops 2000000000 | bytes 4194304 | tf_op jit(solution)/shard_map/flow/pallas_call | solution.py:258
  50.2 3.9 %collective-permute-done.3.refs_1_ = f32[2,4,16]{2,1,0:T(4,128)S(1)} collective-permute-done((f32[2,4,16]{2,1,0:T(4,128)S(1)}, f32[2,4,16]{2,1,0:T(4,128)S(1)}, u32[]{:S(2)}, u32[]{:S(2)}) %collective-permute-start.3) | collective-permute-done | bytes 544 | tf_op jit(solution)/shard_map/ppermute | solution.py:513
  54.1 3.6 %collective-permute-start.5 = (f32[3,8,16]{2,1,0:T(8,128)S(1)}, f32[3,8,16]{2,1,0:T(8,128)S(1)}, u32[]{:S(2)}, u32[]{:S(2)}) collective-permute-start(f32[3,8,16]{2,1,0:T(8,128)S(1)} %pad_maximum_fusion), channel_id=1, source_target_pairs={{1,0},{2,1},{3,2},{4,3},{5,4},{6,5},{7,6},{9,8},{10,9},{11,10},{12... | collective-permute-start | bytes 4616 | tf_op jit(solution)/shard_map/ppermute | solution.py:513
  57.7 3.8 %collective-permute-start.4 = (f32[3,8,16]{2,1,0:T(8,128)S(1)}, f32[3,8,16]{2,1,0:T(8,128)S(1)}, u32[]{:S(2)}, u32[]{:S(2)}) collective-permute-start(f32[3,8,16]{2,1,0:T(8,128)S(1)} %pad_maximum_fusion), channel_id=1, source_target_pairs={{0,1},{1,2},{2,3},{3,4},{4,5},{5,6},{6,7},{8,9},{9,10},{10,11},{11... | collective-permute-start | bytes 4616 | tf_op jit(solution)/shard_map/ppermute | solution.py:513
  61.4 0.0 collective-permute-done.7.off_ref
  61.5 0.0 collective-permute-done.6.on_ref
  61.5 2.3 %edges.1.refs_6_ = f32[8,4,272,128]{3,2,1,0:T(8,128)S(1)} custom-call(s32[2]{0:T(128)S(1)} %pad_add_fusion.tile_ref, s32[8,128]{1,0:T(8,128)S(1)} %get-tuple-element.16.target_ref, f32[8,128]{1,0:T(8,128)S(1)} %get-tuple-element.17.share_ref, bf16[8,2,128,128]{3,2,1,0:T(8,128)(2,1)S(1)} %collective-permute-done.6.on_ref, ...), custom_call_target="tpu_custom_call" | custom-call | flops 5000000 | bytes 4194304 | tf_op jit(solution)/shard_map/edges/pallas_call | solution.py:439
  63.8 1.9 %collective-permute-done.4.refs_3_ = f32[3,8,16]{2,1,0:T(8,128)S(1)} collective-permute-done((f32[3,8,16]{2,1,0:T(8,128)S(1)}, f32[3,8,16]{2,1,0:T(8,128)S(1)}, u32[]{:S(2)}, u32[]{:S(2)}) %collective-permute-start.4) | collective-permute-done | bytes 1568 | tf_op jit(solution)/shard_map/ppermute | solution.py:513
  65.7 7.1 %warp.1 = (bf16[1,8,16,128,128]{4,3,2,1,0:T(8,128)(2,1)}, f32[1,2,8,16]{3,2,1,0:T(8,128)}) custom-call(f32[2,4,16]{2,1,0:T(4,128)S(1)} %flow.2.refs_0_, f32[2,4,16]{2,1,0:T(4,128)S(1)} %collective-permute-done.3.refs_1_, s32[1,8,16]{2,1,0:T(8,128)S(1)} %copy-done.1, f32[3,8,16]{2,1,0:T(8,128)S(1)} %collective-permute-done.4.refs_3_, ...), custom_call_target="tpu_custom_call" | custom-call | flops 20000000 | bytes 12582912 | tf_op jit(solution)/shard_map/warp/pallas_call | solution.py:488
  (11 shorter events, 0.0 us)
Async XLA Ops:
  5.7 13.1 %copy-start.2 = (s32[1,8,16,4]{2,3,1,0:T(4,128)S(1)}, s32[1,8,16,4]{2,3,1,0:T(4,128)}, u32[]{:S(2)}) copy-start(s32[1,8,16,4]{2,3,1,0:T(4,128)} %param.12) | copy-start | bytes 6148
  5.7 13.1 %copy-start.3 = (s32[1,8,16,4]{2,3,1,0:T(4,128)S(1)}, s32[1,8,16,4]{2,3,1,0:T(4,128)}, u32[]{:S(2)}) copy-start(s32[1,8,16,4]{2,3,1,0:T(4,128)} %param.13) | copy-start | bytes 6148
  5.8 13.1 %copy-start.4 = (f32[1,8,16,4]{2,3,1,0:T(4,128)S(1)}, f32[1,8,16,4]{2,3,1,0:T(4,128)}, u32[]{:S(2)}) copy-start(f32[1,8,16,4]{2,3,1,0:T(4,128)} %param.15) | copy-start | bytes 6148
  5.8 13.1 %copy-start.5 = (s32[1,8,16]{2,1,0:T(8,128)S(1)}, s32[1,8,16]{2,1,0:T(8,128)}, u32[]{:S(2)}) copy-start(s32[1,8,16]{2,1,0:T(8,128)} %count_ref.1) | copy-start | bytes 1540
  5.8 29.9 %collective-permute-start.1 = (bf16[65,64,256]{2,1,0:T(8,128)(2,1)S(1)}, bf16[65,64,256]{2,1,0:T(8,128)(2,1)S(1)}, u32[]{:S(2)}, u32[]{:S(2)}) collective-permute-start(bf16[65,64,256]{2,1,0:T(8,128)(2,1)S(1)} %forward.3.own), channel_id=1, source_target_pairs={{0,8},{8,16},{16,24},{24,32},{32,40},{40,48},{48,56},{56,64},{64,7... | collective-permute-start | bytes 6389768 | tf_op jit(solution)/shard_map/ppermute | solution.py:513
  13.0 33.4 %collective-permute-start = (bf16[65,64,256]{2,1,0:T(8,128)(2,1)S(1)}, bf16[65,64,256]{2,1,0:T(8,128)(2,1)S(1)}, u32[]{:S(2)}, u32[]{:S(2)}) collective-permute-start(bf16[65,64,256]{2,1,0:T(8,128)(2,1)S(1)} %get-tuple-element.13.own), channel_id=1, source_target_pairs={{8,0},{16,8},{24,16},{32,24},{40,32},{48,40},{56,48},{64,56},{72,6... | collective-permute-start | bytes 6389768 | tf_op jit(solution)/shard_map/ppermute | solution.py:513
  18.8 11.7 %collective-permute-start.2 = (bf16[8,2,128,128]{3,2,1,0:T(8,128)(2,1)S(1)}, bf16[8,2,128,128]{3,2,1,0:T(8,128)(2,1)S(1)}, u32[]{:S(2)}, u32[]{:S(2)}) collective-permute-start(bf16[8,2,128,128]{3,2,1,0:T(8,128)(2,1)S(1)} %get-tuple-element.15), channel_id=1, source_target_pairs={{0,64},{1,65},{2,66},{3,67},{4,68},{5,69},{6,70},{7,71},{8,72},{9,... | collective-permute-start | bytes 1572872 | tf_op jit(solution)/shard_map/ppermute | solution.py:544
  19.6 16.2 %copy-start = (bf16[256,256]{1,0:T(8,128)(2,1)S(1)}, bf16[256,256]{1,0:T(8,128)(2,1)}, u32[]{:S(2)}) copy-start(bf16[256,256]{1,0:T(8,128)(2,1)} %constant.28.cols_hbm.cols_ref) | copy-start | bytes 393220
  19.6 16.1 %copy-start.6 = (bf16[256,256]{1,0:T(8,128)(2,1)S(1)}, bf16[256,256]{1,0:T(8,128)(2,1)}, u32[]{:S(2)}) copy-start(bf16[256,256]{1,0:T(8,128)(2,1)} %constant.29.back_cols_ref) | copy-start | bytes 393220
  19.6 16.1 %copy-start.7 = (bf16[128,128]{1,0:T(8,128)(2,1)S(1)}, bf16[128,128]{1,0:T(8,128)(2,1)}, u32[]{:S(2)}) copy-start(bf16[128,128]{1,0:T(8,128)(2,1)} %constant.30.back_rows_ref) | copy-start | bytes 98308
  28.3 13.3 %copy-start.1 = (s32[1,8,16]{2,1,0:T(8,128)S(1)}, s32[1,8,16]{2,1,0:T(8,128)}, u32[]{:S(2)}) copy-start(s32[1,8,16]{2,1,0:T(8,128)} %refs_2_.1) | copy-start | bytes 1540
  30.5 30.9 %collective-permute-start.7 = (bf16[8,2,128,128]{3,2,1,0:T(8,128)(2,1)S(1)}, bf16[8,2,128,128]{3,2,1,0:T(8,128)(2,1)S(1)}, u32[]{:S(2)}, u32[]{:S(2)}) collective-permute-start(bf16[8,2,128,128]{3,2,1,0:T(8,128)(2,1)S(1)} %collective-permute-done.2), channel_id=1, source_target_pairs={{64,7},{65,2},{66,1},{67,4},{68,3},{69,6},{70,5},{71,0},{72,15},{7... | collective-permute-start | bytes 1572872 | tf_op jit(solution)/shard_map/ppermute | solution.py:544
  39.4 22.0 %collective-permute-start.6 = (bf16[8,2,128,128]{3,2,1,0:T(8,128)(2,1)S(1)}, bf16[8,2,128,128]{3,2,1,0:T(8,128)(2,1)S(1)}, u32[]{:S(2)}, u32[]{:S(2)}) collective-permute-start(bf16[8,2,128,128]{3,2,1,0:T(8,128)(2,1)S(1)} %get-tuple-element.22), channel_id=1, source_target_pairs={{0,1},{1,0},{2,3},{3,2},{4,5},{5,4},{6,7},{7,6},{8,9},{9,8},{10,11... | collective-permute-start | bytes 1572872 | tf_op jit(solution)/shard_map/ppermute | solution.py:517
  41.6 12.5 %collective-permute-start.3 = (f32[2,4,16]{2,1,0:T(4,128)S(1)}, f32[2,4,16]{2,1,0:T(4,128)S(1)}, u32[]{:S(2)}, u32[]{:S(2)}) collective-permute-start(f32[2,4,16]{2,1,0:T(4,128)S(1)} %flow.3), channel_id=1, source_target_pairs={{8,0},{16,8},{24,16},{32,24},{40,32},{48,40},{56,48},{64,56},{72,6... | collective-permute-start | bytes 1544 | tf_op jit(solution)/shard_map/ppermute | solution.py:513
  54.1 9.7 %collective-permute-start.5 = (f32[3,8,16]{2,1,0:T(8,128)S(1)}, f32[3,8,16]{2,1,0:T(8,128)S(1)}, u32[]{:S(2)}, u32[]{:S(2)}) collective-permute-start(f32[3,8,16]{2,1,0:T(8,128)S(1)} %pad_maximum_fusion), channel_id=1, source_target_pairs={{1,0},{2,1},{3,2},{4,3},{5,4},{6,5},{7,6},{9,8},{10,9},{11,10},{12... | collective-permute-start | bytes 4616 | tf_op jit(solution)/shard_map/ppermute | solution.py:513
  57.7 8.0 %collective-permute-start.4 = (f32[3,8,16]{2,1,0:T(8,128)S(1)}, f32[3,8,16]{2,1,0:T(8,128)S(1)}, u32[]{:S(2)}, u32[]{:S(2)}) collective-permute-start(f32[3,8,16]{2,1,0:T(8,128)S(1)} %pad_maximum_fusion), channel_id=1, source_target_pairs={{0,1},{1,2},{2,3},{3,4},{4,5},{5,6},{6,7},{8,9},{9,10},{10,11},{11... | collective-permute-start | bytes 4616 | tf_op jit(solution)/shard_map/ppermute | solution.py:513

commit v5 on v4

--- a/solution.py
+++ b/solution.py
@@ -81,103 +81,99 @@
             copy.wait()
 
 
-def forward_kernel(start, strips, tile_ref, x_hbm, rows_hbm, cols_hbm, *refs):
-    spec_ref, refs = refs[0], refs[1:]
-    if strips:
-        on_ref, off_ref, on_x, off_x, strip_sems = refs[:2] + refs[-3:]
-        refs = refs[2:-3]
-    x_ref, lines_ref, ends_ref, rows_ref, cols_ref, in_sems, table_sems = refs
+def forward_kernel(start, toward_pair, tile_ref, x_hbm, rows_hbm, cols_hbm, *refs):
+    *_, spec_ref, src_ref, strip_ref, x_ref, rest_ref, lines_ref, ends_ref, rows_ref, cols_ref, in_sems, more_sems = refs
     y = pl.program_id(0)
     count, patches = x_ref.shape[:2]
+    ny = strip_ref.shape[0]
+    odd = tile_ref[0] % 2
+    column = ((1 - odd) if toward_pair else odd) * (patches - HB)
+    rest = (start + count) % ny
     fetch = lambda row: [pltpu.make_async_copy(x_hbm.at[0, start + row], x_ref.at[row], in_sems.at[row])]
-    tables_in = [
-        pltpu.make_async_copy(rows_hbm, rows_ref, table_sems.at[0]),
-        pltpu.make_async_copy(cols_hbm, cols_ref, table_sems.at[1]),
+    more = [
+        pltpu.make_async_copy(rows_hbm, rows_ref, more_sems.at[0]),
+        pltpu.make_async_copy(cols_hbm, cols_ref, more_sems.at[1]),
+        pltpu.make_async_copy(
+            x_hbm.at[0, pl.ds(rest, ny - count), pl.ds(column, HB)], rest_ref, more_sems.at[2]
+        ),
     ]
 
     @pl.when(y == 0)
     def _():
-        for copy in tables_in:
+        for copy in more[:2]:
             copy.start()
 
     ahead(fetch, count, min(DEPTH, count))
 
     @pl.when(y == 0)
     def _():
-        for copy in tables_in:
+        for copy in more[:2]:
             copy.wait()
-
-    if strips:
-        odd = tile_ref[0] % 2
-        strip_copies = [
-            pltpu.make_async_copy(x_hbm.at[0, :, pl.ds(column, HB)], target, strip_sems.at[i])
-            for i, (column, target) in enumerate(
-                (((1 - odd) * (patches - HB), on_x), (odd * (patches - HB), off_x))
-            )
-        ]
-
-        @pl.when(y == 0)
-        def _():
-            for copy in strip_copies:
-                copy.start()
-
-        @pl.when(y == count - 1)
-        def _():
-            for copy in strip_copies:
-                copy.wait()
-            on_ref[...] = on_x[...].astype(jnp.bfloat16)
-            off_ref[...] = off_x[...].astype(jnp.bfloat16)
-
+        more[2].start()
+
+    @pl.when(y == count - 1)
+    def _():
+        more[2].wait()
+        strip_ref[rest : rest + ny - count] = rest_ref[...].astype(jnp.bfloat16)
+
+    for i in range(HB):
+        strip_ref[start + y, i] = x_ref[y, column + i].astype(jnp.bfloat16)
     rows2 = rows_ref[...]
     cols = cols_ref[...]
-    cols2 = jnp.concatenate([cols, cols], axis=0)
     for pair in range(patches // 2):
         x = jnp.concatenate([x_ref[y, 2 * pair], x_ref[y, 2 * pair + 1]], axis=1)
-        both = dot(rows2, jnp.concatenate(split(x), axis=0))
+        high, low = split(x)
+        src_ref[start + y, 2 * pair] = high[:, :N]
+        src_ref[start + y, 2 * pair + 1] = high[:, N:]
+        both = dot(rows2, jnp.concatenate([high, low], axis=0))
         for side in range(2):
             here = both[:, side * N : (side + 1) * N]
             p = 2 * pair + side
             ends_ref[p : p + 1, :N] = here[:1]
             ends_ref[p : p + 1, N:] = here[HALF : HALF + 1]
-            lines = jnp.concatenate([here[:HALF], here[HALF:]], axis=1)
-            high, low = split(lines)
-            lines_ref[p * HALF : (p + 1) * HALF, : 2 * N] = high
-            lines_ref[p * HALF : (p + 1) * HALF, 2 * N :] = low
+            lines_ref[p * HALF : (p + 1) * HALF, :N] = here[:HALF].astype(jnp.bfloat16)
+            lines_ref[p * HALF : (p + 1) * HALF, N:] = here[HALF:].astype(jnp.bfloat16)
     step = 4
     for first in range(0, patches, step):
         lines = lines_ref[first * HALF : (first + step) * HALF, :]
-        freq = dot(lines, cols2).reshape(step, HALF, 2 * N)
+        freq = dot(lines, cols).reshape(step, HALF, 2 * N)
         spec_ref[pl.ds(y * patches + first, step)] = freq.astype(jnp.bfloat16)
     ends = ends_ref[...].astype(jnp.bfloat16)
     spec_ref[count * patches, pl.ds(pl.multiple_of(y * patches, patches), patches), :] = ends
 
 
-def forward(tile, sections, start, count, strips, rows, cols):
+def forward(tile, sections, start, count, toward_pair, source, rows, cols):
     _, ny, nx, _, _ = sections.shape
     rows2 = jnp.concatenate([rows, rows], axis=1).astype(jnp.bfloat16)
     spectra = (count * nx + 1, HALF, 2 * N)
-    strip = (ny, HB, N, N)
-    extra = [pltpu.VMEM(strip, jnp.float32)] * 2 + [pltpu.SemaphoreType.DMA((2,))]
+    before = () if source is None else (in_vmem(source),)
     return pl.pallas_call(
-        functools.partial(forward_kernel, start, strips),
+        functools.partial(forward_kernel, start, toward_pair),
         grid=(count,),
-        in_specs=[pl.BlockSpec(memory_space=pltpu.SMEM)] + [pl.BlockSpec(memory_space=pltpu.HBM)] * 3,
-        out_specs=[pl.BlockSpec(memory_space=pltpu.VMEM)] * (3 if strips else 1),
-        out_shape=[pltpu.VMEM(spectra, jnp.bfloat16)] + [pltpu.VMEM(strip, jnp.bfloat16)] * (2 if strips else 0),
+        in_specs=[pl.BlockSpec(memory_space=pltpu.SMEM)]
+        + [pl.BlockSpec(memory_space=pltpu.HBM)] * 3
+        + [pl.BlockSpec(memory_space=pltpu.VMEM)] * len(before),
+        out_specs=[pl.BlockSpec(memory_space=pltpu.VMEM)] * 3,
+        out_shape=[
+            pltpu.VMEM(spectra, jnp.bfloat16),
+            pltpu.VMEM((ny, nx, N, N), jnp.bfloat16),
+            pltpu.VMEM((ny, HB, N, N), jnp.bfloat16),
+        ],
         scratch_shapes=[
             pltpu.VMEM((count, nx, N, N), jnp.float32),
-            pltpu.VMEM((nx * HALF, 4 * N), jnp.bfloat16),
+            pltpu.VMEM((ny - count, HB, N, N), jnp.float32),
+            pltpu.VMEM((nx * HALF, 2 * N), jnp.bfloat16),
             pltpu.VMEM((nx, 2 * N), jnp.float32),
             pltpu.VMEM((N, 2 * N), jnp.bfloat16),
             pltpu.VMEM((2 * N, 2 * N), jnp.bfloat16),
             pltpu.SemaphoreType.DMA((count,)),
-            pltpu.SemaphoreType.DMA((2,)),
-        ]
-        + (extra if strips else []),
-        compiler_params=pltpu.CompilerParams(vmem_limit_bytes=16 * MIB),
+            pltpu.SemaphoreType.DMA((3,)),
+        ],
+        input_output_aliases={4: 1} if before else {},
+        compiler_params=pltpu.CompilerParams(vmem_limit_bytes=12 * MIB),
         cost_estimate=pl.CostEstimate(flops=2_000_000_000, bytes_accessed=6 * MIB, transcendentals=0),
         name="forward",
-    )(tile, in_hbm(sections), in_hbm(rows2), in_hbm(cols.astype(jnp.bfloat16)))
+    )(tile, in_hbm(sections), in_hbm(rows2), in_hbm(cols.astype(jnp.bfloat16)), *before)
 
 
 def times_conj(a, b, sign):
@@ -273,7 +269,7 @@
             pltpu.VMEM((ny, nx, N), jnp.float32),
         ],
         compiler_params=pltpu.CompilerParams(vmem_limit_bytes=8 * MIB),
-        cost_estimate=pl.CostEstimate(flops=2_000_000_000, bytes_accessed=4 * MIB, transcendentals=0),
+        cost_estimate=pl.CostEstimate(flops=50_000_000_000, bytes_accessed=4 * MIB, transcendentals=0),
         name="flow",
     )(in_vmem(own), in_vmem(other), *(t.astype(jnp.bfloat16) for t in (cols, back_cols, back_rows)))
 
@@ -314,6 +310,7 @@
             jax.ShapeDtypeStruct((ny, N), jnp.float32),
         ],
         compiler_params=pltpu.CompilerParams(vmem_limit_bytes=4 * MIB),
+        cost_estimate=pl.CostEstimate(flops=0, bytes_accessed=0, transcendentals=0),
         name="slots",
     )(tile, slots_first(box_row), slots_first(box_shift), box_count, slots_first(blend_weight))
 
@@ -327,51 +324,35 @@
     return total
 
 
-def blend_kernel(target_ref, share_ref, x_hbm, out_ref, window, staging, in_sems):
+def blend_kernel(target_ref, share_ref, source, out_ref):
     y = pl.program_id(0)
-    ny, nx = staging.shape[:2]
+    nx = source.shape[1]
     border = jnp.zeros((nx, PAD, N), jnp.float32)
     out_ref[y, :, :PAD] = border
     out_ref[y, :, PAD + N :] = border
-
-    @pl.when(y == 0)
-    def _():
-        copies = [
-            pltpu.make_async_copy(x_hbm.at[0, row], staging.at[row], in_sems.at[row]) for row in range(ny)
-        ]
-        for copy in copies:
-            copy.start()
-        for row, copy in enumerate(copies):
-            copy.wait()
-            for x in range(nx):
-                window[row, x] = staging[row, x].astype(jnp.bfloat16)
-
     for x in range(nx):
-        out_ref[y, x, PAD : PAD + N] = blend_cell(y, x, nx, target_ref, share_ref, window)
-
-
-def blend(target, share, sections):
-    _, ny, nx, _, _ = sections.shape
-    shape = sections.shape[1:]
+        out_ref[y, x, PAD : PAD + N] = blend_cell(y, x, nx, target_ref, share_ref, source)
+
+
+def blend(target, share, source):
+    ny, nx = source.shape[:2]
     return pl.pallas_call(
         blend_kernel,
         grid=(ny,),
-        in_specs=[pl.BlockSpec(memory_space=pltpu.SMEM)] * 2 + [pl.BlockSpec(memory_space=pltpu.HBM)],
+        in_specs=[pl.BlockSpec(memory_space=pltpu.SMEM)] * 2 + [pl.BlockSpec(memory_space=pltpu.VMEM)],
         out_specs=pl.BlockSpec(memory_space=pltpu.VMEM),
         out_shape=pltpu.VMEM((ny, nx, N + 2 * PAD, N), jnp.float32),
-        scratch_shapes=[
-            pltpu.VMEM(shape, jnp.bfloat16),
-            pltpu.VMEM(shape, jnp.float32),
-            pltpu.SemaphoreType.DMA((ny,)),
-        ],
-        compiler_params=pltpu.CompilerParams(vmem_limit_bytes=16 * MIB),
-        cost_estimate=pl.CostEstimate(flops=20_000_000, bytes_accessed=16 * MIB, transcendentals=0),
+        compiler_params=pltpu.CompilerParams(vmem_limit_bytes=4 * MIB),
+        cost_estimate=pl.CostEstimate(flops=20_000_000, bytes_accessed=4 * MIB, transcendentals=0),
         name="blend",
-    )(target, share, in_hbm(sections))
-
-
-def relax(low_ref, high_ref, mask_ref, left_ref, right_ref):
+    )(target, share, in_vmem(source))
+
+
+def relax(tile_ref, low_ref, high_ref, mask_ref, on_ref, off_ref):
     ny, nx = mask_ref.shape[1:]
+    even = tile_ref[0] % 2 == 0
+    left_ref = [jnp.where(even, off_ref[i], on_ref[i]) for i in range(3)]
+    right_ref = [jnp.where(even, on_ref[i], off_ref[i]) for i in range(3)]
     rest = jnp.zeros((ny, N - nx - 2 * STEPS), jnp.float32)
 
     def across(left, own, right):
@@ -449,14 +430,14 @@
     )(tile, target, share, in_vmem(on), in_vmem(off), in_vmem(blended))
 
 
-def warp_kernel(*refs):
+def warp_kernel(tile_ref, *refs):
     *flows, padded, edges, out_hbm, field_ref, out, wide, field, sem, out_sems = refs
     y = pl.program_id(0)
     ny, nx = out.shape[:2]
 
     @pl.when(y == 0)
     def _():
-        for component, values in enumerate(relax(*flows)):
+        for component, values in enumerate(relax(tile_ref, *flows)):
             wide[component] = values
             field_ref[0, component] = values[:, STEPS : STEPS + nx]
         scalars = pltpu.make_async_copy(wide, field, sem)
@@ -482,13 +463,15 @@
     wait_all([store(row) for row in range(ny)])
 
 
-def warp(flows, blended, edges):
+def warp(tile, flows, blended, edges):
     ny, nx = blended.shape[:2]
     whole = lambda shape: pl.BlockSpec(shape, lambda y: (0,) * len(shape))
     return pl.pallas_call(
         warp_kernel,
         grid=(ny,),
-        in_specs=[whole(x.shape) for x in flows] + [pl.BlockSpec(memory_space=pltpu.VMEM)] * 2,
+        in_specs=[pl.BlockSpec(memory_space=pltpu.SMEM)]
+        + [whole(x.shape) for x in flows]
+        + [pl.BlockSpec(memory_space=pltpu.VMEM)] * 2,
         out_specs=[pl.BlockSpec(memory_space=pl.ANY), whole((1, 2, ny, nx))],
         out_shape=[
             jax.ShapeDtypeStruct((1, ny, nx, N, N), jnp.bfloat16),
@@ -504,7 +487,7 @@
         compiler_params=pltpu.CompilerParams(vmem_limit_bytes=8 * MIB),
         cost_estimate=pl.CostEstimate(flops=20_000_000, bytes_accessed=12 * MIB, transcendentals=0),
         name="warp",
-    )(*flows, in_vmem(blended), in_vmem(edges))
+    )(tile, *flows, in_vmem(blended), in_vmem(edges))
 
 
 def from_behind(x, axis, by):
@@ -517,7 +500,7 @@
     return lax.ppermute(x, "tile", [(i, i ^ 1) for i in range(lax.axis_size("tile"))])
 
 
-def hops(tiles, sections):
+def hops(tiles, sections, beyond):
     pairs = ([], [])
     for section in range(sections):
         x_low, rest = divmod(section, sections // 2)
@@ -527,7 +510,7 @@
             ends = [section * tiles + tile]
             for hop in (1, 2):
                 x = (2 * x_high + x_low + hop * way) % 4
-                to_z = (z + 2 * x_high - 1) % (tiles // 2) if hop == 2 else z
+                to_z = (z + 2 * x_high - 1) % (tiles // 2) if beyond and hop == 2 else z
                 ends.append((x % 2 * (sections // 2) + rest) * tiles + 2 * to_z + x // 2)
             pairs[0].append((ends[0], ends[1]))
             pairs[1].append((ends[1], ends[2]))
@@ -540,32 +523,34 @@
     half = ny // 2
     tiles, count = lax.axis_size("tile"), lax.axis_size("sec")
     tile = jnp.stack([lax.axis_index("tile"), tiles]).astype(jnp.int32)
-    off_hops = hops(tiles, count)
+    on_hops, off_hops = hops(tiles, count, False), hops(tiles, count, True)
     hop = lambda x, pairs: lax.ppermute(x, ("sec", "tile"), pairs)
 
-    spectra_high, = forward(tile, sections, half, half, False, rows, cols)
+    spectra_high, source, on = forward(tile, sections, half, half, True, None, rows, cols)
     from_last = from_behind(spectra_high, "sec", 1)
-    spectra_low, on, off = forward(tile, sections, 0, half, True, rows, cols)
+    on = hop(on, on_hops[0])
+    spectra_low, source, off = forward(tile, sections, 0, half, False, source, rows, cols)
     from_next = from_behind(spectra_low, "sec", -1)
     off = hop(off, off_hops[0])
     target, share = slots_of(tile, box_row, box_shift, box_count, blend_weight)
-    blended = blend(target, share, sections)
-    off, blended = lax.optimization_barrier((off, blended))
+    on, source = lax.optimization_barrier((on, source))
+    on = hop(on, on_hops[1])
+    blended = blend(target, share, source)
+    from_last, blended = lax.optimization_barrier((from_last, blended))
+
+    flow_high = flow_of(spectra_high, from_last, -1, half, nx, cols, back_cols, back_rows)
+    off, flow_high = lax.optimization_barrier((off, flow_high))
+    flow_high = from_behind(flow_high, "sec", -1)
     off = hop(off, off_hops[1])
-    from_last, blended = lax.optimization_barrier((from_last, blended))
-
-    flow_high = flow_of(spectra_high, from_last, -1, half, nx, cols, back_cols, back_rows)
-    on, flow_high = lax.optimization_barrier((on, flow_high))
-    flow_high = from_behind(flow_high, "sec", -1)
-    on = swapped(on)
     flow_low = flow_of(spectra_low, from_next, 1, half, nx, cols, back_cols, back_rows)
     flow = jnp.concatenate([flow_low, flow_high], axis=1)
     flow = jnp.concatenate([flow, node_mask.astype(jnp.float32) + 1.0], axis=0)
-    flow_left = from_behind(flow, "tile", 1)
-    flow_right = from_behind(flow, "tile", -1)
-    flows = (flow_low, flow_high, node_mask, flow_left, flow_right)
+    beyond = [(i, i + 1) for i in range(1, tiles - 1, 2)]
+    flow_off = lax.ppermute(flow, "tile", beyond + [(j, i) for i, j in beyond])
+    flow_on = swapped(flow)
+    flows = (flow_low, flow_high, node_mask, flow_on, flow_off)
     edges = edges_of(tile, target, share, on, off, blended)
-    return tuple(warp(flows, blended, edges))
+    return tuple(warp(tile, flows, blended, edges))
 
 
 def solution(mesh):

time: 74.2 us -> 71.9 us (0.969)
  the two profiles are of different devices: /device:TPU:66 before, /device:TPU:1 now
where the time goes in v5:
time: 71.9 us; the launch traced here: 71.7 us
  Pallas kernels  33 us (46%)
  starting transfers between devices  22.5 us (31%)
  waiting for transfers between devices  15.3 us (21%)
  between operations  0.81 us (1%)
    ppermute x4, waiting for transfers between devices, per_device(): hop = lambda x, pairs: lax.ppermute(x, ('sec', 'tile'), pairs)  12.2 us
    ppermute x3, starting transfers between devices, from_behind(): return lax.ppermute(x, axis, pairs)  12.1 us
    pallas_call x2, Pallas kernels, forward(): pl.pallas_call(functools.partial(forward_kernel, start, toward_pair), gri...  9.82 us
    pallas_call x1, Pallas kernels, warp(): pl.pallas_call(warp_kernel, grid=(ny,), in_specs=[pl.BlockSpec(memory_spa...  7.83 us
    pallas_call x2, Pallas kernels, flow_of(): pl.pallas_call(functools.partial(flow_kernel, sign), grid=(ny,), in_specs...  7.39 us
    ppermute x4, starting transfers between devices, per_device(): hop = lambda x, pairs: lax.ppermute(x, ('sec', 'tile'), pairs)  5.15 us
    pallas_call x1, Pallas kernels, blend(): pl.pallas_call(blend_kernel, grid=(ny,), in_specs=[pl.BlockSpec(memory_sp...  5 us
    ppermute x1, starting transfers between devices, swapped(): lax.ppermute(x, 'tile', [(i, i ^ 1) for i in range(lax.axis_size('tile'))])  4.59 us
  transfers between devices with their start and end apart: 9, of which 4 were waited for; matrix products, arithmetic and copies ran while one was open for 0% of the time, Pallas kernels for 28%

profile of v5, /device:TPU:1, one launch (start us, length us, event | category | flops | bytes accessed | tf_op | source)
XLA Modules:
  0.0 71.7 jit_solution(6445204334595269995)
XLA Ops:
  0.6 0.1 pad_add_fusion.tile_ref
  0.7 4.9 %forward.2 = (bf16[65,64,256]{2,1,0:T(8,128)(2,1)S(1)}, bf16[8,16,128,128]{3,2,1,0:T(8,128)(2,1)S(1)}, bf16[8,2,128,128]{3,2,1,0:T(8,128)(2,1)S(1)}) custom-call(s32[2]{0:T(128)S(1)} %pad_add_fusion.tile_ref, f32[1,8,16,128,128]{4,3,2,1,0:T(8,128)} %x_hbm.3, bf16[128,256]{1,0:T(8,128)(2,1)} %constant.27.rows_hbm, bf16[256,256]{1,0:T(8,128)(2,1)} %constant.28.cols_hbm.cols_ref), custom_call_target="tpu_custom_call" | custom-call | flops 2000000000 | bytes 6291456 | tf_op jit(solution)/shard_map/forward/pallas_call | solution.py:150
  5.6 4.6 %collective-permute-start.2 = (bf16[65,64,256]{2,1,0:T(8,128)(2,1)S(1)}, bf16[65,64,256]{2,1,0:T(8,128)(2,1)S(1)}, u32[]{:S(2)}, u32[]{:S(2)}) collective-permute-start(bf16[65,64,256]{2,1,0:T(8,128)(2,1)S(1)} %get-tuple-element.19.own), channel_id=1, source_target_pairs={{0,8},{8,16},{16,24},{24,32},{32,40},{40,48},{48,56},{56,64},{64,7... | collective-permute-start | bytes 6389768 | tf_op jit(solution)/shard_map/ppermute | solution.py:496
  10.2 1.3 %collective-permute-start.3 = (bf16[8,2,128,128]{3,2,1,0:T(8,128)(2,1)S(1)}, bf16[8,2,128,128]{3,2,1,0:T(8,128)(2,1)S(1)}, u32[]{:S(2)}, u32[]{:S(2)}) collective-permute-start(bf16[8,2,128,128]{3,2,1,0:T(8,128)(2,1)S(1)} %get-tuple-element.22), channel_id=1, source_target_pairs={{0,64},{1,65},{2,66},{3,67},{4,68},{5,69},{6,70},{7,71},{8,72},{9,... | collective-permute-start | bytes 1572872 | tf_op jit(solution)/shard_map/ppermute | solution.py:527
  11.5 0.0 copy-start.4
  11.5 4.9 %forward.3 = (bf16[65,64,256]{2,1,0:T(8,128)(2,1)S(1)}, bf16[8,16,128,128]{3,2,1,0:T(8,128)(2,1)S(1)}, bf16[8,2,128,128]{3,2,1,0:T(8,128)(2,1)S(1)}) custom-call(s32[2]{0:T(128)S(1)} %pad_add_fusion.tile_ref, f32[1,8,16,128,128]{4,3,2,1,0:T(8,128)} %x_hbm.3, bf16[128,256]{1,0:T(8,128)(2,1)} %constant.27.rows_hbm, ...), custom_call_target="tpu_custom_call", output_to_operand_aliasing={{1}: (4, {})} | custom-call | flops 2000000000 | bytes 6291456 | tf_op jit(solution)/shard_map/forward/pallas_call | solution.py:150
  16.5 1.3 %collective-permute-start.1 = (bf16[8,2,128,128]{3,2,1,0:T(8,128)(2,1)S(1)}, bf16[8,2,128,128]{3,2,1,0:T(8,128)(2,1)S(1)}, u32[]{:S(2)}, u32[]{:S(2)}) collective-permute-start(bf16[8,2,128,128]{3,2,1,0:T(8,128)(2,1)S(1)} %get-tuple-element.18), channel_id=1, source_target_pairs={{0,64},{1,65},{2,66},{3,67},{4,68},{5,69},{6,70},{7,71},{8,72},{9,... | collective-permute-start | bytes 1572872 | tf_op jit(solution)/shard_map/ppermute | solution.py:527
  17.7 1.9 %collective-permute-start = (bf16[65,64,256]{2,1,0:T(8,128)(2,1)S(1)}, bf16[65,64,256]{2,1,0:T(8,128)(2,1)S(1)}, u32[]{:S(2)}, u32[]{:S(2)}) collective-permute-start(bf16[65,64,256]{2,1,0:T(8,128)(2,1)S(1)} %get-tuple-element.17.own), channel_id=1, source_target_pairs={{8,0},{16,8},{24,16},{32,24},{40,32},{48,40},{56,48},{64,56},{72,6... | collective-permute-start | bytes 6389768 | tf_op jit(solution)/shard_map/ppermute | solution.py:496
  19.6 0.0 copy-done.1
  19.7 0.0 copy-done.2
  19.7 0.0 copy-done.3
  19.7 0.6 slots.1
  20.3 0.0 copy-done.4
  20.4 5.1 %collective-permute-done.3 = bf16[8,2,128,128]{3,2,1,0:T(8,128)(2,1)S(1)} collective-permute-done((bf16[8,2,128,128]{3,2,1,0:T(8,128)(2,1)S(1)}, bf16[8,2,128,128]{3,2,1,0:T(8,128)(2,1)S(1)}, u32[]{:S(2)}, u32[]{:S(2)}) %collective-permute-start.3) | collective-permute-done | bytes 524320 | tf_op jit(solution)/shard_map/ppermute | solution.py:527
  25.5 0.0 collective-permute-start.7
  25.5 5.0 %blend.1.padded.refs_5_ = f32[8,16,272,128]{3,2,1,0:T(8,128)S(1)} custom-call(s32[8,128]{1,0:T(8,128)S(1)} %get-tuple-element.20.target_ref, f32[8,128]{1,0:T(8,128)S(1)} %get-tuple-element.21.share_ref, bf16[8,16,128,128]{3,2,1,0:T(8,128)(2,1)S(1)} %get-tuple-element.24.source), custom_call_target="tpu_custom_call" | custom-call | flops 20000000 | bytes 4194304 | tf_op jit(solution)/shard_map/blend/pallas_call | solution.py:339
  30.5 3.0 %collective-permute-done.2.other = bf16[65,64,256]{2,1,0:T(8,128)(2,1)S(1)} collective-permute-done((bf16[65,64,256]{2,1,0:T(8,128)(2,1)S(1)}, bf16[65,64,256]{2,1,0:T(8,128)(2,1)S(1)}, u32[]{:S(2)}, u32[]{:S(2)}) %collective-permute-start.2) | collective-permute-done | bytes 2129952 | tf_op jit(solution)/shard_map/ppermute | solution.py:496
  33.5 3.7 %flow.3 = f32[2,4,16]{2,1,0:T(4,128)S(1)} custom-call(bf16[65,64,256]{2,1,0:T(8,128)(2,1)S(1)} %get-tuple-element.19.own, bf16[65,64,256]{2,1,0:T(8,128)(2,1)S(1)} %collective-permute-done.2.other, bf16[256,256]{1,0:T(8,128)(2,1)S(1)} %copy-done, bf16[256,256]{1,0:T(8,128)(2,1)S(1)} %copy-done.6, bf16[128,128]{1,0:T(8,128)(2,1)S(1)} %copy-done.7), custom_call_target="tpu_custom_call" | custom-call | flops 49999998976 | bytes 4194304 | tf_op jit(solution)/shard_map/flow/pallas_call | solution.py:254
  37.2 0.0 collective-permute-done.1
  37.2 2.6 %collective-permute-start.8 = (bf16[8,2,128,128]{3,2,1,0:T(8,128)(2,1)S(1)}, bf16[8,2,128,128]{3,2,1,0:T(8,128)(2,1)S(1)}, u32[]{:S(2)}, u32[]{:S(2)}) collective-permute-start(bf16[8,2,128,128]{3,2,1,0:T(8,128)(2,1)S(1)} %collective-permute-done.1), channel_id=1, source_target_pairs={{64,7},{65,2},{66,1},{67,4},{68,3},{69,6},{70,5},{71,0},{72,15},{7... | collective-permute-start | bytes 1572872 | tf_op jit(solution)/shard_map/ppermute | solution.py:527
  39.8 5.6 %collective-permute-start.4 = (f32[2,4,16]{2,1,0:T(4,128)S(1)}, f32[2,4,16]{2,1,0:T(4,128)S(1)}, u32[]{:S(2)}, u32[]{:S(2)}) collective-permute-start(f32[2,4,16]{2,1,0:T(4,128)S(1)} %flow.3), channel_id=1, source_target_pairs={{8,0},{16,8},{24,16},{32,24},{40,32},{48,40},{56,48},{64,56},{72,6... | collective-permute-start | bytes 1544 | tf_op jit(solution)/shard_map/ppermute | solution.py:496
  45.4 0.1 collective-permute-done.other
  45.5 3.7 %flow.2.refs_0_ = f32[2,4,16]{2,1,0:T(4,128)S(1)} custom-call(bf16[65,64,256]{2,1,0:T(8,128)(2,1)S(1)} %get-tuple-element.17.own, bf16[65,64,256]{2,1,0:T(8,128)(2,1)S(1)} %collective-permute-done.other, bf16[256,256]{1,0:T(8,128)(2,1)S(1)} %copy-done, bf16[256,256]{1,0:T(8,128)(2,1)S(1)} %copy-done.6, bf16[128,128]{1,0:T(8,128)(2,1)S(1)} %copy-done.7), custom_call_target="tpu_custom_call" | custom-call | flops 49999998976 | bytes 4194304 | tf_op jit(solution)/shard_map/flow/pallas_call | solution.py:254
  49.2 0.0 collective-permute-done.4.refs_1_
  49.3 4.6 %collective-permute-start.5 = (f32[3,8,16]{2,1,0:T(8,128)S(1)}, f32[3,8,16]{2,1,0:T(8,128)S(1)}, u32[]{:S(2)}, u32[]{:S(2)}) collective-permute-start(f32[3,8,16]{2,1,0:T(8,128)S(1)} %pad_maximum_fusion), channel_id=1, source_target_pairs={{0,1},{1,0},{2,3},{3,2},{4,5},{5,4},{6,7},{7,6},{8,9},{9,8},{10,11... | collective-permute-start | bytes 4616 | tf_op jit(solution)/shard_map/ppermute | solution.py:500
  53.8 0.7 collective-permute-start.6
  54.5 0.0 collective-permute-done.7.on_ref
  54.5 7.1 %collective-permute-done.8.off_ref = bf16[8,2,128,128]{3,2,1,0:T(8,128)(2,1)S(1)} collective-permute-done((bf16[8,2,128,128]{3,2,1,0:T(8,128)(2,1)S(1)}, bf16[8,2,128,128]{3,2,1,0:T(8,128)(2,1)S(1)}, u32[]{:S(2)}, u32[]{:S(2)}) %collective-permute-start.8) | collective-permute-done | bytes 524320 | tf_op jit(solution)/shard_map/ppermute | solution.py:527
  61.6 2.3 %edges.1.refs_6_ = f32[8,4,272,128]{3,2,1,0:T(8,128)S(1)} custom-call(s32[2]{0:T(128)S(1)} %pad_add_fusion.tile_ref, s32[8,128]{1,0:T(8,128)S(1)} %get-tuple-element.20.target_ref, f32[8,128]{1,0:T(8,128)S(1)} %get-tuple-element.21.share_ref, bf16[8,2,128,128]{3,2,1,0:T(8,128)(2,1)S(1)} %collective-permute-done.7.on_ref, ...), custom_call_target="tpu_custom_call" | custom-call | flops 5000000 | bytes 4194304 | tf_op jit(solution)/shard_map/edges/pallas_call | solution.py:420
  63.9 0.0 collective-permute-done.5.refs_3_
  63.9 0.0 collective-permute-done.6.refs_4_
  63.9 7.8 %warp.1 = (bf16[1,8,16,128,128]{4,3,2,1,0:T(8,128)(2,1)}, f32[1,2,8,16]{3,2,1,0:T(8,128)}) custom-call(s32[2]{0:T(128)S(1)} %pad_add_fusion.tile_ref, f32[2,4,16]{2,1,0:T(4,128)S(1)} %flow.2.refs_0_, f32[2,4,16]{2,1,0:T(4,128)S(1)} %collective-permute-done.4.refs_1_, s32[1,8,16]{2,1,0:T(8,128)S(1)} %copy-done.4, ...), custom_call_target="tpu_custom_call" | custom-call | flops 20000000 | bytes 12582912 | tf_op jit(solution)/shard_map/warp/pallas_call | solution.py:469
  (13 shorter events, 0.0 us)
Async XLA Ops:
  5.6 27.9 %collective-permute-start.2 = (bf16[65,64,256]{2,1,0:T(8,128)(2,1)S(1)}, bf16[65,64,256]{2,1,0:T(8,128)(2,1)S(1)}, u32[]{:S(2)}, u32[]{:S(2)}) collective-permute-start(bf16[65,64,256]{2,1,0:T(8,128)(2,1)S(1)} %get-tuple-element.19.own), channel_id=1, source_target_pairs={{0,8},{8,16},{16,24},{24,32},{32,40},{40,48},{48,56},{56,64},{64,7... | collective-permute-start | bytes 6389768 | tf_op jit(solution)/shard_map/ppermute | solution.py:496
  10.2 15.2 %collective-permute-start.3 = (bf16[8,2,128,128]{3,2,1,0:T(8,128)(2,1)S(1)}, bf16[8,2,128,128]{3,2,1,0:T(8,128)(2,1)S(1)}, u32[]{:S(2)}, u32[]{:S(2)}) collective-permute-start(bf16[8,2,128,128]{3,2,1,0:T(8,128)(2,1)S(1)} %get-tuple-element.22), channel_id=1, source_target_pairs={{0,64},{1,65},{2,66},{3,67},{4,68},{5,69},{6,70},{7,71},{8,72},{9,... | collective-permute-start | bytes 1572872 | tf_op jit(solution)/shard_map/ppermute | solution.py:527
  11.5 8.1 %copy-start.1 = (s32[1,8,16,4]{2,3,1,0:T(4,128)S(1)}, s32[1,8,16,4]{2,3,1,0:T(4,128)}, u32[]{:S(2)}) copy-start(s32[1,8,16,4]{2,3,1,0:T(4,128)} %param.12) | copy-start | bytes 6148
  11.5 8.2 %copy-start.2 = (s32[1,8,16,4]{2,3,1,0:T(4,128)S(1)}, s32[1,8,16,4]{2,3,1,0:T(4,128)}, u32[]{:S(2)}) copy-start(s32[1,8,16,4]{2,3,1,0:T(4,128)} %param.13) | copy-start | bytes 6148
  11.5 8.2 %copy-start.3 = (f32[1,8,16,4]{2,3,1,0:T(4,128)S(1)}, f32[1,8,16,4]{2,3,1,0:T(4,128)}, u32[]{:S(2)}) copy-start(f32[1,8,16,4]{2,3,1,0:T(4,128)} %param.15) | copy-start | bytes 6148
  11.5 8.2 %copy-start.5 = (s32[1,8,16]{2,1,0:T(8,128)S(1)}, s32[1,8,16]{2,1,0:T(8,128)}, u32[]{:S(2)}) copy-start(s32[1,8,16]{2,1,0:T(8,128)} %count_ref.1) | copy-start | bytes 1540
  11.5 8.8 %copy-start.4 = (s32[1,8,16]{2,1,0:T(8,128)S(1)}, s32[1,8,16]{2,1,0:T(8,128)}, u32[]{:S(2)}) copy-start(s32[1,8,16]{2,1,0:T(8,128)} %refs_2_.1) | copy-start | bytes 1540
  16.5 20.8 %collective-permute-start.1 = (bf16[8,2,128,128]{3,2,1,0:T(8,128)(2,1)S(1)}, bf16[8,2,128,128]{3,2,1,0:T(8,128)(2,1)S(1)}, u32[]{:S(2)}, u32[]{:S(2)}) collective-permute-start(bf16[8,2,128,128]{3,2,1,0:T(8,128)(2,1)S(1)} %get-tuple-element.18), channel_id=1, source_target_pairs={{0,64},{1,65},{2,66},{3,67},{4,68},{5,69},{6,70},{7,71},{8,72},{9,... | collective-permute-start | bytes 1572872 | tf_op jit(solution)/shard_map/ppermute | solution.py:527
  17.7 27.8 %collective-permute-start = (bf16[65,64,256]{2,1,0:T(8,128)(2,1)S(1)}, bf16[65,64,256]{2,1,0:T(8,128)(2,1)S(1)}, u32[]{:S(2)}, u32[]{:S(2)}) collective-permute-start(bf16[65,64,256]{2,1,0:T(8,128)(2,1)S(1)} %get-tuple-element.17.own), channel_id=1, source_target_pairs={{8,0},{16,8},{24,16},{32,24},{40,32},{48,40},{56,48},{64,56},{72,6... | collective-permute-start | bytes 6389768 | tf_op jit(solution)/shard_map/ppermute | solution.py:496
  25.5 29.0 %collective-permute-start.7 = (bf16[8,2,128,128]{3,2,1,0:T(8,128)(2,1)S(1)}, bf16[8,2,128,128]{3,2,1,0:T(8,128)(2,1)S(1)}, u32[]{:S(2)}, u32[]{:S(2)}) collective-permute-start(bf16[8,2,128,128]{3,2,1,0:T(8,128)(2,1)S(1)} %collective-permute-done.3), channel_id=1, source_target_pairs={{64,1},{65,0},{66,3},{67,2},{68,5},{69,4},{70,7},{71,6},{72,9},{73... | collective-permute-start | bytes 1572872 | tf_op jit(solution)/shard_map/ppermute | solution.py:527
  25.5 8.1 %copy-start = (bf16[256,256]{1,0:T(8,128)(2,1)S(1)}, bf16[256,256]{1,0:T(8,128)(2,1)}, u32[]{:S(2)}) copy-start(bf16[256,256]{1,0:T(8,128)(2,1)} %constant.28.cols_hbm.cols_ref) | copy-start | bytes 393220
  25.5 8.1 %copy-start.6 = (bf16[256,256]{1,0:T(8,128)(2,1)S(1)}, bf16[256,256]{1,0:T(8,128)(2,1)}, u32[]{:S(2)}) copy-start(bf16[256,256]{1,0:T(8,128)(2,1)} %constant.29.back_cols_ref) | copy-start | bytes 393220
  25.5 8.1 %copy-start.7 = (bf16[128,128]{1,0:T(8,128)(2,1)S(1)}, bf16[128,128]{1,0:T(8,128)(2,1)}, u32[]{:S(2)}) copy-start(bf16[128,128]{1,0:T(8,128)(2,1)} %constant.30.back_rows_ref) | copy-start | bytes 98308
  37.2 24.3 %collective-permute-start.8 = (bf16[8,2,128,128]{3,2,1,0:T(8,128)(2,1)S(1)}, bf16[8,2,128,128]{3,2,1,0:T(8,128)(2,1)S(1)}, u32[]{:S(2)}, u32[]{:S(2)}) collective-permute-start(bf16[8,2,128,128]{3,2,1,0:T(8,128)(2,1)S(1)} %collective-permute-done.1), channel_id=1, source_target_pairs={{64,7},{65,2},{66,1},{67,4},{68,3},{69,6},{70,5},{71,0},{72,15},{7... | collective-permute-start | bytes 1572872 | tf_op jit(solution)/shard_map/ppermute | solution.py:527
  39.8 9.4 %collective-permute-start.4 = (f32[2,4,16]{2,1,0:T(4,128)S(1)}, f32[2,4,16]{2,1,0:T(4,128)S(1)}, u32[]{:S(2)}, u32[]{:S(2)}) collective-permute-start(f32[2,4,16]{2,1,0:T(4,128)S(1)} %flow.3), channel_id=1, source_target_pairs={{8,0},{16,8},{24,16},{32,24},{40,32},{48,40},{56,48},{64,56},{72,6... | collective-permute-start | bytes 1544 | tf_op jit(solution)/shard_map/ppermute | solution.py:496
  49.3 14.6 %collective-permute-start.5 = (f32[3,8,16]{2,1,0:T(8,128)S(1)}, f32[3,8,16]{2,1,0:T(8,128)S(1)}, u32[]{:S(2)}, u32[]{:S(2)}) collective-permute-start(f32[3,8,16]{2,1,0:T(8,128)S(1)} %pad_maximum_fusion), channel_id=1, source_target_pairs={{0,1},{1,0},{2,3},{3,2},{4,5},{5,4},{6,7},{7,6},{8,9},{9,8},{10,11... | collective-permute-start | bytes 4616 | tf_op jit(solution)/shard_map/ppermute | solution.py:500
  53.8 10.0 %collective-permute-start.6 = (f32[3,8,16]{2,1,0:T(8,128)S(1)}, f32[3,8,16]{2,1,0:T(8,128)S(1)}, u32[]{:S(2)}, u32[]{:S(2)}) collective-permute-start(f32[3,8,16]{2,1,0:T(8,128)S(1)} %pad_maximum_fusion), channel_id=1, source_target_pairs={{1,2},{3,4},{5,6},{2,1},{4,3},{6,5},{9,10},{11,12},{13,14},{10,9},... | collective-permute-start | bytes 4616 | tf_op jit(solution)/shard_map/ppermute | solution.py:549

commit v6 on v5

--- a/solution.py
+++ b/solution.py
@@ -15,7 +15,7 @@
 HALF = N // 2
 PAD = 72
 ROW = 32
-DEPTH = 3
+DEPTH = 2
 SPRING = 0.2
 EPS = 1e-06
 MIB = 1024 * 1024
@@ -430,6 +430,22 @@
     )(tile, target, share, in_vmem(on), in_vmem(off), in_vmem(blended))
 
 
+def warped(cell, down_shift, right_shift):
+    whole_of = lambda shift: (shift + 256.0).astype(jnp.int32) - 256
+    line = lambda value: jnp.full((1, N), value, jnp.float32).astype(jnp.bfloat16)
+    down = jnp.clip(whole_of(down_shift), 4 - PAD, PAD - 6)
+    part = down_shift - down.astype(jnp.float32)
+    upper = cell[pl.ds(PAD + down, N), :]
+    lower = cell[pl.ds(PAD + 1 + down, N), :]
+    image = upper + part * (lower - upper)
+    right = whole_of(right_shift).astype(jnp.float32)
+    apart = lax.broadcasted_iota(jnp.int32, (N, N), 0) - lax.broadcasted_iota(jnp.int32, (N, N), 1)
+    apart = apart.astype(jnp.bfloat16) - line(right)
+    one = jnp.bfloat16(1.0)
+    hat = jnp.maximum(jnp.bfloat16(0.0), one - jnp.abs(apart - line(right_shift - right)))
+    return dot(image.astype(jnp.bfloat16), hat).astype(jnp.bfloat16)
+
+
 def warp_kernel(tile_ref, *refs):
     *flows, padded, edges, out_hbm, field_ref, out, wide, field, sem, out_sems = refs
     y = pl.program_id(0)
@@ -445,19 +461,9 @@
         scalars.wait()
 
     borders = (*range(HB), *range(nx - HB, nx))
-    apart = lax.broadcasted_iota(jnp.int32, (N, N), 0) - lax.broadcasted_iota(jnp.int32, (N, N), 1)
-    apart = apart.astype(jnp.float32)
     for x in range(nx):
         cell = edges.at[y, borders.index(x)] if x in borders else padded.at[y, x]
-        shift = field[0, y, STEPS + x]
-        down = jnp.clip((shift + 256.0).astype(jnp.int32) - 256, 4 - PAD, PAD - 6)
-        part = shift - down.astype(jnp.float32)
-        upper = cell[pl.ds(PAD + down, N), :]
-        lower = cell[pl.ds(PAD + 1 + down, N), :]
-        image = upper + part * (lower - upper)
-        hat = jnp.maximum(0.0, 1.0 - jnp.abs(apart - field[1, y, STEPS + x])).astype(jnp.bfloat16)
-        warped = dot(jnp.concatenate(split(image), axis=1), jnp.concatenate([hat, hat], axis=0))
-        out[y, x] = warped.astype(jnp.bfloat16)
+        out[y, x] = warped(cell, field[0, y, STEPS + x], field[1, y, STEPS + x])
     store = lambda row: pltpu.make_async_copy(out.at[row], out_hbm.at[0, row], out_sems.at[row])
     store(y).start()
     wait_all([store(row) for row in range(ny)])
@@ -500,7 +506,7 @@
     return lax.ppermute(x, "tile", [(i, i ^ 1) for i in range(lax.axis_size("tile"))])
 
 
-def hops(tiles, sections, beyond):
+def hops(tiles, sections):
     pairs = ([], [])
     for section in range(sections):
         x_low, rest = divmod(section, sections // 2)
@@ -510,11 +516,16 @@
             ends = [section * tiles + tile]
             for hop in (1, 2):
                 x = (2 * x_high + x_low + hop * way) % 4
-                to_z = (z + 2 * x_high - 1) % (tiles // 2) if beyond and hop == 2 else z
-                ends.append((x % 2 * (sections // 2) + rest) * tiles + 2 * to_z + x // 2)
+                ends.append((x % 2 * (sections // 2) + rest) * tiles + 2 * z + x // 2)
             pairs[0].append((ends[0], ends[1]))
             pairs[1].append((ends[1], ends[2]))
     return pairs
+
+
+def beyond(x):
+    tiles = lax.axis_size("tile")
+    pairs = [(i, i + 1) for i in range(1, tiles - 1, 2)]
+    return lax.ppermute(x, "tile", pairs + [(j, i) for i, j in pairs])
 
 
 def per_device(sections, node_mask, box_row, box_shift, box_count, blend_weight):
@@ -523,7 +534,7 @@
     half = ny // 2
     tiles, count = lax.axis_size("tile"), lax.axis_size("sec")
     tile = jnp.stack([lax.axis_index("tile"), tiles]).astype(jnp.int32)
-    on_hops, off_hops = hops(tiles, count, False), hops(tiles, count, True)
+    on_hops = hops(tiles, count)
     hop = lambda x, pairs: lax.ppermute(x, ("sec", "tile"), pairs)
 
     spectra_high, source, on = forward(tile, sections, half, half, True, None, rows, cols)
@@ -531,7 +542,6 @@
     on = hop(on, on_hops[0])
     spectra_low, source, off = forward(tile, sections, 0, half, False, source, rows, cols)
     from_next = from_behind(spectra_low, "sec", -1)
-    off = hop(off, off_hops[0])
     target, share = slots_of(tile, box_row, box_shift, box_count, blend_weight)
     on, source = lax.optimization_barrier((on, source))
     on = hop(on, on_hops[1])
@@ -541,12 +551,11 @@
     flow_high = flow_of(spectra_high, from_last, -1, half, nx, cols, back_cols, back_rows)
     off, flow_high = lax.optimization_barrier((off, flow_high))
     flow_high = from_behind(flow_high, "sec", -1)
-    off = hop(off, off_hops[1])
+    off = beyond(off)
     flow_low = flow_of(spectra_low, from_next, 1, half, nx, cols, back_cols, back_rows)
     flow = jnp.concatenate([flow_low, flow_high], axis=1)
     flow = jnp.concatenate([flow, node_mask.astype(jnp.float32) + 1.0], axis=0)
-    beyond = [(i, i + 1) for i in range(1, tiles - 1, 2)]
-    flow_off = lax.ppermute(flow, "tile", beyond + [(j, i) for i, j in beyond])
+    flow_off = beyond(flow)
     flow_on = swapped(flow)
     flows = (flow_low, flow_high, node_mask, flow_on, flow_off)
     edges = edges_of(tile, target, share, on, off, blended)

time: 71.9 us -> 70.5 us (0.981)
  the two profiles are of different devices: /device:TPU:1 before, /device:TPU:66 now
where the time goes in v6:
time: 70.5 us; the launch traced here: 69.4 us
  Pallas kernels  30.8 us (44%)
  starting transfers between devices  20 us (28%)
  waiting for transfers between devices  17.6 us (25%)
  between operations  0.81 us (1%)
    ppermute x3, waiting for transfers between devices, from_behind(): return lax.ppermute(x, axis, pairs)  12.7 us
    pallas_call x2, Pallas kernels, forward(): pl.pallas_call(functools.partial(forward_kernel, start, toward_pair), gri...  9.27 us
    ppermute x3, starting transfers between devices, from_behind(): return lax.ppermute(x, axis, pairs)  8.58 us
    pallas_call x2, Pallas kernels, flow_of(): pl.pallas_call(functools.partial(flow_kernel, sign), grid=(ny,), in_specs...  7.4 us
    ppermute x2, starting transfers between devices, beyond(): return lax.ppermute(x, 'tile', pairs + [(j, i) for i, j in pairs])  6.81 us
    pallas_call x1, Pallas kernels, warp(): pl.pallas_call(warp_kernel, grid=(ny,), in_specs=[pl.BlockSpec(memory_spa...  6.2 us
    pallas_call x1, Pallas kernels, blend(): pl.pallas_call(blend_kernel, grid=(ny,), in_specs=[pl.BlockSpec(memory_sp...  4.98 us
    ppermute x2, starting transfers between devices, per_device(): hop = lambda x, pairs: lax.ppermute(x, ('sec', 'tile'), pairs)  2.91 us
  transfers between devices with their start and end apart: 8, of which 5 were waited for; matrix products, arithmetic and copies ran while one was open for 0% of the time, Pallas kernels for 29%

profile of v6, /device:TPU:66, one launch (start us, length us, event | category | flops | bytes accessed | tf_op | source)
XLA Modules:
  0.0 69.4 jit_solution(15849554252880869589)
XLA Ops:
  0.6 0.1 pad_add_fusion.tile_ref
  0.7 4.6 %forward.2 = (bf16[65,64,256]{2,1,0:T(8,128)(2,1)S(1)}, bf16[8,16,128,128]{3,2,1,0:T(8,128)(2,1)S(1)}, bf16[8,2,128,128]{3,2,1,0:T(8,128)(2,1)S(1)}) custom-call(s32[2]{0:T(128)S(1)} %pad_add_fusion.tile_ref, f32[1,8,16,128,128]{4,3,2,1,0:T(8,128)} %x_hbm.3, bf16[128,256]{1,0:T(8,128)(2,1)} %constant.27.rows_hbm, bf16[256,256]{1,0:T(8,128)(2,1)} %constant.28.cols_hbm.cols_ref), custom_call_target="tpu_custom_call" | custom-call | flops 2000000000 | bytes 6291456 | tf_op jit(solution)/shard_map/forward/pallas_call | solution.py:150
  5.3 1.9 %collective-permute-start.1 = (bf16[65,64,256]{2,1,0:T(8,128)(2,1)S(1)}, bf16[65,64,256]{2,1,0:T(8,128)(2,1)S(1)}, u32[]{:S(2)}, u32[]{:S(2)}) collective-permute-start(bf16[65,64,256]{2,1,0:T(8,128)(2,1)S(1)} %get-tuple-element.19.own), channel_id=1, source_target_pairs={{0,8},{8,16},{16,24},{24,32},{32,40},{40,48},{48,56},{56,64},{64,7... | collective-permute-start | bytes 6389768 | tf_op jit(solution)/shard_map/ppermute | solution.py:502
  7.3 1.5 %collective-permute-start.2 = (bf16[8,2,128,128]{3,2,1,0:T(8,128)(2,1)S(1)}, bf16[8,2,128,128]{3,2,1,0:T(8,128)(2,1)S(1)}, u32[]{:S(2)}, u32[]{:S(2)}) collective-permute-start(bf16[8,2,128,128]{3,2,1,0:T(8,128)(2,1)S(1)} %get-tuple-element.22), channel_id=1, source_target_pairs={{0,64},{1,65},{2,66},{3,67},{4,68},{5,69},{6,70},{7,71},{8,72},{9,... | collective-permute-start | bytes 1572872 | tf_op jit(solution)/shard_map/ppermute | solution.py:538
  8.8 0.0 copy-start.4
  8.8 4.6 %forward.3 = (bf16[65,64,256]{2,1,0:T(8,128)(2,1)S(1)}, bf16[8,16,128,128]{3,2,1,0:T(8,128)(2,1)S(1)}, bf16[8,2,128,128]{3,2,1,0:T(8,128)(2,1)S(1)}) custom-call(s32[2]{0:T(128)S(1)} %pad_add_fusion.tile_ref, f32[1,8,16,128,128]{4,3,2,1,0:T(8,128)} %x_hbm.3, bf16[128,256]{1,0:T(8,128)(2,1)} %constant.27.rows_hbm, ...), custom_call_target="tpu_custom_call", output_to_operand_aliasing={{1}: (4, {})} | custom-call | flops 2000000000 | bytes 6291456 | tf_op jit(solution)/shard_map/forward/pallas_call | solution.py:150
  13.5 4.7 %collective-permute-start = (bf16[65,64,256]{2,1,0:T(8,128)(2,1)S(1)}, bf16[65,64,256]{2,1,0:T(8,128)(2,1)S(1)}, u32[]{:S(2)}, u32[]{:S(2)}) collective-permute-start(bf16[65,64,256]{2,1,0:T(8,128)(2,1)S(1)} %get-tuple-element.17.own), channel_id=1, source_target_pairs={{8,0},{16,8},{24,16},{32,24},{40,32},{48,40},{56,48},{64,56},{72,6... | collective-permute-start | bytes 6389768 | tf_op jit(solution)/shard_map/ppermute | solution.py:502
  18.2 0.0 copy-done.1
  18.2 0.0 copy-done.2
  18.2 0.0 copy-done.3
  18.2 0.0 copy-done.5
  18.2 0.6 slots.1
  18.9 0.0 copy-done.4
  18.9 2.5 %collective-permute-done.2 = bf16[8,2,128,128]{3,2,1,0:T(8,128)(2,1)S(1)} collective-permute-done((bf16[8,2,128,128]{3,2,1,0:T(8,128)(2,1)S(1)}, bf16[8,2,128,128]{3,2,1,0:T(8,128)(2,1)S(1)}, u32[]{:S(2)}, u32[]{:S(2)}) %collective-permute-start.2) | collective-permute-done | bytes 524320 | tf_op jit(solution)/shard_map/ppermute | solution.py:538
  21.5 1.4 %collective-permute-start.6 = (bf16[8,2,128,128]{3,2,1,0:T(8,128)(2,1)S(1)}, bf16[8,2,128,128]{3,2,1,0:T(8,128)(2,1)S(1)}, u32[]{:S(2)}, u32[]{:S(2)}) collective-permute-start(bf16[8,2,128,128]{3,2,1,0:T(8,128)(2,1)S(1)} %collective-permute-done.2), channel_id=1, source_target_pairs={{64,1},{65,0},{66,3},{67,2},{68,5},{69,4},{70,7},{71,6},{72,9},{73... | collective-permute-start | bytes 1572872 | tf_op jit(solution)/shard_map/ppermute | solution.py:538
  22.9 5.0 %blend.1.padded.refs_5_ = f32[8,16,272,128]{3,2,1,0:T(8,128)S(1)} custom-call(s32[8,128]{1,0:T(8,128)S(1)} %get-tuple-element.20.target_ref, f32[8,128]{1,0:T(8,128)S(1)} %get-tuple-element.21.share_ref, bf16[8,16,128,128]{3,2,1,0:T(8,128)(2,1)S(1)} %get-tuple-element.24.source), custom_call_target="tpu_custom_call" | custom-call | flops 20000000 | bytes 4194304 | tf_op jit(solution)/shard_map/blend/pallas_call | solution.py:339
  27.9 7.3 %collective-permute-done.1.other = bf16[65,64,256]{2,1,0:T(8,128)(2,1)S(1)} collective-permute-done((bf16[65,64,256]{2,1,0:T(8,128)(2,1)S(1)}, bf16[65,64,256]{2,1,0:T(8,128)(2,1)S(1)}, u32[]{:S(2)}, u32[]{:S(2)}) %collective-permute-start.1) | collective-permute-done | bytes 2129952 | tf_op jit(solution)/shard_map/ppermute | solution.py:502
  35.2 0.0 copy-done
  35.2 3.7 %flow.3 = f32[2,4,16]{2,1,0:T(4,128)S(1)} custom-call(bf16[65,64,256]{2,1,0:T(8,128)(2,1)S(1)} %get-tuple-element.19.own, bf16[65,64,256]{2,1,0:T(8,128)(2,1)S(1)} %collective-permute-done.1.other, bf16[256,256]{1,0:T(8,128)(2,1)S(1)} %copy-done, bf16[256,256]{1,0:T(8,128)(2,1)S(1)} %copy-done.6, bf16[128,128]{1,0:T(8,128)(2,1)S(1)} %copy-done.7), custom_call_target="tpu_custom_call" | custom-call | flops 49999998976 | bytes 4194304 | tf_op jit(solution)/shard_map/flow/pallas_call | solution.py:254
  38.9 3.6 %collective-permute-start.7 = (bf16[8,2,128,128]{3,2,1,0:T(8,128)(2,1)S(1)}, bf16[8,2,128,128]{3,2,1,0:T(8,128)(2,1)S(1)}, u32[]{:S(2)}, u32[]{:S(2)}) collective-permute-start(bf16[8,2,128,128]{3,2,1,0:T(8,128)(2,1)S(1)} %get-tuple-element.29), channel_id=1, source_target_pairs={{1,2},{3,4},{5,6},{2,1},{4,3},{6,5},{9,10},{11,12},{13,14},{10,9},... | collective-permute-start | bytes 1572872 | tf_op jit(solution)/shard_map/ppermute | solution.py:528
  42.5 1.9 %collective-permute-start.3 = (f32[2,4,16]{2,1,0:T(4,128)S(1)}, f32[2,4,16]{2,1,0:T(4,128)S(1)}, u32[]{:S(2)}, u32[]{:S(2)}) collective-permute-start(f32[2,4,16]{2,1,0:T(4,128)S(1)} %flow.3), channel_id=1, source_target_pairs={{8,0},{16,8},{24,16},{32,24},{40,32},{48,40},{56,48},{64,56},{72,6... | collective-permute-start | bytes 1544 | tf_op jit(solution)/shard_map/ppermute | solution.py:502
  44.4 0.1 collective-permute-done.other
  44.5 3.7 %flow.2.refs_0_ = f32[2,4,16]{2,1,0:T(4,128)S(1)} custom-call(bf16[65,64,256]{2,1,0:T(8,128)(2,1)S(1)} %get-tuple-element.17.own, bf16[65,64,256]{2,1,0:T(8,128)(2,1)S(1)} %collective-permute-done.other, bf16[256,256]{1,0:T(8,128)(2,1)S(1)} %copy-done, bf16[256,256]{1,0:T(8,128)(2,1)S(1)} %copy-done.6, bf16[128,128]{1,0:T(8,128)(2,1)S(1)} %copy-done.7), custom_call_target="tpu_custom_call" | custom-call | flops 49999998976 | bytes 4194304 | tf_op jit(solution)/shard_map/flow/pallas_call | solution.py:254
  48.2 5.3 %collective-permute-done.3.refs_1_ = f32[2,4,16]{2,1,0:T(4,128)S(1)} collective-permute-done((f32[2,4,16]{2,1,0:T(4,128)S(1)}, f32[2,4,16]{2,1,0:T(4,128)S(1)}, u32[]{:S(2)}, u32[]{:S(2)}) %collective-permute-start.3) | collective-permute-done | bytes 544 | tf_op jit(solution)/shard_map/ppermute | solution.py:502
  53.5 1.7 %collective-permute-start.4 = (f32[3,8,16]{2,1,0:T(8,128)S(1)}, f32[3,8,16]{2,1,0:T(8,128)S(1)}, u32[]{:S(2)}, u32[]{:S(2)}) collective-permute-start(f32[3,8,16]{2,1,0:T(8,128)S(1)} %pad_maximum_fusion), channel_id=1, source_target_pairs={{0,1},{1,0},{2,3},{3,2},{4,5},{5,4},{6,7},{7,6},{8,9},{9,8},{10,11... | collective-permute-start | bytes 4616 | tf_op jit(solution)/shard_map/ppermute | solution.py:506
  55.3 3.2 %collective-permute-start.5 = (f32[3,8,16]{2,1,0:T(8,128)S(1)}, f32[3,8,16]{2,1,0:T(8,128)S(1)}, u32[]{:S(2)}, u32[]{:S(2)}) collective-permute-start(f32[3,8,16]{2,1,0:T(8,128)S(1)} %pad_maximum_fusion), channel_id=1, source_target_pairs={{1,2},{3,4},{5,6},{2,1},{4,3},{6,5},{9,10},{11,12},{13,14},{10,9},... | collective-permute-start | bytes 4616 | tf_op jit(solution)/shard_map/ppermute | solution.py:528
  58.5 0.0 collective-permute-done.6.on_ref
  58.5 0.0 collective-permute-done.7.off_ref
  58.5 2.3 %edges.1.refs_6_ = f32[8,4,272,128]{3,2,1,0:T(8,128)S(1)} custom-call(s32[2]{0:T(128)S(1)} %pad_add_fusion.tile_ref, s32[8,128]{1,0:T(8,128)S(1)} %get-tuple-element.20.target_ref, f32[8,128]{1,0:T(8,128)S(1)} %get-tuple-element.21.share_ref, bf16[8,2,128,128]{3,2,1,0:T(8,128)(2,1)S(1)} %collective-permute-done.6.on_ref, ...), custom_call_target="tpu_custom_call" | custom-call | flops 5000000 | bytes 4194304 | tf_op jit(solution)/shard_map/edges/pallas_call | solution.py:420
  60.8 0.0 collective-permute-done.4.refs_3_
  60.8 2.4 %collective-permute-done.5.refs_4_ = f32[3,8,16]{2,1,0:T(8,128)S(1)} collective-permute-done((f32[3,8,16]{2,1,0:T(8,128)S(1)}, f32[3,8,16]{2,1,0:T(8,128)S(1)}, u32[]{:S(2)}, u32[]{:S(2)}) %collective-permute-start.5) | collective-permute-done | bytes 1568 | tf_op jit(solution)/shard_map/ppermute | solution.py:528
  63.2 6.2 %warp.1 = (bf16[1,8,16,128,128]{4,3,2,1,0:T(8,128)(2,1)}, f32[1,2,8,16]{3,2,1,0:T(8,128)}) custom-call(s32[2]{0:T(128)S(1)} %pad_add_fusion.tile_ref, f32[2,4,16]{2,1,0:T(4,128)S(1)} %flow.2.refs_0_, f32[2,4,16]{2,1,0:T(4,128)S(1)} %collective-permute-done.3.refs_1_, s32[1,8,16]{2,1,0:T(8,128)S(1)} %copy-done.4, ...), custom_call_target="tpu_custom_call" | custom-call | flops 20000000 | bytes 12582912 | tf_op jit(solution)/shard_map/warp/pallas_call | solution.py:475
  (11 shorter events, 0.0 us)
Async XLA Ops:
  5.3 29.8 %collective-permute-start.1 = (bf16[65,64,256]{2,1,0:T(8,128)(2,1)S(1)}, bf16[65,64,256]{2,1,0:T(8,128)(2,1)S(1)}, u32[]{:S(2)}, u32[]{:S(2)}) collective-permute-start(bf16[65,64,256]{2,1,0:T(8,128)(2,1)S(1)} %get-tuple-element.19.own), channel_id=1, source_target_pairs={{0,8},{8,16},{16,24},{24,32},{32,40},{40,48},{48,56},{56,64},{64,7... | collective-permute-start | bytes 6389768 | tf_op jit(solution)/shard_map/ppermute | solution.py:502
  7.3 14.2 %collective-permute-start.2 = (bf16[8,2,128,128]{3,2,1,0:T(8,128)(2,1)S(1)}, bf16[8,2,128,128]{3,2,1,0:T(8,128)(2,1)S(1)}, u32[]{:S(2)}, u32[]{:S(2)}) collective-permute-start(bf16[8,2,128,128]{3,2,1,0:T(8,128)(2,1)S(1)} %get-tuple-element.22), channel_id=1, source_target_pairs={{0,64},{1,65},{2,66},{3,67},{4,68},{5,69},{6,70},{7,71},{8,72},{9,... | collective-permute-start | bytes 1572872 | tf_op jit(solution)/shard_map/ppermute | solution.py:538
  8.8 9.4 %copy-start.1 = (s32[1,8,16,4]{2,3,1,0:T(4,128)S(1)}, s32[1,8,16,4]{2,3,1,0:T(4,128)}, u32[]{:S(2)}) copy-start(s32[1,8,16,4]{2,3,1,0:T(4,128)} %param.12) | copy-start | bytes 6148
  8.8 9.4 %copy-start.2 = (s32[1,8,16,4]{2,3,1,0:T(4,128)S(1)}, s32[1,8,16,4]{2,3,1,0:T(4,128)}, u32[]{:S(2)}) copy-start(s32[1,8,16,4]{2,3,1,0:T(4,128)} %param.13) | copy-start | bytes 6148
  8.8 9.4 %copy-start.3 = (f32[1,8,16,4]{2,3,1,0:T(4,128)S(1)}, f32[1,8,16,4]{2,3,1,0:T(4,128)}, u32[]{:S(2)}) copy-start(f32[1,8,16,4]{2,3,1,0:T(4,128)} %param.15) | copy-start | bytes 6148
  8.8 9.4 %copy-start.5 = (s32[1,8,16]{2,1,0:T(8,128)S(1)}, s32[1,8,16]{2,1,0:T(8,128)}, u32[]{:S(2)}) copy-start(s32[1,8,16]{2,1,0:T(8,128)} %count_ref.1) | copy-start | bytes 1540
  8.8 10.1 %copy-start.4 = (s32[1,8,16]{2,1,0:T(8,128)S(1)}, s32[1,8,16]{2,1,0:T(8,128)}, u32[]{:S(2)}) copy-start(s32[1,8,16]{2,1,0:T(8,128)} %refs_2_.1) | copy-start | bytes 1540
  13.5 31.0 %collective-permute-start = (bf16[65,64,256]{2,1,0:T(8,128)(2,1)S(1)}, bf16[65,64,256]{2,1,0:T(8,128)(2,1)S(1)}, u32[]{:S(2)}, u32[]{:S(2)}) collective-permute-start(bf16[65,64,256]{2,1,0:T(8,128)(2,1)S(1)} %get-tuple-element.17.own), channel_id=1, source_target_pairs={{8,0},{16,8},{24,16},{32,24},{40,32},{48,40},{56,48},{64,56},{72,6... | collective-permute-start | bytes 6389768 | tf_op jit(solution)/shard_map/ppermute | solution.py:502
  21.5 37.0 %collective-permute-start.6 = (bf16[8,2,128,128]{3,2,1,0:T(8,128)(2,1)S(1)}, bf16[8,2,128,128]{3,2,1,0:T(8,128)(2,1)S(1)}, u32[]{:S(2)}, u32[]{:S(2)}) collective-permute-start(bf16[8,2,128,128]{3,2,1,0:T(8,128)(2,1)S(1)} %collective-permute-done.2), channel_id=1, source_target_pairs={{64,1},{65,0},{66,3},{67,2},{68,5},{69,4},{70,7},{71,6},{72,9},{73... | collective-permute-start | bytes 1572872 | tf_op jit(solution)/shard_map/ppermute | solution.py:538
  22.9 12.3 %copy-start = (bf16[256,256]{1,0:T(8,128)(2,1)S(1)}, bf16[256,256]{1,0:T(8,128)(2,1)}, u32[]{:S(2)}) copy-start(bf16[256,256]{1,0:T(8,128)(2,1)} %constant.28.cols_hbm.cols_ref) | copy-start | bytes 393220
  22.9 12.3 %copy-start.6 = (bf16[256,256]{1,0:T(8,128)(2,1)S(1)}, bf16[256,256]{1,0:T(8,128)(2,1)}, u32[]{:S(2)}) copy-start(bf16[256,256]{1,0:T(8,128)(2,1)} %constant.29.back_cols_ref) | copy-start | bytes 393220
  22.9 12.3 %copy-start.7 = (bf16[128,128]{1,0:T(8,128)(2,1)S(1)}, bf16[128,128]{1,0:T(8,128)(2,1)}, u32[]{:S(2)}) copy-start(bf16[128,128]{1,0:T(8,128)(2,1)} %constant.30.back_rows_ref) | copy-start | bytes 98308
  38.9 19.6 %collective-permute-start.7 = (bf16[8,2,128,128]{3,2,1,0:T(8,128)(2,1)S(1)}, bf16[8,2,128,128]{3,2,1,0:T(8,128)(2,1)S(1)}, u32[]{:S(2)}, u32[]{:S(2)}) collective-permute-start(bf16[8,2,128,128]{3,2,1,0:T(8,128)(2,1)S(1)} %get-tuple-element.29), channel_id=1, source_target_pairs={{1,2},{3,4},{5,6},{2,1},{4,3},{6,5},{9,10},{11,12},{13,14},{10,9},... | collective-permute-start | bytes 1572872 | tf_op jit(solution)/shard_map/ppermute | solution.py:528
  42.5 11.0 %collective-permute-start.3 = (f32[2,4,16]{2,1,0:T(4,128)S(1)}, f32[2,4,16]{2,1,0:T(4,128)S(1)}, u32[]{:S(2)}, u32[]{:S(2)}) collective-permute-start(f32[2,4,16]{2,1,0:T(4,128)S(1)} %flow.3), channel_id=1, source_target_pairs={{8,0},{16,8},{24,16},{32,24},{40,32},{48,40},{56,48},{64,56},{72,6... | collective-permute-start | bytes 1544 | tf_op jit(solution)/shard_map/ppermute | solution.py:502
  53.5 7.3 %collective-permute-start.4 = (f32[3,8,16]{2,1,0:T(8,128)S(1)}, f32[3,8,16]{2,1,0:T(8,128)S(1)}, u32[]{:S(2)}, u32[]{:S(2)}) collective-permute-start(f32[3,8,16]{2,1,0:T(8,128)S(1)} %pad_maximum_fusion), channel_id=1, source_target_pairs={{0,1},{1,0},{2,3},{3,2},{4,5},{5,4},{6,7},{7,6},{8,9},{9,8},{10,11... | collective-permute-start | bytes 4616 | tf_op jit(solution)/shard_map/ppermute | solution.py:506
  55.3 8.0 %collective-permute-start.5 = (f32[3,8,16]{2,1,0:T(8,128)S(1)}, f32[3,8,16]{2,1,0:T(8,128)S(1)}, u32[]{:S(2)}, u32[]{:S(2)}) collective-permute-start(f32[3,8,16]{2,1,0:T(8,128)S(1)} %pad_maximum_fusion), channel_id=1, source_target_pairs={{1,2},{3,4},{5,6},{2,1},{4,3},{6,5},{9,10},{11,12},{13,14},{10,9},... | collective-permute-start | bytes 4616 | tf_op jit(solution)/shard_map/ppermute | solution.py:528

commit v7 on v6

--- a/solution.py
+++ b/solution.py
@@ -269,7 +269,7 @@
             pltpu.VMEM((ny, nx, N), jnp.float32),
         ],
         compiler_params=pltpu.CompilerParams(vmem_limit_bytes=8 * MIB),
-        cost_estimate=pl.CostEstimate(flops=50_000_000_000, bytes_accessed=4 * MIB, transcendentals=0),
+        cost_estimate=pl.CostEstimate(flops=0 if sign < 0 else 50_000_000_000, bytes_accessed=0, transcendentals=0),
         name="flow",
     )(in_vmem(own), in_vmem(other), *(t.astype(jnp.bfloat16) for t in (cols, back_cols, back_rows)))
 
@@ -343,7 +343,7 @@
         out_specs=pl.BlockSpec(memory_space=pltpu.VMEM),
         out_shape=pltpu.VMEM((ny, nx, N + 2 * PAD, N), jnp.float32),
         compiler_params=pltpu.CompilerParams(vmem_limit_bytes=4 * MIB),
-        cost_estimate=pl.CostEstimate(flops=20_000_000, bytes_accessed=4 * MIB, transcendentals=0),
+        cost_estimate=pl.CostEstimate(flops=20_000_000_000, bytes_accessed=4 * MIB, transcendentals=0),
         name="blend",
     )(target, share, in_vmem(source))
 
@@ -516,7 +516,8 @@
             ends = [section * tiles + tile]
             for hop in (1, 2):
                 x = (2 * x_high + x_low + hop * way) % 4
-                ends.append((x % 2 * (sections // 2) + rest) * tiles + 2 * z + x // 2)
+                to_z = (z + 2 * x_high - 1) % (tiles // 2) if hop == 2 else z
+                ends.append((x % 2 * (sections // 2) + rest) * tiles + 2 * to_z + x // 2)
             pairs[0].append((ends[0], ends[1]))
             pairs[1].append((ends[1], ends[2]))
     return pairs
@@ -534,25 +535,26 @@
     half = ny // 2
     tiles, count = lax.axis_size("tile"), lax.axis_size("sec")
     tile = jnp.stack([lax.axis_index("tile"), tiles]).astype(jnp.int32)
-    on_hops = hops(tiles, count)
+    off_hops = hops(tiles, count)
     hop = lambda x, pairs: lax.ppermute(x, ("sec", "tile"), pairs)
 
-    spectra_high, source, on = forward(tile, sections, half, half, True, None, rows, cols)
+    spectra_high, source, off = forward(tile, sections, half, half, False, None, rows, cols)
     from_last = from_behind(spectra_high, "sec", 1)
-    on = hop(on, on_hops[0])
-    spectra_low, source, off = forward(tile, sections, 0, half, False, source, rows, cols)
+    off = hop(off, off_hops[0])
+    spectra_low, source, on = forward(tile, sections, 0, half, True, source, rows, cols)
     from_next = from_behind(spectra_low, "sec", -1)
     target, share = slots_of(tile, box_row, box_shift, box_count, blend_weight)
-    on, source = lax.optimization_barrier((on, source))
-    on = hop(on, on_hops[1])
+    off, source = lax.optimization_barrier((off, source))
+    off = hop(off, off_hops[1])
     blended = blend(target, share, source)
     from_last, blended = lax.optimization_barrier((from_last, blended))
 
     flow_high = flow_of(spectra_high, from_last, -1, half, nx, cols, back_cols, back_rows)
-    off, flow_high = lax.optimization_barrier((off, flow_high))
+    on, off, flow_high = lax.optimization_barrier((on, off, flow_high))
     flow_high = from_behind(flow_high, "sec", -1)
-    off = beyond(off)
+    from_next, flow_high = lax.optimization_barrier((from_next, flow_high))
     flow_low = flow_of(spectra_low, from_next, 1, half, nx, cols, back_cols, back_rows)
+    on = swapped(on)
     flow = jnp.concatenate([flow_low, flow_high], axis=1)
     flow = jnp.concatenate([flow, node_mask.astype(jnp.float32) + 1.0], axis=0)
     flow_off = beyond(flow)

time: 70.5 us -> 67.4 us (0.956); the launches traced: 69.4 us -> 67.1 us
  starting transfers between devices: 20 us -> 17.5 us
    ppermute x1 -> x2, waiting for transfers between devices: 0.01 us -> 6.12 us  [swapped(): lax.ppermute(x, 'tile', [(i, i ^ 1) for i in range(lax.axis_size('tile'))])]
    ppermute x2 -> x1, starting transfers between devices: 6.81 us -> 2.64 us  [beyond(): return lax.ppermute(x, 'tile', pairs + [(j, i) for i, j in pairs])]
    ppermute x2, waiting for transfers between devices: 2.54 us -> 0.01 us  [per_device(): hop = lambda x, pairs: lax.ppermute(x, ('sec', 'tile'), pairs)]
    ppermute x2 -> x1, waiting for transfers between devices: 2.39 us -> 0.01 us  [beyond(): return lax.ppermute(x, 'tile', pairs + [(j, i) for i, j in pairs])]
    ppermute x1 -> x2, starting transfers between devices: 1.74 us -> 3.6 us  [swapped(): lax.ppermute(x, 'tile', [(i, i ^ 1) for i in range(lax.axis_size('tile'))])]
    ppermute x2, starting transfers between devices: 2.91 us -> 1.68 us  [per_device(): hop = lambda x, pairs: lax.ppermute(x, ('sec', 'tile'), pairs)]
    ppermute x3, waiting for transfers between devices: 12.7 us -> 11.7 us  [from_behind(): return lax.ppermute(x, axis, pairs)]
    ppermute x3, starting transfers between devices: 8.58 us -> 9.59 us  [from_behind(): return lax.ppermute(x, axis, pairs)]
  transfers between devices with their start and end apart: 8 -> 8, of which waited for: 5 -> 3; matrix products, arithmetic and copies ran while one was open for 0% -> 0% of each run, Pallas kernels for 29% -> 30%
where the time goes in v7:
time: 67.4 us; the launch traced here: 67.1 us
  Pallas kernels  30.8 us (46%)
  waiting for transfers between devices  17.8 us (26%)
  starting transfers between devices  17.5 us (26%)
  between operations  0.83 us (1%)
    ppermute x3, waiting for transfers between devices, from_behind(): return lax.ppermute(x, axis, pairs)  11.7 us
    ppermute x3, starting transfers between devices, from_behind(): return lax.ppermute(x, axis, pairs)  9.59 us
    pallas_call x2, Pallas kernels, forward(): pl.pallas_call(functools.partial(forward_kernel, start, toward_pair), gri...  9.27 us
    pallas_call x2, Pallas kernels, flow_of(): pl.pallas_call(functools.partial(flow_kernel, sign), grid=(ny,), in_specs...  7.39 us
    pallas_call x1, Pallas kernels, warp(): pl.pallas_call(warp_kernel, grid=(ny,), in_specs=[pl.BlockSpec(memory_spa...  6.22 us
    ppermute x2, waiting for transfers between devices, swapped(): lax.ppermute(x, 'tile', [(i, i ^ 1) for i in range(lax.axis_size('tile'))])  6.12 us
    pallas_call x1, Pallas kernels, blend(): pl.pallas_call(blend_kernel, grid=(ny,), in_specs=[pl.BlockSpec(memory_sp...  4.99 us
    ppermute x2, starting transfers between devices, swapped(): lax.ppermute(x, 'tile', [(i, i ^ 1) for i in range(lax.axis_size('tile'))])  3.6 us
  transfers between devices with their start and end apart: 8, of which 3 were waited for; matrix products, arithmetic and copies ran while one was open for 0% of the time, Pallas kernels for 30%

profile of v7, /device:TPU:66, one launch (start us, length us, event | category | flops | bytes accessed | tf_op | source)
XLA Modules:
  0.0 67.1 jit_solution(5565449775553224988)
XLA Ops:
  0.6 0.1 pad_add_fusion.tile_ref
  0.7 4.6 %forward.2 = (bf16[65,64,256]{2,1,0:T(8,128)(2,1)S(1)}, bf16[8,16,128,128]{3,2,1,0:T(8,128)(2,1)S(1)}, bf16[8,2,128,128]{3,2,1,0:T(8,128)(2,1)S(1)}) custom-call(s32[2]{0:T(128)S(1)} %pad_add_fusion.tile_ref, f32[1,8,16,128,128]{4,3,2,1,0:T(8,128)} %x_hbm.3, bf16[128,256]{1,0:T(8,128)(2,1)} %constant.27.rows_hbm, bf16[256,256]{1,0:T(8,128)(2,1)} %constant.28.cols_hbm.cols_ref), custom_call_target="tpu_custom_call" | custom-call | flops 2000000000 | bytes 6291456 | tf_op jit(solution)/shard_map/forward/pallas_call | solution.py:150
  5.3 1.6 %collective-permute-start.1 = (bf16[8,2,128,128]{3,2,1,0:T(8,128)(2,1)S(1)}, bf16[8,2,128,128]{3,2,1,0:T(8,128)(2,1)S(1)}, u32[]{:S(2)}, u32[]{:S(2)}) collective-permute-start(bf16[8,2,128,128]{3,2,1,0:T(8,128)(2,1)S(1)} %get-tuple-element.22), channel_id=1, source_target_pairs={{0,64},{1,65},{2,66},{3,67},{4,68},{5,69},{6,70},{7,71},{8,72},{9,... | collective-permute-start | bytes 1572872 | tf_op jit(solution)/shard_map/ppermute | solution.py:539
  6.9 1.9 %collective-permute-start.3 = (bf16[65,64,256]{2,1,0:T(8,128)(2,1)S(1)}, bf16[65,64,256]{2,1,0:T(8,128)(2,1)S(1)}, u32[]{:S(2)}, u32[]{:S(2)}) collective-permute-start(bf16[65,64,256]{2,1,0:T(8,128)(2,1)S(1)} %get-tuple-element.25.own), channel_id=1, source_target_pairs={{0,8},{8,16},{16,24},{24,32},{32,40},{40,48},{48,56},{56,64},{64,7... | collective-permute-start | bytes 6389768 | tf_op jit(solution)/shard_map/ppermute | solution.py:502
  8.8 0.0 copy-start.3
  8.8 0.0 copy-start.4
  8.8 0.0 copy-start.5
  8.9 0.0 copy-start.7
  8.9 4.6 %forward.3 = (bf16[65,64,256]{2,1,0:T(8,128)(2,1)S(1)}, bf16[8,16,128,128]{3,2,1,0:T(8,128)(2,1)S(1)}, bf16[8,2,128,128]{3,2,1,0:T(8,128)(2,1)S(1)}) custom-call(s32[2]{0:T(128)S(1)} %pad_add_fusion.tile_ref, f32[1,8,16,128,128]{4,3,2,1,0:T(8,128)} %x_hbm.3, bf16[128,256]{1,0:T(8,128)(2,1)} %constant.27.rows_hbm, ...), custom_call_target="tpu_custom_call", output_to_operand_aliasing={{1}: (4, {})} | custom-call | flops 2000000000 | bytes 6291456 | tf_op jit(solution)/shard_map/forward/pallas_call | solution.py:150
  13.5 5.8 %collective-permute-start = (bf16[65,64,256]{2,1,0:T(8,128)(2,1)S(1)}, bf16[65,64,256]{2,1,0:T(8,128)(2,1)S(1)}, u32[]{:S(2)}, u32[]{:S(2)}) collective-permute-start(bf16[65,64,256]{2,1,0:T(8,128)(2,1)S(1)} %get-tuple-element.20.own), channel_id=1, source_target_pairs={{8,0},{16,8},{24,16},{32,24},{40,32},{48,40},{56,48},{64,56},{72,6... | collective-permute-start | bytes 6389768 | tf_op jit(solution)/shard_map/ppermute | solution.py:502
  19.3 0.0 copy-done.3
  19.3 0.6 slots.1
  20.0 0.0 collective-permute-done.1
  20.0 0.1 collective-permute-start.2
  20.1 5.0 %blend.1.padded.refs_5_ = f32[8,16,272,128]{3,2,1,0:T(8,128)S(1)} custom-call(s32[8,128]{1,0:T(8,128)S(1)} %get-tuple-element.26.target_ref, f32[8,128]{1,0:T(8,128)S(1)} %get-tuple-element.27.share_ref, bf16[8,16,128,128]{3,2,1,0:T(8,128)(2,1)S(1)} %get-tuple-element.28.source), custom_call_target="tpu_custom_call" | custom-call | flops 20000000000 | bytes 4194304 | tf_op jit(solution)/shard_map/blend/pallas_call | solution.py:339
  25.1 0.0 copy-start.6
  25.1 11.6 %collective-permute-done.3.other = bf16[65,64,256]{2,1,0:T(8,128)(2,1)S(1)} collective-permute-done((bf16[65,64,256]{2,1,0:T(8,128)(2,1)S(1)}, bf16[65,64,256]{2,1,0:T(8,128)(2,1)S(1)}, u32[]{:S(2)}, u32[]{:S(2)}) %collective-permute-start.3) | collective-permute-done | bytes 2129952 | tf_op jit(solution)/shard_map/ppermute | solution.py:502
  36.7 3.7 %flow.2 = f32[2,4,16]{2,1,0:T(4,128)S(1)} custom-call(bf16[65,64,256]{2,1,0:T(8,128)(2,1)S(1)} %get-tuple-element.25.own, bf16[65,64,256]{2,1,0:T(8,128)(2,1)S(1)} %collective-permute-done.3.other, bf16[256,256]{1,0:T(8,128)(2,1)S(1)} %copy-done, bf16[256,256]{1,0:T(8,128)(2,1)S(1)} %copy-done.1, bf16[128,128]{1,0:T(8,128)(2,1)S(1)} %copy-done.2), custom_call_target="tpu_custom_call" | custom-call | tf_op jit(solution)/shard_map/flow/pallas_call | solution.py:254
  40.4 0.0 collective-permute-done.2.off_ref
  40.4 1.9 %collective-permute-start.4 = (f32[2,4,16]{2,1,0:T(4,128)S(1)}, f32[2,4,16]{2,1,0:T(4,128)S(1)}, u32[]{:S(2)}, u32[]{:S(2)}) collective-permute-start(f32[2,4,16]{2,1,0:T(4,128)S(1)} %flow.2), channel_id=1, source_target_pairs={{8,0},{16,8},{24,16},{32,24},{40,32},{48,40},{56,48},{64,56},{72,6... | collective-permute-start | bytes 1544 | tf_op jit(solution)/shard_map/ppermute | solution.py:502
  42.4 0.0 copy-done.6
  42.4 1.2 %collective-permute-start.7 = (bf16[8,2,128,128]{3,2,1,0:T(8,128)(2,1)S(1)}, bf16[8,2,128,128]{3,2,1,0:T(8,128)(2,1)S(1)}, u32[]{:S(2)}, u32[]{:S(2)}) collective-permute-start(bf16[8,2,128,128]{3,2,1,0:T(8,128)(2,1)S(1)} %get-tuple-element.34), channel_id=1, source_target_pairs={{0,1},{1,0},{2,3},{3,2},{4,5},{5,4},{6,7},{7,6},{8,9},{9,8},{10,11... | collective-permute-start | bytes 1572872 | tf_op jit(solution)/shard_map/ppermute | solution.py:506
  43.6 0.0 collective-permute-done.other
  43.6 0.1 collective-permute-done.4.refs_1_
  43.7 3.7 %flow.3.refs_0_ = f32[2,4,16]{2,1,0:T(4,128)S(1)} custom-call(bf16[65,64,256]{2,1,0:T(8,128)(2,1)S(1)} %get-tuple-element.20.own, bf16[65,64,256]{2,1,0:T(8,128)(2,1)S(1)} %collective-permute-done.other, bf16[256,256]{1,0:T(8,128)(2,1)S(1)} %copy-done, bf16[256,256]{1,0:T(8,128)(2,1)S(1)} %copy-done.1, bf16[128,128]{1,0:T(8,128)(2,1)S(1)} %copy-done.2), custom_call_target="tpu_custom_call" | custom-call | flops 49999998976 | tf_op jit(solution)/shard_map/flow/pallas_call | solution.py:254
  47.4 2.4 %collective-permute-start.5 = (f32[3,8,16]{2,1,0:T(8,128)S(1)}, f32[3,8,16]{2,1,0:T(8,128)S(1)}, u32[]{:S(2)}, u32[]{:S(2)}) collective-permute-start(f32[3,8,16]{2,1,0:T(8,128)S(1)} %pad_maximum_fusion), channel_id=1, source_target_pairs={{0,1},{1,0},{2,3},{3,2},{4,5},{5,4},{6,7},{7,6},{8,9},{9,8},{10,11... | collective-permute-start | bytes 4616 | tf_op jit(solution)/shard_map/ppermute | solution.py:506
  49.8 2.6 %collective-permute-start.6 = (f32[3,8,16]{2,1,0:T(8,128)S(1)}, f32[3,8,16]{2,1,0:T(8,128)S(1)}, u32[]{:S(2)}, u32[]{:S(2)}) collective-permute-start(f32[3,8,16]{2,1,0:T(8,128)S(1)} %pad_maximum_fusion), channel_id=1, source_target_pairs={{1,2},{3,4},{5,6},{2,1},{4,3},{6,5},{9,10},{11,12},{13,14},{10,9},... | collective-permute-start | bytes 4616 | tf_op jit(solution)/shard_map/ppermute | solution.py:529
  52.4 6.1 %collective-permute-done.7.on_ref = bf16[8,2,128,128]{3,2,1,0:T(8,128)(2,1)S(1)} collective-permute-done((bf16[8,2,128,128]{3,2,1,0:T(8,128)(2,1)S(1)}, bf16[8,2,128,128]{3,2,1,0:T(8,128)(2,1)S(1)}, u32[]{:S(2)}, u32[]{:S(2)}) %collective-permute-start.7) | collective-permute-done | bytes 524320 | tf_op jit(solution)/shard_map/ppermute | solution.py:506
  58.6 2.3 %edges.1.refs_6_ = f32[8,4,272,128]{3,2,1,0:T(8,128)S(1)} custom-call(s32[2]{0:T(128)S(1)} %pad_add_fusion.tile_ref, s32[8,128]{1,0:T(8,128)S(1)} %get-tuple-element.26.target_ref, f32[8,128]{1,0:T(8,128)S(1)} %get-tuple-element.27.share_ref, bf16[8,2,128,128]{3,2,1,0:T(8,128)(2,1)S(1)} %collective-permute-done.7.on_ref, ...), custom_call_target="tpu_custom_call" | custom-call | flops 5000000 | bytes 4194304 | tf_op jit(solution)/shard_map/edges/pallas_call | solution.py:420
  60.9 0.0 collective-permute-done.5.refs_3_
  60.9 0.0 collective-permute-done.6.refs_4_
  60.9 6.2 %warp.1 = (bf16[1,8,16,128,128]{4,3,2,1,0:T(8,128)(2,1)}, f32[1,2,8,16]{3,2,1,0:T(8,128)}) custom-call(s32[2]{0:T(128)S(1)} %pad_add_fusion.tile_ref, f32[2,4,16]{2,1,0:T(4,128)S(1)} %flow.3.refs_0_, f32[2,4,16]{2,1,0:T(4,128)S(1)} %collective-permute-done.4.refs_1_, s32[1,8,16]{2,1,0:T(8,128)S(1)} %copy-done.6, ...), custom_call_target="tpu_custom_call" | custom-call | flops 20000000 | bytes 12582912 | tf_op jit(solution)/shard_map/warp/pallas_call | solution.py:475
  (11 shorter events, 0.0 us)
Async XLA Ops:
  5.3 14.6 %collective-permute-start.1 = (bf16[8,2,128,128]{3,2,1,0:T(8,128)(2,1)S(1)}, bf16[8,2,128,128]{3,2,1,0:T(8,128)(2,1)S(1)}, u32[]{:S(2)}, u32[]{:S(2)}) collective-permute-start(bf16[8,2,128,128]{3,2,1,0:T(8,128)(2,1)S(1)} %get-tuple-element.22), channel_id=1, source_target_pairs={{0,64},{1,65},{2,66},{3,67},{4,68},{5,69},{6,70},{7,71},{8,72},{9,... | collective-permute-start | bytes 1572872 | tf_op jit(solution)/shard_map/ppermute | solution.py:539
  6.9 29.8 %collective-permute-start.3 = (bf16[65,64,256]{2,1,0:T(8,128)(2,1)S(1)}, bf16[65,64,256]{2,1,0:T(8,128)(2,1)S(1)}, u32[]{:S(2)}, u32[]{:S(2)}) collective-permute-start(bf16[65,64,256]{2,1,0:T(8,128)(2,1)S(1)} %get-tuple-element.25.own), channel_id=1, source_target_pairs={{0,8},{8,16},{16,24},{24,32},{32,40},{40,48},{48,56},{56,64},{64,7... | collective-permute-start | bytes 6389768 | tf_op jit(solution)/shard_map/ppermute | solution.py:502
  8.8 10.5 %copy-start.3 = (s32[1,8,16,4]{2,3,1,0:T(4,128)S(1)}, s32[1,8,16,4]{2,3,1,0:T(4,128)}, u32[]{:S(2)}) copy-start(s32[1,8,16,4]{2,3,1,0:T(4,128)} %param.12) | copy-start | bytes 6148
  8.8 10.5 %copy-start.4 = (s32[1,8,16,4]{2,3,1,0:T(4,128)S(1)}, s32[1,8,16,4]{2,3,1,0:T(4,128)}, u32[]{:S(2)}) copy-start(s32[1,8,16,4]{2,3,1,0:T(4,128)} %param.13) | copy-start | bytes 6148
  8.8 10.5 %copy-start.5 = (f32[1,8,16,4]{2,3,1,0:T(4,128)S(1)}, f32[1,8,16,4]{2,3,1,0:T(4,128)}, u32[]{:S(2)}) copy-start(f32[1,8,16,4]{2,3,1,0:T(4,128)} %param.15) | copy-start | bytes 6148
  8.9 10.5 %copy-start.7 = (s32[1,8,16]{2,1,0:T(8,128)S(1)}, s32[1,8,16]{2,1,0:T(8,128)}, u32[]{:S(2)}) copy-start(s32[1,8,16]{2,1,0:T(8,128)} %count_ref.1) | copy-start | bytes 1540
  13.5 30.1 %collective-permute-start = (bf16[65,64,256]{2,1,0:T(8,128)(2,1)S(1)}, bf16[65,64,256]{2,1,0:T(8,128)(2,1)S(1)}, u32[]{:S(2)}, u32[]{:S(2)}) collective-permute-start(bf16[65,64,256]{2,1,0:T(8,128)(2,1)S(1)} %get-tuple-element.20.own), channel_id=1, source_target_pairs={{8,0},{16,8},{24,16},{32,24},{40,32},{48,40},{56,48},{64,56},{72,6... | collective-permute-start | bytes 6389768 | tf_op jit(solution)/shard_map/ppermute | solution.py:502
  20.0 20.4 %collective-permute-start.2 = (bf16[8,2,128,128]{3,2,1,0:T(8,128)(2,1)S(1)}, bf16[8,2,128,128]{3,2,1,0:T(8,128)(2,1)S(1)}, u32[]{:S(2)}, u32[]{:S(2)}) collective-permute-start(bf16[8,2,128,128]{3,2,1,0:T(8,128)(2,1)S(1)} %collective-permute-done.1), channel_id=1, source_target_pairs={{64,7},{65,2},{66,1},{67,4},{68,3},{69,6},{70,5},{71,0},{72,15},{7... | collective-permute-start | bytes 1572872 | tf_op jit(solution)/shard_map/ppermute | solution.py:539
  20.1 16.6 %copy-start = (bf16[256,256]{1,0:T(8,128)(2,1)S(1)}, bf16[256,256]{1,0:T(8,128)(2,1)}, u32[]{:S(2)}) copy-start(bf16[256,256]{1,0:T(8,128)(2,1)} %constant.28.cols_hbm.cols_ref) | copy-start | bytes 393220
  20.1 16.6 %copy-start.1 = (bf16[256,256]{1,0:T(8,128)(2,1)S(1)}, bf16[256,256]{1,0:T(8,128)(2,1)}, u32[]{:S(2)}) copy-start(bf16[256,256]{1,0:T(8,128)(2,1)} %constant.29.back_cols_ref) | copy-start | bytes 393220
  20.1 16.6 %copy-start.2 = (bf16[128,128]{1,0:T(8,128)(2,1)S(1)}, bf16[128,128]{1,0:T(8,128)(2,1)}, u32[]{:S(2)}) copy-start(bf16[128,128]{1,0:T(8,128)(2,1)} %constant.30.back_rows_ref) | copy-start | bytes 98308
  25.1 17.2 %copy-start.6 = (s32[1,8,16]{2,1,0:T(8,128)S(1)}, s32[1,8,16]{2,1,0:T(8,128)}, u32[]{:S(2)}) copy-start(s32[1,8,16]{2,1,0:T(8,128)} %refs_2_.1) | copy-start | bytes 1540
  40.4 3.2 %collective-permute-start.4 = (f32[2,4,16]{2,1,0:T(4,128)S(1)}, f32[2,4,16]{2,1,0:T(4,128)S(1)}, u32[]{:S(2)}, u32[]{:S(2)}) collective-permute-start(f32[2,4,16]{2,1,0:T(4,128)S(1)} %flow.2), channel_id=1, source_target_pairs={{8,0},{16,8},{24,16},{32,24},{40,32},{48,40},{56,48},{64,56},{72,6... | collective-permute-start | bytes 1544 | tf_op jit(solution)/shard_map/ppermute | solution.py:502
  42.4 16.2 %collective-permute-start.7 = (bf16[8,2,128,128]{3,2,1,0:T(8,128)(2,1)S(1)}, bf16[8,2,128,128]{3,2,1,0:T(8,128)(2,1)S(1)}, u32[]{:S(2)}, u32[]{:S(2)}) collective-permute-start(bf16[8,2,128,128]{3,2,1,0:T(8,128)(2,1)S(1)} %get-tuple-element.34), channel_id=1, source_target_pairs={{0,1},{1,0},{2,3},{3,2},{4,5},{5,4},{6,7},{7,6},{8,9},{9,8},{10,11... | collective-permute-start | bytes 1572872 | tf_op jit(solution)/shard_map/ppermute | solution.py:506
  47.4 13.5 %collective-permute-start.5 = (f32[3,8,16]{2,1,0:T(8,128)S(1)}, f32[3,8,16]{2,1,0:T(8,128)S(1)}, u32[]{:S(2)}, u32[]{:S(2)}) collective-permute-start(f32[3,8,16]{2,1,0:T(8,128)S(1)} %pad_maximum_fusion), channel_id=1, source_target_pairs={{0,1},{1,0},{2,3},{3,2},{4,5},{5,4},{6,7},{7,6},{8,9},{9,8},{10,11... | collective-permute-start | bytes 4616 | tf_op jit(solution)/shard_map/ppermute | solution.py:506
  49.8 11.1 %collective-permute-start.6 = (f32[3,8,16]{2,1,0:T(8,128)S(1)}, f32[3,8,16]{2,1,0:T(8,128)S(1)}, u32[]{:S(2)}, u32[]{:S(2)}) collective-permute-start(f32[3,8,16]{2,1,0:T(8,128)S(1)} %pad_maximum_fusion), channel_id=1, source_target_pairs={{1,2},{3,4},{5,6},{2,1},{4,3},{6,5},{9,10},{11,12},{13,14},{10,9},... | collective-permute-start | bytes 4616 | tf_op jit(solution)/shard_map/ppermute | solution.py:529

commit v8 on v7

--- a/solution.py
+++ b/solution.py
@@ -82,14 +82,16 @@
 
 
 def forward_kernel(start, toward_pair, tile_ref, x_hbm, rows_hbm, cols_hbm, *refs):
-    *_, spec_ref, src_ref, strip_ref, x_ref, rest_ref, lines_ref, ends_ref, rows_ref, cols_ref, in_sems, more_sems = refs
+    *refs, x_ref, rest_ref, lines_ref, ends_ref, rows_ref, cols_ref, in_sems, more_sems = refs
+    spec_ref, src_ref, *strip_refs = refs[-2 - (HB if toward_pair else 1) :]
     y = pl.program_id(0)
     count, patches = x_ref.shape[:2]
-    ny = strip_ref.shape[0]
+    ny = src_ref.shape[0]
     odd = tile_ref[0] % 2
     column = ((1 - odd) if toward_pair else odd) * (patches - HB)
     rest = (start + count) % ny
     fetch = lambda row: [pltpu.make_async_copy(x_hbm.at[0, start + row], x_ref.at[row], in_sems.at[row])]
+    to_strip = lambda i: strip_refs[i].at[:, 0] if toward_pair else strip_refs[0].at[:, i]
     more = [
         pltpu.make_async_copy(rows_hbm, rows_ref, more_sems.at[0]),
         pltpu.make_async_copy(cols_hbm, cols_ref, more_sems.at[1]),
@@ -114,10 +116,11 @@
     @pl.when(y == count - 1)
     def _():
         more[2].wait()
-        strip_ref[rest : rest + ny - count] = rest_ref[...].astype(jnp.bfloat16)
+        for i in range(HB):
+            to_strip(i)[rest : rest + ny - count] = rest_ref[:, i].astype(jnp.bfloat16)
 
     for i in range(HB):
-        strip_ref[start + y, i] = x_ref[y, column + i].astype(jnp.bfloat16)
+        to_strip(i)[start + y] = x_ref[y, column + i].astype(jnp.bfloat16)
     rows2 = rows_ref[...]
     cols = cols_ref[...]
     for pair in range(patches // 2):
@@ -147,17 +150,18 @@
     rows2 = jnp.concatenate([rows, rows], axis=1).astype(jnp.bfloat16)
     spectra = (count * nx + 1, HALF, 2 * N)
     before = () if source is None else (in_vmem(source),)
+    strips = (1,) * HB if toward_pair else (HB,)
     return pl.pallas_call(
         functools.partial(forward_kernel, start, toward_pair),
         grid=(count,),
         in_specs=[pl.BlockSpec(memory_space=pltpu.SMEM)]
         + [pl.BlockSpec(memory_space=pltpu.HBM)] * 3
         + [pl.BlockSpec(memory_space=pltpu.VMEM)] * len(before),
-        out_specs=[pl.BlockSpec(memory_space=pltpu.VMEM)] * 3,
+        out_specs=[pl.BlockSpec(memory_space=pltpu.VMEM)] * (2 + len(strips)),
         out_shape=[
             pltpu.VMEM(spectra, jnp.bfloat16),
             pltpu.VMEM((ny, nx, N, N), jnp.bfloat16),
-            pltpu.VMEM((ny, HB, N, N), jnp.bfloat16),
+            *(pltpu.VMEM((ny, wide, N, N), jnp.bfloat16) for wide in strips),
         ],
         scratch_shapes=[
             pltpu.VMEM((count, nx, N, N), jnp.float32),
@@ -343,7 +347,7 @@
         out_specs=pl.BlockSpec(memory_space=pltpu.VMEM),
         out_shape=pltpu.VMEM((ny, nx, N + 2 * PAD, N), jnp.float32),
         compiler_params=pltpu.CompilerParams(vmem_limit_bytes=4 * MIB),
-        cost_estimate=pl.CostEstimate(flops=20_000_000_000, bytes_accessed=4 * MIB, transcendentals=0),
+        cost_estimate=pl.CostEstimate(flops=16_000_000_000, bytes_accessed=4 * MIB, transcendentals=0),
         name="blend",
     )(target, share, in_vmem(source))
 
@@ -377,14 +381,17 @@
     return fields
 
 
-def edge_kernel(tile_ref, target_ref, share_ref, on_ref, off_ref, padded, out_ref, window, sems):
+def edge_kernel(tile_ref, target_ref, share_ref, first_ref, second_ref, off_ref, padded, out_ref, window, sems):
     y = pl.program_id(0)
     ny, nx = padded.shape[:2]
     even = tile_ref[0] % 2 == 0
-    halos = {True: ((on_ref, HB), (off_ref, 0)), False: ((on_ref, 0), (off_ref, HB))}
+    halos = {
+        side: ((first_ref, on_at), (second_ref, on_at + 1), (off_ref, HB - on_at))
+        for side, on_at in ((True, HB), (False, 0))
+    }
     copies = {
         side: [
-            pltpu.make_async_copy(ref, window.at[:, into : into + HB], sems.at[i])
+            pltpu.make_async_copy(ref, window.at[:, into : into + ref.shape[1]], sems.at[i])
             for i, (ref, into) in enumerate(places)
         ]
         for side, places in halos.items()
@@ -414,20 +421,20 @@
         out_ref[y, i, PAD : PAD + N] = padded[y, x, PAD : PAD + N] + more
 
 
-def edges_of(tile, target, share, on, off, blended):
+def edges_of(tile, target, share, first, second, off, blended):
     ny, _, tall, _ = blended.shape
     vmem = pl.BlockSpec(memory_space=pltpu.VMEM)
     return pl.pallas_call(
         edge_kernel,
         grid=(ny,),
-        in_specs=[pl.BlockSpec(memory_space=pltpu.SMEM)] * 3 + [vmem] * 3,
+        in_specs=[pl.BlockSpec(memory_space=pltpu.SMEM)] * 3 + [vmem] * 4,
         out_specs=vmem,
         out_shape=pltpu.VMEM((ny, 2 * HB, tall, N), jnp.float32),
-        scratch_shapes=[pltpu.VMEM((ny, 2 * HB, N, N), jnp.bfloat16), pltpu.SemaphoreType.DMA((2,))],
+        scratch_shapes=[pltpu.VMEM((ny, 2 * HB, N, N), jnp.bfloat16), pltpu.SemaphoreType.DMA((3,))],
         compiler_params=pltpu.CompilerParams(vmem_limit_bytes=4 * MIB),
         cost_estimate=pl.CostEstimate(flops=5_000_000, bytes_accessed=4 * MIB, transcendentals=0),
         name="edges",
-    )(tile, target, share, in_vmem(on), in_vmem(off), in_vmem(blended))
+    )(tile, target, share, in_vmem(first), in_vmem(second), in_vmem(off), in_vmem(blended))
 
 
 def warped(cell, down_shift, right_shift):
@@ -506,7 +513,7 @@
     return lax.ppermute(x, "tile", [(i, i ^ 1) for i in range(lax.axis_size("tile"))])
 
 
-def hops(tiles, sections):
+def hops(tiles, sections, far):
     pairs = ([], [])
     for section in range(sections):
         x_low, rest = divmod(section, sections // 2)
@@ -516,7 +523,7 @@
             ends = [section * tiles + tile]
             for hop in (1, 2):
                 x = (2 * x_high + x_low + hop * way) % 4
-                to_z = (z + 2 * x_high - 1) % (tiles // 2) if hop == 2 else z
+                to_z = (z + 2 * x_high - 1) % (tiles // 2) if far and hop == 2 else z
                 ends.append((x % 2 * (sections // 2) + rest) * tiles + 2 * to_z + x // 2)
             pairs[0].append((ends[0], ends[1]))
             pairs[1].append((ends[1], ends[2]))
@@ -535,32 +542,34 @@
     half = ny // 2
     tiles, count = lax.axis_size("tile"), lax.axis_size("sec")
     tile = jnp.stack([lax.axis_index("tile"), tiles]).astype(jnp.int32)
-    off_hops = hops(tiles, count)
+    on_hops, off_hops = hops(tiles, count, False), hops(tiles, count, True)
     hop = lambda x, pairs: lax.ppermute(x, ("sec", "tile"), pairs)
 
     spectra_high, source, off = forward(tile, sections, half, half, False, None, rows, cols)
     from_last = from_behind(spectra_high, "sec", 1)
     off = hop(off, off_hops[0])
-    spectra_low, source, on = forward(tile, sections, 0, half, True, source, rows, cols)
+    spectra_low, source, first, second = forward(tile, sections, 0, half, True, source, rows, cols)
     from_next = from_behind(spectra_low, "sec", -1)
+    first = hop(first, on_hops[0])
     target, share = slots_of(tile, box_row, box_shift, box_count, blend_weight)
-    off, source = lax.optimization_barrier((off, source))
+    off, first, source = lax.optimization_barrier((off, first, source))
     off = hop(off, off_hops[1])
+    first = hop(first, on_hops[1])
     blended = blend(target, share, source)
     from_last, blended = lax.optimization_barrier((from_last, blended))
 
     flow_high = flow_of(spectra_high, from_last, -1, half, nx, cols, back_cols, back_rows)
-    on, off, flow_high = lax.optimization_barrier((on, off, flow_high))
+    second, off, flow_high = lax.optimization_barrier((second, off, flow_high))
     flow_high = from_behind(flow_high, "sec", -1)
-    from_next, flow_high = lax.optimization_barrier((from_next, flow_high))
+    second = swapped(second)
+    from_next, flow_high, first = lax.optimization_barrier((from_next, flow_high, first))
     flow_low = flow_of(spectra_low, from_next, 1, half, nx, cols, back_cols, back_rows)
-    on = swapped(on)
     flow = jnp.concatenate([flow_low, flow_high], axis=1)
     flow = jnp.concatenate([flow, node_mask.astype(jnp.float32) + 1.0], axis=0)
     flow_off = beyond(flow)
     flow_on = swapped(flow)
     flows = (flow_low, flow_high, node_mask, flow_on, flow_off)
-    edges = edges_of(tile, target, share, on, off, blended)
+    edges = edges_of(tile, target, share, first, second, off, blended)
     return tuple(warp(tile, flows, blended, edges))
 
 

time: 67.4 us -> 76.8 us (1.14)
  the two profiles are of different devices: /device:TPU:66 before, /device:TPU:22 now
where the time goes in v8:
time: 76.8 us; the launch traced here: 76.5 us
  Pallas kernels  30.8 us (40%)
  waiting for transfers between devices  29.2 us (38%)
  starting transfers between devices  15.6 us (20%)
  between operations  0.81 us (1%)
    ppermute x4, waiting for transfers between devices, per_device(): hop = lambda x, pairs: lax.ppermute(x, ('sec', 'tile'), pairs)  25.5 us
    pallas_call x2, Pallas kernels, forward(): pl.pallas_call(functools.partial(forward_kernel, start, toward_pair), gri...  9.27 us
    pallas_call x2, Pallas kernels, flow_of(): pl.pallas_call(functools.partial(flow_kernel, sign), grid=(ny,), in_specs...  7.39 us
    ppermute x3, starting transfers between devices, from_behind(): return lax.ppermute(x, axis, pairs)  6.84 us
    pallas_call x1, Pallas kernels, warp(): pl.pallas_call(warp_kernel, grid=(ny,), in_specs=[pl.BlockSpec(memory_spa...  6.19 us
    ppermute x4, starting transfers between devices, per_device(): hop = lambda x, pairs: lax.ppermute(x, ('sec', 'tile'), pairs)  5.61 us
    pallas_call x1, Pallas kernels, blend(): pl.pallas_call(blend_kernel, grid=(ny,), in_specs=[pl.BlockSpec(memory_sp...  5 us
    ppermute x1, waiting for transfers between devices, beyond(): return lax.ppermute(x, 'tile', pairs + [(j, i) for i, j in pairs])  2.81 us
  transfers between devices with their start and end apart: 10, of which 5 were waited for; matrix products, arithmetic and copies ran while one was open for 0% of the time, Pallas kernels for 26%

profile of v8, /device:TPU:22, one launch (start us, length us, event | category | flops | bytes accessed | tf_op | source)
XLA Modules:
  0.0 76.5 jit_solution(11588647792728436038)
XLA Ops:
  0.6 0.1 pad_add_fusion.tile_ref
  0.7 4.6 %forward.2 = (bf16[65,64,256]{2,1,0:T(8,128)(2,1)S(1)}, bf16[8,16,128,128]{3,2,1,0:T(8,128)(2,1)S(1)}, bf16[8,2,128,128]{3,2,1,0:T(8,128)(2,1)S(1)}) custom-call(s32[2]{0:T(128)S(1)} %pad_add_fusion.tile_ref, f32[1,8,16,128,128]{4,3,2,1,0:T(8,128)} %x_hbm.3, bf16[128,256]{1,0:T(8,128)(2,1)} %constant.27.rows_hbm, bf16[256,256]{1,0:T(8,128)(2,1)} %constant.28.cols_hbm.cols_ref), custom_call_target="tpu_custom_call" | custom-call | flops 2000000000 | bytes 6291456 | tf_op jit(solution)/shard_map/forward/pallas_call | solution.py:154
  5.3 1.9 %collective-permute-start.4 = (bf16[65,64,256]{2,1,0:T(8,128)(2,1)S(1)}, bf16[65,64,256]{2,1,0:T(8,128)(2,1)S(1)}, u32[]{:S(2)}, u32[]{:S(2)}) collective-permute-start(bf16[65,64,256]{2,1,0:T(8,128)(2,1)S(1)} %get-tuple-element.29.own), channel_id=1, source_target_pairs={{0,8},{8,16},{16,24},{24,32},{32,40},{40,48},{48,56},{56,64},{64,7... | collective-permute-start | bytes 6389768 | tf_op jit(solution)/shard_map/ppermute | solution.py:509
  7.3 0.9 %collective-permute-start.1 = (bf16[8,2,128,128]{3,2,1,0:T(8,128)(2,1)S(1)}, bf16[8,2,128,128]{3,2,1,0:T(8,128)(2,1)S(1)}, u32[]{:S(2)}, u32[]{:S(2)}) collective-permute-start(bf16[8,2,128,128]{3,2,1,0:T(8,128)(2,1)S(1)} %get-tuple-element.25), channel_id=1, source_target_pairs={{0,64},{1,65},{2,66},{3,67},{4,68},{5,69},{6,70},{7,71},{8,72},{9,... | collective-permute-start | bytes 1572872 | tf_op jit(solution)/shard_map/ppermute | solution.py:546
  8.2 4.6 %forward.3 = (bf16[65,64,256]{2,1,0:T(8,128)(2,1)S(1)}, bf16[8,16,128,128]{3,2,1,0:T(8,128)(2,1)S(1)}, bf16[8,1,128,128]{3,2,1,0:T(8,128)(2,1)S(1)}, bf16[8,1,128,128]{3,2,1,0:T(8,128)(2,1)S(1)}) custom-call(s32[2]{0:T(128)S(1)} %pad_add_fusion.tile_ref, f32[1,8,16,128,128]{4,3,2,1,0:T(8,128)} %x_hbm.3, ...), custom_call_target="tpu_custom_call", output_to_operand_aliasing={{1}: (4, {})} | custom-call | flops 2000000000 | bytes 6291456 | tf_op jit(solution)/shard_map/forward/pallas_call | solution.py:154
  12.8 3.0 %collective-permute-start = (bf16[65,64,256]{2,1,0:T(8,128)(2,1)S(1)}, bf16[65,64,256]{2,1,0:T(8,128)(2,1)S(1)}, u32[]{:S(2)}, u32[]{:S(2)}) collective-permute-start(bf16[65,64,256]{2,1,0:T(8,128)(2,1)S(1)} %get-tuple-element.23.own), channel_id=1, source_target_pairs={{8,0},{16,8},{24,16},{32,24},{40,32},{48,40},{56,48},{64,56},{72,6... | collective-permute-start | bytes 6389768 | tf_op jit(solution)/shard_map/ppermute | solution.py:509
  15.8 1.6 %collective-permute-start.2 = (bf16[8,1,128,128]{3,2,1,0:T(8,128)(2,1)S(1)}, bf16[8,1,128,128]{3,2,1,0:T(8,128)(2,1)S(1)}, u32[]{:S(2)}, u32[]{:S(2)}) collective-permute-start(bf16[8,1,128,128]{3,2,1,0:T(8,128)(2,1)S(1)} %get-tuple-element.26), channel_id=1, source_target_pairs={{0,64},{1,65},{2,66},{3,67},{4,68},{5,69},{6,70},{7,71},{8,72},{9,... | collective-permute-start | bytes 786440 | tf_op jit(solution)/shard_map/ppermute | solution.py:546
  17.5 0.0 copy-done.3
  17.5 0.0 copy-done.4
  17.5 0.6 slots.1
  18.1 10.5 %collective-permute-done.2 = bf16[8,1,128,128]{3,2,1,0:T(8,128)(2,1)S(1)} collective-permute-done((bf16[8,1,128,128]{3,2,1,0:T(8,128)(2,1)S(1)}, bf16[8,1,128,128]{3,2,1,0:T(8,128)(2,1)S(1)}, u32[]{:S(2)}, u32[]{:S(2)}) %collective-permute-start.2) | collective-permute-done | bytes 262176 | tf_op jit(solution)/shard_map/ppermute | solution.py:546
  28.6 0.0 collective-permute-done.1
  28.6 3.1 %collective-permute-start.3 = (bf16[8,2,128,128]{3,2,1,0:T(8,128)(2,1)S(1)}, bf16[8,2,128,128]{3,2,1,0:T(8,128)(2,1)S(1)}, u32[]{:S(2)}, u32[]{:S(2)}) collective-permute-start(bf16[8,2,128,128]{3,2,1,0:T(8,128)(2,1)S(1)} %collective-permute-done.1), channel_id=1, source_target_pairs={{64,7},{65,2},{66,1},{67,4},{68,3},{69,6},{70,5},{71,0},{72,15},{7... | collective-permute-start | bytes 1572872 | tf_op jit(solution)/shard_map/ppermute | solution.py:546
  31.7 0.0 collective-permute-start.6
  31.7 5.0 %blend.1.padded.refs_5_ = f32[8,16,272,128]{3,2,1,0:T(8,128)S(1)} custom-call(s32[8,128]{1,0:T(8,128)S(1)} %get-tuple-element.30.target_ref, f32[8,128]{1,0:T(8,128)S(1)} %get-tuple-element.31.share_ref, bf16[8,16,128,128]{3,2,1,0:T(8,128)(2,1)S(1)} %get-tuple-element.32.source), custom_call_target="tpu_custom_call" | custom-call | flops 16000000000 | bytes 4194304 | tf_op jit(solution)/shard_map/blend/pallas_call | solution.py:343
  36.7 0.0 copy-start.6
  36.8 0.0 collective-permute-done.4.other
  36.8 3.7 %flow.2 = f32[2,4,16]{2,1,0:T(4,128)S(1)} custom-call(bf16[65,64,256]{2,1,0:T(8,128)(2,1)S(1)} %get-tuple-element.29.own, bf16[65,64,256]{2,1,0:T(8,128)(2,1)S(1)} %collective-permute-done.4.other, bf16[256,256]{1,0:T(8,128)(2,1)S(1)} %copy-done, bf16[256,256]{1,0:T(8,128)(2,1)S(1)} %copy-done.1, bf16[128,128]{1,0:T(8,128)(2,1)S(1)} %copy-done.2), custom_call_target="tpu_custom_call" | custom-call | tf_op jit(solution)/shard_map/flow/pallas_call | solution.py:258
  40.5 5.0 %collective-permute-done.3.off_ref = bf16[8,2,128,128]{3,2,1,0:T(8,128)(2,1)S(1)} collective-permute-done((bf16[8,2,128,128]{3,2,1,0:T(8,128)(2,1)S(1)}, bf16[8,2,128,128]{3,2,1,0:T(8,128)(2,1)S(1)}, u32[]{:S(2)}, u32[]{:S(2)}) %collective-permute-start.3) | collective-permute-done | bytes 524320 | tf_op jit(solution)/shard_map/ppermute | solution.py:546
  45.5 1.9 %collective-permute-start.5 = (f32[2,4,16]{2,1,0:T(4,128)S(1)}, f32[2,4,16]{2,1,0:T(4,128)S(1)}, u32[]{:S(2)}, u32[]{:S(2)}) collective-permute-start(f32[2,4,16]{2,1,0:T(4,128)S(1)} %flow.2), channel_id=1, source_target_pairs={{8,0},{16,8},{24,16},{32,24},{40,32},{48,40},{56,48},{64,56},{72,6... | collective-permute-start | bytes 1544 | tf_op jit(solution)/shard_map/ppermute | solution.py:509
  47.5 1.1 %collective-permute-start.9 = (bf16[8,1,128,128]{3,2,1,0:T(8,128)(2,1)S(1)}, bf16[8,1,128,128]{3,2,1,0:T(8,128)(2,1)S(1)}, u32[]{:S(2)}, u32[]{:S(2)}) collective-permute-start(bf16[8,1,128,128]{3,2,1,0:T(8,128)(2,1)S(1)} %get-tuple-element.40), channel_id=1, source_target_pairs={{0,1},{1,0},{2,3},{3,2},{4,5},{5,4},{6,7},{7,6},{8,9},{9,8},{10,11... | collective-permute-start | bytes 786440 | tf_op jit(solution)/shard_map/ppermute | solution.py:513
  48.6 10.0 %collective-permute-done.6.first_ref = bf16[8,1,128,128]{3,2,1,0:T(8,128)(2,1)S(1)} collective-permute-done((bf16[8,1,128,128]{3,2,1,0:T(8,128)(2,1)S(1)}, bf16[8,1,128,128]{3,2,1,0:T(8,128)(2,1)S(1)}, u32[]{:S(2)}, u32[]{:S(2)}) %collective-permute-start.6) | collective-permute-done | bytes 262176 | tf_op jit(solution)/shard_map/ppermute | solution.py:546
  58.5 0.0 collective-permute-done.other
  58.5 0.0 collective-permute-done.5.refs_1_
  58.5 3.7 %flow.3.refs_0_ = f32[2,4,16]{2,1,0:T(4,128)S(1)} custom-call(bf16[65,64,256]{2,1,0:T(8,128)(2,1)S(1)} %get-tuple-element.23.own, bf16[65,64,256]{2,1,0:T(8,128)(2,1)S(1)} %collective-permute-done.other, bf16[256,256]{1,0:T(8,128)(2,1)S(1)} %copy-done, bf16[256,256]{1,0:T(8,128)(2,1)S(1)} %copy-done.1, bf16[128,128]{1,0:T(8,128)(2,1)S(1)} %copy-done.2), custom_call_target="tpu_custom_call" | custom-call | flops 49999998976 | tf_op jit(solution)/shard_map/flow/pallas_call | solution.py:258
  62.3 0.1 collective-permute-start.7
  62.4 1.9 %collective-permute-start.8 = (f32[3,8,16]{2,1,0:T(8,128)S(1)}, f32[3,8,16]{2,1,0:T(8,128)S(1)}, u32[]{:S(2)}, u32[]{:S(2)}) collective-permute-start(f32[3,8,16]{2,1,0:T(8,128)S(1)} %pad_maximum_fusion), channel_id=1, source_target_pairs={{1,2},{3,4},{5,6},{2,1},{4,3},{6,5},{9,10},{11,12},{13,14},{10,9},... | collective-permute-start | bytes 4616 | tf_op jit(solution)/shard_map/ppermute | solution.py:536
  64.3 0.0 collective-permute-done.9.second_ref
  64.3 2.3 %edges.1.refs_6_ = f32[8,4,272,128]{3,2,1,0:T(8,128)S(1)} custom-call(s32[2]{0:T(128)S(1)} %pad_add_fusion.tile_ref, s32[8,128]{1,0:T(8,128)S(1)} %get-tuple-element.30.target_ref, f32[8,128]{1,0:T(8,128)S(1)} %get-tuple-element.31.share_ref, bf16[8,1,128,128]{3,2,1,0:T(8,128)(2,1)S(1)} %collective-permute-done.6.first_ref, ...), custom_call_target="tpu_custom_call" | custom-call | flops 5000000 | bytes 4194304 | tf_op jit(solution)/shard_map/edges/pallas_call | solution.py:427
  66.6 0.9 %collective-permute-done.7.refs_3_ = f32[3,8,16]{2,1,0:T(8,128)S(1)} collective-permute-done((f32[3,8,16]{2,1,0:T(8,128)S(1)}, f32[3,8,16]{2,1,0:T(8,128)S(1)}, u32[]{:S(2)}, u32[]{:S(2)}) %collective-permute-start.7) | collective-permute-done | bytes 1568 | tf_op jit(solution)/shard_map/ppermute | solution.py:513
  67.5 2.8 %collective-permute-done.8.refs_4_ = f32[3,8,16]{2,1,0:T(8,128)S(1)} collective-permute-done((f32[3,8,16]{2,1,0:T(8,128)S(1)}, f32[3,8,16]{2,1,0:T(8,128)S(1)}, u32[]{:S(2)}, u32[]{:S(2)}) %collective-permute-start.8) | collective-permute-done | bytes 1568 | tf_op jit(solution)/shard_map/ppermute | solution.py:536
  70.3 6.2 %warp.1 = (bf16[1,8,16,128,128]{4,3,2,1,0:T(8,128)(2,1)}, f32[1,2,8,16]{3,2,1,0:T(8,128)}) custom-call(s32[2]{0:T(128)S(1)} %pad_add_fusion.tile_ref, f32[2,4,16]{2,1,0:T(4,128)S(1)} %flow.3.refs_0_, f32[2,4,16]{2,1,0:T(4,128)S(1)} %collective-permute-done.5.refs_1_, s32[1,8,16]{2,1,0:T(8,128)S(1)} %copy-done.6, ...), custom_call_target="tpu_custom_call" | custom-call | flops 20000000 | bytes 12582912 | tf_op jit(solution)/shard_map/warp/pallas_call | solution.py:482
  (15 shorter events, 0.1 us)
Async XLA Ops:
  5.3 31.4 %collective-permute-start.4 = (bf16[65,64,256]{2,1,0:T(8,128)(2,1)S(1)}, bf16[65,64,256]{2,1,0:T(8,128)(2,1)S(1)}, u32[]{:S(2)}, u32[]{:S(2)}) collective-permute-start(bf16[65,64,256]{2,1,0:T(8,128)(2,1)S(1)} %get-tuple-element.29.own), channel_id=1, source_target_pairs={{0,8},{8,16},{16,24},{24,32},{32,40},{40,48},{48,56},{56,64},{64,7... | collective-permute-start | bytes 6389768 | tf_op jit(solution)/shard_map/ppermute | solution.py:509
  7.3 21.4 %collective-permute-start.1 = (bf16[8,2,128,128]{3,2,1,0:T(8,128)(2,1)S(1)}, bf16[8,2,128,128]{3,2,1,0:T(8,128)(2,1)S(1)}, u32[]{:S(2)}, u32[]{:S(2)}) collective-permute-start(bf16[8,2,128,128]{3,2,1,0:T(8,128)(2,1)S(1)} %get-tuple-element.25), channel_id=1, source_target_pairs={{0,64},{1,65},{2,66},{3,67},{4,68},{5,69},{6,70},{7,71},{8,72},{9,... | collective-permute-start | bytes 1572872 | tf_op jit(solution)/shard_map/ppermute | solution.py:546
  8.2 9.3 %copy-start.3 = (s32[1,8,16,4]{2,3,1,0:T(4,128)S(1)}, s32[1,8,16,4]{2,3,1,0:T(4,128)}, u32[]{:S(2)}) copy-start(s32[1,8,16,4]{2,3,1,0:T(4,128)} %param.12) | copy-start | bytes 6148
  8.2 9.3 %copy-start.4 = (s32[1,8,16,4]{2,3,1,0:T(4,128)S(1)}, s32[1,8,16,4]{2,3,1,0:T(4,128)}, u32[]{:S(2)}) copy-start(s32[1,8,16,4]{2,3,1,0:T(4,128)} %param.13) | copy-start | bytes 6148
  8.2 9.3 %copy-start.5 = (f32[1,8,16,4]{2,3,1,0:T(4,128)S(1)}, f32[1,8,16,4]{2,3,1,0:T(4,128)}, u32[]{:S(2)}) copy-start(f32[1,8,16,4]{2,3,1,0:T(4,128)} %param.15) | copy-start | bytes 6148
  8.2 9.3 %copy-start.7 = (s32[1,8,16]{2,1,0:T(8,128)S(1)}, s32[1,8,16]{2,1,0:T(8,128)}, u32[]{:S(2)}) copy-start(s32[1,8,16]{2,1,0:T(8,128)} %count_ref.1) | copy-start | bytes 1540
  12.8 45.7 %collective-permute-start = (bf16[65,64,256]{2,1,0:T(8,128)(2,1)S(1)}, bf16[65,64,256]{2,1,0:T(8,128)(2,1)S(1)}, u32[]{:S(2)}, u32[]{:S(2)}) collective-permute-start(bf16[65,64,256]{2,1,0:T(8,128)(2,1)S(1)} %get-tuple-element.23.own), channel_id=1, source_target_pairs={{8,0},{16,8},{24,16},{32,24},{40,32},{48,40},{56,48},{64,56},{72,6... | collective-permute-start | bytes 6389768 | tf_op jit(solution)/shard_map/ppermute | solution.py:509
  15.8 12.8 %collective-permute-start.2 = (bf16[8,1,128,128]{3,2,1,0:T(8,128)(2,1)S(1)}, bf16[8,1,128,128]{3,2,1,0:T(8,128)(2,1)S(1)}, u32[]{:S(2)}, u32[]{:S(2)}) collective-permute-start(bf16[8,1,128,128]{3,2,1,0:T(8,128)(2,1)S(1)} %get-tuple-element.26), channel_id=1, source_target_pairs={{0,64},{1,65},{2,66},{3,67},{4,68},{5,69},{6,70},{7,71},{8,72},{9,... | collective-permute-start | bytes 786440 | tf_op jit(solution)/shard_map/ppermute | solution.py:546
  28.6 16.9 %collective-permute-start.3 = (bf16[8,2,128,128]{3,2,1,0:T(8,128)(2,1)S(1)}, bf16[8,2,128,128]{3,2,1,0:T(8,128)(2,1)S(1)}, u32[]{:S(2)}, u32[]{:S(2)}) collective-permute-start(bf16[8,2,128,128]{3,2,1,0:T(8,128)(2,1)S(1)} %collective-permute-done.1), channel_id=1, source_target_pairs={{64,7},{65,2},{66,1},{67,4},{68,3},{69,6},{70,5},{71,0},{72,15},{7... | collective-permute-start | bytes 1572872 | tf_op jit(solution)/shard_map/ppermute | solution.py:546
  31.7 26.8 %collective-permute-start.6 = (bf16[8,1,128,128]{3,2,1,0:T(8,128)(2,1)S(1)}, bf16[8,1,128,128]{3,2,1,0:T(8,128)(2,1)S(1)}, u32[]{:S(2)}, u32[]{:S(2)}) collective-permute-start(bf16[8,1,128,128]{3,2,1,0:T(8,128)(2,1)S(1)} %collective-permute-done.2), channel_id=1, source_target_pairs={{64,1},{65,0},{66,3},{67,2},{68,5},{69,4},{70,7},{71,6},{72,9},{73... | collective-permute-start | bytes 786440 | tf_op jit(solution)/shard_map/ppermute | solution.py:546
  31.7 5.0 %copy-start = (bf16[256,256]{1,0:T(8,128)(2,1)S(1)}, bf16[256,256]{1,0:T(8,128)(2,1)}, u32[]{:S(2)}) copy-start(bf16[256,256]{1,0:T(8,128)(2,1)} %constant.28.cols_hbm.cols_ref) | copy-start | bytes 393220
  31.7 5.1 %copy-start.1 = (bf16[256,256]{1,0:T(8,128)(2,1)S(1)}, bf16[256,256]{1,0:T(8,128)(2,1)}, u32[]{:S(2)}) copy-start(bf16[256,256]{1,0:T(8,128)(2,1)} %constant.29.back_cols_ref) | copy-start | bytes 393220
  31.7 5.1 %copy-start.2 = (bf16[128,128]{1,0:T(8,128)(2,1)S(1)}, bf16[128,128]{1,0:T(8,128)(2,1)}, u32[]{:S(2)}) copy-start(bf16[128,128]{1,0:T(8,128)(2,1)} %constant.30.back_rows_ref) | copy-start | bytes 98308
  36.7 10.7 %copy-start.6 = (s32[1,8,16]{2,1,0:T(8,128)S(1)}, s32[1,8,16]{2,1,0:T(8,128)}, u32[]{:S(2)}) copy-start(s32[1,8,16]{2,1,0:T(8,128)} %refs_2_.1) | copy-start | bytes 1540
  45.5 13.0 %collective-permute-start.5 = (f32[2,4,16]{2,1,0:T(4,128)S(1)}, f32[2,4,16]{2,1,0:T(4,128)S(1)}, u32[]{:S(2)}, u32[]{:S(2)}) collective-permute-start(f32[2,4,16]{2,1,0:T(4,128)S(1)} %flow.2), channel_id=1, source_target_pairs={{8,0},{16,8},{24,16},{32,24},{40,32},{48,40},{56,48},{64,56},{72,6... | collective-permute-start | bytes 1544 | tf_op jit(solution)/shard_map/ppermute | solution.py:509
  47.5 16.8 %collective-permute-start.9 = (bf16[8,1,128,128]{3,2,1,0:T(8,128)(2,1)S(1)}, bf16[8,1,128,128]{3,2,1,0:T(8,128)(2,1)S(1)}, u32[]{:S(2)}, u32[]{:S(2)}) collective-permute-start(bf16[8,1,128,128]{3,2,1,0:T(8,128)(2,1)S(1)} %get-tuple-element.40), channel_id=1, source_target_pairs={{0,1},{1,0},{2,3},{3,2},{4,5},{5,4},{6,7},{7,6},{8,9},{9,8},{10,11... | collective-permute-start | bytes 786440 | tf_op jit(solution)/shard_map/ppermute | solution.py:513
  62.3 5.3 %collective-permute-start.7 = (f32[3,8,16]{2,1,0:T(8,128)S(1)}, f32[3,8,16]{2,1,0:T(8,128)S(1)}, u32[]{:S(2)}, u32[]{:S(2)}) collective-permute-start(f32[3,8,16]{2,1,0:T(8,128)S(1)} %pad_maximum_fusion), channel_id=1, source_target_pairs={{0,1},{1,0},{2,3},{3,2},{4,5},{5,4},{6,7},{7,6},{8,9},{9,8},{10,11... | collective-permute-start | bytes 4616 | tf_op jit(solution)/shard_map/ppermute | solution.py:513
  62.4 8.0 %collective-permute-start.8 = (f32[3,8,16]{2,1,0:T(8,128)S(1)}, f32[3,8,16]{2,1,0:T(8,128)S(1)}, u32[]{:S(2)}, u32[]{:S(2)}) collective-permute-start(f32[3,8,16]{2,1,0:T(8,128)S(1)} %pad_maximum_fusion), channel_id=1, source_target_pairs={{1,2},{3,4},{5,6},{2,1},{4,3},{6,5},{9,10},{11,12},{13,14},{10,9},... | collective-permute-start | bytes 4616 | tf_op jit(solution)/shard_map/ppermute | solution.py:536

commit v9 on v7

--- a/solution.py
+++ b/solution.py
@@ -377,57 +377,38 @@
     return fields
 
 
-def edge_kernel(tile_ref, target_ref, share_ref, on_ref, off_ref, padded, out_ref, window, sems):
+def halo_cell(y, x, nx, target_ref, share_ref, strip):
+    total = None
+    for k in range(K):
+        at = (K + k) * nx + x
+        spot = target_ref[y, at]
+        piece = strip[spot // ROW, spot % HB].astype(jnp.float32) * share_ref[y, at]
+        total = piece if total is None else total + piece
+    return total
+
+
+def beyond_kernel(tile_ref, target_ref, share_ref, strip, _, out_ref):
     y = pl.program_id(0)
-    ny, nx = padded.shape[:2]
-    even = tile_ref[0] % 2 == 0
-    halos = {True: ((on_ref, HB), (off_ref, 0)), False: ((on_ref, 0), (off_ref, HB))}
-    copies = {
-        side: [
-            pltpu.make_async_copy(ref, window.at[:, into : into + HB], sems.at[i])
-            for i, (ref, into) in enumerate(places)
-        ]
-        for side, places in halos.items()
-    }
-
-    @pl.when((y == 0) & even)
-    def _():
-        for copy in copies[True]:
-            copy.start()
-
-    @pl.when((y == 0) & jnp.logical_not(even))
-    def _():
-        for copy in copies[False]:
-            copy.start()
-
-    border = jnp.zeros((2 * HB, PAD, N), jnp.float32)
-    out_ref[y, :, :PAD] = border
-    out_ref[y, :, PAD + N :] = border
-
-    @pl.when(y == 0)
-    def _():
-        for copy in copies[True]:
-            copy.wait()
-
-    for i, x in enumerate((*range(HB), *range(nx - HB, nx))):
-        more = blend_cell(y, K * nx + x, nx, target_ref, share_ref, window)
-        out_ref[y, i, PAD : PAD + N] = padded[y, x, PAD : PAD + N] + more
-
-
-def edges_of(tile, target, share, on, off, blended):
-    ny, _, tall, _ = blended.shape
+    nx = out_ref.shape[1]
+    first = tile_ref[0] % 2 * (nx - HB)
+    for i in range(HB):
+        x = first + i
+        out_ref[y, x, PAD : PAD + N] += halo_cell(y, x, nx, target_ref, share_ref, strip)
+
+
+def with_beyond(tile, target, share, off, blended):
     vmem = pl.BlockSpec(memory_space=pltpu.VMEM)
     return pl.pallas_call(
-        edge_kernel,
-        grid=(ny,),
-        in_specs=[pl.BlockSpec(memory_space=pltpu.SMEM)] * 3 + [vmem] * 3,
+        beyond_kernel,
+        grid=(blended.shape[0],),
+        in_specs=[pl.BlockSpec(memory_space=pltpu.SMEM)] * 3 + [vmem] * 2,
         out_specs=vmem,
-        out_shape=pltpu.VMEM((ny, 2 * HB, tall, N), jnp.float32),
-        scratch_shapes=[pltpu.VMEM((ny, 2 * HB, N, N), jnp.bfloat16), pltpu.SemaphoreType.DMA((2,))],
+        out_shape=pltpu.VMEM(blended.shape, jnp.float32),
+        input_output_aliases={4: 0},
         compiler_params=pltpu.CompilerParams(vmem_limit_bytes=4 * MIB),
-        cost_estimate=pl.CostEstimate(flops=5_000_000, bytes_accessed=4 * MIB, transcendentals=0),
-        name="edges",
-    )(tile, target, share, in_vmem(on), in_vmem(off), in_vmem(blended))
+        cost_estimate=pl.CostEstimate(flops=0, bytes_accessed=0, transcendentals=0),
+        name="beyond",
+    )(tile, target, share, in_vmem(off), in_vmem(blended))
 
 
 def warped(cell, down_shift, right_shift):
@@ -447,29 +428,32 @@
 
 
 def warp_kernel(tile_ref, *refs):
-    *flows, padded, edges, out_hbm, field_ref, out, wide, field, sem, out_sems = refs
+    *flows, padded, out_hbm, field_ref, wide_ref, out, field, sem, out_sems = refs
     y = pl.program_id(0)
-    ny, nx = out.shape[:2]
+    ny, count = out.shape[:2]
+    nx = padded.shape[1]
+    first = tile_ref[0] % 2 * HB
 
     @pl.when(y == 0)
     def _():
         for component, values in enumerate(relax(tile_ref, *flows)):
-            wide[component] = values
+            wide_ref[component] = values
             field_ref[0, component] = values[:, STEPS : STEPS + nx]
-        scalars = pltpu.make_async_copy(wide, field, sem)
+        scalars = pltpu.make_async_copy(wide_ref, field, sem)
         scalars.start()
         scalars.wait()
 
-    borders = (*range(HB), *range(nx - HB, nx))
-    for x in range(nx):
-        cell = edges.at[y, borders.index(x)] if x in borders else padded.at[y, x]
-        out[y, x] = warped(cell, field[0, y, STEPS + x], field[1, y, STEPS + x])
-    store = lambda row: pltpu.make_async_copy(out.at[row], out_hbm.at[0, row], out_sems.at[row])
+    for i in range(count):
+        x = first + i
+        out[y, i] = warped(padded.at[y, x], field[0, y, STEPS + x], field[1, y, STEPS + x])
+    store = lambda row: pltpu.make_async_copy(
+        out.at[row], out_hbm.at[0, row, pl.ds(first, count)], out_sems.at[row]
+    )
     store(y).start()
     wait_all([store(row) for row in range(ny)])
 
 
-def warp(tile, flows, blended, edges):
+def warp(tile, flows, blended):
     ny, nx = blended.shape[:2]
     whole = lambda shape: pl.BlockSpec(shape, lambda y: (0,) * len(shape))
     return pl.pallas_call(
@@ -477,15 +461,19 @@
         grid=(ny,),
         in_specs=[pl.BlockSpec(memory_space=pltpu.SMEM)]
         + [whole(x.shape) for x in flows]
-        + [pl.BlockSpec(memory_space=pltpu.VMEM)] * 2,
-        out_specs=[pl.BlockSpec(memory_space=pl.ANY), whole((1, 2, ny, nx))],
+        + [pl.BlockSpec(memory_space=pltpu.VMEM)],
+        out_specs=[
+            pl.BlockSpec(memory_space=pltpu.HBM),
+            whole((1, 2, ny, nx)),
+            pl.BlockSpec(memory_space=pltpu.VMEM),
+        ],
         out_shape=[
             jax.ShapeDtypeStruct((1, ny, nx, N, N), jnp.bfloat16),
             jax.ShapeDtypeStruct((1, 2, ny, nx), jnp.float32),
+            pltpu.VMEM((2, ny, N), jnp.float32),
         ],
         scratch_shapes=[
-            pltpu.VMEM((ny, nx, N, N), jnp.bfloat16),
-            pltpu.VMEM((2, ny, N), jnp.float32),
+            pltpu.VMEM((ny, nx - HB, N, N), jnp.bfloat16),
             pltpu.SMEM((2, ny, N), jnp.float32),
             pltpu.SemaphoreType.DMA,
             pltpu.SemaphoreType.DMA((ny,)),
@@ -493,7 +481,66 @@
         compiler_params=pltpu.CompilerParams(vmem_limit_bytes=8 * MIB),
         cost_estimate=pl.CostEstimate(flops=20_000_000, bytes_accessed=12 * MIB, transcendentals=0),
         name="warp",
-    )(tile, *flows, in_vmem(blended), in_vmem(edges))
+    )(tile, *flows, in_vmem(blended))
+
+
+def pair_kernel(tile_ref, target_ref, share_ref, wide, strip, padded, _, out_hbm, cells, out, field, sem, out_sems):
+    step = pl.program_id(0)
+    ny, nx = padded.shape[:2]
+    rows = cells.shape[0] // HB
+    first = (1 - tile_ref[0] % 2) * (nx - HB)
+    scalars = pltpu.make_async_copy(wide, field, sem)
+
+    @pl.when(step == 0)
+    def _():
+        scalars.start()
+        border = jnp.zeros((rows * HB, PAD, N), jnp.float32)
+        cells[:, :PAD] = border
+        cells[:, PAD + N :] = border
+
+    places = [(step * rows + row, i, row * HB + i) for row in range(rows) for i in range(HB)]
+    for y, i, at in places:
+        more = halo_cell(y, first + i, nx, target_ref, share_ref, strip)
+        cells[at, PAD : PAD + N] = padded[y, first + i, PAD : PAD + N] + more
+
+    @pl.when(step == 0)
+    def _():
+        scalars.wait()
+
+    for y, i, at in places:
+        column = STEPS + first + i
+        out[y, i] = warped(cells.at[at], field[0, y, column], field[1, y, column])
+    store = lambda row: pltpu.make_async_copy(
+        out.at[row], out_hbm.at[0, row, pl.ds(first, HB)], out_sems.at[row]
+    )
+    for row in range(rows):
+        store(step * rows + row).start()
+    wait_all([store(row) for row in range(ny)])
+
+
+def warp_pair(tile, target, share, wide, on, blended, rendered):
+    ny, _, tall, _ = blended.shape
+    rows = 2
+    vmem = pl.BlockSpec(memory_space=pltpu.VMEM)
+    hbm = pl.BlockSpec(memory_space=pltpu.HBM)
+    return pl.pallas_call(
+        pair_kernel,
+        grid=(ny // rows,),
+        in_specs=[pl.BlockSpec(memory_space=pltpu.SMEM)] * 3 + [vmem] * 3 + [hbm],
+        out_specs=hbm,
+        out_shape=jax.ShapeDtypeStruct(rendered.shape, rendered.dtype),
+        scratch_shapes=[
+            pltpu.VMEM((rows * HB, tall, N), jnp.float32),
+            pltpu.VMEM((ny, HB, N, N), jnp.bfloat16),
+            pltpu.SMEM((2, ny, N), jnp.float32),
+            pltpu.SemaphoreType.DMA,
+            pltpu.SemaphoreType.DMA((ny,)),
+        ],
+        input_output_aliases={6: 0},
+        compiler_params=pltpu.CompilerParams(vmem_limit_bytes=8 * MIB),
+        cost_estimate=pl.CostEstimate(flops=5_000_000, bytes_accessed=4 * MIB, transcendentals=0),
+        name="pair",
+    )(tile, target, share, in_vmem(wide), in_vmem(on), in_vmem(blended), rendered)
 
 
 def from_behind(x, axis, by):
@@ -547,10 +594,11 @@
     off, source = lax.optimization_barrier((off, source))
     off = hop(off, off_hops[1])
     blended = blend(target, share, source)
+    blended = with_beyond(tile, target, share, off, blended)
     from_last, blended = lax.optimization_barrier((from_last, blended))
 
     flow_high = flow_of(spectra_high, from_last, -1, half, nx, cols, back_cols, back_rows)
-    on, off, flow_high = lax.optimization_barrier((on, off, flow_high))
+    on, flow_high = lax.optimization_barrier((on, flow_high))
     flow_high = from_behind(flow_high, "sec", -1)
     from_next, flow_high = lax.optimization_barrier((from_next, flow_high))
     flow_low = flow_of(spectra_low, from_next, 1, half, nx, cols, back_cols, back_rows)
@@ -560,8 +608,9 @@
     flow_off = beyond(flow)
     flow_on = swapped(flow)
     flows = (flow_low, flow_high, node_mask, flow_on, flow_off)
-    edges = edges_of(tile, target, share, on, off, blended)
-    return tuple(warp(tile, flows, blended, edges))
+    rendered, field, wide = warp(tile, flows, blended)
+    on, rendered = lax.optimization_barrier((on, rendered))
+    return (warp_pair(tile, target, share, wide, on, blended, rendered), field)
 
 
 def solution(mesh):

time: 67.4 us -> 71 us (1.053)
  the two profiles are of different devices: /device:TPU:66 before, /device:TPU:86 now
where the time goes in v9:
time: 71 us; the launch traced here: 70.7 us
  Pallas kernels  33.4 us (47%)
  waiting for transfers between devices  20.1 us (28%)
  starting transfers between devices  16.2 us (23%)
  between operations  0.89 us (1%)
    ppermute x2, waiting for transfers between devices, per_device(): hop = lambda x, pairs: lax.ppermute(x, ('sec', 'tile'), pairs)  12.9 us
    pallas_call x2, Pallas kernels, forward(): pl.pallas_call(functools.partial(forward_kernel, start, toward_pair), gri...  9.27 us
    ppermute x3, starting transfers between devices, from_behind(): return lax.ppermute(x, axis, pairs)  7.48 us
    pallas_call x2, Pallas kernels, flow_of(): pl.pallas_call(functools.partial(flow_kernel, sign), grid=(ny,), in_specs...  7.39 us
    pallas_call x1, Pallas kernels, warp(): pl.pallas_call(warp_kernel, grid=(ny,), in_specs=[pl.BlockSpec(memory_spa...  5.94 us
    ppermute x1, starting transfers between devices, beyond(): return lax.ppermute(x, 'tile', pairs + [(j, i) for i, j in pairs])  5.37 us
    pallas_call x1, Pallas kernels, blend(): pl.pallas_call(blend_kernel, grid=(ny,), in_specs=[pl.BlockSpec(memory_sp...  4.98 us
    pallas_call x1, Pallas kernels, warp_pair(): pl.pallas_call(pair_kernel, grid=(ny // rows,), in_specs=[pl.BlockSpec(me...  3.52 us
  transfers between devices with their start and end apart: 8, of which 5 were waited for; matrix products, arithmetic and copies ran while one was open for 0% of the time, Pallas kernels for 36%

profile of v9, /device:TPU:86, one launch (start us, length us, event | category | flops | bytes accessed | tf_op | source)
XLA Modules:
  0.0 70.7 jit_solution(11614165716529050826)
XLA Ops:
  0.6 0.1 pad_add_fusion.tile_ref
  0.7 4.6 %forward.2 = (bf16[65,64,256]{2,1,0:T(8,128)(2,1)S(1)}, bf16[8,16,128,128]{3,2,1,0:T(8,128)(2,1)S(1)}, bf16[8,2,128,128]{3,2,1,0:T(8,128)(2,1)S(1)}) custom-call(s32[2]{0:T(128)S(1)} %pad_add_fusion.tile_ref, f32[1,8,16,128,128]{4,3,2,1,0:T(8,128)} %x_hbm.3, bf16[128,256]{1,0:T(8,128)(2,1)} %constant.27.rows_hbm, bf16[256,256]{1,0:T(8,128)(2,1)} %constant.28.cols_hbm.cols_ref), custom_call_target="tpu_custom_call" | custom-call | flops 2000000000 | bytes 6291456 | tf_op jit(solution)/shard_map/forward/pallas_call | solution.py:150
  5.3 0.9 %collective-permute-start.2 = (bf16[8,2,128,128]{3,2,1,0:T(8,128)(2,1)S(1)}, bf16[8,2,128,128]{3,2,1,0:T(8,128)(2,1)S(1)}, u32[]{:S(2)}, u32[]{:S(2)}) collective-permute-start(bf16[8,2,128,128]{3,2,1,0:T(8,128)(2,1)S(1)} %get-tuple-element.29), channel_id=1, source_target_pairs={{0,64},{1,65},{2,66},{3,67},{4,68},{5,69},{6,70},{7,71},{8,72},{9,... | collective-permute-start | bytes 1572872 | tf_op jit(solution)/shard_map/ppermute | solution.py:586
  6.2 1.9 %collective-permute-start.1 = (bf16[65,64,256]{2,1,0:T(8,128)(2,1)S(1)}, bf16[65,64,256]{2,1,0:T(8,128)(2,1)S(1)}, u32[]{:S(2)}, u32[]{:S(2)}) collective-permute-start(bf16[65,64,256]{2,1,0:T(8,128)(2,1)S(1)} %get-tuple-element.28.own), channel_id=1, source_target_pairs={{0,8},{8,16},{16,24},{24,32},{32,40},{40,48},{48,56},{56,64},{64,7... | collective-permute-start | bytes 6389768 | tf_op jit(solution)/shard_map/ppermute | solution.py:549
  8.2 0.0 copy-start.3
  8.2 0.0 copy-start.4
  8.2 0.0 copy-start.5
  8.2 0.0 copy-start.7
  8.2 4.6 %forward.3 = (bf16[65,64,256]{2,1,0:T(8,128)(2,1)S(1)}, bf16[8,16,128,128]{3,2,1,0:T(8,128)(2,1)S(1)}, bf16[8,2,128,128]{3,2,1,0:T(8,128)(2,1)S(1)}) custom-call(s32[2]{0:T(128)S(1)} %pad_add_fusion.tile_ref, f32[1,8,16,128,128]{4,3,2,1,0:T(8,128)} %x_hbm.3, bf16[128,256]{1,0:T(8,128)(2,1)} %constant.27.rows_hbm, ...), custom_call_target="tpu_custom_call", output_to_operand_aliasing={{1}: (4, {})} | custom-call | flops 2000000000 | bytes 6291456 | tf_op jit(solution)/shard_map/forward/pallas_call | solution.py:150
  12.9 3.6 %collective-permute-start = (bf16[65,64,256]{2,1,0:T(8,128)(2,1)S(1)}, bf16[65,64,256]{2,1,0:T(8,128)(2,1)S(1)}, u32[]{:S(2)}, u32[]{:S(2)}) collective-permute-start(bf16[65,64,256]{2,1,0:T(8,128)(2,1)S(1)} %get-tuple-element.26.own), channel_id=1, source_target_pairs={{8,0},{16,8},{24,16},{32,24},{40,32},{48,40},{56,48},{64,56},{72,6... | collective-permute-start | bytes 6389768 | tf_op jit(solution)/shard_map/ppermute | solution.py:549
  16.5 0.6 slots.1
  17.2 3.1 %collective-permute-done.2 = bf16[8,2,128,128]{3,2,1,0:T(8,128)(2,1)S(1)} collective-permute-done((bf16[8,2,128,128]{3,2,1,0:T(8,128)(2,1)S(1)}, bf16[8,2,128,128]{3,2,1,0:T(8,128)(2,1)S(1)}, u32[]{:S(2)}, u32[]{:S(2)}) %collective-permute-start.2) | collective-permute-done | bytes 524320 | tf_op jit(solution)/shard_map/ppermute | solution.py:586
  20.3 5.0 %blend.1._ = f32[8,16,272,128]{3,2,1,0:T(8,128)S(1)} custom-call(s32[8,128]{1,0:T(8,128)S(1)} %get-tuple-element.23.target_ref, f32[8,128]{1,0:T(8,128)S(1)} %get-tuple-element.24.share_ref, bf16[8,16,128,128]{3,2,1,0:T(8,128)(2,1)S(1)} %get-tuple-element.32.source), custom_call_target="tpu_custom_call" | custom-call | flops 20000000000 | bytes 4194304 | tf_op jit(solution)/shard_map/blend/pallas_call | solution.py:339
  25.3 0.0 copy-start
  25.3 0.0 copy-start.1
  25.3 0.0 copy-start.2
  25.3 9.9 %collective-permute-done.3.strip = bf16[8,2,128,128]{3,2,1,0:T(8,128)(2,1)S(1)} collective-permute-done((bf16[8,2,128,128]{3,2,1,0:T(8,128)(2,1)S(1)}, bf16[8,2,128,128]{3,2,1,0:T(8,128)(2,1)S(1)}, u32[]{:S(2)}, u32[]{:S(2)}) %collective-permute-start.3) | collective-permute-done | bytes 524320 | tf_op jit(solution)/shard_map/ppermute | solution.py:586
  35.2 1.6 %beyond.1.refs_5_.padded = f32[8,16,272,128]{3,2,1,0:T(8,128)S(1)} custom-call(s32[2]{0:T(128)S(1)} %pad_add_fusion.tile_ref, s32[8,128]{1,0:T(8,128)S(1)} %get-tuple-element.23.target_ref, f32[8,128]{1,0:T(8,128)S(1)} %get-tuple-element.24.share_ref, bf16[8,2,128,128]{3,2,1,0:T(8,128)(2,1)S(1)} %collective-permute-done.3.strip, ...), custom_call_target="tpu_custom_call", output_to_operand_aliasing={{}: (4, {})} | custom-call | tf_op jit(solution)/shard_map/beyond/pallas_call | solution.py:401
  36.8 0.0 copy-start.6
  36.8 0.0 collective-permute-done.1.other
  36.9 3.7 %flow.2 = f32[2,4,16]{2,1,0:T(4,128)S(1)} custom-call(bf16[65,64,256]{2,1,0:T(8,128)(2,1)S(1)} %get-tuple-element.28.own, bf16[65,64,256]{2,1,0:T(8,128)(2,1)S(1)} %collective-permute-done.1.other, bf16[256,256]{1,0:T(8,128)(2,1)S(1)} %copy-done, bf16[256,256]{1,0:T(8,128)(2,1)S(1)} %copy-done.1, bf16[128,128]{1,0:T(8,128)(2,1)S(1)} %copy-done.2), custom_call_target="tpu_custom_call" | custom-call | tf_op jit(solution)/shard_map/flow/pallas_call | solution.py:254
  40.6 1.9 %collective-permute-start.4 = (f32[2,4,16]{2,1,0:T(4,128)S(1)}, f32[2,4,16]{2,1,0:T(4,128)S(1)}, u32[]{:S(2)}, u32[]{:S(2)}) collective-permute-start(f32[2,4,16]{2,1,0:T(4,128)S(1)} %flow.2), channel_id=1, source_target_pairs={{8,0},{16,8},{24,16},{32,24},{40,32},{48,40},{56,48},{64,56},{72,6... | collective-permute-start | bytes 1544 | tf_op jit(solution)/shard_map/ppermute | solution.py:549
  42.5 0.1 collective-permute-start.7
  42.6 0.0 collective-permute-done.other
  42.6 1.2 %collective-permute-done.4.refs_1_ = f32[2,4,16]{2,1,0:T(4,128)S(1)} collective-permute-done((f32[2,4,16]{2,1,0:T(4,128)S(1)}, f32[2,4,16]{2,1,0:T(4,128)S(1)}, u32[]{:S(2)}, u32[]{:S(2)}) %collective-permute-start.4) | collective-permute-done | bytes 544 | tf_op jit(solution)/shard_map/ppermute | solution.py:549
  43.8 3.7 %flow.3.refs_0_ = f32[2,4,16]{2,1,0:T(4,128)S(1)} custom-call(bf16[65,64,256]{2,1,0:T(8,128)(2,1)S(1)} %get-tuple-element.26.own, bf16[65,64,256]{2,1,0:T(8,128)(2,1)S(1)} %collective-permute-done.other, bf16[256,256]{1,0:T(8,128)(2,1)S(1)} %copy-done, bf16[256,256]{1,0:T(8,128)(2,1)S(1)} %copy-done.1, bf16[128,128]{1,0:T(8,128)(2,1)S(1)} %copy-done.2), custom_call_target="tpu_custom_call" | custom-call | flops 49999998976 | tf_op jit(solution)/shard_map/flow/pallas_call | solution.py:254
  47.5 2.4 %collective-permute-start.5 = (f32[3,8,16]{2,1,0:T(8,128)S(1)}, f32[3,8,16]{2,1,0:T(8,128)S(1)}, u32[]{:S(2)}, u32[]{:S(2)}) collective-permute-start(f32[3,8,16]{2,1,0:T(8,128)S(1)} %pad_maximum_fusion), channel_id=1, source_target_pairs={{0,1},{1,0},{2,3},{3,2},{4,5},{5,4},{6,7},{7,6},{8,9},{9,8},{10,11... | collective-permute-start | bytes 4616 | tf_op jit(solution)/shard_map/ppermute | solution.py:553
  49.9 5.4 %collective-permute-start.6 = (f32[3,8,16]{2,1,0:T(8,128)S(1)}, f32[3,8,16]{2,1,0:T(8,128)S(1)}, u32[]{:S(2)}, u32[]{:S(2)}) collective-permute-start(f32[3,8,16]{2,1,0:T(8,128)S(1)} %pad_maximum_fusion), channel_id=1, source_target_pairs={{1,2},{3,4},{5,6},{2,1},{4,3},{6,5},{9,10},{11,12},{13,14},{10,9},... | collective-permute-start | bytes 4616 | tf_op jit(solution)/shard_map/ppermute | solution.py:576
  55.3 3.5 %collective-permute-done.5.refs_3_ = f32[3,8,16]{2,1,0:T(8,128)S(1)} collective-permute-done((f32[3,8,16]{2,1,0:T(8,128)S(1)}, f32[3,8,16]{2,1,0:T(8,128)S(1)}, u32[]{:S(2)}, u32[]{:S(2)}) %collective-permute-start.5) | collective-permute-done | bytes 1568 | tf_op jit(solution)/shard_map/ppermute | solution.py:553
  58.8 2.4 %collective-permute-done.6.refs_4_ = f32[3,8,16]{2,1,0:T(8,128)S(1)} collective-permute-done((f32[3,8,16]{2,1,0:T(8,128)S(1)}, f32[3,8,16]{2,1,0:T(8,128)S(1)}, u32[]{:S(2)}, u32[]{:S(2)}) %collective-permute-start.6) | collective-permute-done | bytes 1568 | tf_op jit(solution)/shard_map/ppermute | solution.py:576
  61.2 5.9 %warp.1 = (bf16[1,8,16,128,128]{4,3,2,1,0:T(8,128)(2,1)}, f32[1,2,8,16]{3,2,1,0:T(8,128)}, f32[2,8,128]{2,1,0:T(8,128)S(1)}) custom-call(s32[2]{0:T(128)S(1)} %pad_add_fusion.tile_ref, f32[2,4,16]{2,1,0:T(4,128)S(1)} %flow.3.refs_0_, f32[2,4,16]{2,1,0:T(4,128)S(1)} %collective-permute-done.4.refs_1_, s32[1,8,16]{2,1,0:T(8,128)S(1)} %copy-done.6, ...), custom_call_target="tpu_custom_call" | custom-call | flops 20000000 | bytes 12582912 | tf_op jit(solution)/shard_map/warp/pallas_call | solution.py:459
  67.2 3.5 %pair.1 = bf16[1,8,16,128,128]{4,3,2,1,0:T(8,128)(2,1)} custom-call(s32[2]{0:T(128)S(1)} %pad_add_fusion.tile_ref, s32[8,128]{1,0:T(8,128)S(1)} %get-tuple-element.23.target_ref, f32[8,128]{1,0:T(8,128)S(1)} %get-tuple-element.24.share_ref, f32[2,8,128]{2,1,0:T(8,128)S(1)} %get-tuple-element.38.wide, ...), custom_call_target="tpu_custom_call", output_to_operand_aliasing={{}: (6, {})} | custom-call | flops 5000000 | bytes 4194304 | tf_op jit(solution)/shard_map/pair/pallas_call | solution.py:526
  (12 shorter events, 0.1 us)
Async XLA Ops:
  5.3 14.9 %collective-permute-start.2 = (bf16[8,2,128,128]{3,2,1,0:T(8,128)(2,1)S(1)}, bf16[8,2,128,128]{3,2,1,0:T(8,128)(2,1)S(1)}, u32[]{:S(2)}, u32[]{:S(2)}) collective-permute-start(bf16[8,2,128,128]{3,2,1,0:T(8,128)(2,1)S(1)} %get-tuple-element.29), channel_id=1, source_target_pairs={{0,64},{1,65},{2,66},{3,67},{4,68},{5,69},{6,70},{7,71},{8,72},{9,... | collective-permute-start | bytes 1572872 | tf_op jit(solution)/shard_map/ppermute | solution.py:586
  6.2 30.6 %collective-permute-start.1 = (bf16[65,64,256]{2,1,0:T(8,128)(2,1)S(1)}, bf16[65,64,256]{2,1,0:T(8,128)(2,1)S(1)}, u32[]{:S(2)}, u32[]{:S(2)}) collective-permute-start(bf16[65,64,256]{2,1,0:T(8,128)(2,1)S(1)} %get-tuple-element.28.own), channel_id=1, source_target_pairs={{0,8},{8,16},{16,24},{24,32},{32,40},{40,48},{48,56},{56,64},{64,7... | collective-permute-start | bytes 6389768 | tf_op jit(solution)/shard_map/ppermute | solution.py:549
  8.2 8.4 %copy-start.3 = (s32[1,8,16,4]{2,3,1,0:T(4,128)S(1)}, s32[1,8,16,4]{2,3,1,0:T(4,128)}, u32[]{:S(2)}) copy-start(s32[1,8,16,4]{2,3,1,0:T(4,128)} %param.12) | copy-start | bytes 6148
  8.2 8.4 %copy-start.4 = (s32[1,8,16,4]{2,3,1,0:T(4,128)S(1)}, s32[1,8,16,4]{2,3,1,0:T(4,128)}, u32[]{:S(2)}) copy-start(s32[1,8,16,4]{2,3,1,0:T(4,128)} %param.13) | copy-start | bytes 6148
  8.2 8.3 %copy-start.5 = (f32[1,8,16,4]{2,3,1,0:T(4,128)S(1)}, f32[1,8,16,4]{2,3,1,0:T(4,128)}, u32[]{:S(2)}) copy-start(f32[1,8,16,4]{2,3,1,0:T(4,128)} %param.15) | copy-start | bytes 6148
  8.2 8.3 %copy-start.7 = (s32[1,8,16]{2,1,0:T(8,128)S(1)}, s32[1,8,16]{2,1,0:T(8,128)}, u32[]{:S(2)}) copy-start(s32[1,8,16]{2,1,0:T(8,128)} %count_ref.1) | copy-start | bytes 1540
  12.9 29.8 %collective-permute-start = (bf16[65,64,256]{2,1,0:T(8,128)(2,1)S(1)}, bf16[65,64,256]{2,1,0:T(8,128)(2,1)S(1)}, u32[]{:S(2)}, u32[]{:S(2)}) collective-permute-start(bf16[65,64,256]{2,1,0:T(8,128)(2,1)S(1)} %get-tuple-element.26.own), channel_id=1, source_target_pairs={{8,0},{16,8},{24,16},{32,24},{40,32},{48,40},{56,48},{64,56},{72,6... | collective-permute-start | bytes 6389768 | tf_op jit(solution)/shard_map/ppermute | solution.py:549
  20.3 14.9 %collective-permute-start.3 = (bf16[8,2,128,128]{3,2,1,0:T(8,128)(2,1)S(1)}, bf16[8,2,128,128]{3,2,1,0:T(8,128)(2,1)S(1)}, u32[]{:S(2)}, u32[]{:S(2)}) collective-permute-start(bf16[8,2,128,128]{3,2,1,0:T(8,128)(2,1)S(1)} %collective-permute-done.2), channel_id=1, source_target_pairs={{64,7},{65,2},{66,1},{67,4},{68,3},{69,6},{70,5},{71,0},{72,15},{7... | collective-permute-start | bytes 1572872 | tf_op jit(solution)/shard_map/ppermute | solution.py:586
  25.3 11.5 %copy-start = (bf16[256,256]{1,0:T(8,128)(2,1)S(1)}, bf16[256,256]{1,0:T(8,128)(2,1)}, u32[]{:S(2)}) copy-start(bf16[256,256]{1,0:T(8,128)(2,1)} %constant.28.cols_hbm.cols_ref) | copy-start | bytes 393220
  25.3 11.5 %copy-start.1 = (bf16[256,256]{1,0:T(8,128)(2,1)S(1)}, bf16[256,256]{1,0:T(8,128)(2,1)}, u32[]{:S(2)}) copy-start(bf16[256,256]{1,0:T(8,128)(2,1)} %constant.29.back_cols_ref) | copy-start | bytes 393220
  25.3 11.5 %copy-start.2 = (bf16[128,128]{1,0:T(8,128)(2,1)S(1)}, bf16[128,128]{1,0:T(8,128)(2,1)}, u32[]{:S(2)}) copy-start(bf16[128,128]{1,0:T(8,128)(2,1)} %constant.30.back_rows_ref) | copy-start | bytes 98308
  36.8 5.7 %copy-start.6 = (s32[1,8,16]{2,1,0:T(8,128)S(1)}, s32[1,8,16]{2,1,0:T(8,128)}, u32[]{:S(2)}) copy-start(s32[1,8,16]{2,1,0:T(8,128)} %refs_2_.1) | copy-start | bytes 1540
  40.6 3.2 %collective-permute-start.4 = (f32[2,4,16]{2,1,0:T(4,128)S(1)}, f32[2,4,16]{2,1,0:T(4,128)S(1)}, u32[]{:S(2)}, u32[]{:S(2)}) collective-permute-start(f32[2,4,16]{2,1,0:T(4,128)S(1)} %flow.2), channel_id=1, source_target_pairs={{8,0},{16,8},{24,16},{32,24},{40,32},{48,40},{56,48},{64,56},{72,6... | collective-permute-start | bytes 1544 | tf_op jit(solution)/shard_map/ppermute | solution.py:549
  42.5 24.7 %collective-permute-start.7 = (bf16[8,2,128,128]{3,2,1,0:T(8,128)(2,1)S(1)}, bf16[8,2,128,128]{3,2,1,0:T(8,128)(2,1)S(1)}, u32[]{:S(2)}, u32[]{:S(2)}) collective-permute-start(bf16[8,2,128,128]{3,2,1,0:T(8,128)(2,1)S(1)} %get-tuple-element.39), channel_id=1, source_target_pairs={{0,1},{1,0},{2,3},{3,2},{4,5},{5,4},{6,7},{7,6},{8,9},{9,8},{10,11... | collective-permute-start | bytes 1572872 | tf_op jit(solution)/shard_map/ppermute | solution.py:553
  47.5 11.3 %collective-permute-start.5 = (f32[3,8,16]{2,1,0:T(8,128)S(1)}, f32[3,8,16]{2,1,0:T(8,128)S(1)}, u32[]{:S(2)}, u32[]{:S(2)}) collective-permute-start(f32[3,8,16]{2,1,0:T(8,128)S(1)} %pad_maximum_fusion), channel_id=1, source_target_pairs={{0,1},{1,0},{2,3},{3,2},{4,5},{5,4},{6,7},{7,6},{8,9},{9,8},{10,11... | collective-permute-start | bytes 4616 | tf_op jit(solution)/shard_map/ppermute | solution.py:553
  49.9 11.3 %collective-permute-start.6 = (f32[3,8,16]{2,1,0:T(8,128)S(1)}, f32[3,8,16]{2,1,0:T(8,128)S(1)}, u32[]{:S(2)}, u32[]{:S(2)}) collective-permute-start(f32[3,8,16]{2,1,0:T(8,128)S(1)} %pad_maximum_fusion), channel_id=1, source_target_pairs={{1,2},{3,4},{5,6},{2,1},{4,3},{6,5},{9,10},{11,12},{13,14},{10,9},... | collective-permute-start | bytes 4616 | tf_op jit(solution)/shard_map/ppermute | solution.py:576

commit v10 on v8

--- a/solution.py
+++ b/solution.py
@@ -552,17 +552,18 @@
     from_next = from_behind(spectra_low, "sec", -1)
     first = hop(first, on_hops[0])
     target, share = slots_of(tile, box_row, box_shift, box_count, blend_weight)
-    off, first, source = lax.optimization_barrier((off, first, source))
+    off, source = lax.optimization_barrier((off, source))
     off = hop(off, off_hops[1])
+    blended = blend(target, share, source)
+    first, blended = lax.optimization_barrier((first, blended))
     first = hop(first, on_hops[1])
-    blended = blend(target, share, source)
     from_last, blended = lax.optimization_barrier((from_last, blended))
 
     flow_high = flow_of(spectra_high, from_last, -1, half, nx, cols, back_cols, back_rows)
-    second, off, flow_high = lax.optimization_barrier((second, off, flow_high))
+    second, flow_high = lax.optimization_barrier((second, flow_high))
     flow_high = from_behind(flow_high, "sec", -1)
     second = swapped(second)
-    from_next, flow_high, first = lax.optimization_barrier((from_next, flow_high, first))
+    from_next, flow_high, off, first = lax.optimization_barrier((from_next, flow_high, off, first))
     flow_low = flow_of(spectra_low, from_next, 1, half, nx, cols, back_cols, back_rows)
     flow = jnp.concatenate([flow_low, flow_high], axis=1)
     flow = jnp.concatenate([flow, node_mask.astype(jnp.float32) + 1.0], axis=0)

time: 76.8 us -> 71.8 us (0.935)
  waiting for transfers between devices: 29.2 us -> 19.5 us
  starting transfers between devices: 15.6 us -> 20.3 us
    ppermute x4, waiting for transfers between devices: 25.5 us -> 16.4 us  [per_device(): hop = lambda x, pairs: lax.ppermute(x, ('sec', 'tile'), pairs)]
    ppermute x1, starting transfers between devices: 1.92 us -> 4.33 us  [beyond(): return lax.ppermute(x, 'tile', pairs + [(j, i) for i, j in pairs])]
    ppermute x2, starting transfers between devices: 1.22 us -> 3.4 us  [swapped(): lax.ppermute(x, 'tile', [(i, i ^ 1) for i in range(lax.axis_size('tile'))])]
    ppermute x3, waiting for transfers between devices: 0.01 us -> 1.85 us  [from_behind(): return lax.ppermute(x, axis, pairs)]
    ppermute x1, waiting for transfers between devices: 2.81 us -> 1.28 us  [beyond(): return lax.ppermute(x, 'tile', pairs + [(j, i) for i, j in pairs])]
    ppermute x2, waiting for transfers between devices: 0.9 us -> 0.01 us  [swapped(): lax.ppermute(x, 'tile', [(i, i ^ 1) for i in range(lax.axis_size('tile'))])]
  transfers between devices with their start and end apart: 10 -> 10, of which waited for: 5 -> 4; matrix products, arithmetic and copies ran while one was open for 0% -> 0% of each run, Pallas kernels for 26% -> 28%
where the time goes in v10:
time: 71.8 us; the launch traced here: 71.6 us
  Pallas kernels  30.8 us (43%)
  starting transfers between devices  20.3 us (28%)
  waiting for transfers between devices  19.5 us (27%)
  between operations  0.8 us (1%)
    ppermute x4, waiting for transfers between devices, per_device(): hop = lambda x, pairs: lax.ppermute(x, ('sec', 'tile'), pairs)  16.4 us
    pallas_call x2, Pallas kernels, forward(): pl.pallas_call(functools.partial(forward_kernel, start, toward_pair), gri...  9.27 us
    pallas_call x2, Pallas kernels, flow_of(): pl.pallas_call(functools.partial(flow_kernel, sign), grid=(ny,), in_specs...  7.4 us
    ppermute x3, starting transfers between devices, from_behind(): return lax.ppermute(x, axis, pairs)  6.86 us
    pallas_call x1, Pallas kernels, warp(): pl.pallas_call(warp_kernel, grid=(ny,), in_specs=[pl.BlockSpec(memory_spa...  6.19 us
    ppermute x4, starting transfers between devices, per_device(): hop = lambda x, pairs: lax.ppermute(x, ('sec', 'tile'), pairs)  5.68 us
    pallas_call x1, Pallas kernels, blend(): pl.pallas_call(blend_kernel, grid=(ny,), in_specs=[pl.BlockSpec(memory_sp...  4.98 us
    ppermute x1, starting transfers between devices, beyond(): return lax.ppermute(x, 'tile', pairs + [(j, i) for i, j in pairs])  4.33 us
  transfers between devices with their start and end apart: 10, of which 4 were waited for; matrix products, arithmetic and copies ran while one was open for 0% of the time, Pallas kernels for 28%

profile of v10, /device:TPU:22, one launch (start us, length us, event | category | flops | bytes accessed | tf_op | source)
XLA Modules:
  0.0 71.6 jit_solution(4997786496703602885)
XLA Ops:
  0.6 0.1 pad_add_fusion.tile_ref
  0.7 4.6 %forward.2 = (bf16[65,64,256]{2,1,0:T(8,128)(2,1)S(1)}, bf16[8,16,128,128]{3,2,1,0:T(8,128)(2,1)S(1)}, bf16[8,2,128,128]{3,2,1,0:T(8,128)(2,1)S(1)}) custom-call(s32[2]{0:T(128)S(1)} %pad_add_fusion.tile_ref, f32[1,8,16,128,128]{4,3,2,1,0:T(8,128)} %x_hbm.3, bf16[128,256]{1,0:T(8,128)(2,1)} %constant.27.rows_hbm, bf16[256,256]{1,0:T(8,128)(2,1)} %constant.28.cols_hbm.cols_ref), custom_call_target="tpu_custom_call" | custom-call | flops 2000000000 | bytes 6291456 | tf_op jit(solution)/shard_map/forward/pallas_call | solution.py:154
  5.3 1.9 %collective-permute-start.1 = (bf16[65,64,256]{2,1,0:T(8,128)(2,1)S(1)}, bf16[65,64,256]{2,1,0:T(8,128)(2,1)S(1)}, u32[]{:S(2)}, u32[]{:S(2)}) collective-permute-start(bf16[65,64,256]{2,1,0:T(8,128)(2,1)S(1)} %get-tuple-element.26.own), channel_id=1, source_target_pairs={{0,8},{8,16},{16,24},{24,32},{32,40},{40,48},{48,56},{56,64},{64,7... | collective-permute-start | bytes 6389768 | tf_op jit(solution)/shard_map/ppermute | solution.py:509
  7.3 0.9 %collective-permute-start.3 = (bf16[8,2,128,128]{3,2,1,0:T(8,128)(2,1)S(1)}, bf16[8,2,128,128]{3,2,1,0:T(8,128)(2,1)S(1)}, u32[]{:S(2)}, u32[]{:S(2)}) collective-permute-start(bf16[8,2,128,128]{3,2,1,0:T(8,128)(2,1)S(1)} %get-tuple-element.30), channel_id=1, source_target_pairs={{0,64},{1,65},{2,66},{3,67},{4,68},{5,69},{6,70},{7,71},{8,72},{9,... | collective-permute-start | bytes 1572872 | tf_op jit(solution)/shard_map/ppermute | solution.py:546
  8.2 4.6 %forward.3 = (bf16[65,64,256]{2,1,0:T(8,128)(2,1)S(1)}, bf16[8,16,128,128]{3,2,1,0:T(8,128)(2,1)S(1)}, bf16[8,1,128,128]{3,2,1,0:T(8,128)(2,1)S(1)}, bf16[8,1,128,128]{3,2,1,0:T(8,128)(2,1)S(1)}) custom-call(s32[2]{0:T(128)S(1)} %pad_add_fusion.tile_ref, f32[1,8,16,128,128]{4,3,2,1,0:T(8,128)} %x_hbm.3, ...), custom_call_target="tpu_custom_call", output_to_operand_aliasing={{1}: (4, {})} | custom-call | flops 2000000000 | bytes 6291456 | tf_op jit(solution)/shard_map/forward/pallas_call | solution.py:154
  12.8 3.0 %collective-permute-start = (bf16[65,64,256]{2,1,0:T(8,128)(2,1)S(1)}, bf16[65,64,256]{2,1,0:T(8,128)(2,1)S(1)}, u32[]{:S(2)}, u32[]{:S(2)}) collective-permute-start(bf16[65,64,256]{2,1,0:T(8,128)(2,1)S(1)} %get-tuple-element.24.own), channel_id=1, source_target_pairs={{8,0},{16,8},{24,16},{32,24},{40,32},{48,40},{56,48},{64,56},{72,6... | collective-permute-start | bytes 6389768 | tf_op jit(solution)/shard_map/ppermute | solution.py:509
  15.8 1.6 %collective-permute-start.2 = (bf16[8,1,128,128]{3,2,1,0:T(8,128)(2,1)S(1)}, bf16[8,1,128,128]{3,2,1,0:T(8,128)(2,1)S(1)}, u32[]{:S(2)}, u32[]{:S(2)}) collective-permute-start(bf16[8,1,128,128]{3,2,1,0:T(8,128)(2,1)S(1)} %get-tuple-element.27), channel_id=1, source_target_pairs={{0,64},{1,65},{2,66},{3,67},{4,68},{5,69},{6,70},{7,71},{8,72},{9,... | collective-permute-start | bytes 786440 | tf_op jit(solution)/shard_map/ppermute | solution.py:546
  17.5 0.0 copy-done.3
  17.5 0.6 slots.1
  18.1 4.9 %collective-permute-done.3 = bf16[8,2,128,128]{3,2,1,0:T(8,128)(2,1)S(1)} collective-permute-done((bf16[8,2,128,128]{3,2,1,0:T(8,128)(2,1)S(1)}, bf16[8,2,128,128]{3,2,1,0:T(8,128)(2,1)S(1)}, u32[]{:S(2)}, u32[]{:S(2)}) %collective-permute-start.3) | collective-permute-done | bytes 524320 | tf_op jit(solution)/shard_map/ppermute | solution.py:546
  23.0 3.1 %collective-permute-start.5 = (bf16[8,2,128,128]{3,2,1,0:T(8,128)(2,1)S(1)}, bf16[8,2,128,128]{3,2,1,0:T(8,128)(2,1)S(1)}, u32[]{:S(2)}, u32[]{:S(2)}) collective-permute-start(bf16[8,2,128,128]{3,2,1,0:T(8,128)(2,1)S(1)} %collective-permute-done.3), channel_id=1, source_target_pairs={{64,7},{65,2},{66,1},{67,4},{68,3},{69,6},{70,5},{71,0},{72,15},{7... | collective-permute-start | bytes 1572872 | tf_op jit(solution)/shard_map/ppermute | solution.py:546
  26.1 5.0 %blend.1.padded.refs_5_ = f32[8,16,272,128]{3,2,1,0:T(8,128)S(1)} custom-call(s32[8,128]{1,0:T(8,128)S(1)} %get-tuple-element.28.target_ref, f32[8,128]{1,0:T(8,128)S(1)} %get-tuple-element.29.share_ref, bf16[8,16,128,128]{3,2,1,0:T(8,128)(2,1)S(1)} %get-tuple-element.32.source), custom_call_target="tpu_custom_call" | custom-call | flops 16000000000 | bytes 4194304 | tf_op jit(solution)/shard_map/blend/pallas_call | solution.py:343
  31.1 0.0 copy-start.6
  31.1 0.0 collective-permute-done.2
  31.1 0.1 collective-permute-start.6
  31.2 1.8 %collective-permute-done.1.other = bf16[65,64,256]{2,1,0:T(8,128)(2,1)S(1)} collective-permute-done((bf16[65,64,256]{2,1,0:T(8,128)(2,1)S(1)}, bf16[65,64,256]{2,1,0:T(8,128)(2,1)S(1)}, u32[]{:S(2)}, u32[]{:S(2)}) %collective-permute-start.1) | collective-permute-done | bytes 2129952 | tf_op jit(solution)/shard_map/ppermute | solution.py:509
  33.0 0.0 copy-done.2
  33.1 3.7 %flow.2 = f32[2,4,16]{2,1,0:T(4,128)S(1)} custom-call(bf16[65,64,256]{2,1,0:T(8,128)(2,1)S(1)} %get-tuple-element.26.own, bf16[65,64,256]{2,1,0:T(8,128)(2,1)S(1)} %collective-permute-done.1.other, bf16[256,256]{1,0:T(8,128)(2,1)S(1)} %copy-done, bf16[256,256]{1,0:T(8,128)(2,1)S(1)} %copy-done.1, bf16[128,128]{1,0:T(8,128)(2,1)S(1)} %copy-done.2), custom_call_target="tpu_custom_call" | custom-call | tf_op jit(solution)/shard_map/flow/pallas_call | solution.py:258
  36.8 1.9 %collective-permute-start.4 = (f32[2,4,16]{2,1,0:T(4,128)S(1)}, f32[2,4,16]{2,1,0:T(4,128)S(1)}, u32[]{:S(2)}, u32[]{:S(2)}) collective-permute-start(f32[2,4,16]{2,1,0:T(4,128)S(1)} %flow.2), channel_id=1, source_target_pairs={{8,0},{16,8},{24,16},{32,24},{40,32},{48,40},{56,48},{64,56},{72,6... | collective-permute-start | bytes 1544 | tf_op jit(solution)/shard_map/ppermute | solution.py:509
  38.7 3.3 %collective-permute-start.9 = (bf16[8,1,128,128]{3,2,1,0:T(8,128)(2,1)S(1)}, bf16[8,1,128,128]{3,2,1,0:T(8,128)(2,1)S(1)}, u32[]{:S(2)}, u32[]{:S(2)}) collective-permute-start(bf16[8,1,128,128]{3,2,1,0:T(8,128)(2,1)S(1)} %get-tuple-element.42), channel_id=1, source_target_pairs={{0,1},{1,0},{2,3},{3,2},{4,5},{5,4},{6,7},{7,6},{8,9},{9,8},{10,11... | collective-permute-start | bytes 786440 | tf_op jit(solution)/shard_map/ppermute | solution.py:513
  42.0 11.5 %collective-permute-done.6.first_ref = bf16[8,1,128,128]{3,2,1,0:T(8,128)(2,1)S(1)} collective-permute-done((bf16[8,1,128,128]{3,2,1,0:T(8,128)(2,1)S(1)}, bf16[8,1,128,128]{3,2,1,0:T(8,128)(2,1)S(1)}, u32[]{:S(2)}, u32[]{:S(2)}) %collective-permute-start.6) | collective-permute-done | bytes 262176 | tf_op jit(solution)/shard_map/ppermute | solution.py:546
  53.5 0.0 collective-permute-done.5.off_ref
  53.5 0.0 collective-permute-done.other
  53.5 0.0 collective-permute-done.4.refs_1_
  53.6 3.7 %flow.3.refs_0_ = f32[2,4,16]{2,1,0:T(4,128)S(1)} custom-call(bf16[65,64,256]{2,1,0:T(8,128)(2,1)S(1)} %get-tuple-element.24.own, bf16[65,64,256]{2,1,0:T(8,128)(2,1)S(1)} %collective-permute-done.other, bf16[256,256]{1,0:T(8,128)(2,1)S(1)} %copy-done, bf16[256,256]{1,0:T(8,128)(2,1)S(1)} %copy-done.1, bf16[128,128]{1,0:T(8,128)(2,1)S(1)} %copy-done.2), custom_call_target="tpu_custom_call" | custom-call | flops 49999998976 | tf_op jit(solution)/shard_map/flow/pallas_call | solution.py:258
  57.3 0.1 collective-permute-start.7
  57.4 4.3 %collective-permute-start.8 = (f32[3,8,16]{2,1,0:T(8,128)S(1)}, f32[3,8,16]{2,1,0:T(8,128)S(1)}, u32[]{:S(2)}, u32[]{:S(2)}) collective-permute-start(f32[3,8,16]{2,1,0:T(8,128)S(1)} %pad_maximum_fusion), channel_id=1, source_target_pairs={{1,2},{3,4},{5,6},{2,1},{4,3},{6,5},{9,10},{11,12},{13,14},{10,9},... | collective-permute-start | bytes 4616 | tf_op jit(solution)/shard_map/ppermute | solution.py:536
  61.7 0.0 collective-permute-done.9.second_ref
  61.7 2.3 %edges.1.refs_6_ = f32[8,4,272,128]{3,2,1,0:T(8,128)S(1)} custom-call(s32[2]{0:T(128)S(1)} %pad_add_fusion.tile_ref, s32[8,128]{1,0:T(8,128)S(1)} %get-tuple-element.28.target_ref, f32[8,128]{1,0:T(8,128)S(1)} %get-tuple-element.29.share_ref, bf16[8,1,128,128]{3,2,1,0:T(8,128)(2,1)S(1)} %collective-permute-done.6.first_ref, ...), custom_call_target="tpu_custom_call" | custom-call | flops 5000000 | bytes 4194304 | tf_op jit(solution)/shard_map/edges/pallas_call | solution.py:427
  64.1 0.0 collective-permute-done.7.refs_3_
  64.1 1.3 %collective-permute-done.8.refs_4_ = f32[3,8,16]{2,1,0:T(8,128)S(1)} collective-permute-done((f32[3,8,16]{2,1,0:T(8,128)S(1)}, f32[3,8,16]{2,1,0:T(8,128)S(1)}, u32[]{:S(2)}, u32[]{:S(2)}) %collective-permute-start.8) | collective-permute-done | bytes 1568 | tf_op jit(solution)/shard_map/ppermute | solution.py:536
  65.4 6.2 %warp.1 = (bf16[1,8,16,128,128]{4,3,2,1,0:T(8,128)(2,1)}, f32[1,2,8,16]{3,2,1,0:T(8,128)}) custom-call(s32[2]{0:T(128)S(1)} %pad_add_fusion.tile_ref, f32[2,4,16]{2,1,0:T(4,128)S(1)} %flow.3.refs_0_, f32[2,4,16]{2,1,0:T(4,128)S(1)} %collective-permute-done.4.refs_1_, s32[1,8,16]{2,1,0:T(8,128)S(1)} %copy-done.6, ...), custom_call_target="tpu_custom_call" | custom-call | flops 20000000 | bytes 12582912 | tf_op jit(solution)/shard_map/warp/pallas_call | solution.py:482
  (15 shorter events, 0.1 us)
Async XLA Ops:
  5.3 27.7 %collective-permute-start.1 = (bf16[65,64,256]{2,1,0:T(8,128)(2,1)S(1)}, bf16[65,64,256]{2,1,0:T(8,128)(2,1)S(1)}, u32[]{:S(2)}, u32[]{:S(2)}) collective-permute-start(bf16[65,64,256]{2,1,0:T(8,128)(2,1)S(1)} %get-tuple-element.26.own), channel_id=1, source_target_pairs={{0,8},{8,16},{16,24},{24,32},{32,40},{40,48},{48,56},{56,64},{64,7... | collective-permute-start | bytes 6389768 | tf_op jit(solution)/shard_map/ppermute | solution.py:509
  7.3 15.7 %collective-permute-start.3 = (bf16[8,2,128,128]{3,2,1,0:T(8,128)(2,1)S(1)}, bf16[8,2,128,128]{3,2,1,0:T(8,128)(2,1)S(1)}, u32[]{:S(2)}, u32[]{:S(2)}) collective-permute-start(bf16[8,2,128,128]{3,2,1,0:T(8,128)(2,1)S(1)} %get-tuple-element.30), channel_id=1, source_target_pairs={{0,64},{1,65},{2,66},{3,67},{4,68},{5,69},{6,70},{7,71},{8,72},{9,... | collective-permute-start | bytes 1572872 | tf_op jit(solution)/shard_map/ppermute | solution.py:546
  8.2 9.3 %copy-start.3 = (s32[1,8,16,4]{2,3,1,0:T(4,128)S(1)}, s32[1,8,16,4]{2,3,1,0:T(4,128)}, u32[]{:S(2)}) copy-start(s32[1,8,16,4]{2,3,1,0:T(4,128)} %param.12) | copy-start | bytes 6148
  8.2 9.3 %copy-start.4 = (s32[1,8,16,4]{2,3,1,0:T(4,128)S(1)}, s32[1,8,16,4]{2,3,1,0:T(4,128)}, u32[]{:S(2)}) copy-start(s32[1,8,16,4]{2,3,1,0:T(4,128)} %param.13) | copy-start | bytes 6148
  8.2 9.3 %copy-start.5 = (f32[1,8,16,4]{2,3,1,0:T(4,128)S(1)}, f32[1,8,16,4]{2,3,1,0:T(4,128)}, u32[]{:S(2)}) copy-start(f32[1,8,16,4]{2,3,1,0:T(4,128)} %param.15) | copy-start | bytes 6148
  8.2 9.3 %copy-start.7 = (s32[1,8,16]{2,1,0:T(8,128)S(1)}, s32[1,8,16]{2,1,0:T(8,128)}, u32[]{:S(2)}) copy-start(s32[1,8,16]{2,1,0:T(8,128)} %count_ref.1) | copy-start | bytes 1540
  12.8 40.7 %collective-permute-start = (bf16[65,64,256]{2,1,0:T(8,128)(2,1)S(1)}, bf16[65,64,256]{2,1,0:T(8,128)(2,1)S(1)}, u32[]{:S(2)}, u32[]{:S(2)}) collective-permute-start(bf16[65,64,256]{2,1,0:T(8,128)(2,1)S(1)} %get-tuple-element.24.own), channel_id=1, source_target_pairs={{8,0},{16,8},{24,16},{32,24},{40,32},{48,40},{56,48},{64,56},{72,6... | collective-permute-start | bytes 6389768 | tf_op jit(solution)/shard_map/ppermute | solution.py:509
  15.8 15.3 %collective-permute-start.2 = (bf16[8,1,128,128]{3,2,1,0:T(8,128)(2,1)S(1)}, bf16[8,1,128,128]{3,2,1,0:T(8,128)(2,1)S(1)}, u32[]{:S(2)}, u32[]{:S(2)}) collective-permute-start(bf16[8,1,128,128]{3,2,1,0:T(8,128)(2,1)S(1)} %get-tuple-element.27), channel_id=1, source_target_pairs={{0,64},{1,65},{2,66},{3,67},{4,68},{5,69},{6,70},{7,71},{8,72},{9,... | collective-permute-start | bytes 786440 | tf_op jit(solution)/shard_map/ppermute | solution.py:546
  23.0 30.5 %collective-permute-start.5 = (bf16[8,2,128,128]{3,2,1,0:T(8,128)(2,1)S(1)}, bf16[8,2,128,128]{3,2,1,0:T(8,128)(2,1)S(1)}, u32[]{:S(2)}, u32[]{:S(2)}) collective-permute-start(bf16[8,2,128,128]{3,2,1,0:T(8,128)(2,1)S(1)} %collective-permute-done.3), channel_id=1, source_target_pairs={{64,7},{65,2},{66,1},{67,4},{68,3},{69,6},{70,5},{71,0},{72,15},{7... | collective-permute-start | bytes 1572872 | tf_op jit(solution)/shard_map/ppermute | solution.py:546
  26.1 6.9 %copy-start = (bf16[256,256]{1,0:T(8,128)(2,1)S(1)}, bf16[256,256]{1,0:T(8,128)(2,1)}, u32[]{:S(2)}) copy-start(bf16[256,256]{1,0:T(8,128)(2,1)} %constant.28.cols_hbm.cols_ref) | copy-start | bytes 393220
  26.1 6.9 %copy-start.1 = (bf16[256,256]{1,0:T(8,128)(2,1)S(1)}, bf16[256,256]{1,0:T(8,128)(2,1)}, u32[]{:S(2)}) copy-start(bf16[256,256]{1,0:T(8,128)(2,1)} %constant.29.back_cols_ref) | copy-start | bytes 393220
  26.1 6.9 %copy-start.2 = (bf16[128,128]{1,0:T(8,128)(2,1)S(1)}, bf16[128,128]{1,0:T(8,128)(2,1)}, u32[]{:S(2)}) copy-start(bf16[128,128]{1,0:T(8,128)(2,1)} %constant.30.back_rows_ref) | copy-start | bytes 98308
  31.1 7.6 %copy-start.6 = (s32[1,8,16]{2,1,0:T(8,128)S(1)}, s32[1,8,16]{2,1,0:T(8,128)}, u32[]{:S(2)}) copy-start(s32[1,8,16]{2,1,0:T(8,128)} %refs_2_.1) | copy-start | bytes 1540
  31.1 22.4 %collective-permute-start.6 = (bf16[8,1,128,128]{3,2,1,0:T(8,128)(2,1)S(1)}, bf16[8,1,128,128]{3,2,1,0:T(8,128)(2,1)S(1)}, u32[]{:S(2)}, u32[]{:S(2)}) collective-permute-start(bf16[8,1,128,128]{3,2,1,0:T(8,128)(2,1)S(1)} %collective-permute-done.2), channel_id=1, source_target_pairs={{64,1},{65,0},{66,3},{67,2},{68,5},{69,4},{70,7},{71,6},{72,9},{73... | collective-permute-start | bytes 786440 | tf_op jit(solution)/shard_map/ppermute | solution.py:546
  36.8 16.8 %collective-permute-start.4 = (f32[2,4,16]{2,1,0:T(4,128)S(1)}, f32[2,4,16]{2,1,0:T(4,128)S(1)}, u32[]{:S(2)}, u32[]{:S(2)}) collective-permute-start(f32[2,4,16]{2,1,0:T(4,128)S(1)} %flow.2), channel_id=1, source_target_pairs={{8,0},{16,8},{24,16},{32,24},{40,32},{48,40},{56,48},{64,56},{72,6... | collective-permute-start | bytes 1544 | tf_op jit(solution)/shard_map/ppermute | solution.py:509
  38.7 23.0 %collective-permute-start.9 = (bf16[8,1,128,128]{3,2,1,0:T(8,128)(2,1)S(1)}, bf16[8,1,128,128]{3,2,1,0:T(8,128)(2,1)S(1)}, u32[]{:S(2)}, u32[]{:S(2)}) collective-permute-start(bf16[8,1,128,128]{3,2,1,0:T(8,128)(2,1)S(1)} %get-tuple-element.42), channel_id=1, source_target_pairs={{0,1},{1,0},{2,3},{3,2},{4,5},{5,4},{6,7},{7,6},{8,9},{9,8},{10,11... | collective-permute-start | bytes 786440 | tf_op jit(solution)/shard_map/ppermute | solution.py:513
  57.3 6.8 %collective-permute-start.7 = (f32[3,8,16]{2,1,0:T(8,128)S(1)}, f32[3,8,16]{2,1,0:T(8,128)S(1)}, u32[]{:S(2)}, u32[]{:S(2)}) collective-permute-start(f32[3,8,16]{2,1,0:T(8,128)S(1)} %pad_maximum_fusion), channel_id=1, source_target_pairs={{0,1},{1,0},{2,3},{3,2},{4,5},{5,4},{6,7},{7,6},{8,9},{9,8},{10,11... | collective-permute-start | bytes 4616 | tf_op jit(solution)/shard_map/ppermute | solution.py:513
  57.4 8.0 %collective-permute-start.8 = (f32[3,8,16]{2,1,0:T(8,128)S(1)}, f32[3,8,16]{2,1,0:T(8,128)S(1)}, u32[]{:S(2)}, u32[]{:S(2)}) collective-permute-start(f32[3,8,16]{2,1,0:T(8,128)S(1)} %pad_maximum_fusion), channel_id=1, source_target_pairs={{1,2},{3,4},{5,6},{2,1},{4,3},{6,5},{9,10},{11,12},{13,14},{10,9},... | collective-permute-start | bytes 4616 | tf_op jit(solution)/shard_map/ppermute | solution.py:536

commit v11 on v10

--- a/solution.py
+++ b/solution.py
@@ -273,7 +273,7 @@
             pltpu.VMEM((ny, nx, N), jnp.float32),
         ],
         compiler_params=pltpu.CompilerParams(vmem_limit_bytes=8 * MIB),
-        cost_estimate=pl.CostEstimate(flops=0 if sign < 0 else 50_000_000_000, bytes_accessed=0, transcendentals=0),
+        cost_estimate=pl.CostEstimate(flops=0 if sign < 0 else 0, bytes_accessed=0, transcendentals=0),
         name="flow",
     )(in_vmem(own), in_vmem(other), *(t.astype(jnp.bfloat16) for t in (cols, back_cols, back_rows)))
 
@@ -520,10 +520,12 @@
         way = 1 if rest < sections // 4 else -1
         for tile in range(tiles):
             z, x_high = divmod(tile, 2)
+            if far and not 0 <= z + 2 * x_high - 1 < tiles // 2:
+                continue
             ends = [section * tiles + tile]
             for hop in (1, 2):
                 x = (2 * x_high + x_low + hop * way) % 4
-                to_z = (z + 2 * x_high - 1) % (tiles // 2) if far and hop == 2 else z
+                to_z = z + 2 * x_high - 1 if far and hop == 2 else z
                 ends.append((x % 2 * (sections // 2) + rest) * tiles + 2 * to_z + x // 2)
             pairs[0].append((ends[0], ends[1]))
             pairs[1].append((ends[1], ends[2]))
@@ -563,7 +565,7 @@
     second, flow_high = lax.optimization_barrier((second, flow_high))
     flow_high = from_behind(flow_high, "sec", -1)
     second = swapped(second)
-    from_next, flow_high, off, first = lax.optimization_barrier((from_next, flow_high, off, first))
+    from_next, flow_high, off = lax.optimization_barrier((from_next, flow_high, off))
     flow_low = flow_of(spectra_low, from_next, 1, half, nx, cols, back_cols, back_rows)
     flow = jnp.concatenate([flow_low, flow_high], axis=1)
     flow = jnp.concatenate([flow, node_mask.astype(jnp.float32) + 1.0], axis=0)

time: 71.8 us -> 65.4 us (0.911)
  the two profiles are of different devices: /device:TPU:22 before, /device:TPU:66 now
where the time goes in v11:
time: 65.4 us; the launch traced here: 64.3 us
  Pallas kernels  30.8 us (47%)
  starting transfers between devices  24.2 us (37%)
  waiting for transfers between devices  8.25 us (13%)
  between operations  0.87 us (1%)
    ppermute x3, starting transfers between devices, from_behind(): return lax.ppermute(x, axis, pairs)  9.69 us
    pallas_call x2, Pallas kernels, forward(): pl.pallas_call(functools.partial(forward_kernel, start, toward_pair), gri...  9.27 us
    ppermute x4, starting transfers between devices, per_device(): hop = lambda x, pairs: lax.ppermute(x, ('sec', 'tile'), pairs)  7.63 us
    pallas_call x2, Pallas kernels, flow_of(): pl.pallas_call(functools.partial(flow_kernel, sign), grid=(ny,), in_specs...  7.39 us
    pallas_call x1, Pallas kernels, warp(): pl.pallas_call(warp_kernel, grid=(ny,), in_specs=[pl.BlockSpec(memory_spa...  6.19 us
    pallas_call x1, Pallas kernels, blend(): pl.pallas_call(blend_kernel, grid=(ny,), in_specs=[pl.BlockSpec(memory_sp...  5 us
    ppermute x2, starting transfers between devices, swapped(): lax.ppermute(x, 'tile', [(i, i ^ 1) for i in range(lax.axis_size('tile'))])  3.88 us
    ppermute x3, waiting for transfers between devices, from_behind(): return lax.ppermute(x, axis, pairs)  3.18 us
  transfers between devices with their start and end apart: 10, of which 5 were waited for; matrix products, arithmetic and copies ran while one was open for 0% of the time, Pallas kernels for 31%

profile of v11, /device:TPU:66, one launch (start us, length us, event | category | flops | bytes accessed | tf_op | source)
XLA Modules:
  0.0 64.3 jit_solution(2788963238731453171)
XLA Ops:
  0.6 0.1 pad_add_fusion.tile_ref
  0.7 4.6 %forward.2 = (bf16[65,64,256]{2,1,0:T(8,128)(2,1)S(1)}, bf16[8,16,128,128]{3,2,1,0:T(8,128)(2,1)S(1)}, bf16[8,2,128,128]{3,2,1,0:T(8,128)(2,1)S(1)}) custom-call(s32[2]{0:T(128)S(1)} %pad_add_fusion.tile_ref, f32[1,8,16,128,128]{4,3,2,1,0:T(8,128)} %x_hbm.3, bf16[128,256]{1,0:T(8,128)(2,1)} %constant.27.rows_hbm, bf16[256,256]{1,0:T(8,128)(2,1)} %constant.28.cols_hbm.cols_ref), custom_call_target="tpu_custom_call" | custom-call | flops 2000000000 | bytes 6291456 | tf_op jit(solution)/shard_map/forward/pallas_call | solution.py:154
  5.3 1.9 %collective-permute-start.1 = (bf16[65,64,256]{2,1,0:T(8,128)(2,1)S(1)}, bf16[65,64,256]{2,1,0:T(8,128)(2,1)S(1)}, u32[]{:S(2)}, u32[]{:S(2)}) collective-permute-start(bf16[65,64,256]{2,1,0:T(8,128)(2,1)S(1)} %get-tuple-element.25.own), channel_id=1, source_target_pairs={{0,8},{8,16},{16,24},{24,32},{32,40},{40,48},{48,56},{56,64},{64,7... | collective-permute-start | bytes 6389768 | tf_op jit(solution)/shard_map/ppermute | solution.py:509
  7.3 3.4 %collective-permute-start.3 = (bf16[8,2,128,128]{3,2,1,0:T(8,128)(2,1)S(1)}, bf16[8,2,128,128]{3,2,1,0:T(8,128)(2,1)S(1)}, u32[]{:S(2)}, u32[]{:S(2)}) collective-permute-start(bf16[8,2,128,128]{3,2,1,0:T(8,128)(2,1)S(1)} %get-tuple-element.29), channel_id=1, source_target_pairs={{1,65},{2,66},{3,67},{4,68},{5,69},{6,70},{9,73},{10,74},{11,75},{... | collective-permute-start | bytes 1572872 | tf_op jit(solution)/shard_map/ppermute | solution.py:548
  10.6 0.0 copy-start.3
  10.6 0.0 copy-start.4
  10.7 0.0 copy-start.5
  10.7 0.0 copy-start.7
  10.7 4.6 %forward.3 = (bf16[65,64,256]{2,1,0:T(8,128)(2,1)S(1)}, bf16[8,16,128,128]{3,2,1,0:T(8,128)(2,1)S(1)}, bf16[8,1,128,128]{3,2,1,0:T(8,128)(2,1)S(1)}, bf16[8,1,128,128]{3,2,1,0:T(8,128)(2,1)S(1)}) custom-call(s32[2]{0:T(128)S(1)} %pad_add_fusion.tile_ref, f32[1,8,16,128,128]{4,3,2,1,0:T(8,128)} %x_hbm.3, ...), custom_call_target="tpu_custom_call", output_to_operand_aliasing={{1}: (4, {})} | custom-call | flops 2000000000 | bytes 6291456 | tf_op jit(solution)/shard_map/forward/pallas_call | solution.py:154
  15.3 4.7 %collective-permute-start = (bf16[65,64,256]{2,1,0:T(8,128)(2,1)S(1)}, bf16[65,64,256]{2,1,0:T(8,128)(2,1)S(1)}, u32[]{:S(2)}, u32[]{:S(2)}) collective-permute-start(bf16[65,64,256]{2,1,0:T(8,128)(2,1)S(1)} %get-tuple-element.23.own), channel_id=1, source_target_pairs={{8,0},{16,8},{24,16},{32,24},{40,32},{48,40},{56,48},{64,56},{72,6... | collective-permute-start | bytes 6389768 | tf_op jit(solution)/shard_map/ppermute | solution.py:509
  20.1 0.1 collective-permute-start.2
  20.2 0.6 %slots.1 = (s32[8,128]{1,0:T(8,128)S(1)}, f32[8,128]{1,0:T(8,128)S(1)}) custom-call(s32[2]{0:T(128)S(1)} %pad_add_fusion.tile_ref, s32[1,8,4,16]{3,2,1,0:T(4,128)S(1)} %bitcast.4, s32[1,8,4,16]{3,2,1,0:T(4,128)S(1)} %bitcast.5, s32[1,8,16]{2,1,0:T(8,128)S(1)} %copy-done.7, f32[1,8,4,16]{3,2,1,0:T(4,128)S(1)} %bitcast.6), custom_call_target="tpu_custom_call" | custom-call | tf_op jit(solution)/shard_map/slots/pallas_call | solution.py:309
  20.9 2.4 %collective-permute-done.3 = bf16[8,2,128,128]{3,2,1,0:T(8,128)(2,1)S(1)} collective-permute-done((bf16[8,2,128,128]{3,2,1,0:T(8,128)(2,1)S(1)}, bf16[8,2,128,128]{3,2,1,0:T(8,128)(2,1)S(1)}, u32[]{:S(2)}, u32[]{:S(2)}) %collective-permute-start.3) | collective-permute-done | bytes 524320 | tf_op jit(solution)/shard_map/ppermute | solution.py:548
  23.3 2.8 %collective-permute-start.5 = (bf16[8,2,128,128]{3,2,1,0:T(8,128)(2,1)S(1)}, bf16[8,2,128,128]{3,2,1,0:T(8,128)(2,1)S(1)}, u32[]{:S(2)}, u32[]{:S(2)}) collective-permute-start(bf16[8,2,128,128]{3,2,1,0:T(8,128)(2,1)S(1)} %collective-permute-done.3), channel_id=1, source_target_pairs={{65,2},{66,1},{67,4},{68,3},{69,6},{70,5},{73,10},{74,9},{75,12},{... | collective-permute-start | bytes 1572872 | tf_op jit(solution)/shard_map/ppermute | solution.py:548
  26.1 0.0 copy-start
  26.1 0.0 copy-start.1
  26.2 0.0 copy-start.2
  26.2 5.0 %blend.1.padded.refs_5_ = f32[8,16,272,128]{3,2,1,0:T(8,128)S(1)} custom-call(s32[8,128]{1,0:T(8,128)S(1)} %get-tuple-element.27.target_ref, f32[8,128]{1,0:T(8,128)S(1)} %get-tuple-element.28.share_ref, bf16[8,16,128,128]{3,2,1,0:T(8,128)(2,1)S(1)} %get-tuple-element.31.source), custom_call_target="tpu_custom_call" | custom-call | flops 16000000000 | bytes 4194304 | tf_op jit(solution)/shard_map/blend/pallas_call | solution.py:343
  31.2 0.0 copy-start.6
  31.2 1.4 %collective-permute-start.8 = (bf16[8,1,128,128]{3,2,1,0:T(8,128)(2,1)S(1)}, bf16[8,1,128,128]{3,2,1,0:T(8,128)(2,1)S(1)}, u32[]{:S(2)}, u32[]{:S(2)}) collective-permute-start(bf16[8,1,128,128]{3,2,1,0:T(8,128)(2,1)S(1)} %collective-permute-done.2), channel_id=1, source_target_pairs={{64,1},{65,0},{66,3},{67,2},{68,5},{69,4},{70,7},{71,6},{72,9},{73... | collective-permute-start | bytes 786440 | tf_op jit(solution)/shard_map/ppermute | solution.py:548
  32.6 2.6 %collective-permute-done.1.other = bf16[65,64,256]{2,1,0:T(8,128)(2,1)S(1)} collective-permute-done((bf16[65,64,256]{2,1,0:T(8,128)(2,1)S(1)}, bf16[65,64,256]{2,1,0:T(8,128)(2,1)S(1)}, u32[]{:S(2)}, u32[]{:S(2)}) %collective-permute-start.1) | collective-permute-done | bytes 2129952 | tf_op jit(solution)/shard_map/ppermute | solution.py:509
  35.2 3.7 %flow.2 = f32[2,4,16]{2,1,0:T(4,128)S(1)} custom-call(bf16[65,64,256]{2,1,0:T(8,128)(2,1)S(1)} %get-tuple-element.25.own, bf16[65,64,256]{2,1,0:T(8,128)(2,1)S(1)} %collective-permute-done.1.other, bf16[256,256]{1,0:T(8,128)(2,1)S(1)} %copy-done, bf16[256,256]{1,0:T(8,128)(2,1)S(1)} %copy-done.1, bf16[128,128]{1,0:T(8,128)(2,1)S(1)} %copy-done.2), custom_call_target="tpu_custom_call" | custom-call | tf_op jit(solution)/shard_map/flow/pallas_call | solution.py:258
  38.9 3.0 %collective-permute-start.4 = (f32[2,4,16]{2,1,0:T(4,128)S(1)}, f32[2,4,16]{2,1,0:T(4,128)S(1)}, u32[]{:S(2)}, u32[]{:S(2)}) collective-permute-start(f32[2,4,16]{2,1,0:T(4,128)S(1)} %flow.2), channel_id=1, source_target_pairs={{8,0},{16,8},{24,16},{32,24},{40,32},{48,40},{56,48},{64,56},{72,6... | collective-permute-start | bytes 1544 | tf_op jit(solution)/shard_map/ppermute | solution.py:509
  41.9 1.8 %collective-permute-start.9 = (bf16[8,1,128,128]{3,2,1,0:T(8,128)(2,1)S(1)}, bf16[8,1,128,128]{3,2,1,0:T(8,128)(2,1)S(1)}, u32[]{:S(2)}, u32[]{:S(2)}) collective-permute-start(bf16[8,1,128,128]{3,2,1,0:T(8,128)(2,1)S(1)} %get-tuple-element.40), channel_id=1, source_target_pairs={{0,1},{1,0},{2,3},{3,2},{4,5},{5,4},{6,7},{7,6},{8,9},{9,8},{10,11... | collective-permute-start | bytes 786440 | tf_op jit(solution)/shard_map/ppermute | solution.py:513
  43.7 0.5 collective-permute-done.other
  44.2 0.1 collective-permute-done.4.refs_1_
  44.3 3.7 %flow.3.refs_0_ = f32[2,4,16]{2,1,0:T(4,128)S(1)} custom-call(bf16[65,64,256]{2,1,0:T(8,128)(2,1)S(1)} %get-tuple-element.23.own, bf16[65,64,256]{2,1,0:T(8,128)(2,1)S(1)} %collective-permute-done.other, bf16[256,256]{1,0:T(8,128)(2,1)S(1)} %copy-done, bf16[256,256]{1,0:T(8,128)(2,1)S(1)} %copy-done.1, bf16[128,128]{1,0:T(8,128)(2,1)S(1)} %copy-done.2), custom_call_target="tpu_custom_call" | custom-call | tf_op jit(solution)/shard_map/flow/pallas_call | solution.py:258
  48.0 2.1 %collective-permute-start.6 = (f32[3,8,16]{2,1,0:T(8,128)S(1)}, f32[3,8,16]{2,1,0:T(8,128)S(1)}, u32[]{:S(2)}, u32[]{:S(2)}) collective-permute-start(f32[3,8,16]{2,1,0:T(8,128)S(1)} %pad_maximum_fusion), channel_id=1, source_target_pairs={{0,1},{1,0},{2,3},{3,2},{4,5},{5,4},{6,7},{7,6},{8,9},{9,8},{10,11... | collective-permute-start | bytes 4616 | tf_op jit(solution)/shard_map/ppermute | solution.py:513
  50.1 3.0 %collective-permute-start.7 = (f32[3,8,16]{2,1,0:T(8,128)S(1)}, f32[3,8,16]{2,1,0:T(8,128)S(1)}, u32[]{:S(2)}, u32[]{:S(2)}) collective-permute-start(f32[3,8,16]{2,1,0:T(8,128)S(1)} %pad_maximum_fusion), channel_id=1, source_target_pairs={{1,2},{3,4},{5,6},{2,1},{4,3},{6,5},{9,10},{11,12},{13,14},{10,9},... | collective-permute-start | bytes 4616 | tf_op jit(solution)/shard_map/ppermute | solution.py:538
  53.1 2.3 %edges.1.refs_6_ = f32[8,4,272,128]{3,2,1,0:T(8,128)S(1)} custom-call(s32[2]{0:T(128)S(1)} %pad_add_fusion.tile_ref, s32[8,128]{1,0:T(8,128)S(1)} %get-tuple-element.27.target_ref, f32[8,128]{1,0:T(8,128)S(1)} %get-tuple-element.28.share_ref, bf16[8,1,128,128]{3,2,1,0:T(8,128)(2,1)S(1)} %collective-permute-done.8.first_ref, ...), custom_call_target="tpu_custom_call" | custom-call | flops 5000000 | bytes 4194304 | tf_op jit(solution)/shard_map/edges/pallas_call | solution.py:427
  55.5 2.6 %collective-permute-done.7.refs_4_ = f32[3,8,16]{2,1,0:T(8,128)S(1)} collective-permute-done((f32[3,8,16]{2,1,0:T(8,128)S(1)}, f32[3,8,16]{2,1,0:T(8,128)S(1)}, u32[]{:S(2)}, u32[]{:S(2)}) %collective-permute-start.7) | collective-permute-done | bytes 1568 | tf_op jit(solution)/shard_map/ppermute | solution.py:538
  58.1 6.2 %warp.1 = (bf16[1,8,16,128,128]{4,3,2,1,0:T(8,128)(2,1)}, f32[1,2,8,16]{3,2,1,0:T(8,128)}) custom-call(s32[2]{0:T(128)S(1)} %pad_add_fusion.tile_ref, f32[2,4,16]{2,1,0:T(4,128)S(1)} %flow.3.refs_0_, f32[2,4,16]{2,1,0:T(4,128)S(1)} %collective-permute-done.4.refs_1_, s32[1,8,16]{2,1,0:T(8,128)S(1)} %copy-done.6, ...), custom_call_target="tpu_custom_call" | custom-call | flops 20000000 | bytes 12582912 | tf_op jit(solution)/shard_map/warp/pallas_call | solution.py:482
  (15 shorter events, 0.1 us)
Async XLA Ops:
  5.3 29.8 %collective-permute-start.1 = (bf16[65,64,256]{2,1,0:T(8,128)(2,1)S(1)}, bf16[65,64,256]{2,1,0:T(8,128)(2,1)S(1)}, u32[]{:S(2)}, u32[]{:S(2)}) collective-permute-start(bf16[65,64,256]{2,1,0:T(8,128)(2,1)S(1)} %get-tuple-element.25.own), channel_id=1, source_target_pairs={{0,8},{8,16},{16,24},{24,32},{32,40},{40,48},{48,56},{56,64},{64,7... | collective-permute-start | bytes 6389768 | tf_op jit(solution)/shard_map/ppermute | solution.py:509
  7.3 16.0 %collective-permute-start.3 = (bf16[8,2,128,128]{3,2,1,0:T(8,128)(2,1)S(1)}, bf16[8,2,128,128]{3,2,1,0:T(8,128)(2,1)S(1)}, u32[]{:S(2)}, u32[]{:S(2)}) collective-permute-start(bf16[8,2,128,128]{3,2,1,0:T(8,128)(2,1)S(1)} %get-tuple-element.29), channel_id=1, source_target_pairs={{1,65},{2,66},{3,67},{4,68},{5,69},{6,70},{9,73},{10,74},{11,75},{... | collective-permute-start | bytes 1572872 | tf_op jit(solution)/shard_map/ppermute | solution.py:548
  10.6 9.5 %copy-start.3 = (s32[1,8,16,4]{2,3,1,0:T(4,128)S(1)}, s32[1,8,16,4]{2,3,1,0:T(4,128)}, u32[]{:S(2)}) copy-start(s32[1,8,16,4]{2,3,1,0:T(4,128)} %param.12) | copy-start | bytes 6148
  10.6 9.5 %copy-start.4 = (s32[1,8,16,4]{2,3,1,0:T(4,128)S(1)}, s32[1,8,16,4]{2,3,1,0:T(4,128)}, u32[]{:S(2)}) copy-start(s32[1,8,16,4]{2,3,1,0:T(4,128)} %param.13) | copy-start | bytes 6148
  10.7 9.5 %copy-start.5 = (f32[1,8,16,4]{2,3,1,0:T(4,128)S(1)}, f32[1,8,16,4]{2,3,1,0:T(4,128)}, u32[]{:S(2)}) copy-start(f32[1,8,16,4]{2,3,1,0:T(4,128)} %param.15) | copy-start | bytes 6148
  10.7 9.5 %copy-start.7 = (s32[1,8,16]{2,1,0:T(8,128)S(1)}, s32[1,8,16]{2,1,0:T(8,128)}, u32[]{:S(2)}) copy-start(s32[1,8,16]{2,1,0:T(8,128)} %count_ref.1) | copy-start | bytes 1540
  15.3 28.9 %collective-permute-start = (bf16[65,64,256]{2,1,0:T(8,128)(2,1)S(1)}, bf16[65,64,256]{2,1,0:T(8,128)(2,1)S(1)}, u32[]{:S(2)}, u32[]{:S(2)}) collective-permute-start(bf16[65,64,256]{2,1,0:T(8,128)(2,1)S(1)} %get-tuple-element.23.own), channel_id=1, source_target_pairs={{8,0},{16,8},{24,16},{32,24},{40,32},{48,40},{56,48},{64,56},{72,6... | collective-permute-start | bytes 6389768 | tf_op jit(solution)/shard_map/ppermute | solution.py:509
  20.1 11.1 %collective-permute-start.2 = (bf16[8,1,128,128]{3,2,1,0:T(8,128)(2,1)S(1)}, bf16[8,1,128,128]{3,2,1,0:T(8,128)(2,1)S(1)}, u32[]{:S(2)}, u32[]{:S(2)}) collective-permute-start(bf16[8,1,128,128]{3,2,1,0:T(8,128)(2,1)S(1)} %get-tuple-element.26), channel_id=1, source_target_pairs={{0,64},{1,65},{2,66},{3,67},{4,68},{5,69},{6,70},{7,71},{8,72},{9,... | collective-permute-start | bytes 786440 | tf_op jit(solution)/shard_map/ppermute | solution.py:548
  23.3 20.4 %collective-permute-start.5 = (bf16[8,2,128,128]{3,2,1,0:T(8,128)(2,1)S(1)}, bf16[8,2,128,128]{3,2,1,0:T(8,128)(2,1)S(1)}, u32[]{:S(2)}, u32[]{:S(2)}) collective-permute-start(bf16[8,2,128,128]{3,2,1,0:T(8,128)(2,1)S(1)} %collective-permute-done.3), channel_id=1, source_target_pairs={{65,2},{66,1},{67,4},{68,3},{69,6},{70,5},{73,10},{74,9},{75,12},{... | collective-permute-start | bytes 1572872 | tf_op jit(solution)/shard_map/ppermute | solution.py:548
  26.1 9.0 %copy-start = (bf16[256,256]{1,0:T(8,128)(2,1)S(1)}, bf16[256,256]{1,0:T(8,128)(2,1)}, u32[]{:S(2)}) copy-start(bf16[256,256]{1,0:T(8,128)(2,1)} %constant.28.cols_hbm.cols_ref) | copy-start | bytes 393220
  26.1 9.0 %copy-start.1 = (bf16[256,256]{1,0:T(8,128)(2,1)S(1)}, bf16[256,256]{1,0:T(8,128)(2,1)}, u32[]{:S(2)}) copy-start(bf16[256,256]{1,0:T(8,128)(2,1)} %constant.29.back_cols_ref) | copy-start | bytes 393220
  26.2 9.0 %copy-start.2 = (bf16[128,128]{1,0:T(8,128)(2,1)S(1)}, bf16[128,128]{1,0:T(8,128)(2,1)}, u32[]{:S(2)}) copy-start(bf16[128,128]{1,0:T(8,128)(2,1)} %constant.30.back_rows_ref) | copy-start | bytes 98308
  31.2 12.5 %copy-start.6 = (s32[1,8,16]{2,1,0:T(8,128)S(1)}, s32[1,8,16]{2,1,0:T(8,128)}, u32[]{:S(2)}) copy-start(s32[1,8,16]{2,1,0:T(8,128)} %refs_2_.1) | copy-start | bytes 1540
  31.2 21.9 %collective-permute-start.8 = (bf16[8,1,128,128]{3,2,1,0:T(8,128)(2,1)S(1)}, bf16[8,1,128,128]{3,2,1,0:T(8,128)(2,1)S(1)}, u32[]{:S(2)}, u32[]{:S(2)}) collective-permute-start(bf16[8,1,128,128]{3,2,1,0:T(8,128)(2,1)S(1)} %collective-permute-done.2), channel_id=1, source_target_pairs={{64,1},{65,0},{66,3},{67,2},{68,5},{69,4},{70,7},{71,6},{72,9},{73... | collective-permute-start | bytes 786440 | tf_op jit(solution)/shard_map/ppermute | solution.py:548
  38.9 5.4 %collective-permute-start.4 = (f32[2,4,16]{2,1,0:T(4,128)S(1)}, f32[2,4,16]{2,1,0:T(4,128)S(1)}, u32[]{:S(2)}, u32[]{:S(2)}) collective-permute-start(f32[2,4,16]{2,1,0:T(4,128)S(1)} %flow.2), channel_id=1, source_target_pairs={{8,0},{16,8},{24,16},{32,24},{40,32},{48,40},{56,48},{64,56},{72,6... | collective-permute-start | bytes 1544 | tf_op jit(solution)/shard_map/ppermute | solution.py:509
  41.9 11.2 %collective-permute-start.9 = (bf16[8,1,128,128]{3,2,1,0:T(8,128)(2,1)S(1)}, bf16[8,1,128,128]{3,2,1,0:T(8,128)(2,1)S(1)}, u32[]{:S(2)}, u32[]{:S(2)}) collective-permute-start(bf16[8,1,128,128]{3,2,1,0:T(8,128)(2,1)S(1)} %get-tuple-element.40), channel_id=1, source_target_pairs={{0,1},{1,0},{2,3},{3,2},{4,5},{5,4},{6,7},{7,6},{8,9},{9,8},{10,11... | collective-permute-start | bytes 786440 | tf_op jit(solution)/shard_map/ppermute | solution.py:513
  48.0 7.4 %collective-permute-start.6 = (f32[3,8,16]{2,1,0:T(8,128)S(1)}, f32[3,8,16]{2,1,0:T(8,128)S(1)}, u32[]{:S(2)}, u32[]{:S(2)}) collective-permute-start(f32[3,8,16]{2,1,0:T(8,128)S(1)} %pad_maximum_fusion), channel_id=1, source_target_pairs={{0,1},{1,0},{2,3},{3,2},{4,5},{5,4},{6,7},{7,6},{8,9},{9,8},{10,11... | collective-permute-start | bytes 4616 | tf_op jit(solution)/shard_map/ppermute | solution.py:513
  50.1 8.0 %collective-permute-start.7 = (f32[3,8,16]{2,1,0:T(8,128)S(1)}, f32[3,8,16]{2,1,0:T(8,128)S(1)}, u32[]{:S(2)}, u32[]{:S(2)}) collective-permute-start(f32[3,8,16]{2,1,0:T(8,128)S(1)} %pad_maximum_fusion), channel_id=1, source_target_pairs={{1,2},{3,4},{5,6},{2,1},{4,3},{6,5},{9,10},{11,12},{13,14},{10,9},... | collective-permute-start | bytes 4616 | tf_op jit(solution)/shard_map/ppermute | solution.py:538

commit v12 on v11

--- a/solution.py
+++ b/solution.py
@@ -520,15 +520,14 @@
         way = 1 if rest < sections // 4 else -1
         for tile in range(tiles):
             z, x_high = divmod(tile, 2)
-            if far and not 0 <= z + 2 * x_high - 1 < tiles // 2:
-                continue
+            to_z = z + 2 * x_high - 1 if far else z
             ends = [section * tiles + tile]
             for hop in (1, 2):
                 x = (2 * x_high + x_low + hop * way) % 4
-                to_z = z + 2 * x_high - 1 if far and hop == 2 else z
-                ends.append((x % 2 * (sections // 2) + rest) * tiles + 2 * to_z + x // 2)
+                ends.append((x % 2 * (sections // 2) + rest) * tiles + 2 * (to_z if hop == 2 else z) + x // 2)
             pairs[0].append((ends[0], ends[1]))
-            pairs[1].append((ends[1], ends[2]))
+            if 0 <= to_z < tiles // 2:
+                pairs[1].append((ends[1], ends[2]))
     return pairs
 
 

time: 65.4 us -> 63 us (0.963)
  starting transfers between devices: 24.2 us -> 21.6 us
  waiting for transfers between devices: 8.25 us -> 8.96 us
    ppermute x4, starting transfers between devices: 7.63 us -> 5.79 us  [per_device(): hop = lambda x, pairs: lax.ppermute(x, ('sec', 'tile'), pairs)]
    ppermute x3, waiting for transfers between devices: 3.18 us -> 4.42 us  [from_behind(): return lax.ppermute(x, axis, pairs)]
    ppermute x3, starting transfers between devices: 9.69 us -> 8.59 us  [from_behind(): return lax.ppermute(x, axis, pairs)]
  transfers between devices with their start and end apart: 10 -> 10, of which waited for: 5 -> 3; matrix products, arithmetic and copies ran while one was open for 0% -> 0% of each run, Pallas kernels for 31% -> 32%
where the time goes in v12:
time: 63 us; the launch traced here: 62.4 us
  Pallas kernels  30.9 us (49%)
  starting transfers between devices  21.6 us (34%)
  waiting for transfers between devices  8.96 us (14%)
  between operations  0.86 us (1%)
    pallas_call x2, Pallas kernels, forward(): pl.pallas_call(functools.partial(forward_kernel, start, toward_pair), gri...  9.27 us
    ppermute x3, starting transfers between devices, from_behind(): return lax.ppermute(x, axis, pairs)  8.59 us
    pallas_call x2, Pallas kernels, flow_of(): pl.pallas_call(functools.partial(flow_kernel, sign), grid=(ny,), in_specs...  7.41 us
    pallas_call x1, Pallas kernels, warp(): pl.pallas_call(warp_kernel, grid=(ny,), in_specs=[pl.BlockSpec(memory_spa...  6.19 us
    ppermute x4, starting transfers between devices, per_device(): hop = lambda x, pairs: lax.ppermute(x, ('sec', 'tile'), pairs)  5.79 us
    pallas_call x1, Pallas kernels, blend(): pl.pallas_call(blend_kernel, grid=(ny,), in_specs=[pl.BlockSpec(memory_sp...  5 us
    ppermute x3, waiting for transfers between devices, from_behind(): return lax.ppermute(x, axis, pairs)  4.42 us
    ppermute x2, starting transfers between devices, swapped(): lax.ppermute(x, 'tile', [(i, i ^ 1) for i in range(lax.axis_size('tile'))])  3.69 us
  transfers between devices with their start and end apart: 10, of which 3 were waited for; matrix products, arithmetic and copies ran while one was open for 0% of the time, Pallas kernels for 32%

profile of v12, /device:TPU:66, one launch (start us, length us, event | category | flops | bytes accessed | tf_op | source)
XLA Modules:
  0.0 62.4 jit_solution(11213212233663124133)
XLA Ops:
  0.6 0.1 pad_add_fusion.tile_ref
  0.7 4.6 %forward.2 = (bf16[65,64,256]{2,1,0:T(8,128)(2,1)S(1)}, bf16[8,16,128,128]{3,2,1,0:T(8,128)(2,1)S(1)}, bf16[8,2,128,128]{3,2,1,0:T(8,128)(2,1)S(1)}) custom-call(s32[2]{0:T(128)S(1)} %pad_add_fusion.tile_ref, f32[1,8,16,128,128]{4,3,2,1,0:T(8,128)} %x_hbm.3, bf16[128,256]{1,0:T(8,128)(2,1)} %constant.27.rows_hbm, bf16[256,256]{1,0:T(8,128)(2,1)} %constant.28.cols_hbm.cols_ref), custom_call_target="tpu_custom_call" | custom-call | flops 2000000000 | bytes 6291456 | tf_op jit(solution)/shard_map/forward/pallas_call | solution.py:154
  5.3 1.9 %collective-permute-start.1 = (bf16[65,64,256]{2,1,0:T(8,128)(2,1)S(1)}, bf16[65,64,256]{2,1,0:T(8,128)(2,1)S(1)}, u32[]{:S(2)}, u32[]{:S(2)}) collective-permute-start(bf16[65,64,256]{2,1,0:T(8,128)(2,1)S(1)} %get-tuple-element.25.own), channel_id=1, source_target_pairs={{0,8},{8,16},{16,24},{24,32},{32,40},{40,48},{48,56},{56,64},{64,7... | collective-permute-start | bytes 6389768 | tf_op jit(solution)/shard_map/ppermute | solution.py:509
  7.3 1.5 %collective-permute-start.3 = (bf16[8,2,128,128]{3,2,1,0:T(8,128)(2,1)S(1)}, bf16[8,2,128,128]{3,2,1,0:T(8,128)(2,1)S(1)}, u32[]{:S(2)}, u32[]{:S(2)}) collective-permute-start(bf16[8,2,128,128]{3,2,1,0:T(8,128)(2,1)S(1)} %get-tuple-element.29), channel_id=1, source_target_pairs={{0,64},{1,65},{2,66},{3,67},{4,68},{5,69},{6,70},{7,71},{8,72},{9,... | collective-permute-start | bytes 1572872 | tf_op jit(solution)/shard_map/ppermute | solution.py:547
  8.8 4.6 %forward.3 = (bf16[65,64,256]{2,1,0:T(8,128)(2,1)S(1)}, bf16[8,16,128,128]{3,2,1,0:T(8,128)(2,1)S(1)}, bf16[8,1,128,128]{3,2,1,0:T(8,128)(2,1)S(1)}, bf16[8,1,128,128]{3,2,1,0:T(8,128)(2,1)S(1)}) custom-call(s32[2]{0:T(128)S(1)} %pad_add_fusion.tile_ref, f32[1,8,16,128,128]{4,3,2,1,0:T(8,128)} %x_hbm.3, ...), custom_call_target="tpu_custom_call", output_to_operand_aliasing={{1}: (4, {})} | custom-call | flops 2000000000 | bytes 6291456 | tf_op jit(solution)/shard_map/forward/pallas_call | solution.py:154
  13.4 4.7 %collective-permute-start = (bf16[65,64,256]{2,1,0:T(8,128)(2,1)S(1)}, bf16[65,64,256]{2,1,0:T(8,128)(2,1)S(1)}, u32[]{:S(2)}, u32[]{:S(2)}) collective-permute-start(bf16[65,64,256]{2,1,0:T(8,128)(2,1)S(1)} %get-tuple-element.23.own), channel_id=1, source_target_pairs={{8,0},{16,8},{24,16},{32,24},{40,32},{48,40},{56,48},{64,56},{72,6... | collective-permute-start | bytes 6389768 | tf_op jit(solution)/shard_map/ppermute | solution.py:509
  18.2 0.1 collective-permute-start.2
  18.3 0.6 %slots.1 = (s32[8,128]{1,0:T(8,128)S(1)}, f32[8,128]{1,0:T(8,128)S(1)}) custom-call(s32[2]{0:T(128)S(1)} %pad_add_fusion.tile_ref, s32[1,8,4,16]{3,2,1,0:T(4,128)S(1)} %bitcast.4, s32[1,8,4,16]{3,2,1,0:T(4,128)S(1)} %bitcast.5, s32[1,8,16]{2,1,0:T(8,128)S(1)} %copy-done.7, f32[1,8,4,16]{3,2,1,0:T(4,128)S(1)} %bitcast.6), custom_call_target="tpu_custom_call" | custom-call | tf_op jit(solution)/shard_map/slots/pallas_call | solution.py:309
  19.0 2.5 %collective-permute-done.3 = bf16[8,2,128,128]{3,2,1,0:T(8,128)(2,1)S(1)} collective-permute-done((bf16[8,2,128,128]{3,2,1,0:T(8,128)(2,1)S(1)}, bf16[8,2,128,128]{3,2,1,0:T(8,128)(2,1)S(1)}, u32[]{:S(2)}, u32[]{:S(2)}) %collective-permute-start.3) | collective-permute-done | bytes 524320 | tf_op jit(solution)/shard_map/ppermute | solution.py:547
  21.5 2.8 %collective-permute-start.5 = (bf16[8,2,128,128]{3,2,1,0:T(8,128)(2,1)S(1)}, bf16[8,2,128,128]{3,2,1,0:T(8,128)(2,1)S(1)}, u32[]{:S(2)}, u32[]{:S(2)}) collective-permute-start(bf16[8,2,128,128]{3,2,1,0:T(8,128)(2,1)S(1)} %collective-permute-done.3), channel_id=1, source_target_pairs={{65,2},{66,1},{67,4},{68,3},{69,6},{70,5},{73,10},{74,9},{75,12},{... | collective-permute-start | bytes 1572872 | tf_op jit(solution)/shard_map/ppermute | solution.py:547
  24.3 0.0 copy-start
  24.3 0.0 copy-start.1
  24.3 0.0 copy-start.2
  24.3 5.0 %blend.1.padded.refs_5_ = f32[8,16,272,128]{3,2,1,0:T(8,128)S(1)} custom-call(s32[8,128]{1,0:T(8,128)S(1)} %get-tuple-element.27.target_ref, f32[8,128]{1,0:T(8,128)S(1)} %get-tuple-element.28.share_ref, bf16[8,16,128,128]{3,2,1,0:T(8,128)(2,1)S(1)} %get-tuple-element.31.source), custom_call_target="tpu_custom_call" | custom-call | flops 16000000000 | bytes 4194304 | tf_op jit(solution)/shard_map/blend/pallas_call | solution.py:343
  29.4 0.0 copy-start.6
  29.4 0.0 collective-permute-done.2
  29.4 1.4 %collective-permute-start.8 = (bf16[8,1,128,128]{3,2,1,0:T(8,128)(2,1)S(1)}, bf16[8,1,128,128]{3,2,1,0:T(8,128)(2,1)S(1)}, u32[]{:S(2)}, u32[]{:S(2)}) collective-permute-start(bf16[8,1,128,128]{3,2,1,0:T(8,128)(2,1)S(1)} %collective-permute-done.2), channel_id=1, source_target_pairs={{64,1},{65,0},{66,3},{67,2},{68,5},{69,4},{70,7},{71,6},{72,9},{73... | collective-permute-start | bytes 786440 | tf_op jit(solution)/shard_map/ppermute | solution.py:547
  30.7 4.4 %collective-permute-done.1.other = bf16[65,64,256]{2,1,0:T(8,128)(2,1)S(1)} collective-permute-done((bf16[65,64,256]{2,1,0:T(8,128)(2,1)S(1)}, bf16[65,64,256]{2,1,0:T(8,128)(2,1)S(1)}, u32[]{:S(2)}, u32[]{:S(2)}) %collective-permute-start.1) | collective-permute-done | bytes 2129952 | tf_op jit(solution)/shard_map/ppermute | solution.py:509
  35.2 3.7 %flow.2 = f32[2,4,16]{2,1,0:T(4,128)S(1)} custom-call(bf16[65,64,256]{2,1,0:T(8,128)(2,1)S(1)} %get-tuple-element.25.own, bf16[65,64,256]{2,1,0:T(8,128)(2,1)S(1)} %collective-permute-done.1.other, bf16[256,256]{1,0:T(8,128)(2,1)S(1)} %copy-done, bf16[256,256]{1,0:T(8,128)(2,1)S(1)} %copy-done.1, bf16[128,128]{1,0:T(8,128)(2,1)S(1)} %copy-done.2), custom_call_target="tpu_custom_call" | custom-call | tf_op jit(solution)/shard_map/flow/pallas_call | solution.py:258
  38.9 1.9 %collective-permute-start.4 = (f32[2,4,16]{2,1,0:T(4,128)S(1)}, f32[2,4,16]{2,1,0:T(4,128)S(1)}, u32[]{:S(2)}, u32[]{:S(2)}) collective-permute-start(f32[2,4,16]{2,1,0:T(4,128)S(1)} %flow.2), channel_id=1, source_target_pairs={{8,0},{16,8},{24,16},{32,24},{40,32},{48,40},{56,48},{64,56},{72,6... | collective-permute-start | bytes 1544 | tf_op jit(solution)/shard_map/ppermute | solution.py:509
  40.8 2.2 %collective-permute-start.9 = (bf16[8,1,128,128]{3,2,1,0:T(8,128)(2,1)S(1)}, bf16[8,1,128,128]{3,2,1,0:T(8,128)(2,1)S(1)}, u32[]{:S(2)}, u32[]{:S(2)}) collective-permute-start(bf16[8,1,128,128]{3,2,1,0:T(8,128)(2,1)S(1)} %get-tuple-element.40), channel_id=1, source_target_pairs={{0,1},{1,0},{2,3},{3,2},{4,5},{5,4},{6,7},{7,6},{8,9},{9,8},{10,11... | collective-permute-start | bytes 786440 | tf_op jit(solution)/shard_map/ppermute | solution.py:513
  43.0 0.0 collective-permute-done.5.off_ref
  43.0 0.0 collective-permute-done.other
  43.0 0.0 collective-permute-done.4.refs_1_
  43.0 3.7 %flow.3.refs_0_ = f32[2,4,16]{2,1,0:T(4,128)S(1)} custom-call(bf16[65,64,256]{2,1,0:T(8,128)(2,1)S(1)} %get-tuple-element.23.own, bf16[65,64,256]{2,1,0:T(8,128)(2,1)S(1)} %collective-permute-done.other, bf16[256,256]{1,0:T(8,128)(2,1)S(1)} %copy-done, bf16[256,256]{1,0:T(8,128)(2,1)S(1)} %copy-done.1, bf16[128,128]{1,0:T(8,128)(2,1)S(1)} %copy-done.2), custom_call_target="tpu_custom_call" | custom-call | tf_op jit(solution)/shard_map/flow/pallas_call | solution.py:258
  46.8 1.5 %collective-permute-start.6 = (f32[3,8,16]{2,1,0:T(8,128)S(1)}, f32[3,8,16]{2,1,0:T(8,128)S(1)}, u32[]{:S(2)}, u32[]{:S(2)}) collective-permute-start(f32[3,8,16]{2,1,0:T(8,128)S(1)} %pad_maximum_fusion), channel_id=1, source_target_pairs={{0,1},{1,0},{2,3},{3,2},{4,5},{5,4},{6,7},{7,6},{8,9},{9,8},{10,11... | collective-permute-start | bytes 4616 | tf_op jit(solution)/shard_map/ppermute | solution.py:513
  48.3 3.6 %collective-permute-start.7 = (f32[3,8,16]{2,1,0:T(8,128)S(1)}, f32[3,8,16]{2,1,0:T(8,128)S(1)}, u32[]{:S(2)}, u32[]{:S(2)}) collective-permute-start(f32[3,8,16]{2,1,0:T(8,128)S(1)} %pad_maximum_fusion), channel_id=1, source_target_pairs={{1,2},{3,4},{5,6},{2,1},{4,3},{6,5},{9,10},{11,12},{13,14},{10,9},... | collective-permute-start | bytes 4616 | tf_op jit(solution)/shard_map/ppermute | solution.py:537
  51.8 0.0 collective-permute-done.8.first_ref
  51.9 2.3 %edges.1.refs_6_ = f32[8,4,272,128]{3,2,1,0:T(8,128)S(1)} custom-call(s32[2]{0:T(128)S(1)} %pad_add_fusion.tile_ref, s32[8,128]{1,0:T(8,128)S(1)} %get-tuple-element.27.target_ref, f32[8,128]{1,0:T(8,128)S(1)} %get-tuple-element.28.share_ref, bf16[8,1,128,128]{3,2,1,0:T(8,128)(2,1)S(1)} %collective-permute-done.8.first_ref, ...), custom_call_target="tpu_custom_call" | custom-call | flops 5000000 | bytes 4194304 | tf_op jit(solution)/shard_map/edges/pallas_call | solution.py:427
  54.2 0.0 collective-permute-done.6.refs_3_
  54.2 2.0 %collective-permute-done.7.refs_4_ = f32[3,8,16]{2,1,0:T(8,128)S(1)} collective-permute-done((f32[3,8,16]{2,1,0:T(8,128)S(1)}, f32[3,8,16]{2,1,0:T(8,128)S(1)}, u32[]{:S(2)}, u32[]{:S(2)}) %collective-permute-start.7) | collective-permute-done | bytes 1568 | tf_op jit(solution)/shard_map/ppermute | solution.py:537
  56.2 6.2 %warp.1 = (bf16[1,8,16,128,128]{4,3,2,1,0:T(8,128)(2,1)}, f32[1,2,8,16]{3,2,1,0:T(8,128)}) custom-call(s32[2]{0:T(128)S(1)} %pad_add_fusion.tile_ref, f32[2,4,16]{2,1,0:T(4,128)S(1)} %flow.3.refs_0_, f32[2,4,16]{2,1,0:T(4,128)S(1)} %collective-permute-done.4.refs_1_, s32[1,8,16]{2,1,0:T(8,128)S(1)} %copy-done.6, ...), custom_call_target="tpu_custom_call" | custom-call | flops 20000000 | bytes 12582912 | tf_op jit(solution)/shard_map/warp/pallas_call | solution.py:482
  (15 shorter events, 0.1 us)
Async XLA Ops:
  5.3 29.8 %collective-permute-start.1 = (bf16[65,64,256]{2,1,0:T(8,128)(2,1)S(1)}, bf16[65,64,256]{2,1,0:T(8,128)(2,1)S(1)}, u32[]{:S(2)}, u32[]{:S(2)}) collective-permute-start(bf16[65,64,256]{2,1,0:T(8,128)(2,1)S(1)} %get-tuple-element.25.own), channel_id=1, source_target_pairs={{0,8},{8,16},{16,24},{24,32},{32,40},{40,48},{48,56},{56,64},{64,7... | collective-permute-start | bytes 6389768 | tf_op jit(solution)/shard_map/ppermute | solution.py:509
  7.3 14.2 %collective-permute-start.3 = (bf16[8,2,128,128]{3,2,1,0:T(8,128)(2,1)S(1)}, bf16[8,2,128,128]{3,2,1,0:T(8,128)(2,1)S(1)}, u32[]{:S(2)}, u32[]{:S(2)}) collective-permute-start(bf16[8,2,128,128]{3,2,1,0:T(8,128)(2,1)S(1)} %get-tuple-element.29), channel_id=1, source_target_pairs={{0,64},{1,65},{2,66},{3,67},{4,68},{5,69},{6,70},{7,71},{8,72},{9,... | collective-permute-start | bytes 1572872 | tf_op jit(solution)/shard_map/ppermute | solution.py:547
  8.8 9.5 %copy-start.3 = (s32[1,8,16,4]{2,3,1,0:T(4,128)S(1)}, s32[1,8,16,4]{2,3,1,0:T(4,128)}, u32[]{:S(2)}) copy-start(s32[1,8,16,4]{2,3,1,0:T(4,128)} %param.12) | copy-start | bytes 6148
  8.8 9.5 %copy-start.4 = (s32[1,8,16,4]{2,3,1,0:T(4,128)S(1)}, s32[1,8,16,4]{2,3,1,0:T(4,128)}, u32[]{:S(2)}) copy-start(s32[1,8,16,4]{2,3,1,0:T(4,128)} %param.13) | copy-start | bytes 6148
  8.8 9.5 %copy-start.5 = (f32[1,8,16,4]{2,3,1,0:T(4,128)S(1)}, f32[1,8,16,4]{2,3,1,0:T(4,128)}, u32[]{:S(2)}) copy-start(f32[1,8,16,4]{2,3,1,0:T(4,128)} %param.15) | copy-start | bytes 6148
  8.8 9.5 %copy-start.7 = (s32[1,8,16]{2,1,0:T(8,128)S(1)}, s32[1,8,16]{2,1,0:T(8,128)}, u32[]{:S(2)}) copy-start(s32[1,8,16]{2,1,0:T(8,128)} %count_ref.1) | copy-start | bytes 1540
  13.4 29.6 %collective-permute-start = (bf16[65,64,256]{2,1,0:T(8,128)(2,1)S(1)}, bf16[65,64,256]{2,1,0:T(8,128)(2,1)S(1)}, u32[]{:S(2)}, u32[]{:S(2)}) collective-permute-start(bf16[65,64,256]{2,1,0:T(8,128)(2,1)S(1)} %get-tuple-element.23.own), channel_id=1, source_target_pairs={{8,0},{16,8},{24,16},{32,24},{40,32},{48,40},{56,48},{64,56},{72,6... | collective-permute-start | bytes 6389768 | tf_op jit(solution)/shard_map/ppermute | solution.py:509
  18.2 11.2 %collective-permute-start.2 = (bf16[8,1,128,128]{3,2,1,0:T(8,128)(2,1)S(1)}, bf16[8,1,128,128]{3,2,1,0:T(8,128)(2,1)S(1)}, u32[]{:S(2)}, u32[]{:S(2)}) collective-permute-start(bf16[8,1,128,128]{3,2,1,0:T(8,128)(2,1)S(1)} %get-tuple-element.26), channel_id=1, source_target_pairs={{0,64},{1,65},{2,66},{3,67},{4,68},{5,69},{6,70},{7,71},{8,72},{9,... | collective-permute-start | bytes 786440 | tf_op jit(solution)/shard_map/ppermute | solution.py:547
  21.5 21.6 %collective-permute-start.5 = (bf16[8,2,128,128]{3,2,1,0:T(8,128)(2,1)S(1)}, bf16[8,2,128,128]{3,2,1,0:T(8,128)(2,1)S(1)}, u32[]{:S(2)}, u32[]{:S(2)}) collective-permute-start(bf16[8,2,128,128]{3,2,1,0:T(8,128)(2,1)S(1)} %collective-permute-done.3), channel_id=1, source_target_pairs={{65,2},{66,1},{67,4},{68,3},{69,6},{70,5},{73,10},{74,9},{75,12},{... | collective-permute-start | bytes 1572872 | tf_op jit(solution)/shard_map/ppermute | solution.py:547
  24.3 10.8 %copy-start = (bf16[256,256]{1,0:T(8,128)(2,1)S(1)}, bf16[256,256]{1,0:T(8,128)(2,1)}, u32[]{:S(2)}) copy-start(bf16[256,256]{1,0:T(8,128)(2,1)} %constant.28.cols_hbm.cols_ref) | copy-start | bytes 393220
  24.3 10.8 %copy-start.1 = (bf16[256,256]{1,0:T(8,128)(2,1)S(1)}, bf16[256,256]{1,0:T(8,128)(2,1)}, u32[]{:S(2)}) copy-start(bf16[256,256]{1,0:T(8,128)(2,1)} %constant.29.back_cols_ref) | copy-start | bytes 393220
  24.3 10.8 %copy-start.2 = (bf16[128,128]{1,0:T(8,128)(2,1)S(1)}, bf16[128,128]{1,0:T(8,128)(2,1)}, u32[]{:S(2)}) copy-start(bf16[128,128]{1,0:T(8,128)(2,1)} %constant.30.back_rows_ref) | copy-start | bytes 98308
  29.4 13.7 %copy-start.6 = (s32[1,8,16]{2,1,0:T(8,128)S(1)}, s32[1,8,16]{2,1,0:T(8,128)}, u32[]{:S(2)}) copy-start(s32[1,8,16]{2,1,0:T(8,128)} %refs_2_.1) | copy-start | bytes 1540
  29.4 22.5 %collective-permute-start.8 = (bf16[8,1,128,128]{3,2,1,0:T(8,128)(2,1)S(1)}, bf16[8,1,128,128]{3,2,1,0:T(8,128)(2,1)S(1)}, u32[]{:S(2)}, u32[]{:S(2)}) collective-permute-start(bf16[8,1,128,128]{3,2,1,0:T(8,128)(2,1)S(1)} %collective-permute-done.2), channel_id=1, source_target_pairs={{64,1},{65,0},{66,3},{67,2},{68,5},{69,4},{70,7},{71,6},{72,9},{73... | collective-permute-start | bytes 786440 | tf_op jit(solution)/shard_map/ppermute | solution.py:547
  38.9 4.2 %collective-permute-start.4 = (f32[2,4,16]{2,1,0:T(4,128)S(1)}, f32[2,4,16]{2,1,0:T(4,128)S(1)}, u32[]{:S(2)}, u32[]{:S(2)}) collective-permute-start(f32[2,4,16]{2,1,0:T(4,128)S(1)} %flow.2), channel_id=1, source_target_pairs={{8,0},{16,8},{24,16},{32,24},{40,32},{48,40},{56,48},{64,56},{72,6... | collective-permute-start | bytes 1544 | tf_op jit(solution)/shard_map/ppermute | solution.py:509
  40.8 11.0 %collective-permute-start.9 = (bf16[8,1,128,128]{3,2,1,0:T(8,128)(2,1)S(1)}, bf16[8,1,128,128]{3,2,1,0:T(8,128)(2,1)S(1)}, u32[]{:S(2)}, u32[]{:S(2)}) collective-permute-start(bf16[8,1,128,128]{3,2,1,0:T(8,128)(2,1)S(1)} %get-tuple-element.40), channel_id=1, source_target_pairs={{0,1},{1,0},{2,3},{3,2},{4,5},{5,4},{6,7},{7,6},{8,9},{9,8},{10,11... | collective-permute-start | bytes 786440 | tf_op jit(solution)/shard_map/ppermute | solution.py:513
  46.8 7.4 %collective-permute-start.6 = (f32[3,8,16]{2,1,0:T(8,128)S(1)}, f32[3,8,16]{2,1,0:T(8,128)S(1)}, u32[]{:S(2)}, u32[]{:S(2)}) collective-permute-start(f32[3,8,16]{2,1,0:T(8,128)S(1)} %pad_maximum_fusion), channel_id=1, source_target_pairs={{0,1},{1,0},{2,3},{3,2},{4,5},{5,4},{6,7},{7,6},{8,9},{9,8},{10,11... | collective-permute-start | bytes 4616 | tf_op jit(solution)/shard_map/ppermute | solution.py:513
  48.3 8.0 %collective-permute-start.7 = (f32[3,8,16]{2,1,0:T(8,128)S(1)}, f32[3,8,16]{2,1,0:T(8,128)S(1)}, u32[]{:S(2)}, u32[]{:S(2)}) collective-permute-start(f32[3,8,16]{2,1,0:T(8,128)S(1)} %pad_maximum_fusion), channel_id=1, source_target_pairs={{1,2},{3,4},{5,6},{2,1},{4,3},{6,5},{9,10},{11,12},{13,14},{10,9},... | collective-permute-start | bytes 4616 | tf_op jit(solution)/shard_map/ppermute | solution.py:537

commit v13 on v12

--- a/solution.py
+++ b/solution.py
@@ -355,8 +355,9 @@
 def relax(tile_ref, low_ref, high_ref, mask_ref, on_ref, off_ref):
     ny, nx = mask_ref.shape[1:]
     even = tile_ref[0] % 2 == 0
-    left_ref = [jnp.where(even, off_ref[i], on_ref[i]) for i in range(3)]
-    right_ref = [jnp.where(even, on_ref[i], off_ref[i]) for i in range(3)]
+    inner = jnp.where((tile_ref[0] == 0) | (tile_ref[0] == tile_ref[1] - 1), 0.0, 1.0)
+    left_ref = [jnp.where(even, off_ref[i] * inner, on_ref[i]) for i in range(3)]
+    right_ref = [jnp.where(even, on_ref[i], off_ref[i] * inner) for i in range(3)]
     rest = jnp.zeros((ny, N - nx - 2 * STEPS), jnp.float32)
 
     def across(left, own, right):
@@ -534,7 +535,8 @@
 def beyond(x):
     tiles = lax.axis_size("tile")
     pairs = [(i, i + 1) for i in range(1, tiles - 1, 2)]
-    return lax.ppermute(x, "tile", pairs + [(j, i) for i, j in pairs])
+    ends = [(i, i) for i in (0, tiles - 1)]
+    return lax.ppermute(x, "tile", ends + pairs + [(j, i) for i, j in pairs])
 
 
 def per_device(sections, node_mask, box_row, box_shift, box_count, blend_weight):
@@ -562,7 +564,7 @@
 
     flow_high = flow_of(spectra_high, from_last, -1, half, nx, cols, back_cols, back_rows)
     second, flow_high = lax.optimization_barrier((second, flow_high))
-    flow_high = from_behind(flow_high, "sec", -1)
+    flow_high = lax.ppermute(flow_high, "sec", [(i, (i - 1) % count) for i in range(count)])
     second = swapped(second)
     from_next, flow_high, off = lax.optimization_barrier((from_next, flow_high, off))
     flow_low = flow_of(spectra_low, from_next, 1, half, nx, cols, back_cols, back_rows)

time: 63 us -> 64 us (1.016)
  the two profiles are of different devices: /device:TPU:66 before, /device:TPU:32 now
where the time goes in v13:
time: 64 us; the launch traced here: 63.7 us
  Pallas kernels  30.8 us (48%)
  starting transfers between devices  24.3 us (38%)
  waiting for transfers between devices  7.6 us (12%)
  between operations  0.84 us (1%)
    ppermute x4, starting transfers between devices, per_device(): hop = lambda x, pairs: lax.ppermute(x, ('sec', 'tile'), pairs)  10.3 us
    pallas_call x2, Pallas kernels, forward(): pl.pallas_call(functools.partial(forward_kernel, start, toward_pair), gri...  9.27 us
    pallas_call x2, Pallas kernels, flow_of(): pl.pallas_call(functools.partial(flow_kernel, sign), grid=(ny,), in_specs...  7.39 us
    pallas_call x1, Pallas kernels, warp(): pl.pallas_call(warp_kernel, grid=(ny,), in_specs=[pl.BlockSpec(memory_spa...  6.19 us
    pallas_call x1, Pallas kernels, blend(): pl.pallas_call(blend_kernel, grid=(ny,), in_specs=[pl.BlockSpec(memory_sp...  5 us
    ppermute x2, starting transfers between devices, swapped(): lax.ppermute(x, 'tile', [(i, i ^ 1) for i in range(lax.axis_size('tile'))])  4.13 us
    ppermute x1, starting transfers between devices, per_device(): lax.ppermute(flow_high, 'sec', [(i, (i - 1) % count) for i in range(count)])  3.39 us
    ppermute x1, starting transfers between devices, beyond(): return lax.ppermute(x, 'tile', ends + pairs + [(j, i) for i, j in pairs])  3.36 us
  transfers between devices with their start and end apart: 10, of which 3 were waited for; matrix products, arithmetic and copies ran while one was open for 0% of the time, Pallas kernels for 31%

profile of v13, /device:TPU:32, one launch (start us, length us, event | category | flops | bytes accessed | tf_op | source)
XLA Modules:
  0.0 63.7 jit_solution(10861894517739046291)
XLA Ops:
  0.6 0.1 pad_add_fusion.tile_ref
  0.7 4.6 %forward.2 = (bf16[65,64,256]{2,1,0:T(8,128)(2,1)S(1)}, bf16[8,16,128,128]{3,2,1,0:T(8,128)(2,1)S(1)}, bf16[8,2,128,128]{3,2,1,0:T(8,128)(2,1)S(1)}) custom-call(s32[2]{0:T(128)S(1)} %pad_add_fusion.tile_ref, f32[1,8,16,128,128]{4,3,2,1,0:T(8,128)} %x_hbm.3, bf16[128,256]{1,0:T(8,128)(2,1)} %constant.27.rows_hbm, bf16[256,256]{1,0:T(8,128)(2,1)} %constant.28.cols_hbm.cols_ref), custom_call_target="tpu_custom_call" | custom-call | flops 2000000000 | bytes 6291456 | tf_op jit(solution)/shard_map/forward/pallas_call | solution.py:154
  5.3 1.9 %collective-permute-start.1 = (bf16[65,64,256]{2,1,0:T(8,128)(2,1)S(1)}, bf16[65,64,256]{2,1,0:T(8,128)(2,1)S(1)}, u32[]{:S(2)}, u32[]{:S(2)}) collective-permute-start(bf16[65,64,256]{2,1,0:T(8,128)(2,1)S(1)} %get-tuple-element.25.own), channel_id=1, source_target_pairs={{0,8},{8,16},{16,24},{24,32},{32,40},{40,48},{48,56},{56,64},{64,7... | collective-permute-start | bytes 6389768 | tf_op jit(solution)/shard_map/ppermute | solution.py:510
  7.2 1.6 %collective-permute-start.3 = (bf16[8,2,128,128]{3,2,1,0:T(8,128)(2,1)S(1)}, bf16[8,2,128,128]{3,2,1,0:T(8,128)(2,1)S(1)}, u32[]{:S(2)}, u32[]{:S(2)}) collective-permute-start(bf16[8,2,128,128]{3,2,1,0:T(8,128)(2,1)S(1)} %get-tuple-element.29), channel_id=1, source_target_pairs={{0,64},{1,65},{2,66},{3,67},{4,68},{5,69},{6,70},{7,71},{8,72},{9,... | collective-permute-start | bytes 1572872 | tf_op jit(solution)/shard_map/ppermute | solution.py:549
  8.8 4.6 %forward.3 = (bf16[65,64,256]{2,1,0:T(8,128)(2,1)S(1)}, bf16[8,16,128,128]{3,2,1,0:T(8,128)(2,1)S(1)}, bf16[8,1,128,128]{3,2,1,0:T(8,128)(2,1)S(1)}, bf16[8,1,128,128]{3,2,1,0:T(8,128)(2,1)S(1)}) custom-call(s32[2]{0:T(128)S(1)} %pad_add_fusion.tile_ref, f32[1,8,16,128,128]{4,3,2,1,0:T(8,128)} %x_hbm.3, ...), custom_call_target="tpu_custom_call", output_to_operand_aliasing={{1}: (4, {})} | custom-call | flops 2000000000 | bytes 6291456 | tf_op jit(solution)/shard_map/forward/pallas_call | solution.py:154
  13.5 1.3 %collective-permute-start = (bf16[65,64,256]{2,1,0:T(8,128)(2,1)S(1)}, bf16[65,64,256]{2,1,0:T(8,128)(2,1)S(1)}, u32[]{:S(2)}, u32[]{:S(2)}) collective-permute-start(bf16[65,64,256]{2,1,0:T(8,128)(2,1)S(1)} %get-tuple-element.23.own), channel_id=1, source_target_pairs={{8,0},{16,8},{24,16},{32,24},{40,32},{48,40},{56,48},{64,56},{72,6... | collective-permute-start | bytes 6389768 | tf_op jit(solution)/shard_map/ppermute | solution.py:510
  14.8 5.0 %collective-permute-start.2 = (bf16[8,1,128,128]{3,2,1,0:T(8,128)(2,1)S(1)}, bf16[8,1,128,128]{3,2,1,0:T(8,128)(2,1)S(1)}, u32[]{:S(2)}, u32[]{:S(2)}) collective-permute-start(bf16[8,1,128,128]{3,2,1,0:T(8,128)(2,1)S(1)} %get-tuple-element.26), channel_id=1, source_target_pairs={{0,64},{1,65},{2,66},{3,67},{4,68},{5,69},{6,70},{7,71},{8,72},{9,... | collective-permute-start | bytes 786440 | tf_op jit(solution)/shard_map/ppermute | solution.py:549
  19.8 0.6 %slots.1 = (s32[8,128]{1,0:T(8,128)S(1)}, f32[8,128]{1,0:T(8,128)S(1)}) custom-call(s32[2]{0:T(128)S(1)} %pad_add_fusion.tile_ref, s32[1,8,4,16]{3,2,1,0:T(4,128)S(1)} %bitcast.4, s32[1,8,4,16]{3,2,1,0:T(4,128)S(1)} %bitcast.5, s32[1,8,16]{2,1,0:T(8,128)S(1)} %copy-done.7, f32[1,8,4,16]{3,2,1,0:T(4,128)S(1)} %bitcast.6), custom_call_target="tpu_custom_call" | custom-call | tf_op jit(solution)/shard_map/slots/pallas_call | solution.py:309
  20.4 2.2 %collective-permute-done.3 = bf16[8,2,128,128]{3,2,1,0:T(8,128)(2,1)S(1)} collective-permute-done((bf16[8,2,128,128]{3,2,1,0:T(8,128)(2,1)S(1)}, bf16[8,2,128,128]{3,2,1,0:T(8,128)(2,1)S(1)}, u32[]{:S(2)}, u32[]{:S(2)}) %collective-permute-start.3) | collective-permute-done | bytes 524320 | tf_op jit(solution)/shard_map/ppermute | solution.py:549
  22.6 3.6 %collective-permute-start.5 = (bf16[8,2,128,128]{3,2,1,0:T(8,128)(2,1)S(1)}, bf16[8,2,128,128]{3,2,1,0:T(8,128)(2,1)S(1)}, u32[]{:S(2)}, u32[]{:S(2)}) collective-permute-start(bf16[8,2,128,128]{3,2,1,0:T(8,128)(2,1)S(1)} %collective-permute-done.3), channel_id=1, source_target_pairs={{65,2},{66,1},{67,4},{68,3},{69,6},{70,5},{73,10},{74,9},{75,12},{... | collective-permute-start | bytes 1572872 | tf_op jit(solution)/shard_map/ppermute | solution.py:549
  26.2 0.0 copy-start
  26.2 0.0 copy-start.1
  26.2 0.0 copy-start.2
  26.3 5.0 %blend.1.padded.refs_5_ = f32[8,16,272,128]{3,2,1,0:T(8,128)S(1)} custom-call(s32[8,128]{1,0:T(8,128)S(1)} %get-tuple-element.27.target_ref, f32[8,128]{1,0:T(8,128)S(1)} %get-tuple-element.28.share_ref, bf16[8,16,128,128]{3,2,1,0:T(8,128)(2,1)S(1)} %get-tuple-element.31.source), custom_call_target="tpu_custom_call" | custom-call | flops 16000000000 | bytes 4194304 | tf_op jit(solution)/shard_map/blend/pallas_call | solution.py:343
  31.3 0.0 copy-start.6
  31.3 0.0 collective-permute-done.2
  31.3 0.1 collective-permute-start.8
  31.4 0.0 collective-permute-done.1.other
  31.4 3.7 %flow.2 = f32[2,4,16]{2,1,0:T(4,128)S(1)} custom-call(bf16[65,64,256]{2,1,0:T(8,128)(2,1)S(1)} %get-tuple-element.25.own, bf16[65,64,256]{2,1,0:T(8,128)(2,1)S(1)} %collective-permute-done.1.other, bf16[256,256]{1,0:T(8,128)(2,1)S(1)} %copy-done, bf16[256,256]{1,0:T(8,128)(2,1)S(1)} %copy-done.1, bf16[128,128]{1,0:T(8,128)(2,1)S(1)} %copy-done.2), custom_call_target="tpu_custom_call" | custom-call | tf_op jit(solution)/shard_map/flow/pallas_call | solution.py:258
  35.1 3.4 %collective-permute-start.4 = (f32[2,4,16]{2,1,0:T(4,128)S(1)}, f32[2,4,16]{2,1,0:T(4,128)S(1)}, u32[]{:S(2)}, u32[]{:S(2)}) collective-permute-start(f32[2,4,16]{2,1,0:T(4,128)S(1)} %flow.2), channel_id=1, source_target_pairs={{0,120},{8,0},{16,8},{24,16},{32,24},{40,32},{48,40},{56,48},{64,5... | collective-permute-start | bytes 1544 | tf_op jit(solution)/shard_map/ppermute | solution.py:567
  38.5 2.4 %collective-permute-start.9 = (bf16[8,1,128,128]{3,2,1,0:T(8,128)(2,1)S(1)}, bf16[8,1,128,128]{3,2,1,0:T(8,128)(2,1)S(1)}, u32[]{:S(2)}, u32[]{:S(2)}) collective-permute-start(bf16[8,1,128,128]{3,2,1,0:T(8,128)(2,1)S(1)} %get-tuple-element.40), channel_id=1, source_target_pairs={{0,1},{1,0},{2,3},{3,2},{4,5},{5,4},{6,7},{7,6},{8,9},{9,8},{10,11... | collective-permute-start | bytes 786440 | tf_op jit(solution)/shard_map/ppermute | solution.py:514
  41.0 0.0 collective-permute-done.5.off_ref
  41.0 0.0 collective-permute-done.other
  41.0 3.2 %collective-permute-done.4.refs_1_ = f32[2,4,16]{2,1,0:T(4,128)S(1)} collective-permute-done((f32[2,4,16]{2,1,0:T(4,128)S(1)}, f32[2,4,16]{2,1,0:T(4,128)S(1)}, u32[]{:S(2)}, u32[]{:S(2)}) %collective-permute-start.4) | collective-permute-done | bytes 544 | tf_op jit(solution)/shard_map/ppermute | solution.py:567
  44.2 3.7 %flow.3.refs_0_ = f32[2,4,16]{2,1,0:T(4,128)S(1)} custom-call(bf16[65,64,256]{2,1,0:T(8,128)(2,1)S(1)} %get-tuple-element.23.own, bf16[65,64,256]{2,1,0:T(8,128)(2,1)S(1)} %collective-permute-done.other, bf16[256,256]{1,0:T(8,128)(2,1)S(1)} %copy-done, bf16[256,256]{1,0:T(8,128)(2,1)S(1)} %copy-done.1, bf16[128,128]{1,0:T(8,128)(2,1)S(1)} %copy-done.2), custom_call_target="tpu_custom_call" | custom-call | tf_op jit(solution)/shard_map/flow/pallas_call | solution.py:258
  47.9 1.7 %collective-permute-start.6 = (f32[3,8,16]{2,1,0:T(8,128)S(1)}, f32[3,8,16]{2,1,0:T(8,128)S(1)}, u32[]{:S(2)}, u32[]{:S(2)}) collective-permute-start(f32[3,8,16]{2,1,0:T(8,128)S(1)} %pad_maximum_fusion), channel_id=1, source_target_pairs={{0,1},{1,0},{2,3},{3,2},{4,5},{5,4},{6,7},{7,6},{8,9},{9,8},{10,11... | collective-permute-start | bytes 4616 | tf_op jit(solution)/shard_map/ppermute | solution.py:514
  49.6 3.4 %collective-permute-start.7 = (f32[3,8,16]{2,1,0:T(8,128)S(1)}, f32[3,8,16]{2,1,0:T(8,128)S(1)}, u32[]{:S(2)}, u32[]{:S(2)}) collective-permute-start(f32[3,8,16]{2,1,0:T(8,128)S(1)} %pad_maximum_fusion), channel_id=1, source_target_pairs={{0,0},{7,7},{1,2},{3,4},{5,6},{2,1},{4,3},{6,5},{8,8},{15,15},{9,1... | collective-permute-start | bytes 4616 | tf_op jit(solution)/shard_map/ppermute | solution.py:539
  52.9 0.0 collective-permute-done.8.first_ref
  52.9 0.0 collective-permute-done.9.second_ref
  53.0 2.3 %edges.1.refs_6_ = f32[8,4,272,128]{3,2,1,0:T(8,128)S(1)} custom-call(s32[2]{0:T(128)S(1)} %pad_add_fusion.tile_ref, s32[8,128]{1,0:T(8,128)S(1)} %get-tuple-element.27.target_ref, f32[8,128]{1,0:T(8,128)S(1)} %get-tuple-element.28.share_ref, bf16[8,1,128,128]{3,2,1,0:T(8,128)(2,1)S(1)} %collective-permute-done.8.first_ref, ...), custom_call_target="tpu_custom_call" | custom-call | flops 5000000 | bytes 4194304 | tf_op jit(solution)/shard_map/edges/pallas_call | solution.py:428
  55.3 2.2 %collective-permute-done.7.refs_4_ = f32[3,8,16]{2,1,0:T(8,128)S(1)} collective-permute-done((f32[3,8,16]{2,1,0:T(8,128)S(1)}, f32[3,8,16]{2,1,0:T(8,128)S(1)}, u32[]{:S(2)}, u32[]{:S(2)}) %collective-permute-start.7) | collective-permute-done | bytes 1568 | tf_op jit(solution)/shard_map/ppermute | solution.py:539
  57.5 6.2 %warp.1 = (bf16[1,8,16,128,128]{4,3,2,1,0:T(8,128)(2,1)}, f32[1,2,8,16]{3,2,1,0:T(8,128)}) custom-call(s32[2]{0:T(128)S(1)} %pad_add_fusion.tile_ref, f32[2,4,16]{2,1,0:T(4,128)S(1)} %flow.3.refs_0_, f32[2,4,16]{2,1,0:T(4,128)S(1)} %collective-permute-done.4.refs_1_, s32[1,8,16]{2,1,0:T(8,128)S(1)} %copy-done.6, ...), custom_call_target="tpu_custom_call" | custom-call | flops 20000000 | bytes 12582912 | tf_op jit(solution)/shard_map/warp/pallas_call | solution.py:483
  (15 shorter events, 0.1 us)
Async XLA Ops:
  5.3 26.0 %collective-permute-start.1 = (bf16[65,64,256]{2,1,0:T(8,128)(2,1)S(1)}, bf16[65,64,256]{2,1,0:T(8,128)(2,1)S(1)}, u32[]{:S(2)}, u32[]{:S(2)}) collective-permute-start(bf16[65,64,256]{2,1,0:T(8,128)(2,1)S(1)} %get-tuple-element.25.own), channel_id=1, source_target_pairs={{0,8},{8,16},{16,24},{24,32},{32,40},{40,48},{48,56},{56,64},{64,7... | collective-permute-start | bytes 6389768 | tf_op jit(solution)/shard_map/ppermute | solution.py:510
  7.2 15.4 %collective-permute-start.3 = (bf16[8,2,128,128]{3,2,1,0:T(8,128)(2,1)S(1)}, bf16[8,2,128,128]{3,2,1,0:T(8,128)(2,1)S(1)}, u32[]{:S(2)}, u32[]{:S(2)}) collective-permute-start(bf16[8,2,128,128]{3,2,1,0:T(8,128)(2,1)S(1)} %get-tuple-element.29), channel_id=1, source_target_pairs={{0,64},{1,65},{2,66},{3,67},{4,68},{5,69},{6,70},{7,71},{8,72},{9,... | collective-permute-start | bytes 1572872 | tf_op jit(solution)/shard_map/ppermute | solution.py:549
  8.8 10.9 %copy-start.3 = (s32[1,8,16,4]{2,3,1,0:T(4,128)S(1)}, s32[1,8,16,4]{2,3,1,0:T(4,128)}, u32[]{:S(2)}) copy-start(s32[1,8,16,4]{2,3,1,0:T(4,128)} %param.12) | copy-start | bytes 6148
  8.8 10.9 %copy-start.4 = (s32[1,8,16,4]{2,3,1,0:T(4,128)S(1)}, s32[1,8,16,4]{2,3,1,0:T(4,128)}, u32[]{:S(2)}) copy-start(s32[1,8,16,4]{2,3,1,0:T(4,128)} %param.13) | copy-start | bytes 6148
  8.8 10.9 %copy-start.5 = (f32[1,8,16,4]{2,3,1,0:T(4,128)S(1)}, f32[1,8,16,4]{2,3,1,0:T(4,128)}, u32[]{:S(2)}) copy-start(f32[1,8,16,4]{2,3,1,0:T(4,128)} %param.15) | copy-start | bytes 6148
  8.8 10.9 %copy-start.7 = (s32[1,8,16]{2,1,0:T(8,128)S(1)}, s32[1,8,16]{2,1,0:T(8,128)}, u32[]{:S(2)}) copy-start(s32[1,8,16]{2,1,0:T(8,128)} %count_ref.1) | copy-start | bytes 1540
  13.5 27.5 %collective-permute-start = (bf16[65,64,256]{2,1,0:T(8,128)(2,1)S(1)}, bf16[65,64,256]{2,1,0:T(8,128)(2,1)S(1)}, u32[]{:S(2)}, u32[]{:S(2)}) collective-permute-start(bf16[65,64,256]{2,1,0:T(8,128)(2,1)S(1)} %get-tuple-element.23.own), channel_id=1, source_target_pairs={{8,0},{16,8},{24,16},{32,24},{40,32},{48,40},{56,48},{64,56},{72,6... | collective-permute-start | bytes 6389768 | tf_op jit(solution)/shard_map/ppermute | solution.py:510
  14.8 16.5 %collective-permute-start.2 = (bf16[8,1,128,128]{3,2,1,0:T(8,128)(2,1)S(1)}, bf16[8,1,128,128]{3,2,1,0:T(8,128)(2,1)S(1)}, u32[]{:S(2)}, u32[]{:S(2)}) collective-permute-start(bf16[8,1,128,128]{3,2,1,0:T(8,128)(2,1)S(1)} %get-tuple-element.26), channel_id=1, source_target_pairs={{0,64},{1,65},{2,66},{3,67},{4,68},{5,69},{6,70},{7,71},{8,72},{9,... | collective-permute-start | bytes 786440 | tf_op jit(solution)/shard_map/ppermute | solution.py:549
  22.6 18.4 %collective-permute-start.5 = (bf16[8,2,128,128]{3,2,1,0:T(8,128)(2,1)S(1)}, bf16[8,2,128,128]{3,2,1,0:T(8,128)(2,1)S(1)}, u32[]{:S(2)}, u32[]{:S(2)}) collective-permute-start(bf16[8,2,128,128]{3,2,1,0:T(8,128)(2,1)S(1)} %collective-permute-done.3), channel_id=1, source_target_pairs={{65,2},{66,1},{67,4},{68,3},{69,6},{70,5},{73,10},{74,9},{75,12},{... | collective-permute-start | bytes 1572872 | tf_op jit(solution)/shard_map/ppermute | solution.py:549
  26.2 5.2 %copy-start = (bf16[256,256]{1,0:T(8,128)(2,1)S(1)}, bf16[256,256]{1,0:T(8,128)(2,1)}, u32[]{:S(2)}) copy-start(bf16[256,256]{1,0:T(8,128)(2,1)} %constant.28.cols_hbm.cols_ref) | copy-start | bytes 393220
  26.2 5.2 %copy-start.1 = (bf16[256,256]{1,0:T(8,128)(2,1)S(1)}, bf16[256,256]{1,0:T(8,128)(2,1)}, u32[]{:S(2)}) copy-start(bf16[256,256]{1,0:T(8,128)(2,1)} %constant.29.back_cols_ref) | copy-start | bytes 393220
  26.2 5.2 %copy-start.2 = (bf16[128,128]{1,0:T(8,128)(2,1)S(1)}, bf16[128,128]{1,0:T(8,128)(2,1)}, u32[]{:S(2)}) copy-start(bf16[128,128]{1,0:T(8,128)(2,1)} %constant.30.back_rows_ref) | copy-start | bytes 98308
  31.3 9.7 %copy-start.6 = (s32[1,8,16]{2,1,0:T(8,128)S(1)}, s32[1,8,16]{2,1,0:T(8,128)}, u32[]{:S(2)}) copy-start(s32[1,8,16]{2,1,0:T(8,128)} %refs_2_.1) | copy-start | bytes 1540
  31.3 21.7 %collective-permute-start.8 = (bf16[8,1,128,128]{3,2,1,0:T(8,128)(2,1)S(1)}, bf16[8,1,128,128]{3,2,1,0:T(8,128)(2,1)S(1)}, u32[]{:S(2)}, u32[]{:S(2)}) collective-permute-start(bf16[8,1,128,128]{3,2,1,0:T(8,128)(2,1)S(1)} %collective-permute-done.2), channel_id=1, source_target_pairs={{64,1},{65,0},{66,3},{67,2},{68,5},{69,4},{70,7},{71,6},{72,9},{73... | collective-permute-start | bytes 786440 | tf_op jit(solution)/shard_map/ppermute | solution.py:549
  35.1 9.0 %collective-permute-start.4 = (f32[2,4,16]{2,1,0:T(4,128)S(1)}, f32[2,4,16]{2,1,0:T(4,128)S(1)}, u32[]{:S(2)}, u32[]{:S(2)}) collective-permute-start(f32[2,4,16]{2,1,0:T(4,128)S(1)} %flow.2), channel_id=1, source_target_pairs={{0,120},{8,0},{16,8},{24,16},{32,24},{40,32},{48,40},{56,48},{64,5... | collective-permute-start | bytes 1544 | tf_op jit(solution)/shard_map/ppermute | solution.py:567
  38.5 14.4 %collective-permute-start.9 = (bf16[8,1,128,128]{3,2,1,0:T(8,128)(2,1)S(1)}, bf16[8,1,128,128]{3,2,1,0:T(8,128)(2,1)S(1)}, u32[]{:S(2)}, u32[]{:S(2)}) collective-permute-start(bf16[8,1,128,128]{3,2,1,0:T(8,128)(2,1)S(1)} %get-tuple-element.40), channel_id=1, source_target_pairs={{0,1},{1,0},{2,3},{3,2},{4,5},{5,4},{6,7},{7,6},{8,9},{9,8},{10,11... | collective-permute-start | bytes 786440 | tf_op jit(solution)/shard_map/ppermute | solution.py:514
  47.9 7.4 %collective-permute-start.6 = (f32[3,8,16]{2,1,0:T(8,128)S(1)}, f32[3,8,16]{2,1,0:T(8,128)S(1)}, u32[]{:S(2)}, u32[]{:S(2)}) collective-permute-start(f32[3,8,16]{2,1,0:T(8,128)S(1)} %pad_maximum_fusion), channel_id=1, source_target_pairs={{0,1},{1,0},{2,3},{3,2},{4,5},{5,4},{6,7},{7,6},{8,9},{9,8},{10,11... | collective-permute-start | bytes 4616 | tf_op jit(solution)/shard_map/ppermute | solution.py:514
  49.6 8.0 %collective-permute-start.7 = (f32[3,8,16]{2,1,0:T(8,128)S(1)}, f32[3,8,16]{2,1,0:T(8,128)S(1)}, u32[]{:S(2)}, u32[]{:S(2)}) collective-permute-start(f32[3,8,16]{2,1,0:T(8,128)S(1)} %pad_maximum_fusion), channel_id=1, source_target_pairs={{0,0},{7,7},{1,2},{3,4},{5,6},{2,1},{4,3},{6,5},{8,8},{15,15},{9,1... | collective-permute-start | bytes 4616 | tf_op jit(solution)/shard_map/ppermute | solution.py:539

commit v14 on v12

--- a/solution.py
+++ b/solution.py
@@ -125,10 +125,10 @@
     cols = cols_ref[...]
     for pair in range(patches // 2):
         x = jnp.concatenate([x_ref[y, 2 * pair], x_ref[y, 2 * pair + 1]], axis=1)
-        high, low = split(x)
+        high = x.astype(jnp.bfloat16)
         src_ref[start + y, 2 * pair] = high[:, :N]
         src_ref[start + y, 2 * pair + 1] = high[:, N:]
-        both = dot(rows2, jnp.concatenate([high, low], axis=0))
+        both = dot(rows2[:, :N], high)
         for side in range(2):
             here = both[:, side * N : (side + 1) * N]
             p = 2 * pair + side

time: 63 us -> 62.9 us (level)
  no operation moved by 1% of the time
where the time goes in v14:
time: 62.9 us; the launch traced here: 62.3 us
  Pallas kernels  30.5 us (48%)
  starting transfers between devices  21.6 us (34%)
  waiting for transfers between devices  9.1 us (14%)
  between operations  0.86 us (1%)
    pallas_call x2, Pallas kernels, forward(): pl.pallas_call(functools.partial(forward_kernel, start, toward_pair), gri...  8.95 us
    ppermute x3, starting transfers between devices, from_behind(): return lax.ppermute(x, axis, pairs)  8.59 us
    pallas_call x2, Pallas kernels, flow_of(): pl.pallas_call(functools.partial(flow_kernel, sign), grid=(ny,), in_specs...  7.41 us
    pallas_call x1, Pallas kernels, warp(): pl.pallas_call(warp_kernel, grid=(ny,), in_specs=[pl.BlockSpec(memory_spa...  6.19 us
    ppermute x4, starting transfers between devices, per_device(): hop = lambda x, pairs: lax.ppermute(x, ('sec', 'tile'), pairs)  5.8 us
    pallas_call x1, Pallas kernels, blend(): pl.pallas_call(blend_kernel, grid=(ny,), in_specs=[pl.BlockSpec(memory_sp...  5 us
    ppermute x3, waiting for transfers between devices, from_behind(): return lax.ppermute(x, axis, pairs)  4.41 us
    ppermute x2, starting transfers between devices, swapped(): lax.ppermute(x, 'tile', [(i, i ^ 1) for i in range(lax.axis_size('tile'))])  3.69 us
  transfers between devices with their start and end apart: 10, of which 3 were waited for; matrix products, arithmetic and copies ran while one was open for 0% of the time, Pallas kernels for 32%

profile of v14, /device:TPU:66, one launch (start us, length us, event | category | flops | bytes accessed | tf_op | source)
XLA Modules:
  0.0 62.3 jit_solution(12750259763539727294)
XLA Ops:
  0.6 0.1 pad_add_fusion.tile_ref
  0.7 4.5 %forward.2 = (bf16[65,64,256]{2,1,0:T(8,128)(2,1)S(1)}, bf16[8,16,128,128]{3,2,1,0:T(8,128)(2,1)S(1)}, bf16[8,2,128,128]{3,2,1,0:T(8,128)(2,1)S(1)}) custom-call(s32[2]{0:T(128)S(1)} %pad_add_fusion.tile_ref, f32[1,8,16,128,128]{4,3,2,1,0:T(8,128)} %x_hbm.3, bf16[128,256]{1,0:T(8,128)(2,1)} %constant.27.rows_hbm, bf16[256,256]{1,0:T(8,128)(2,1)} %constant.28.cols_hbm.cols_ref), custom_call_target="tpu_custom_call" | custom-call | flops 2000000000 | bytes 6291456 | tf_op jit(solution)/shard_map/forward/pallas_call | solution.py:154
  5.2 1.9 %collective-permute-start.1 = (bf16[65,64,256]{2,1,0:T(8,128)(2,1)S(1)}, bf16[65,64,256]{2,1,0:T(8,128)(2,1)S(1)}, u32[]{:S(2)}, u32[]{:S(2)}) collective-permute-start(bf16[65,64,256]{2,1,0:T(8,128)(2,1)S(1)} %get-tuple-element.25.own), channel_id=1, source_target_pairs={{0,8},{8,16},{16,24},{24,32},{32,40},{40,48},{48,56},{56,64},{64,7... | collective-permute-start | bytes 6389768 | tf_op jit(solution)/shard_map/ppermute | solution.py:509
  7.1 1.5 %collective-permute-start.3 = (bf16[8,2,128,128]{3,2,1,0:T(8,128)(2,1)S(1)}, bf16[8,2,128,128]{3,2,1,0:T(8,128)(2,1)S(1)}, u32[]{:S(2)}, u32[]{:S(2)}) collective-permute-start(bf16[8,2,128,128]{3,2,1,0:T(8,128)(2,1)S(1)} %get-tuple-element.29), channel_id=1, source_target_pairs={{0,64},{1,65},{2,66},{3,67},{4,68},{5,69},{6,70},{7,71},{8,72},{9,... | collective-permute-start | bytes 1572872 | tf_op jit(solution)/shard_map/ppermute | solution.py:547
  8.6 4.5 %forward.3 = (bf16[65,64,256]{2,1,0:T(8,128)(2,1)S(1)}, bf16[8,16,128,128]{3,2,1,0:T(8,128)(2,1)S(1)}, bf16[8,1,128,128]{3,2,1,0:T(8,128)(2,1)S(1)}, bf16[8,1,128,128]{3,2,1,0:T(8,128)(2,1)S(1)}) custom-call(s32[2]{0:T(128)S(1)} %pad_add_fusion.tile_ref, f32[1,8,16,128,128]{4,3,2,1,0:T(8,128)} %x_hbm.3, ...), custom_call_target="tpu_custom_call", output_to_operand_aliasing={{1}: (4, {})} | custom-call | flops 2000000000 | bytes 6291456 | tf_op jit(solution)/shard_map/forward/pallas_call | solution.py:154
  13.1 4.7 %collective-permute-start = (bf16[65,64,256]{2,1,0:T(8,128)(2,1)S(1)}, bf16[65,64,256]{2,1,0:T(8,128)(2,1)S(1)}, u32[]{:S(2)}, u32[]{:S(2)}) collective-permute-start(bf16[65,64,256]{2,1,0:T(8,128)(2,1)S(1)} %get-tuple-element.23.own), channel_id=1, source_target_pairs={{8,0},{16,8},{24,16},{32,24},{40,32},{48,40},{56,48},{64,56},{72,6... | collective-permute-start | bytes 6389768 | tf_op jit(solution)/shard_map/ppermute | solution.py:509
  17.9 0.1 collective-permute-start.2
  18.0 0.6 %slots.1 = (s32[8,128]{1,0:T(8,128)S(1)}, f32[8,128]{1,0:T(8,128)S(1)}) custom-call(s32[2]{0:T(128)S(1)} %pad_add_fusion.tile_ref, s32[1,8,4,16]{3,2,1,0:T(4,128)S(1)} %bitcast.4, s32[1,8,4,16]{3,2,1,0:T(4,128)S(1)} %bitcast.5, s32[1,8,16]{2,1,0:T(8,128)S(1)} %copy-done.7, f32[1,8,4,16]{3,2,1,0:T(4,128)S(1)} %bitcast.6), custom_call_target="tpu_custom_call" | custom-call | tf_op jit(solution)/shard_map/slots/pallas_call | solution.py:309
  18.7 2.7 %collective-permute-done.3 = bf16[8,2,128,128]{3,2,1,0:T(8,128)(2,1)S(1)} collective-permute-done((bf16[8,2,128,128]{3,2,1,0:T(8,128)(2,1)S(1)}, bf16[8,2,128,128]{3,2,1,0:T(8,128)(2,1)S(1)}, u32[]{:S(2)}, u32[]{:S(2)}) %collective-permute-start.3) | collective-permute-done | bytes 524320 | tf_op jit(solution)/shard_map/ppermute | solution.py:547
  21.3 2.8 %collective-permute-start.5 = (bf16[8,2,128,128]{3,2,1,0:T(8,128)(2,1)S(1)}, bf16[8,2,128,128]{3,2,1,0:T(8,128)(2,1)S(1)}, u32[]{:S(2)}, u32[]{:S(2)}) collective-permute-start(bf16[8,2,128,128]{3,2,1,0:T(8,128)(2,1)S(1)} %collective-permute-done.3), channel_id=1, source_target_pairs={{65,2},{66,1},{67,4},{68,3},{69,6},{70,5},{73,10},{74,9},{75,12},{... | collective-permute-start | bytes 1572872 | tf_op jit(solution)/shard_map/ppermute | solution.py:547
  24.2 0.0 copy-start
  24.2 0.0 copy-start.1
  24.2 0.0 copy-start.2
  24.2 5.0 %blend.1.padded.refs_5_ = f32[8,16,272,128]{3,2,1,0:T(8,128)S(1)} custom-call(s32[8,128]{1,0:T(8,128)S(1)} %get-tuple-element.27.target_ref, f32[8,128]{1,0:T(8,128)S(1)} %get-tuple-element.28.share_ref, bf16[8,16,128,128]{3,2,1,0:T(8,128)(2,1)S(1)} %get-tuple-element.31.source), custom_call_target="tpu_custom_call" | custom-call | flops 16000000000 | bytes 4194304 | tf_op jit(solution)/shard_map/blend/pallas_call | solution.py:343
  29.2 0.0 copy-start.6
  29.2 0.0 collective-permute-done.2
  29.2 1.4 %collective-permute-start.8 = (bf16[8,1,128,128]{3,2,1,0:T(8,128)(2,1)S(1)}, bf16[8,1,128,128]{3,2,1,0:T(8,128)(2,1)S(1)}, u32[]{:S(2)}, u32[]{:S(2)}) collective-permute-start(bf16[8,1,128,128]{3,2,1,0:T(8,128)(2,1)S(1)} %collective-permute-done.2), channel_id=1, source_target_pairs={{64,1},{65,0},{66,3},{67,2},{68,5},{69,4},{70,7},{71,6},{72,9},{73... | collective-permute-start | bytes 786440 | tf_op jit(solution)/shard_map/ppermute | solution.py:547
  30.6 4.4 %collective-permute-done.1.other = bf16[65,64,256]{2,1,0:T(8,128)(2,1)S(1)} collective-permute-done((bf16[65,64,256]{2,1,0:T(8,128)(2,1)S(1)}, bf16[65,64,256]{2,1,0:T(8,128)(2,1)S(1)}, u32[]{:S(2)}, u32[]{:S(2)}) %collective-permute-start.1) | collective-permute-done | bytes 2129952 | tf_op jit(solution)/shard_map/ppermute | solution.py:509
  35.0 3.7 %flow.2 = f32[2,4,16]{2,1,0:T(4,128)S(1)} custom-call(bf16[65,64,256]{2,1,0:T(8,128)(2,1)S(1)} %get-tuple-element.25.own, bf16[65,64,256]{2,1,0:T(8,128)(2,1)S(1)} %collective-permute-done.1.other, bf16[256,256]{1,0:T(8,128)(2,1)S(1)} %copy-done, bf16[256,256]{1,0:T(8,128)(2,1)S(1)} %copy-done.1, bf16[128,128]{1,0:T(8,128)(2,1)S(1)} %copy-done.2), custom_call_target="tpu_custom_call" | custom-call | tf_op jit(solution)/shard_map/flow/pallas_call | solution.py:258
  38.7 1.9 %collective-permute-start.4 = (f32[2,4,16]{2,1,0:T(4,128)S(1)}, f32[2,4,16]{2,1,0:T(4,128)S(1)}, u32[]{:S(2)}, u32[]{:S(2)}) collective-permute-start(f32[2,4,16]{2,1,0:T(4,128)S(1)} %flow.2), channel_id=1, source_target_pairs={{8,0},{16,8},{24,16},{32,24},{40,32},{48,40},{56,48},{64,56},{72,6... | collective-permute-start | bytes 1544 | tf_op jit(solution)/shard_map/ppermute | solution.py:509
  40.6 2.2 %collective-permute-start.9 = (bf16[8,1,128,128]{3,2,1,0:T(8,128)(2,1)S(1)}, bf16[8,1,128,128]{3,2,1,0:T(8,128)(2,1)S(1)}, u32[]{:S(2)}, u32[]{:S(2)}) collective-permute-start(bf16[8,1,128,128]{3,2,1,0:T(8,128)(2,1)S(1)} %get-tuple-element.40), channel_id=1, source_target_pairs={{0,1},{1,0},{2,3},{3,2},{4,5},{5,4},{6,7},{7,6},{8,9},{9,8},{10,11... | collective-permute-start | bytes 786440 | tf_op jit(solution)/shard_map/ppermute | solution.py:513
  42.9 0.0 collective-permute-done.5.off_ref
  42.9 0.0 collective-permute-done.other
  42.9 0.0 collective-permute-done.4.refs_1_
  42.9 3.7 %flow.3.refs_0_ = f32[2,4,16]{2,1,0:T(4,128)S(1)} custom-call(bf16[65,64,256]{2,1,0:T(8,128)(2,1)S(1)} %get-tuple-element.23.own, bf16[65,64,256]{2,1,0:T(8,128)(2,1)S(1)} %collective-permute-done.other, bf16[256,256]{1,0:T(8,128)(2,1)S(1)} %copy-done, bf16[256,256]{1,0:T(8,128)(2,1)S(1)} %copy-done.1, bf16[128,128]{1,0:T(8,128)(2,1)S(1)} %copy-done.2), custom_call_target="tpu_custom_call" | custom-call | tf_op jit(solution)/shard_map/flow/pallas_call | solution.py:258
  46.6 1.5 %collective-permute-start.6 = (f32[3,8,16]{2,1,0:T(8,128)S(1)}, f32[3,8,16]{2,1,0:T(8,128)S(1)}, u32[]{:S(2)}, u32[]{:S(2)}) collective-permute-start(f32[3,8,16]{2,1,0:T(8,128)S(1)} %pad_maximum_fusion), channel_id=1, source_target_pairs={{0,1},{1,0},{2,3},{3,2},{4,5},{5,4},{6,7},{7,6},{8,9},{9,8},{10,11... | collective-permute-start | bytes 4616 | tf_op jit(solution)/shard_map/ppermute | solution.py:513
  48.1 3.6 %collective-permute-start.7 = (f32[3,8,16]{2,1,0:T(8,128)S(1)}, f32[3,8,16]{2,1,0:T(8,128)S(1)}, u32[]{:S(2)}, u32[]{:S(2)}) collective-permute-start(f32[3,8,16]{2,1,0:T(8,128)S(1)} %pad_maximum_fusion), channel_id=1, source_target_pairs={{1,2},{3,4},{5,6},{2,1},{4,3},{6,5},{9,10},{11,12},{13,14},{10,9},... | collective-permute-start | bytes 4616 | tf_op jit(solution)/shard_map/ppermute | solution.py:537
  51.7 0.0 collective-permute-done.8.first_ref
  51.7 2.3 %edges.1.refs_6_ = f32[8,4,272,128]{3,2,1,0:T(8,128)S(1)} custom-call(s32[2]{0:T(128)S(1)} %pad_add_fusion.tile_ref, s32[8,128]{1,0:T(8,128)S(1)} %get-tuple-element.27.target_ref, f32[8,128]{1,0:T(8,128)S(1)} %get-tuple-element.28.share_ref, bf16[8,1,128,128]{3,2,1,0:T(8,128)(2,1)S(1)} %collective-permute-done.8.first_ref, ...), custom_call_target="tpu_custom_call" | custom-call | flops 5000000 | bytes 4194304 | tf_op jit(solution)/shard_map/edges/pallas_call | solution.py:427
  54.1 0.0 collective-permute-done.6.refs_3_
  54.1 2.0 %collective-permute-done.7.refs_4_ = f32[3,8,16]{2,1,0:T(8,128)S(1)} collective-permute-done((f32[3,8,16]{2,1,0:T(8,128)S(1)}, f32[3,8,16]{2,1,0:T(8,128)S(1)}, u32[]{:S(2)}, u32[]{:S(2)}) %collective-permute-start.7) | collective-permute-done | bytes 1568 | tf_op jit(solution)/shard_map/ppermute | solution.py:537
  56.1 6.2 %warp.1 = (bf16[1,8,16,128,128]{4,3,2,1,0:T(8,128)(2,1)}, f32[1,2,8,16]{3,2,1,0:T(8,128)}) custom-call(s32[2]{0:T(128)S(1)} %pad_add_fusion.tile_ref, f32[2,4,16]{2,1,0:T(4,128)S(1)} %flow.3.refs_0_, f32[2,4,16]{2,1,0:T(4,128)S(1)} %collective-permute-done.4.refs_1_, s32[1,8,16]{2,1,0:T(8,128)S(1)} %copy-done.6, ...), custom_call_target="tpu_custom_call" | custom-call | flops 20000000 | bytes 12582912 | tf_op jit(solution)/shard_map/warp/pallas_call | solution.py:482
  (15 shorter events, 0.1 us)
Async XLA Ops:
  5.2 29.8 %collective-permute-start.1 = (bf16[65,64,256]{2,1,0:T(8,128)(2,1)S(1)}, bf16[65,64,256]{2,1,0:T(8,128)(2,1)S(1)}, u32[]{:S(2)}, u32[]{:S(2)}) collective-permute-start(bf16[65,64,256]{2,1,0:T(8,128)(2,1)S(1)} %get-tuple-element.25.own), channel_id=1, source_target_pairs={{0,8},{8,16},{16,24},{24,32},{32,40},{40,48},{48,56},{56,64},{64,7... | collective-permute-start | bytes 6389768 | tf_op jit(solution)/shard_map/ppermute | solution.py:509
  7.1 14.2 %collective-permute-start.3 = (bf16[8,2,128,128]{3,2,1,0:T(8,128)(2,1)S(1)}, bf16[8,2,128,128]{3,2,1,0:T(8,128)(2,1)S(1)}, u32[]{:S(2)}, u32[]{:S(2)}) collective-permute-start(bf16[8,2,128,128]{3,2,1,0:T(8,128)(2,1)S(1)} %get-tuple-element.29), channel_id=1, source_target_pairs={{0,64},{1,65},{2,66},{3,67},{4,68},{5,69},{6,70},{7,71},{8,72},{9,... | collective-permute-start | bytes 1572872 | tf_op jit(solution)/shard_map/ppermute | solution.py:547
  8.6 9.3 %copy-start.3 = (s32[1,8,16,4]{2,3,1,0:T(4,128)S(1)}, s32[1,8,16,4]{2,3,1,0:T(4,128)}, u32[]{:S(2)}) copy-start(s32[1,8,16,4]{2,3,1,0:T(4,128)} %param.12) | copy-start | bytes 6148
  8.6 9.3 %copy-start.4 = (s32[1,8,16,4]{2,3,1,0:T(4,128)S(1)}, s32[1,8,16,4]{2,3,1,0:T(4,128)}, u32[]{:S(2)}) copy-start(s32[1,8,16,4]{2,3,1,0:T(4,128)} %param.13) | copy-start | bytes 6148
  8.6 9.4 %copy-start.5 = (f32[1,8,16,4]{2,3,1,0:T(4,128)S(1)}, f32[1,8,16,4]{2,3,1,0:T(4,128)}, u32[]{:S(2)}) copy-start(f32[1,8,16,4]{2,3,1,0:T(4,128)} %param.15) | copy-start | bytes 6148
  8.6 9.4 %copy-start.7 = (s32[1,8,16]{2,1,0:T(8,128)S(1)}, s32[1,8,16]{2,1,0:T(8,128)}, u32[]{:S(2)}) copy-start(s32[1,8,16]{2,1,0:T(8,128)} %count_ref.1) | copy-start | bytes 1540
  13.1 29.7 %collective-permute-start = (bf16[65,64,256]{2,1,0:T(8,128)(2,1)S(1)}, bf16[65,64,256]{2,1,0:T(8,128)(2,1)S(1)}, u32[]{:S(2)}, u32[]{:S(2)}) collective-permute-start(bf16[65,64,256]{2,1,0:T(8,128)(2,1)S(1)} %get-tuple-element.23.own), channel_id=1, source_target_pairs={{8,0},{16,8},{24,16},{32,24},{40,32},{48,40},{56,48},{64,56},{72,6... | collective-permute-start | bytes 6389768 | tf_op jit(solution)/shard_map/ppermute | solution.py:509
  17.9 11.3 %collective-permute-start.2 = (bf16[8,1,128,128]{3,2,1,0:T(8,128)(2,1)S(1)}, bf16[8,1,128,128]{3,2,1,0:T(8,128)(2,1)S(1)}, u32[]{:S(2)}, u32[]{:S(2)}) collective-permute-start(bf16[8,1,128,128]{3,2,1,0:T(8,128)(2,1)S(1)} %get-tuple-element.26), channel_id=1, source_target_pairs={{0,64},{1,65},{2,66},{3,67},{4,68},{5,69},{6,70},{7,71},{8,72},{9,... | collective-permute-start | bytes 786440 | tf_op jit(solution)/shard_map/ppermute | solution.py:547
  21.3 21.6 %collective-permute-start.5 = (bf16[8,2,128,128]{3,2,1,0:T(8,128)(2,1)S(1)}, bf16[8,2,128,128]{3,2,1,0:T(8,128)(2,1)S(1)}, u32[]{:S(2)}, u32[]{:S(2)}) collective-permute-start(bf16[8,2,128,128]{3,2,1,0:T(8,128)(2,1)S(1)} %collective-permute-done.3), channel_id=1, source_target_pairs={{65,2},{66,1},{67,4},{68,3},{69,6},{70,5},{73,10},{74,9},{75,12},{... | collective-permute-start | bytes 1572872 | tf_op jit(solution)/shard_map/ppermute | solution.py:547
  24.2 10.8 %copy-start = (bf16[256,256]{1,0:T(8,128)(2,1)S(1)}, bf16[256,256]{1,0:T(8,128)(2,1)}, u32[]{:S(2)}) copy-start(bf16[256,256]{1,0:T(8,128)(2,1)} %constant.28.cols_hbm.cols_ref) | copy-start | bytes 393220
  24.2 10.8 %copy-start.1 = (bf16[256,256]{1,0:T(8,128)(2,1)S(1)}, bf16[256,256]{1,0:T(8,128)(2,1)}, u32[]{:S(2)}) copy-start(bf16[256,256]{1,0:T(8,128)(2,1)} %constant.29.back_cols_ref) | copy-start | bytes 393220
  24.2 10.8 %copy-start.2 = (bf16[128,128]{1,0:T(8,128)(2,1)S(1)}, bf16[128,128]{1,0:T(8,128)(2,1)}, u32[]{:S(2)}) copy-start(bf16[128,128]{1,0:T(8,128)(2,1)} %constant.30.back_rows_ref) | copy-start | bytes 98308
  29.2 13.7 %copy-start.6 = (s32[1,8,16]{2,1,0:T(8,128)S(1)}, s32[1,8,16]{2,1,0:T(8,128)}, u32[]{:S(2)}) copy-start(s32[1,8,16]{2,1,0:T(8,128)} %refs_2_.1) | copy-start | bytes 1540
  29.2 22.5 %collective-permute-start.8 = (bf16[8,1,128,128]{3,2,1,0:T(8,128)(2,1)S(1)}, bf16[8,1,128,128]{3,2,1,0:T(8,128)(2,1)S(1)}, u32[]{:S(2)}, u32[]{:S(2)}) collective-permute-start(bf16[8,1,128,128]{3,2,1,0:T(8,128)(2,1)S(1)} %collective-permute-done.2), channel_id=1, source_target_pairs={{64,1},{65,0},{66,3},{67,2},{68,5},{69,4},{70,7},{71,6},{72,9},{73... | collective-permute-start | bytes 786440 | tf_op jit(solution)/shard_map/ppermute | solution.py:547
  38.7 4.2 %collective-permute-start.4 = (f32[2,4,16]{2,1,0:T(4,128)S(1)}, f32[2,4,16]{2,1,0:T(4,128)S(1)}, u32[]{:S(2)}, u32[]{:S(2)}) collective-permute-start(f32[2,4,16]{2,1,0:T(4,128)S(1)} %flow.2), channel_id=1, source_target_pairs={{8,0},{16,8},{24,16},{32,24},{40,32},{48,40},{56,48},{64,56},{72,6... | collective-permute-start | bytes 1544 | tf_op jit(solution)/shard_map/ppermute | solution.py:509
  40.6 11.1 %collective-permute-start.9 = (bf16[8,1,128,128]{3,2,1,0:T(8,128)(2,1)S(1)}, bf16[8,1,128,128]{3,2,1,0:T(8,128)(2,1)S(1)}, u32[]{:S(2)}, u32[]{:S(2)}) collective-permute-start(bf16[8,1,128,128]{3,2,1,0:T(8,128)(2,1)S(1)} %get-tuple-element.40), channel_id=1, source_target_pairs={{0,1},{1,0},{2,3},{3,2},{4,5},{5,4},{6,7},{7,6},{8,9},{9,8},{10,11... | collective-permute-start | bytes 786440 | tf_op jit(solution)/shard_map/ppermute | solution.py:513
  46.6 7.4 %collective-permute-start.6 = (f32[3,8,16]{2,1,0:T(8,128)S(1)}, f32[3,8,16]{2,1,0:T(8,128)S(1)}, u32[]{:S(2)}, u32[]{:S(2)}) collective-permute-start(f32[3,8,16]{2,1,0:T(8,128)S(1)} %pad_maximum_fusion), channel_id=1, source_target_pairs={{0,1},{1,0},{2,3},{3,2},{4,5},{5,4},{6,7},{7,6},{8,9},{9,8},{10,11... | collective-permute-start | bytes 4616 | tf_op jit(solution)/shard_map/ppermute | solution.py:513
  48.1 8.0 %collective-permute-start.7 = (f32[3,8,16]{2,1,0:T(8,128)S(1)}, f32[3,8,16]{2,1,0:T(8,128)S(1)}, u32[]{:S(2)}, u32[]{:S(2)}) collective-permute-start(f32[3,8,16]{2,1,0:T(8,128)S(1)} %pad_maximum_fusion), channel_id=1, source_target_pairs={{1,2},{3,4},{5,6},{2,1},{4,3},{6,5},{9,10},{11,12},{13,14},{10,9},... | collective-permute-start | bytes 4616 | tf_op jit(solution)/shard_map/ppermute | solution.py:537
